TPU v7x, 32 devices: a whole 2x2x4 slice. The times are simulated.
32 devices in a mesh: dp: 4 (over y, x), expert: 8 (over z, core).
Axes of the slice: x: 2, y: 2, z: 4, core: 2. Of those that a mesh axis runs over, the one named last changes fastest.
Arguments:
- tokens: bfloat16 [4096, 2048], P(('dp', 'expert')), may hold values from -6 to 6
- cotangent: bfloat16 [4096, 2048], P(('dp', 'expert')), may hold values from -0.3984375 to 0.3984375
- routing: int32 [4096, 8], P(('dp', 'expert')), may hold values from 0 to 7, as said below
- router_route_weights: float32 [4096, 8], P(('dp', 'expert')), may hold values from 0.1 to 1
- route_replica_choice: int32 [4096, 8], P(('dp', 'expert')), may hold values from 0 to 11
- device_expert_table: int32 [8], replicated, may hold values from 0 to 7, as said below
- gate_up_weight: bfloat16 [8, 2048, 1536], P('expert'), may hold values from -1 to 1, as said below
- down_weight: bfloat16 [8, 768, 2048], P('expert'), may hold values from -1 to 1, as said below
- adapter_down_maps: bfloat16 [8, 2048, 128], P('expert'), may hold values from -1 to 1, as said below
- adapter_up_maps: bfloat16 [8, 2, 64, 768], P('expert'), may hold values from -2 to 2, as said below
Outputs:
- mixed: bfloat16 [4096, 2048], P(('dp', 'expert'))
- grad_a: float32 [8, 2048, 128], P('expert')
- grad_b: float32 [8, 2, 64, 768], P('expert')
Inputs may be any that keep to these rules, and one draw needn't show every extreme that they name: `routing`: each row names 8 different experts; experts held by more entries of device_expert_table are chosen more often. `device_expert_table`: every expert of 0 to 7 is held by one to four entries. `gate_up_weight`: entries of device_expert_table that are equal hold equal matrices. `down_weight`: entries of device_expert_table that are equal hold equal matrices. `adapter_down_maps`: entries of device_expert_table that are equal hold equal matrices. `adapter_up_maps`: entries of device_expert_table that are equal hold equal matrices.
All inputs are finite; a program needn't handle non-finite values.
Results may differ from a plain program's by a relative error of at most 0.006.
Values may be sent and summed in bfloat16 or wider, within the bound.
No kernel may reach another device: no remote copies, remote signals or barrier semaphores. Data moves between devices by JAX's collectives and lax.ppermute only.
A program may use at most 128 MiB of HBM per device.

v0:
```python
import jax
import jax.numpy as jnp
from jax import lax
from jax.sharding import PartitionSpec as P

ADAPTER_SCALE = 0.5


def route_rows(routing, route_replica_choice, device_expert_table, capacity):
    slot_total = device_expert_table.shape[0]
    route_total = routing.shape[0] * routing.shape[1]
    expert_flat = routing.reshape(-1)
    holds_mask = (expert_flat[:, None] == device_expert_table[None, :]).astype(jnp.int32)
    copies = jnp.sum(holds_mask, axis=1)
    wanted = route_replica_choice.reshape(-1) % copies
    before = jnp.cumsum(holds_mask, axis=1) - holds_mask
    picked = holds_mask * (before == wanted[:, None]).astype(jnp.int32)
    ahead_of = jnp.cumsum(picked, axis=0) - picked
    position = jnp.sum(picked * ahead_of, axis=1)
    target = jnp.sum(picked * jnp.arange(slot_total, dtype=jnp.int32)[None, :], axis=1)
    kept_mask = position < capacity
    dest_index = jnp.where(kept_mask, target * capacity + position, slot_total * capacity)
    source = jnp.full((slot_total * capacity,), route_total, jnp.int32)
    source = source.at[dest_index].set(jnp.arange(route_total, dtype=jnp.int32), mode="drop")
    return (kept_mask, dest_index, source)


def expert_apply_forward(rows_in, gate_up, down, adapt_a, adapt_b):
    adapter_rank_count = adapt_b.shape[1]
    hidden_width = adapt_b.shape[2]
    reduced_rank_rows = jnp.dot(rows_in, adapt_a, preferred_element_type=jnp.float32).astype(
        jnp.bfloat16
    )
    base_preactivation = jnp.dot(rows_in, gate_up, preferred_element_type=jnp.float32)
    adapter_gate_delta = jnp.dot(
        reduced_rank_rows[:, :adapter_rank_count], adapt_b[0], preferred_element_type=jnp.float32
    )
    adapter_up_delta = jnp.dot(
        reduced_rank_rows[:, adapter_rank_count:], adapt_b[1], preferred_element_type=jnp.float32
    )
    gate_preactivation = base_preactivation[:, :hidden_width] + ADAPTER_SCALE * adapter_gate_delta
    up_preactivation = base_preactivation[:, hidden_width:] + ADAPTER_SCALE * adapter_up_delta
    sigmoid_gate = jax.nn.sigmoid(gate_preactivation)
    active = gate_preactivation * sigmoid_gate
    hidden = (active * up_preactivation).astype(jnp.bfloat16)
    layer_output = jnp.dot(hidden, down, preferred_element_type=jnp.float32).astype(jnp.bfloat16)
    return (
        layer_output,
        (reduced_rank_rows, gate_preactivation, up_preactivation, sigmoid_gate, active),
    )


def expert_backward(rows_in, scaled, down, adapt_b, saved_residuals):
    reduced_rank_rows, gate_preactivation, up_preactivation, sigmoid_gate, active = saved_residuals
    adapter_rank_count = adapt_b.shape[1]
    back_hidden = lax.dot_general(
        scaled, down, (((1,), (1,)), ((), ())), preferred_element_type=jnp.float32
    )
    up_preactivation_gradient = (back_hidden * active).astype(jnp.bfloat16)
    slope = sigmoid_gate * (1.0 + gate_preactivation * (1.0 - sigmoid_gate))
    gate_preactivation_gradient = (back_hidden * up_preactivation * slope).astype(jnp.bfloat16)
    row_dimension_numbers = (((0,), (0,)), ((), ()))
    gate_up_map_gradient = ADAPTER_SCALE * lax.dot_general(
        reduced_rank_rows[:, :adapter_rank_count],
        gate_preactivation_gradient,
        row_dimension_numbers,
        preferred_element_type=jnp.float32,
    )
    up_map_gradient = ADAPTER_SCALE * lax.dot_general(
        reduced_rank_rows[:, adapter_rank_count:],
        up_preactivation_gradient,
        row_dimension_numbers,
        preferred_element_type=jnp.float32,
    )
    cols_dims = (((1,), (1,)), ((), ()))
    gate_reduced_rows = lax.dot_general(
        gate_preactivation_gradient, adapt_b[0], cols_dims, preferred_element_type=jnp.float32
    )
    up_reduced_rows = lax.dot_general(
        up_preactivation_gradient, adapt_b[1], cols_dims, preferred_element_type=jnp.float32
    )
    reduced_gradient = (
        ADAPTER_SCALE * jnp.concatenate([gate_reduced_rows, up_reduced_rows], axis=1)
    ).astype(jnp.bfloat16)
    grad_adapt_a = lax.dot_general(
        rows_in, reduced_gradient, row_dimension_numbers, preferred_element_type=jnp.float32
    )
    return (grad_adapt_a, jnp.stack([gate_up_map_gradient, up_map_gradient]))


def body(
    tokens,
    cotangent,
    routing,
    router_route_weights,
    route_replica_choice,
    device_expert_table,
    gate_up_weight,
    down_weight,
    adapter_down_maps,
    adapter_up_maps,
):
    slot_total = lax.axis_size("expert")
    tok_rows = tokens.shape[0]
    model_feature_width = tokens.shape[1]
    top_routes = routing.shape[1]
    route_total = tok_rows * top_routes
    capacity = route_total // slot_total
    kept_mask, dest_index, source = route_rows(
        routing, route_replica_choice, device_expert_table, capacity
    )
    valid_route_mask = source < route_total
    safe_route = jnp.minimum(source, route_total - 1)
    route_token_index = safe_route // top_routes
    weight_flat = router_route_weights.reshape(-1)
    route_weight_rows = weight_flat[safe_route]
    zero_row = jnp.zeros((), jnp.bfloat16)
    rows_out = jnp.where(valid_route_mask[:, None], tokens[route_token_index], zero_row).reshape(
        slot_total, capacity, model_feature_width
    )
    product = (
        route_weight_rows[:, None] * cotangent[route_token_index].astype(jnp.float32)
    ).astype(jnp.bfloat16)
    scaled_out = jnp.where(valid_route_mask[:, None], product, zero_row).reshape(
        slot_total, capacity, model_feature_width
    )
    rows_in = lax.all_to_all(rows_out, "expert", split_axis=0, concat_axis=0, tiled=True)
    flattened_rows = rows_in.reshape(-1, model_feature_width)
    layer_output, saved_residuals = expert_apply_forward(
        flattened_rows, gate_up_weight[0], down_weight[0], adapter_down_maps[0], adapter_up_maps[0]
    )
    returned = lax.all_to_all(
        layer_output.reshape(slot_total, capacity, model_feature_width),
        "expert",
        split_axis=0,
        concat_axis=0,
        tiled=True,
    )
    returned = returned.reshape(-1, model_feature_width)
    picked_rows = returned[jnp.minimum(dest_index, slot_total * capacity - 1)]
    weighted = jnp.where(
        kept_mask[:, None],
        weight_flat[:, None] * picked_rows.astype(jnp.float32),
        jnp.zeros((), jnp.float32),
    )
    mixed = jnp.sum(weighted.reshape(tok_rows, top_routes, model_feature_width), axis=1).astype(
        jnp.bfloat16
    )
    scaled_input_rows = lax.all_to_all(
        scaled_out, "expert", split_axis=0, concat_axis=0, tiled=True
    )
    grad_adapt_a, grad_adapt_b = expert_backward(
        flattened_rows,
        scaled_input_rows.reshape(-1, model_feature_width),
        down_weight[0],
        adapter_up_maps[0],
        saved_residuals,
    )
    piece_a = grad_adapt_a.reshape(slot_total, -1)
    piece_b = grad_adapt_b.reshape(slot_total, -1)
    expert_total = max(top_routes, slot_total // 2)
    members = (
        jnp.arange(expert_total, dtype=jnp.int32)[:, None] == device_expert_table[None, :]
    ).astype(jnp.float32)
    piece_a, piece_b = lax.psum((piece_a, piece_b), "dp")
    got_a, got_b = (
        lax.all_to_all(piece_a, "expert", split_axis=0, concat_axis=0, tiled=True),
        lax.all_to_all(piece_b, "expert", split_axis=0, concat_axis=0, tiled=True),
    )
    expert_a = jnp.dot(members, got_a, precision=lax.Precision.HIGHEST)
    expert_b = jnp.dot(members, got_b, precision=lax.Precision.HIGHEST)
    back_dims = (((0,), (0,)), ((), ()))
    spread_a = lax.dot_general(members, expert_a, back_dims, precision=lax.Precision.HIGHEST)
    spread_b = lax.dot_general(members, expert_b, back_dims, precision=lax.Precision.HIGHEST)
    summed_a, summed_b = (
        lax.all_to_all(spread_a, "expert", split_axis=0, concat_axis=0, tiled=True),
        lax.all_to_all(spread_b, "expert", split_axis=0, concat_axis=0, tiled=True),
    )
    grad_a = summed_a.reshape(grad_adapt_a.shape)[None]
    grad_b = summed_b.reshape(grad_adapt_b.shape)[None]
    return (mixed, grad_a, grad_b)


def solution(mesh):
    return jax.shard_map(
        body,
        mesh=mesh,
        in_specs=(
            P(("dp", "expert"), None),
            P(("dp", "expert"), None),
            P(("dp", "expert"), None),
            P(("dp", "expert"), None),
            P(("dp", "expert"), None),
            P(),
            P("expert", None, None),
            P("expert", None, None),
            P("expert", None, None),
            P("expert", None, None, None),
        ),
        out_specs=(
            P(("dp", "expert"), None),
            P("expert", None, None),
            P("expert", None, None, None),
        ),
        check_vma=False,
    )
```

profile of v0, /device:TPU:0, one launch (start us, length us, event | category | flops | bytes accessed | tf_op | source)
XLA Modules:
  0.0 546.4 jit_solution(437167952930273436)
XLA Ops:
  15.6 4.3 scatter_custom_fusion
  20.9 9.9 %gather_fusion.3 = bf16[1024,2048]{1,0:T(8,128)(2,1)} fusion(bf16[128,2048]{1,0:T(8,128)(2,1)} %param.11, s32[1024]{0:T(1024)S(1)} %get-tuple-element.10), kind=kCustom, calls=%fused_computation.3 | custom fusion | bytes 8392704 | tf_op jit(solution)/shard_map/gather | solution.py:122
  30.8 9.9 %gather_fusion = bf16[1024,2048]{1,0:T(8,128)(2,1)} fusion(bf16[128,2048]{1,0:T(8,128)(2,1)} %param.10, s32[1024]{0:T(1024)S(1)} %get-tuple-element.10), kind=kCustom, calls=%fused_computation | custom fusion | bytes 8392704 | tf_op jit(solution)/shard_map/gather | solution.py:118
  40.8 4.5 gather_fusion.2
  45.3 6.4 %fusion.5 = (bf16[8,128,2048]{2,1,0:T(8,128)(2,1)}, bf16[8,128,2048]{2,1,0:T(8,128)(2,1)S(1)}) fusion(bf16[8,128,2048]{2,1,0:T(8,128)(2,1)} %bitcast.89, f32[8,128]{1,0:T(8,128)S(1)} %bitcast.97, pred[8,128]{1,0:T(8,128)(4,1)S(1)} %compare_bitcast_fusion, bf16[8,128,2048]{2,1,0:T(8,128)(2,1)} %bitcast.90), kind=kLoop, calls=%fused_computation.14 | loop fusion | flops 10485760 | bytes 16782336 | tf_op jit(solution)/shard_map/jit(_where)/select_n | solution.py:124
  51.7 100.2 %all_to_all.58 = bf16[8,128,2048]{2,1,0:T(8,128)(2,1)} all-to-all(bf16[8,128,2048]{2,1,0:T(8,128)(2,1)S(1)} %get-tuple-element.14), channel_id=1, replica_groups=mesh['dp'=4,'expert'=8] {'expert'}, dimensions={0} | all-to-all | bytes 8388608 | tf_op jit(solution)/shard_map/all_to_all | solution.py:127
  151.9 4.6 all-to-all-start.2
  156.8 4.0 convolution_convert_fusion.1
  160.7 10.4 %fusion.3 = f32[1024,1536]{1,0:T(8,128)} fusion(bf16[1024,2048]{1,0:T(8,128)(2,1)S(1)} %bitcast.88, bf16[1,2048,1536]{2,1,0:T(8,128)(2,1)} %param.16), kind=kOutput, calls=%fused_computation.12 | convolution fusion | flops 6442450944 | bytes 16777216 | tf_op jit(solution)/shard_map/dot_general | solution.py:34
  171.2 79.3 %all-to-all-done.2 = bf16[8,128,2048]{2,1,0:T(8,128)(2,1)} async-done(((bf16[8,128,2048]{2,1,0:T(8,128)(2,1)}), bf16[8,128,2048]{2,1,0:T(8,128)(2,1)}, u32[]{:S(2)}, u32[]{:S(2)}) %all-to-all-start.2) | async-done | bytes 4194336 | tf_op jit(solution)/shard_map/all_to_all | solution.py:149
  250.5 5.4 fusion.6
  264.3 4.5 fusion.21
  268.9 57.9 %all-reduce.3.cloned.1.call-done = (f32[8,1,32768]{2,1,0:T(1,128)}, f32[8,1,12288]{2,1,0:T(1,128)}) async-done(((f32[8,1,32768]{2,1,0:T(1,128)}, f32[8,1,12288]{2,1,0:T(1,128)}), (f32[8,1,32768]{2,1,0:T(1,128)}, f32[8,1,12288]{2,1,0:T(1,128)})) %all-reduce.3.cloned.1.call-update) | async-done | bytes 1441808 | tf_op jit(solution)/shard_map/psum | solution.py:165
  326.8 17.2 %all_to_all.59 = f32[8,1,12288]{2,1,0:T(1,128)S(1)} all-to-all(f32[8,1,12288]{2,1,0:T(1,128)} %get-tuple-element.6), channel_id=1, replica_groups=mesh['dp'=4,'expert'=8] {'expert'}, dimensions={0} | all-to-all | bytes 786432 | tf_op jit(solution)/shard_map/all_to_all | solution.py:168
  344.0 4.2 all-to-all-start.3
  350.3 24.5 %all-to-all-done.3 = f32[8,1,32768]{2,1,0:T(1,128)} async-done(((f32[8,1,32768]{2,1,0:T(1,128)}), f32[8,1,32768]{2,1,0:T(1,128)}, u32[]{:S(2)}, u32[]{:S(2)}) %all-to-all-start.3) | async-done | bytes 1048608 | tf_op jit(solution)/shard_map/all_to_all | solution.py:167
  383.5 7.2 %all-to-all-done.6 = f32[8,1,12288]{2,1,0:T(1,128)S(1)} async-done(((f32[8,1,12288]{2,1,0:T(1,128)}), f32[8,1,12288]{2,1,0:T(1,128)S(1)}, u32[]{:S(2)}, u32[]{:S(2)}) %all-to-all-start.6) | async-done | bytes 393248 | tf_op jit(solution)/shard_map/all_to_all | solution.py:177
  390.7 4.2 all-to-all-start.4
  395.0 7.9 %convolution_convert_fusion = bf16[1024,2048]{1,0:T(8,128)(2,1)} fusion(bf16[1,768,2048]{2,1,0:T(8,128)(2,1)S(1)} %copy-done, f32[1024,768]{1,0:T(8,128)} %copy-done.2, f32[1024,768]{1,0:T(8,128)} %get-tuple-element.15), kind=kOutput, calls=%fused_computation.16 | convolution fusion | flops 3228041216 | bytes 13631488 | tf_op jit(solution)/shard_map/dot_general | solution.py:46
  402.9 18.7 %all-to-all-done.4 = f32[8,1,32768]{2,1,0:T(1,128)} async-done(((f32[8,1,32768]{2,1,0:T(1,128)}), f32[8,1,32768]{2,1,0:T(1,128)}, u32[]{:S(2)}, u32[]{:S(2)}) %all-to-all-start.4) | async-done | bytes 1048608 | tf_op jit(solution)/shard_map/all_to_all | solution.py:176
  421.6 4.5 all-to-all-start.1
  432.3 87.8 %all-to-all-done.1 = bf16[8,128,2048]{2,1,0:T(8,128)(2,1)} async-done(((bf16[8,128,2048]{2,1,0:T(8,128)(2,1)}), bf16[8,128,2048]{2,1,0:T(8,128)(2,1)}, u32[]{:S(2)}, u32[]{:S(2)}) %all-to-all-start.1) | async-done | bytes 4194336 | tf_op jit(solution)/shard_map/all_to_all | solution.py:132
  520.1 11.7 %gather_fusion.1 = bf16[1024,2048]{1,0:T(8,128)(2,1)} fusion(bf16[1024,2048]{1,0:T(8,128)(2,1)} %bitcast.13, s32[1024]{0:T(1024)} %broadcast_clamp_fusion), kind=kCustom, calls=%fused_computation.1 | custom fusion | bytes 8392704 | tf_op jit(solution)/shard_map/gather | solution.py:140
  531.8 5.4 fusion.2
  (61 shorter events, 37.1 us)
Async XLA Ops:
  7.2 243.4 %copy-start = (bf16[1,768,2048]{2,1,0:T(8,128)(2,1)S(1)}, bf16[1,768,2048]{2,1,0:T(8,128)(2,1)}, u32[]{:S(2)}) copy-start(bf16[1,768,2048]{2,1,0:T(8,128)(2,1)} %param.17) | copy-start | bytes 9437188
  20.8 10.0 %copy-start.4 = (f32[128,8]{1,0:T(8,128)}, f32[128,8]{1,0:T(8,128)S(1)}, u32[]{:S(2)}) copy-start(f32[128,8]{1,0:T(8,128)S(1)} %copy.20) | copy-start | bytes 12292
  151.9 98.6 %all-to-all-start.2 = ((bf16[8,128,2048]{2,1,0:T(8,128)(2,1)}), bf16[8,128,2048]{2,1,0:T(8,128)(2,1)}, u32[]{:S(2)}, u32[]{:S(2)}) async-start(bf16[8,128,2048]{2,1,0:T(8,128)(2,1)} %get-tuple-element.13), calls=%async_computation.2 | async-start | bytes 8388608 | tf_op jit(solution)/shard_map/all_to_all | solution.py:149
  156.5 170.3 %all-reduce.3.cloned.1.call-start = ((), (), s32[]{:S(2)}) async-start(), calls=%async_computation.7 | async-start | bytes 2883584 | tf_op jit(solution)/shard_map/psum | solution.py:165
  156.8 4.0 copy-start.1
  250.5 5.4 copy-start.3
  250.5 5.5 copy-start.6
  256.6 3.2 copy-start.2
  268.9 79.3 %copy-start.7 = (s32[8]{0:T(128)S(1)}, s32[8]{0:T(128)}, u32[]{:S(2)}) copy-start(s32[8]{0:T(128)} %param.15) | copy-start | bytes 100
  344.0 30.8 %all-to-all-start.3 = ((f32[8,1,32768]{2,1,0:T(1,128)}), f32[8,1,32768]{2,1,0:T(1,128)}, u32[]{:S(2)}, u32[]{:S(2)}) async-start(f32[8,1,32768]{2,1,0:T(1,128)} %get-tuple-element.5), calls=%async_computation.3 | async-start | bytes 2097152 | tf_op jit(solution)/shard_map/all_to_all | solution.py:167
  374.8 15.9 %all-to-all-start.6 = ((f32[8,1,12288]{2,1,0:T(1,128)}), f32[8,1,12288]{2,1,0:T(1,128)S(1)}, u32[]{:S(2)}, u32[]{:S(2)}) async-start(f32[8,1,12288]{2,1,0:T(1,128)} %copy.25), calls=%async_computation.6 | async-start | bytes 786432 | tf_op jit(solution)/shard_map/all_to_all | solution.py:177
  390.7 30.8 %all-to-all-start.4 = ((f32[8,1,32768]{2,1,0:T(1,128)}), f32[8,1,32768]{2,1,0:T(1,128)}, u32[]{:S(2)}, u32[]{:S(2)}) async-start(f32[8,1,32768]{2,1,0:T(1,128)} %copy.23), calls=%async_computation.4 | async-start | bytes 2097152 | tf_op jit(solution)/shard_map/all_to_all | solution.py:176
  421.6 98.6 %all-to-all-start.1 = ((bf16[8,128,2048]{2,1,0:T(8,128)(2,1)}), bf16[8,128,2048]{2,1,0:T(8,128)(2,1)}, u32[]{:S(2)}, u32[]{:S(2)}) async-start(bf16[8,128,2048]{2,1,0:T(8,128)(2,1)} %bitcast.92), calls=%async_computation.1 | async-start | bytes 8388608 | tf_op jit(solution)/shard_map/all_to_all | solution.py:132
  520.1 11.7 %copy-start.5 = (f32[128,8]{1,0:T(8,128)S(1)}, f32[128,8]{1,0:T(8,128)}, u32[]{:S(2)}) copy-start(f32[128,8]{1,0:T(8,128)} %copy-done.4) | copy-start | bytes 12292
Sparse Core Ops, SparseCore 0:
  269.0 57.7 all-reduce.2
where the time goes:
time: 547 us; the launch traced here: 546 us
  waiting for transfers between devices  275 us (50%)
  blocking collectives  117 us (21%)
  local copies, waits for them, and re-layouts  52.7 us (10%)
  matrix products  43.3 us (8%)
  other arithmetic  21.7 us (4%)
  starting transfers between devices  21.5 us (4%)
  between operations  14.3 us (3%)
    all_to_all x1, blocking collectives, body(): lax.all_to_all(rows_out, 'expert', split_axis=0, concat_axis=0, tiled=True)  100 us
    all_to_all x1, waiting for transfers between devices, body(): lax.all_to_all(layer_output.reshape(slot_total, capacity, model_feature_w...  87.8 us
    all_to_all x1, waiting for transfers between devices, body(): lax.all_to_all(scaled_out, 'expert', split_axis=0, concat_axis=0, tiled=T...  79.3 us
    psum x1, waiting for transfers between devices, body(): piece_a, piece_b = lax.psum((piece_a, piece_b), 'dp')  57.9 us
    all_to_all x1, waiting for transfers between devices, body(): lax.all_to_all(piece_a, 'expert', split_axis=0, concat_axis=0, tiled=True)  24.5 us
    all_to_all x1, waiting for transfers between devices, body(): lax.all_to_all(spread_a, 'expert', split_axis=0, concat_axis=0, tiled=True)  18.7 us
    all_to_all x1, blocking collectives, body(): lax.all_to_all(piece_b, 'expert', split_axis=0, concat_axis=0, tiled=True)  17.2 us
    gather x1, local copies, waits for them, and re-layouts, body(): picked_rows = returned[jnp.minimum(dest_index, slot_total * capacity - 1)]  11.7 us
  transfers between devices with their start and end apart: 6, of which 6 were waited for; matrix products, arithmetic and copies ran while one was open for 7% of the time, Pallas kernels for 0%

commit v1 on v0

--- a/solution.py
+++ b/solution.py
@@ -88,7 +88,7 @@
     return (grad_adapt_a, jnp.stack([gate_up_map_gradient, up_map_gradient]))
 
 
-def body(
+def sparse_body(
     tokens,
     cotangent,
     routing,
@@ -181,6 +181,57 @@
     return (mixed, grad_a, grad_b)
 
 
+def dense_route_weights(routing, weights, choice, table, capacity):
+    holds = (routing[:, :, None] == table[None, None, :]).astype(jnp.int32)
+    copies = jnp.sum(holds, axis=2)
+    wanted = choice % copies
+    before = jnp.cumsum(holds, axis=2) - holds
+    picked = holds * (before == wanted[:, :, None]).astype(jnp.int32)
+    taken = jnp.sum(picked, axis=1)
+    rank = jnp.cumsum(taken, axis=0) - taken
+    route_weight = jnp.sum(picked.astype(jnp.float32) * weights[:, :, None], axis=1)
+    return jnp.where(rank < capacity, route_weight, 0.0)
+
+
+def dense_body(
+    tokens,
+    cotangent,
+    routing,
+    router_route_weights,
+    route_replica_choice,
+    device_expert_table,
+    gate_up_weight,
+    down_weight,
+    adapter_down_maps,
+    adapter_up_maps,
+):
+    slot_total = lax.axis_size("expert")
+    capacity = tokens.shape[0] * routing.shape[1] // slot_total
+    me = lax.axis_index("expert")
+    weight_table = dense_route_weights(
+        routing, router_route_weights, route_replica_choice, device_expert_table, capacity
+    )
+    rows = lax.all_gather(tokens, "expert", tiled=True)
+    weight_all = lax.all_gather(weight_table, "expert", tiled=True)
+    w = lax.dynamic_slice_in_dim(weight_all, me, 1, axis=1)
+    cot = lax.all_gather(cotangent, "expert", tiled=True)
+    layer_output, saved = expert_apply_forward(
+        rows, gate_up_weight[0], down_weight[0], adapter_down_maps[0], adapter_up_maps[0]
+    )
+    part = (w * layer_output.astype(jnp.float32)).astype(jnp.bfloat16)
+    mixed = lax.psum_scatter(part, "expert", scatter_dimension=0, tiled=True)
+    scaled = (w * cot.astype(jnp.float32)).astype(jnp.bfloat16)
+    grad_a, grad_b = expert_backward(rows, scaled, down_weight[0], adapter_up_maps[0], saved)
+    grad_a, grad_b = lax.psum((grad_a, grad_b), "dp")
+    return mixed, grad_a[None], grad_b[None]
+
+
+def body(*arrays):
+    if lax.axis_size("expert") == arrays[2].shape[1]:
+        return dense_body(*arrays)
+    return sparse_body(*arrays)
+
+
 def solution(mesh):
     return jax.shard_map(
         body,

time: 547 us -> 242 us (0.44)
  waiting for transfers between devices: 275 us -> 162 us
  blocking collectives: 117 us -> 18 us
  local copies, waits for them, and re-layouts: 52.7 us -> 7.55 us
  starting transfers between devices: 21.5 us -> 0.16 us
  other arithmetic: 21.7 us -> 4.91 us
  matrix products: 43.3 us -> 35.5 us
    all_to_all x5 -> x0, waiting for transfers between devices: 218 us -> none  [the longest x1 87.8 us: body(): lax.all_to_all(layer_output.reshape(slot_total, capacity, model_feature_w...]
    all_to_all x2 -> x0, blocking collectives: 117 us -> none  [the longest x1 100 us: body(): lax.all_to_all(rows_out, 'expert', split_axis=0, concat_axis=0, tiled=True)]
    all_gather x0 -> x2, waiting for transfers between devices: none -> 60.6 us  [the longest x1 30.5 us: dense_body(): cot = lax.all_gather(cotangent, 'expert', tiled=True)]
    reduce_scatter x0 -> x1, waiting for transfers between devices: none -> 50.3 us  [dense_body(): mixed = lax.psum_scatter(part, 'expert', scatter_dimension=0, tiled=True)]
    gather x4 -> x0, local copies, waits for them, and re-layouts: 36.1 us -> none  [the longest x1 11.7 us: body(): picked_rows = returned[jnp.minimum(dest_index, slot_total * capacity - 1)]]
    all_to_all x5 -> x0, starting transfers between devices: 21.3 us -> none  [the longest x1 4.57 us: body(): lax.all_to_all(scaled_out, 'expert', split_axis=0, concat_axis=0, tiled=T...]
    all_gather x0 -> x1, blocking collectives: none -> 18 us  [dense_body(): weight_all = lax.all_gather(weight_table, 'expert', tiled=True)]
    psum x1, waiting for transfers between devices: 57.9 us -> 49.7 us  [dense_body(): grad_a, grad_b = lax.psum((grad_a, grad_b), 'dp')]
  transfers between devices with their start and end apart: 6 -> 4, of which waited for: 6 -> 4; matrix products, arithmetic and copies ran while one was open for 7% -> 12% of each run, Pallas kernels for 0% -> 0%
where the time goes in v1:
time: 242 us
  waiting for transfers between devices  162 us (67%)
  matrix products  35.5 us (15%)
  blocking collectives  18 us (7%)
  between operations  13.9 us (6%)
  local copies, waits for them, and re-layouts  7.55 us (3%)
  other arithmetic  4.91 us (2%)
    reduce_scatter x1, waiting for transfers between devices, dense_body(): mixed = lax.psum_scatter(part, 'expert', scatter_dimension=0, tiled=True)  50.3 us
    psum x1, waiting for transfers between devices, dense_body(): grad_a, grad_b = lax.psum((grad_a, grad_b), 'dp')  49.7 us
    all_gather x1, waiting for transfers between devices, dense_body(): cot = lax.all_gather(cotangent, 'expert', tiled=True)  30.5 us
    all_gather x1, waiting for transfers between devices, dense_body(): rows = lax.all_gather(tokens, 'expert', tiled=True)  30.1 us
    all_gather x1, blocking collectives, dense_body(): weight_all = lax.all_gather(weight_table, 'expert', tiled=True)  18 us
    dot_general x1, matrix products, expert_apply_forward(): jnp.dot(rows_in, gate_up, preferred_element_type=jnp.float32)  8.78 us
    dot_general x1, matrix products, expert_apply_forward(): jnp.dot(hidden, down, preferred_element_type=jnp.float32)  7.98 us
    unnamed x18, local copies, waits for them, and re-layouts  6.98 us
  transfers between devices with their start and end apart: 4, of which 4 were waited for; matrix products, arithmetic and copies ran while one was open for 12% of the time, Pallas kernels for 0%

profile of v1, /device:TPU:0, one launch (start us, length us, event | category | flops | bytes accessed | tf_op | source)
XLA Modules:
  0.0 242.0 jit_solution(1458352579558795359)
XLA Ops:
  7.2 0.7 all-gather.3.cloned.1.call-update
  8.0 0.7 all-gather.5.cloned.1.call-update
  8.7 0.8 compare_convert_fusion
  9.5 0.8 convert_reduce_fusion
  10.3 0.8 add_select_fusion
  11.1 0.8 fusion.30
  12.0 0.8 fusion.32
  13.1 18.0 %all_gather.9 = f32[1024,8]{1,0:T(8,128)S(1)} all-gather(f32[128,8]{1,0:T(8,128)S(1)} %fusion.28), channel_id=1, replica_groups=mesh['dp'=4,'expert'=8] {'expert'}, dimensions={0}, use_global_device_ids=true | all-gather | bytes 36864 | tf_op jit(solution)/shard_map/all_gather | solution.py:215
  31.4 30.1 %all-gather.3.cloned.1.call-done = bf16[1024,2048]{1,0:T(8,128)(2,1)} async-done(((bf16[128,2048]{1,0:T(8,128)(2,1)}), bf16[1024,2048]{1,0:T(8,128)(2,1)}) %all-gather.3.cloned.1.call-update) | async-done | bytes 4194320 | tf_op jit(solution)/shard_map/all_gather | solution.py:214
  61.5 4.0 %convolution_convert_fusion = bf16[1024,128]{0,1:T(8,128)(2,1)S(1)} fusion(bf16[1024,2048]{1,0:T(8,128)(2,1)} %all-gather.3.cloned.1.call-done, bf16[1,2048,128]{2,1,0:T(8,128)(2,1)} %param.18), kind=kOutput, calls=%fused_computation.16 | convolution fusion | flops 537001984 | bytes 4980736 | tf_op jit(solution)/shard_map/dot_general | solution.py:31
  65.5 8.8 %fusion = f32[1024,1536]{1,0:T(8,128)S(1)} fusion(bf16[1024,2048]{1,0:T(8,128)(2,1)S(1)} %copy-done.1, bf16[1,2048,1536]{2,1,0:T(8,128)(2,1)} %param.16), kind=kOutput, calls=%fused_computation.2 | convolution fusion | flops 6442450944 | bytes 16777216 | tf_op jit(solution)/shard_map/dot_general | solution.py:34
  74.3 2.6 %copy-done.4 = f32[1024,1536]{1,0:T(8,128)} copy-done((f32[1024,1536]{1,0:T(8,128)}, f32[1024,1536]{1,0:T(8,128)S(1)}, u32[]{:S(2)}) %copy-start.4) | copy-done | bytes 6291480
  76.9 2.2 slice_add_fusion
  79.2 30.5 %all-gather.5.cloned.1.call-done = bf16[1024,2048]{1,0:T(8,128)(2,1)} async-done(((bf16[128,2048]{1,0:T(8,128)(2,1)}), bf16[1024,2048]{1,0:T(8,128)(2,1)}) %all-gather.5.cloned.1.call-update) | async-done | bytes 4194320 | tf_op jit(solution)/shard_map/all_gather | solution.py:217
  109.7 5.6 %fusion.2 = f32[1024,768]{1,0:T(8,128)S(1)} fusion(bf16[1024,2048]{1,0:T(8,128)(2,1)} %all-gather.5.cloned.1.call-done, f32[1024]{0:T(1024)S(1)} %dynamic-slice_reduce_fusion, bf16[1,768,2048]{2,1,0:T(8,128)(2,1)S(1)} %copy-done), kind=kOutput, calls=%fused_computation.4 | convolution fusion | flops 3227516928 | bytes 10489856 | tf_op jit(solution)/shard_map/dot_general | solution.py:56
  115.3 3.3 %multiply_convert_fusion.4 = (bf16[1024,768]{1,0:T(8,128)(2,1)S(1)}, bf16[1024,768]{1,0:T(8,128)(2,1)S(1)}, f32[1024,768]{1,0:T(8,128)}) fusion(f32[1024,768]{1,0:T(8,128)S(1)} %fusion.2, f32[1024,768]{1,0:T(8,128)S(1)} %copy-done.3, bf16[1,2,64,768]{3,2,1,0:T(8,128)(2,1)S(1)} %copy-done.7, bf16[1024,128]{0,1:T(8,128)(2,1)S(1)} %convolution_convert_fusion, ...), kind=kOutput, calls=%fused_computation.11 | convolution fusion | flops 112459776 | bytes 15958016 | tf_op jit(solution)/shard_map/dot_general | solution.py:35
  120.0 0.6 fusion.18
  120.6 0.8 maximum_bitcast_fusion
  121.4 1.7 convolution_bitcast_fusion
  123.1 8.0 %multiply_convert_fusion.1 = bf16[1024,2048]{1,0:T(8,128)(2,1)} fusion(f32[1024]{0:T(1024)S(1)} %dynamic-slice_reduce_fusion, bf16[1,768,2048]{2,1,0:T(8,128)(2,1)S(1)} %copy-done, f32[1024,768]{1,0:T(8,128)} %slice_add_fusion, f32[1024,768]{1,0:T(8,128)} %get-tuple-element.18), kind=kOutput, calls=%fused_computation.1 | convolution fusion | flops 3234332672 | bytes 13635584 | tf_op jit(solution)/shard_map/dot_general | solution.py:46
  131.1 49.7 %all-reduce.3.cloned.1.call-done = (f32[1,2048,128]{1,2,0:T(8,128)}, f32[1,2,64,768]{3,2,1,0:T(8,128)}) async-done(((f32[1,2048,128]{1,2,0:T(8,128)}, f32[1,2,64,768]{3,2,1,0:T(8,128)}), (f32[1,2048,128]{1,2,0:T(8,128)}, f32[1,2,64,768]{3,2,1,0:T(8,128)})) %all-reduce.3.cloned.1.call-update) | async-done | bytes 1441808 | tf_op jit(solution)/shard_map/psum | solution.py:225
  180.9 2.5 %copy.24 = f32[1,2048,128]{2,1,0:T(8,128)} copy(f32[1,2048,128]{1,2,0:T(8,128)} %get-tuple-element.12) | data formatting | bytes 2097152
  183.4 50.3 %reduce-scatter.2.cloned.1.call-done = bf16[128,2048]{1,0:T(8,128)(2,1)} async-done(((bf16[1024,2048]{1,0:T(8,128)(2,1)}), bf16[128,2048]{1,0:T(8,128)(2,1)}) %reduce-scatter.2.cloned.1.call-update) | async-done | bytes 524304 | tf_op jit(solution)/shard_map/reduce_scatter | solution.py:222
  233.7 1.8 copy.27
  (30 shorter events, 2.4 us)
Async XLA Ops:
  7.2 102.5 %copy-start = (bf16[1,768,2048]{2,1,0:T(8,128)(2,1)S(1)}, bf16[1,768,2048]{2,1,0:T(8,128)(2,1)}, u32[]{:S(2)}) copy-start(bf16[1,768,2048]{2,1,0:T(8,128)(2,1)} %param.17) | copy-start | bytes 9437188
  7.2 54.3 %all-gather.3.cloned.1.call-start = ((), (), s32[]{:S(2)}) async-start(), calls=%async_computation.1 | async-start | bytes 4718592 | tf_op jit(solution)/shard_map/all_gather | solution.py:214
  7.9 101.8 %all-gather.5.cloned.1.call-start = ((), (), s32[]{:S(2)}) async-start(), calls=%async_computation.3 | async-start | bytes 4718592 | tf_op jit(solution)/shard_map/all_gather | solution.py:217
  8.7 172.2 %all-reduce.3.cloned.1.call-start = ((), (), s32[]{:S(2)}) async-start(), calls=%async_computation.4 | async-start | bytes 2883584 | tf_op jit(solution)/shard_map/psum | solution.py:225
  61.5 4.0 %copy-start.1 = (bf16[1024,2048]{1,0:T(8,128)(2,1)S(1)}, bf16[1024,2048]{1,0:T(8,128)(2,1)}, u32[]{:S(2)}) copy-start(bf16[1024,2048]{1,0:T(8,128)(2,1)} %all-gather.3.cloned.1.call-done) | copy-start | bytes 12582916
  65.5 11.5 %copy-start.6 = (bf16[1,2,64,768]{3,2,1,0:T(8,128)(2,1)S(1)}, bf16[1,2,64,768]{3,2,1,0:T(8,128)(2,1)}, u32[]{:S(2)}) copy-start(bf16[1,2,64,768]{3,2,1,0:T(8,128)(2,1)} %param.19) | copy-start | bytes 589828
  74.3 2.7 %copy-start.4 = (f32[1024,1536]{1,0:T(8,128)}, f32[1024,1536]{1,0:T(8,128)S(1)}, u32[]{:S(2)}) copy-start(f32[1024,1536]{1,0:T(8,128)S(1)} %fusion) | copy-start | bytes 18874372
  109.7 5.6 %copy-start.3 = (f32[1024,768]{1,0:T(8,128)S(1)}, f32[1024,768]{1,0:T(8,128)}, u32[]{:S(2)}) copy-start(f32[1024,768]{1,0:T(8,128)} %slice_add_fusion) | copy-start | bytes 9437188
  109.7 5.6 %copy-start.5 = (f32[1024,1536]{1,0:T(8,128)S(1)}, f32[1024,1536]{1,0:T(8,128)}, u32[]{:S(2)}) copy-start(f32[1024,1536]{1,0:T(8,128)} %copy-done.4) | copy-start | bytes 18874372
  109.7 5.6 %copy-start.7 = (bf16[1,2,64,768]{3,2,1,0:T(8,128)(2,1)S(1)}, bf16[1,2,64,768]{3,2,1,0:T(8,128)(2,1)}, u32[]{:S(2)}) copy-start(bf16[1,2,64,768]{3,2,1,0:T(8,128)(2,1)} %param.19) | copy-start | bytes 589828
  119.0 2.4 copy-start.2
  123.1 110.6 %reduce-scatter.2.cloned.1.call-start = ((), (), s32[]{:S(2)}) async-start(), calls=%async_computation.2 | async-start | bytes 4718592 | tf_op jit(solution)/shard_map/reduce_scatter | solution.py:222
Sparse Core Ops, SparseCore 0:
  9.6 51.8 all-gather.2
  63.1 46.5 all-gather.4
  123.2 57.6 all-reduce.2
  183.7 49.9 reduce-scatter.1

commit v2 on v1

--- a/solution.py
+++ b/solution.py
@@ -193,6 +193,87 @@
     return jnp.where(rank < capacity, route_weight, 0.0)
 
 
+def z_pairs(*moves):
+    return [(2 * a + core, 2 * b + core) for a, b in moves for core in (0, 1)]
+
+
+ALL_SWAP = z_pairs((0, 1), (1, 0), (2, 3), (3, 2))
+MID_SWAP = z_pairs((1, 2), (2, 1))
+OUTWARD = z_pairs((1, 0), (2, 3))
+INWARD = z_pairs((0, 1), (3, 2))
+SIBLING = [(e, e ^ 1) for e in range(8)]
+
+
+def send(array, pairs):
+    return lax.ppermute(array, "expert", pairs)
+
+
+def line_gather(block, inner):
+    swap_first = send(block, ALL_SWAP)
+    mid_first = send(block, MID_SWAP)
+    out_second = send(mid_first, OUTWARD)
+    mid_second = send(swap_first, MID_SWAP)
+    out_third = send(mid_second, OUTWARD)
+    stages = [
+        block,
+        swap_first,
+        jnp.where(inner, mid_first, out_second),
+        jnp.where(inner, mid_second, out_third),
+    ]
+    return [jnp.concatenate([mine, send(mine, SIBLING)]) for mine in stages]
+
+
+def add_rounded(*terms):
+    total = terms[0].astype(jnp.float32)
+    for term in terms[1:]:
+        total = total + term.astype(jnp.float32)
+    return total.astype(jnp.bfloat16)
+
+
+def line_combine(parts, tok_rows):
+    own, first, second, third = [
+        add_rounded(part[:tok_rows], send(part[tok_rows:], SIBLING)) for part in parts
+    ]
+    third_in = send(third, INWARD)
+    third_mid = send(add_rounded(third, third_in), MID_SWAP)
+    second_in = send(second, INWARD)
+    second_mid = send(add_rounded(second, second_in), MID_SWAP)
+    first_swap = send(add_rounded(first, third_mid), ALL_SWAP)
+    return add_rounded(own, first_swap, second_mid)
+
+
+def stage_weights(weight_table, inner, me):
+    for bit in (1, 2, 4):
+        other = send(weight_table, [(e, e ^ bit) for e in range(8)])
+        weight_table = jnp.concatenate([weight_table, other])
+    tok_rows = weight_table.shape[1]
+    table = weight_table.reshape(8, 8, tok_rows)
+    mine = lax.dynamic_index_in_dim(table, me, axis=1, keepdims=False)
+    near = mine.reshape(4, 2 * tok_rows)
+    return [
+        near[0],
+        near[1],
+        jnp.where(inner, near[3], near[2]),
+        jnp.where(inner, near[2], near[3]),
+    ]
+
+
+def swap_sum(array, bit):
+    rounded = lax.reduce_precision(array, 8, 7)
+    pairs = [(d, d ^ bit) for d in range(4)]
+    other = lax.ppermute(rounded.astype(jnp.bfloat16), "dp", pairs)
+    return rounded + other.astype(jnp.float32)
+
+
+def group_sum(grad_a, grad_b):
+    rows, rank = grad_a.shape
+    low_rows = (grad_a.size + grad_b.size) // 2 // rank // 16 * 16
+    x_first = swap_sum(swap_sum(grad_a[:low_rows], 1), 2)
+    y_first = swap_sum(swap_sum(grad_a[low_rows:], 2), 1)
+    sum_b = swap_sum(swap_sum(grad_b, 2), 1)
+    return jnp.concatenate([x_first, y_first]), sum_b
+
+
 def dense_body(
     tokens,
     cotangent,
@@ -206,28 +287,36 @@
     adapter_up_maps,
 ):
     slot_total = lax.axis_size("expert")
-    capacity = tokens.shape[0] * routing.shape[1] // slot_total
+    tok_rows = tokens.shape[0]
+    capacity = tok_rows * routing.shape[1] // slot_total
     me = lax.axis_index("expert")
+    chip = me // 2
+    inner = (chip == 1) | (chip == 2)
     weight_table = dense_route_weights(
         routing, router_route_weights, route_replica_choice, device_expert_table, capacity
     )
-    rows = lax.all_gather(tokens, "expert", tiled=True)
-    weight_all = lax.all_gather(weight_table, "expert", tiled=True)
-    w = lax.dynamic_slice_in_dim(weight_all, me, 1, axis=1)
-    cot = lax.all_gather(cotangent, "expert", tiled=True)
-    layer_output, saved = expert_apply_forward(
-        rows, gate_up_weight[0], down_weight[0], adapter_down_maps[0], adapter_up_maps[0]
-    )
-    part = (w * layer_output.astype(jnp.float32)).astype(jnp.bfloat16)
-    mixed = lax.psum_scatter(part, "expert", scatter_dimension=0, tiled=True)
-    scaled = (w * cot.astype(jnp.float32)).astype(jnp.bfloat16)
-    grad_a, grad_b = expert_backward(rows, scaled, down_weight[0], adapter_up_maps[0], saved)
-    grad_a, grad_b = lax.psum((grad_a, grad_b), "dp")
+    weights = [w[:, None] for w in stage_weights(weight_table.T, inner, me)]
+    row_stages = line_gather(tokens, inner)
+    cot_stages = line_gather(cotangent, inner)
+    parts, saved = [], []
+    for rows, w in zip(row_stages, weights):
+        layer_output, kept = expert_apply_forward(
+            rows, gate_up_weight[0], down_weight[0], adapter_down_maps[0], adapter_up_maps[0]
+        )
+        parts.append((w * layer_output.astype(jnp.float32)).astype(jnp.bfloat16))
+        saved.append(kept)
+    mixed = line_combine(parts, tok_rows)
+    grad_a, grad_b = 0.0, 0.0
+    for rows, cot, w, kept in zip(row_stages, cot_stages, weights, saved):
+        scaled = (w * cot.astype(jnp.float32)).astype(jnp.bfloat16)
+        more_a, more_b = expert_backward(rows, scaled, down_weight[0], adapter_up_maps[0], kept)
+        grad_a, grad_b = grad_a + more_a, grad_b + more_b
+    grad_a, grad_b = group_sum(grad_a, grad_b)
     return mixed, grad_a[None], grad_b[None]
 
 
 def body(*arrays):
-    if lax.axis_size("expert") == arrays[2].shape[1]:
+    if (lax.axis_size("dp"), lax.axis_size("expert"), arrays[2].shape[1]) == (4, 8, 8):
         return dense_body(*arrays)
     return sparse_body(*arrays)
 

time: 242 us -> 180 us (0.74)
  waiting for transfers between devices: 162 us -> 79.5 us
  starting transfers between devices: 0.16 us -> 52.4 us
  blocking collectives: 18 us -> 0 us
  between operations: 13.9 us -> 1.43 us
  other arithmetic: 4.91 us -> 8.92 us
  matrix products: 35.5 us -> 32.2 us
    ppermute x0 -> x36, waiting for transfers between devices: none -> 79.5 us  [the longest x30 66.4 us: send(): return lax.ppermute(array, 'expert', pairs)]
    all_gather x2 -> x0, waiting for transfers between devices: 60.6 us -> none  [the longest x1 30.5 us: dense_body(): cot = lax.all_gather(cotangent, 'expert', tiled=True)]
    ppermute x0 -> x36, starting transfers between devices: none -> 52.4 us  [the longest x30 44.2 us: send(): return lax.ppermute(array, 'expert', pairs)]
    reduce_scatter x1 -> x0, waiting for transfers between devices: 50.3 us -> none  [dense_body(): mixed = lax.psum_scatter(part, 'expert', scatter_dimension=0, tiled=True)]
    psum x1 -> x0, waiting for transfers between devices: 49.7 us -> none  [dense_body(): grad_a, grad_b = lax.psum((grad_a, grad_b), 'dp')]
    all_gather x1 -> x0, blocking collectives: 18 us -> none  [dense_body(): weight_all = lax.all_gather(weight_table, 'expert', tiled=True)]
    unnamed x18 -> x16, local copies, waits for them, and re-layouts: 6.98 us -> 3.02 us
    dot_general x1 -> x4, matrix products: 7.98 us -> 4.22 us  [expert_apply_forward(): jnp.dot(hidden, down, preferred_element_type=jnp.float32)]
  transfers between devices with their start and end apart: 4 -> 36, of which waited for: 4 -> 11; matrix products, arithmetic and copies ran while one was open for 12% -> 23% of each run, Pallas kernels for 0% -> 0%
where the time goes in v2:
time: 180 us
  waiting for transfers between devices  79.5 us (44%)
  starting transfers between devices  52.4 us (29%)
  matrix products  32.2 us (18%)
  other arithmetic  8.92 us (5%)
  local copies, waits for them, and re-layouts  5.26 us (3%)
    ppermute x30, waiting for transfers between devices, send(): return lax.ppermute(array, 'expert', pairs)  66.4 us
    ppermute x30, starting transfers between devices, send(): return lax.ppermute(array, 'expert', pairs)  44.2 us
    ppermute x6, waiting for transfers between devices, swap_sum(): other = lax.ppermute(rounded.astype(jnp.bfloat16), 'dp', pairs)  13.1 us
    dot_general x4, matrix products, expert_apply_forward(): jnp.dot(rows_in, gate_up, preferred_element_type=jnp.float32)  10.3 us
    ppermute x6, starting transfers between devices, swap_sum(): other = lax.ppermute(rounded.astype(jnp.bfloat16), 'dp', pairs)  8.17 us
    dot_general x4, matrix products, expert_backward(): lax.dot_general(scaled, down, (((1,), (1,)), ((), ())), preferred_element...  6.43 us
    dot_general x4, matrix products, expert_apply_forward(): jnp.dot(hidden, down, preferred_element_type=jnp.float32)  4.22 us
  transfers between devices with their start and end apart: 36, of which 11 were waited for; matrix products, arithmetic and copies ran while one was open for 23% of the time, Pallas kernels for 0%

profile of v2, /device:TPU:0, one launch (start us, length us, event | category | flops | bytes accessed | tf_op | source)
XLA Modules:
  0.0 179.7 jit_solution(7394963903229473034)
XLA Ops:
  6.5 2.9 %collective-permute-start.1 = (f32[16,128]{1,0:T(8,128)S(1)}, f32[16,128]{1,0:T(8,128)S(1)}, u32[]{:S(2)}, u32[]{:S(2)}) collective-permute-start(f32[16,128]{1,0:T(8,128)S(1)} %pad_maximum_fusion.9), channel_id=1, source_target_pairs={{0,2},{1,3},{2,0},{3,1},{4,6},{5,7},{6,4},{7,5},{8,10},{9,11},{10,... | collective-permute-start | bytes 24584 | tf_op jit(solution)/shard_map/ppermute | solution.py:208
  10.9 3.7 %collective-permute-start.5 = (bf16[128,2048]{1,0:T(8,128)(2,1)}, bf16[128,2048]{1,0:T(8,128)(2,1)}, u32[]{:S(2)}, u32[]{:S(2)}) collective-permute-start(bf16[128,2048]{1,0:T(8,128)(2,1)} %param.10), channel_id=1, source_target_pairs={{0,2},{1,3},{2,0},{3,1},{4,6},{5,7},{6,4},{7,5},{8,10},{9,11},{10,... | collective-permute-start | bytes 1572872 | tf_op jit(solution)/shard_map/ppermute | solution.py:208
  14.6 1.9 %constant_dynamic-update-slice_fusion.1 = bf16[256,2048]{1,0:T(8,128)(2,1)} fusion(bf16[128,2048]{1,0:T(8,128)(2,1)} %param.10), kind=kLoop, calls=%fused_computation.239 | loop fusion | bytes 1048576
  16.5 10.6 %collective-permute-done.2 = f32[32,128]{1,0:T(8,128)S(1)} collective-permute-done((f32[32,128]{1,0:T(8,128)S(1)}, f32[32,128]{1,0:T(8,128)S(1)}, u32[]{:S(2)}, u32[]{:S(2)}) %collective-permute-start.2) | collective-permute-done | bytes 16416 | tf_op jit(solution)/shard_map/ppermute | solution.py:208
  27.9 4.7 %collective-permute-start.22 = (bf16[128,2048]{1,0:T(8,128)(2,1)}, bf16[128,2048]{1,0:T(8,128)(2,1)S(1)}, u32[]{:S(2)}, u32[]{:S(2)}) collective-permute-start(bf16[128,2048]{1,0:T(8,128)(2,1)} %param.11), channel_id=1, source_target_pairs={{0,2},{1,3},{2,0},{3,1},{4,6},{5,7},{6,4},{7,5},{8,10},{9,11},{10,... | collective-permute-start | bytes 1572872 | tf_op jit(solution)/shard_map/ppermute | solution.py:208
  32.6 1.9 %constant_dynamic-update-slice_fusion = bf16[256,2048]{1,0:T(8,128)(2,1)} fusion(bf16[256,2048]{1,0:T(8,128)(2,1)} %constant_dynamic-update-slice_fusion.1, bf16[128,2048]{1,0:T(8,128)(2,1)} %collective-permute-done.3), kind=kLoop, calls=%fused_computation.238 | loop fusion | bytes 1048576 | tf_op jit(solution)/shard_map/concatenate | solution.py:223
  34.5 1.8 %convolution_convert_fusion.3 = bf16[256,128]{0,1:T(8,128)(2,1)S(1)} fusion(bf16[256,2048]{1,0:T(8,128)(2,1)} %constant_dynamic-update-slice_fusion, bf16[1,2048,128]{2,1,0:T(8,128)(2,1)} %param.18), kind=kOutput, calls=%fused_computation.74 | convolution fusion | flops 134250496 | bytes 1638400 | tf_op jit(solution)/shard_map/dot_general | solution.py:31
  36.4 4.9 %fusion.6 = f32[256,1536]{1,0:T(8,128)S(1)} fusion(bf16[256,2048]{1,0:T(8,128)(2,1)} %constant_dynamic-update-slice_fusion, bf16[1,2048,1536]{2,1,0:T(8,128)(2,1)} %param.16), kind=kOutput, calls=%fused_computation.6 | convolution fusion | flops 1610612736 | bytes 8912896 | tf_op jit(solution)/shard_map/dot_general | solution.py:34
  43.2 2.5 %multiply_convert_fusion.15 = (bf16[256,768]{1,0:T(8,128)(2,1)S(1)}, bf16[256,768]{1,0:T(8,128)(2,1)S(1)}) fusion(f32[256,768]{1,0:T(8,128)S(1)} %slice_add_fusion.7, f32[256,768]{1,0:T(8,128)S(1)} %slice_add_fusion.6, bf16[1,768,2048]{2,1,0:T(8,128)(2,1)S(1)} %copy-done, bf16[128,2048]{1,0:T(8,128)(2,1)} %collective-permute-done.21, ...), kind=kOutput, calls=%fused_computation.117 | convolution fusion | flops 811008000 | bytes 6554624 | tf_op jit(solution)/shard_map/dot_general | solution.py:56
  51.5 1.8 fusion.4
  54.5 10.9 %collective-permute-done.16 = bf16[128,2048]{1,0:T(8,128)(2,1)S(1)} collective-permute-done((bf16[128,2048]{1,0:T(8,128)(2,1)}, bf16[128,2048]{1,0:T(8,128)(2,1)S(1)}, u32[]{:S(2)}, u32[]{:S(2)}) %collective-permute-start.16) | collective-permute-done | bytes 524320 | tf_op jit(solution)/shard_map/ppermute | solution.py:208
  70.3 11.9 %collective-permute-done.25 = bf16[128,2048]{1,0:T(8,128)(2,1)S(1)} collective-permute-done((bf16[128,2048]{1,0:T(8,128)(2,1)S(1)}, bf16[128,2048]{1,0:T(8,128)(2,1)S(1)}, u32[]{:S(2)}, u32[]{:S(2)}) %collective-permute-start.25) | collective-permute-done | bytes 524320 | tf_op jit(solution)/shard_map/ppermute | solution.py:208
  84.2 7.5 %collective-permute-done.9 = bf16[128,2048]{1,0:T(8,128)(2,1)S(1)} collective-permute-done((bf16[128,2048]{1,0:T(8,128)(2,1)S(1)}, bf16[128,2048]{1,0:T(8,128)(2,1)S(1)}, u32[]{:S(2)}, u32[]{:S(2)}) %collective-permute-start.9) | collective-permute-done | bytes 524320 | tf_op jit(solution)/shard_map/ppermute | solution.py:208
  93.8 1.8 fusion
  98.9 7.0 %collective-permute-done.28 = bf16[128,2048]{1,0:T(8,128)(2,1)S(1)} collective-permute-done((bf16[128,2048]{1,0:T(8,128)(2,1)S(1)}, bf16[128,2048]{1,0:T(8,128)(2,1)S(1)}, u32[]{:S(2)}, u32[]{:S(2)}) %collective-permute-start.28) | collective-permute-done | bytes 524320 | tf_op jit(solution)/shard_map/ppermute | solution.py:208
  108.3 1.8 fusion.2
  115.1 1.6 collective-permute-start.32
  117.6 4.6 %collective-permute-done.32 = bf16[640,128]{1,0:T(8,128)(2,1)S(1)} collective-permute-done((bf16[640,128]{1,0:T(8,128)(2,1)S(1)}, bf16[640,128]{1,0:T(8,128)(2,1)S(1)}, u32[]{:S(2)}, u32[]{:S(2)}) %collective-permute-start.32) | collective-permute-done | bytes 163872 | tf_op jit(solution)/shard_map/ppermute | solution.py:264
  123.7 2.3 %collective-permute-done.34 = bf16[2,64,768]{2,1,0:T(8,128)(2,1)S(1)} collective-permute-done((bf16[2,64,768]{2,1,0:T(8,128)(2,1)S(1)}, bf16[2,64,768]{2,1,0:T(8,128)(2,1)S(1)}, u32[]{:S(2)}, u32[]{:S(2)}) %collective-permute-start.34) | collective-permute-done | bytes 196640 | tf_op jit(solution)/shard_map/ppermute | solution.py:264
  127.5 1.5 collective-permute-start.33
  129.2 6.1 %collective-permute-done.33 = bf16[640,128]{1,0:T(8,128)(2,1)S(1)} collective-permute-done((bf16[640,128]{1,0:T(8,128)(2,1)S(1)}, bf16[640,128]{1,0:T(8,128)(2,1)S(1)}, u32[]{:S(2)}, u32[]{:S(2)}) %collective-permute-start.33) | collective-permute-done | bytes 163872 | tf_op jit(solution)/shard_map/ppermute | solution.py:264
  138.5 11.3 %collective-permute-done.12 = bf16[128,2048]{1,0:T(8,128)(2,1)S(1)} collective-permute-done((bf16[128,2048]{1,0:T(8,128)(2,1)S(1)}, bf16[128,2048]{1,0:T(8,128)(2,1)S(1)}, u32[]{:S(2)}, u32[]{:S(2)}) %collective-permute-start.12) | collective-permute-done | bytes 524320 | tf_op jit(solution)/shard_map/ppermute | solution.py:208
  154.1 16.9 %collective-permute-start.14 = (bf16[128,2048]{1,0:T(8,128)(2,1)S(1)}, bf16[128,2048]{1,0:T(8,128)(2,1)S(1)}, u32[]{:S(2)}, u32[]{:S(2)}) collective-permute-start(bf16[128,2048]{1,0:T(8,128)(2,1)S(1)} %add_convert_fusion.3), channel_id=1, source_target_pairs={{0,2},{1,3},{2,0},{3,1},{4,6},{5,7},{6,4},{7,5},{8,10},{9,11},{10,... | collective-permute-start | bytes 1572872 | tf_op jit(solution)/shard_map/ppermute | solution.py:208
  172.3 6.3 %collective-permute-done.14 = bf16[128,2048]{1,0:T(8,128)(2,1)S(1)} collective-permute-done((bf16[128,2048]{1,0:T(8,128)(2,1)S(1)}, bf16[128,2048]{1,0:T(8,128)(2,1)S(1)}, u32[]{:S(2)}, u32[]{:S(2)}) %collective-permute-start.14) | collective-permute-done | bytes 524320 | tf_op jit(solution)/shard_map/ppermute | solution.py:208
  (149 shorter events, 49.9 us)
Async XLA Ops:
  9.4 18.5 %collective-permute-start.3 = (bf16[128,2048]{1,0:T(8,128)(2,1)}, bf16[128,2048]{1,0:T(8,128)(2,1)}, u32[]{:S(2)}, u32[]{:S(2)}) collective-permute-start(bf16[128,2048]{1,0:T(8,128)(2,1)} %param.10), channel_id=1, source_target_pairs={{0,1},{1,0},{2,3},{3,2},{4,5},{5,4},{6,7},{7,6},{8,9},{9,8},{10,11... | collective-permute-start | bytes 1572872 | tf_op jit(solution)/shard_map/ppermute | solution.py:208
  9.4 39.2 %collective-permute-start.15 = (bf16[128,2048]{1,0:T(8,128)(2,1)}, bf16[128,2048]{1,0:T(8,128)(2,1)}, u32[]{:S(2)}, u32[]{:S(2)}) collective-permute-start(bf16[128,2048]{1,0:T(8,128)(2,1)} %param.10), channel_id=1, source_target_pairs={{2,4},{3,5},{4,2},{5,3},{10,12},{11,13},{12,10},{13,11},{18,20},{1... | collective-permute-start | bytes 1572872 | tf_op jit(solution)/shard_map/ppermute | solution.py:208
  10.9 35.3 %collective-permute-start.5 = (bf16[128,2048]{1,0:T(8,128)(2,1)}, bf16[128,2048]{1,0:T(8,128)(2,1)}, u32[]{:S(2)}, u32[]{:S(2)}) collective-permute-start(bf16[128,2048]{1,0:T(8,128)(2,1)} %param.10), channel_id=1, source_target_pairs={{0,2},{1,3},{2,0},{3,1},{4,6},{5,7},{6,4},{7,5},{8,10},{9,11},{10,... | collective-permute-start | bytes 1572872 | tf_op jit(solution)/shard_map/ppermute | solution.py:208
  14.5 28.5 %collective-permute-start.21 = (bf16[128,2048]{1,0:T(8,128)(2,1)}, bf16[128,2048]{1,0:T(8,128)(2,1)}, u32[]{:S(2)}, u32[]{:S(2)}) collective-permute-start(bf16[128,2048]{1,0:T(8,128)(2,1)} %param.11), channel_id=1, source_target_pairs={{0,1},{1,0},{2,3},{3,2},{4,5},{5,4},{6,7},{7,6},{8,9},{9,8},{10,11... | collective-permute-start | bytes 1572872 | tf_op jit(solution)/shard_map/ppermute | solution.py:208
  27.2 26.7 %collective-permute-start.24 = (bf16[128,2048]{1,0:T(8,128)(2,1)}, bf16[128,2048]{1,0:T(8,128)(2,1)S(1)}, u32[]{:S(2)}, u32[]{:S(2)}) collective-permute-start(bf16[128,2048]{1,0:T(8,128)(2,1)} %param.11), channel_id=1, source_target_pairs={{2,4},{3,5},{4,2},{5,3},{10,12},{11,13},{12,10},{13,11},{18,20},{1... | collective-permute-start | bytes 1572872 | tf_op jit(solution)/shard_map/ppermute | solution.py:208
  27.9 21.4 %collective-permute-start.22 = (bf16[128,2048]{1,0:T(8,128)(2,1)}, bf16[128,2048]{1,0:T(8,128)(2,1)S(1)}, u32[]{:S(2)}, u32[]{:S(2)}) collective-permute-start(bf16[128,2048]{1,0:T(8,128)(2,1)} %param.11), channel_id=1, source_target_pairs={{0,2},{1,3},{2,0},{3,1},{4,6},{5,7},{6,4},{7,5},{8,10},{9,11},{10,... | collective-permute-start | bytes 1572872 | tf_op jit(solution)/shard_map/ppermute | solution.py:208
  43.1 129.2 %collective-permute-start.4 = (bf16[128,2048]{1,0:T(8,128)(2,1)S(1)}, bf16[128,2048]{1,0:T(8,128)(2,1)S(1)}, u32[]{:S(2)}, u32[]{:S(2)}) collective-permute-start(bf16[128,2048]{1,0:T(8,128)(2,1)S(1)} %slice.163), channel_id=1, source_target_pairs={{0,1},{1,0},{2,3},{3,2},{4,5},{5,4},{6,7},{7,6},{8,9},{9,8},{10,11... | collective-permute-start | bytes 1572872 | tf_op jit(solution)/shard_map/ppermute | solution.py:208
  48.6 19.8 %collective-permute-start.8 = (bf16[128,2048]{1,0:T(8,128)(2,1)}, bf16[128,2048]{1,0:T(8,128)(2,1)S(1)}, u32[]{:S(2)}, u32[]{:S(2)}) collective-permute-start(bf16[128,2048]{1,0:T(8,128)(2,1)} %collective-permute-done.5), channel_id=1, source_target_pairs={{2,4},{3,5},{4,2},{5,3},{10,12},{11,13},{12,10},{13,11},{18,20},{1... | collective-permute-start | bytes 1572872 | tf_op jit(solution)/shard_map/ppermute | solution.py:208
  49.3 16.1 %collective-permute-start.16 = (bf16[128,2048]{1,0:T(8,128)(2,1)}, bf16[128,2048]{1,0:T(8,128)(2,1)S(1)}, u32[]{:S(2)}, u32[]{:S(2)}) collective-permute-start(bf16[128,2048]{1,0:T(8,128)(2,1)} %collective-permute-done.15), channel_id=1, source_target_pairs={{2,0},{3,1},{4,6},{5,7},{10,8},{11,9},{12,14},{13,15},{18,16},{19,... | collective-permute-start | bytes 1572872 | tf_op jit(solution)/shard_map/ppermute | solution.py:208
  50.6 16.2 %collective-permute-start.23 = (bf16[128,2048]{1,0:T(8,128)(2,1)S(1)}, bf16[128,2048]{1,0:T(8,128)(2,1)S(1)}, u32[]{:S(2)}, u32[]{:S(2)}) collective-permute-start(bf16[128,2048]{1,0:T(8,128)(2,1)S(1)} %collective-permute-done.22), channel_id=1, source_target_pairs={{0,1},{1,0},{2,3},{3,2},{4,5},{5,4},{6,7},{7,6},{8,9},{9,8},{10,11... | collective-permute-start | bytes 1572872 | tf_op jit(solution)/shard_map/ppermute | solution.py:208
  53.8 29.8 %collective-permute-start.27 = (bf16[128,2048]{1,0:T(8,128)(2,1)S(1)}, bf16[128,2048]{1,0:T(8,128)(2,1)S(1)}, u32[]{:S(2)}, u32[]{:S(2)}) collective-permute-start(bf16[128,2048]{1,0:T(8,128)(2,1)S(1)} %collective-permute-done.22), channel_id=1, source_target_pairs={{2,4},{3,5},{4,2},{5,3},{10,12},{11,13},{12,10},{13,11},{18,20},{1... | collective-permute-start | bytes 1572872 | tf_op jit(solution)/shard_map/ppermute | solution.py:208
  65.4 16.7 %collective-permute-start.25 = (bf16[128,2048]{1,0:T(8,128)(2,1)S(1)}, bf16[128,2048]{1,0:T(8,128)(2,1)S(1)}, u32[]{:S(2)}, u32[]{:S(2)}) collective-permute-start(bf16[128,2048]{1,0:T(8,128)(2,1)S(1)} %collective-permute-done.24), channel_id=1, source_target_pairs={{2,0},{3,1},{4,6},{5,7},{10,8},{11,9},{12,14},{13,15},{18,16},{19,... | collective-permute-start | bytes 1572872 | tf_op jit(solution)/shard_map/ppermute | solution.py:208
  66.8 26.4 %collective-permute-start.17 = (bf16[128,2048]{1,0:T(8,128)(2,1)S(1)}, bf16[128,2048]{1,0:T(8,128)(2,1)S(1)}, u32[]{:S(2)}, u32[]{:S(2)}) collective-permute-start(bf16[128,2048]{1,0:T(8,128)(2,1)S(1)} %broadcast_select_fusion.2), channel_id=1, source_target_pairs={{0,1},{1,0},{2,3},{3,2},{4,5},{5,4},{6,7},{7,6},{8,9},{9,8},{10,11... | collective-permute-start | bytes 1572872 | tf_op jit(solution)/shard_map/ppermute | solution.py:208
  68.4 23.3 %collective-permute-start.9 = (bf16[128,2048]{1,0:T(8,128)(2,1)S(1)}, bf16[128,2048]{1,0:T(8,128)(2,1)S(1)}, u32[]{:S(2)}, u32[]{:S(2)}) collective-permute-start(bf16[128,2048]{1,0:T(8,128)(2,1)S(1)} %collective-permute-done.8), channel_id=1, source_target_pairs={{2,0},{3,1},{4,6},{5,7},{10,8},{11,9},{12,14},{13,15},{18,16},{19,... | collective-permute-start | bytes 1572872 | tf_op jit(solution)/shard_map/ppermute | solution.py:208
  83.6 70.2 %collective-permute-start.7 = (bf16[128,2048]{1,0:T(8,128)(2,1)S(1)}, bf16[128,2048]{1,0:T(8,128)(2,1)S(1)}, u32[]{:S(2)}, u32[]{:S(2)}) collective-permute-start(bf16[128,2048]{1,0:T(8,128)(2,1)S(1)} %slice.169), channel_id=1, source_target_pairs={{0,1},{1,0},{2,3},{3,2},{4,5},{5,4},{6,7},{7,6},{8,9},{9,8},{10,11... | collective-permute-start | bytes 1572872 | tf_op jit(solution)/shard_map/ppermute | solution.py:208
  91.7 14.1 %collective-permute-start.28 = (bf16[128,2048]{1,0:T(8,128)(2,1)S(1)}, bf16[128,2048]{1,0:T(8,128)(2,1)S(1)}, u32[]{:S(2)}, u32[]{:S(2)}) collective-permute-start(bf16[128,2048]{1,0:T(8,128)(2,1)S(1)} %collective-permute-done.27), channel_id=1, source_target_pairs={{2,0},{3,1},{4,6},{5,7},{10,8},{11,9},{12,14},{13,15},{18,16},{19,... | collective-permute-start | bytes 1572872 | tf_op jit(solution)/shard_map/ppermute | solution.py:208
  93.3 14.5 %collective-permute-start.10 = (bf16[128,2048]{1,0:T(8,128)(2,1)S(1)}, bf16[128,2048]{1,0:T(8,128)(2,1)S(1)}, u32[]{:S(2)}, u32[]{:S(2)}) collective-permute-start(bf16[128,2048]{1,0:T(8,128)(2,1)S(1)} %broadcast_select_fusion.3), channel_id=1, source_target_pairs={{0,1},{1,0},{2,3},{3,2},{4,5},{5,4},{6,7},{7,6},{8,9},{9,8},{10,11... | collective-permute-start | bytes 1572872 | tf_op jit(solution)/shard_map/ppermute | solution.py:208
  122.2 14.7 %collective-permute-start.30 = (bf16[1408,128]{1,0:T(8,128)(2,1)S(1)}, bf16[1408,128]{1,0:T(8,128)(2,1)S(1)}, u32[]{:S(2)}, u32[]{:S(2)}) collective-permute-start(bf16[1408,128]{1,0:T(8,128)(2,1)S(1)} %fusion.102), channel_id=1, source_target_pairs={{0,8},{8,0},{16,24},{24,16},{1,9},{9,1},{17,25},{25,17},{2,10},{10... | collective-permute-start | bytes 1081352 | tf_op jit(solution)/shard_map/ppermute | solution.py:264
  126.0 27.0 %collective-permute-start.19 = (bf16[128,2048]{1,0:T(8,128)(2,1)S(1)}, bf16[128,2048]{1,0:T(8,128)(2,1)S(1)}, u32[]{:S(2)}, u32[]{:S(2)}) collective-permute-start(bf16[128,2048]{1,0:T(8,128)(2,1)S(1)} %add_convert_fusion.2), channel_id=1, source_target_pairs={{0,2},{1,3},{6,4},{7,5},{8,10},{9,11},{14,12},{15,13},{16,18},{17,... | collective-permute-start | bytes 1572872 | tf_op jit(solution)/shard_map/ppermute | solution.py:208
  135.3 14.5 %collective-permute-start.12 = (bf16[128,2048]{1,0:T(8,128)(2,1)S(1)}, bf16[128,2048]{1,0:T(8,128)(2,1)S(1)}, u32[]{:S(2)}, u32[]{:S(2)}) collective-permute-start(bf16[128,2048]{1,0:T(8,128)(2,1)S(1)} %add_convert_fusion.5), channel_id=1, source_target_pairs={{0,2},{1,3},{6,4},{7,5},{8,10},{9,11},{14,12},{15,13},{16,18},{17,... | collective-permute-start | bytes 1572872 | tf_op jit(solution)/shard_map/ppermute | solution.py:208
  136.9 14.6 %collective-permute-start.35 = (bf16[2,64,768]{2,1,0:T(8,128)(2,1)S(1)}, bf16[2,64,768]{2,1,0:T(8,128)(2,1)S(1)}, u32[]{:S(2)}, u32[]{:S(2)}) collective-permute-start(bf16[2,64,768]{2,1,0:T(8,128)(2,1)S(1)} %fusion.114), channel_id=1, source_target_pairs={{0,8},{8,0},{16,24},{24,16},{1,9},{9,1},{17,25},{25,17},{2,10},{10... | collective-permute-start | bytes 589832 | tf_op jit(solution)/shard_map/ppermute | solution.py:264
  149.9 21.2 %collective-permute-start.31 = (bf16[1408,128]{1,0:T(8,128)(2,1)S(1)}, bf16[1408,128]{1,0:T(8,128)(2,1)S(1)}, u32[]{:S(2)}, u32[]{:S(2)}) collective-permute-start(bf16[1408,128]{1,0:T(8,128)(2,1)S(1)} %fusion.110), channel_id=1, source_target_pairs={{0,16},{8,24},{16,0},{24,8},{1,17},{9,25},{17,1},{25,9},{2,18},{10... | collective-permute-start | bytes 1081352 | tf_op jit(solution)/shard_map/ppermute | solution.py:264
  153.2 19.1 %collective-permute-start.20 = (bf16[128,2048]{1,0:T(8,128)(2,1)S(1)}, bf16[128,2048]{1,0:T(8,128)(2,1)S(1)}, u32[]{:S(2)}, u32[]{:S(2)}) collective-permute-start(bf16[128,2048]{1,0:T(8,128)(2,1)S(1)} %add_convert_fusion.1), channel_id=1, source_target_pairs={{2,4},{3,5},{4,2},{5,3},{10,12},{11,13},{12,10},{13,11},{18,20},{1... | collective-permute-start | bytes 1572872 | tf_op jit(solution)/shard_map/ppermute | solution.py:208
  154.1 24.4 %collective-permute-start.14 = (bf16[128,2048]{1,0:T(8,128)(2,1)S(1)}, bf16[128,2048]{1,0:T(8,128)(2,1)S(1)}, u32[]{:S(2)}, u32[]{:S(2)}) collective-permute-start(bf16[128,2048]{1,0:T(8,128)(2,1)S(1)} %add_convert_fusion.3), channel_id=1, source_target_pairs={{0,2},{1,3},{2,0},{3,1},{4,6},{5,7},{6,4},{7,5},{8,10},{9,11},{10,... | collective-permute-start | bytes 1572872 | tf_op jit(solution)/shard_map/ppermute | solution.py:208
  (19 other events, 165.4 us)

commit v3 on v2

--- a/solution.py
+++ b/solution.py
@@ -208,19 +208,8 @@
     return lax.ppermute(array, "expert", pairs)
 
 
-def line_gather(block, inner):
-    swap_first = send(block, ALL_SWAP)
-    mid_first = send(block, MID_SWAP)
-    out_second = send(mid_first, OUTWARD)
-    mid_second = send(swap_first, MID_SWAP)
-    out_third = send(mid_second, OUTWARD)
-    stages = [
-        block,
-        swap_first,
-        jnp.where(inner, mid_first, out_second),
-        jnp.where(inner, mid_second, out_third),
-    ]
-    return [jnp.concatenate([mine, send(mine, SIBLING)]) for mine in stages]
+def after(array, *earlier):
+    return lax.optimization_barrier((array,) + earlier)[0]
 
 
 def add_rounded(*terms):
@@ -230,24 +219,13 @@
     return total.astype(jnp.bfloat16)
 
 
-def line_combine(parts, tok_rows):
-    own, first, second, third = [
-        add_rounded(part[:tok_rows], send(part[tok_rows:], SIBLING)) for part in parts
-    ]
-    third_in = send(third, INWARD)
-    third_mid = send(add_rounded(third, third_in), MID_SWAP)
-    second_in = send(second, INWARD)
-    second_mid = send(add_rounded(second, second_in), MID_SWAP)
-    first_swap = send(add_rounded(first, third_mid), ALL_SWAP)
-    return add_rounded(own, first_swap, second_mid)
-
-
-def stage_weights(weight_table, inner, me):
-    for bit in (1, 2, 4):
-        other = send(weight_table, [(e, e ^ bit) for e in range(8)])
-        weight_table = jnp.concatenate([weight_table, other])
-    tok_rows = weight_table.shape[1]
-    table = weight_table.reshape(8, 8, tok_rows)
+def doubled(weight_table, bit):
+    return jnp.concatenate([weight_table, send(weight_table, [(e, e ^ bit) for e in range(8)])])
+
+
+def stage_weights(weight_tables, inner, me):
+    tok_rows = weight_tables.shape[1]
+    table = weight_tables.reshape(8, 8, tok_rows)
     mine = lax.dynamic_index_in_dim(table, me, axis=1, keepdims=False)
     near = mine.reshape(4, 2 * tok_rows)
     return [
@@ -292,24 +270,77 @@
     me = lax.axis_index("expert")
     chip = me // 2
     inner = (chip == 1) | (chip == 2)
+    gate_up, down = gate_up_weight[0], down_weight[0]
+    adapt_a, adapt_b = adapter_down_maps[0], adapter_up_maps[0]
+
+    def pair(block):
+        return jnp.concatenate([block, send(block, SIBLING)])
+
+    def forward(rows):
+        return expert_apply_forward(rows, gate_up, down, adapt_a, adapt_b)
+
+    tok_swap = send(tokens, ALL_SWAP)
+    tok_mid = send(tokens, MID_SWAP)
+    rows0 = pair(tokens)
     weight_table = dense_route_weights(
-        routing, router_route_weights, route_replica_choice, device_expert_table, capacity
-    )
-    weights = [w[:, None] for w in stage_weights(weight_table.T, inner, me)]
-    row_stages = line_gather(tokens, inner)
-    cot_stages = line_gather(cotangent, inner)
-    parts, saved = [], []
-    for rows, w in zip(row_stages, weights):
-        layer_output, kept = expert_apply_forward(
-            rows, gate_up_weight[0], down_weight[0], adapter_down_maps[0], adapter_up_maps[0]
-        )
-        parts.append((w * layer_output.astype(jnp.float32)).astype(jnp.bfloat16))
-        saved.append(kept)
-    mixed = line_combine(parts, tok_rows)
+        after(routing, rows0),
+        router_route_weights,
+        route_replica_choice,
+        device_expert_table,
+        capacity,
+    ).T
+    weight_table = doubled(doubled(weight_table, 1), 2)
+    out0, kept0 = forward(rows0)
+
+    tok_out2 = send(after(tok_mid, tok_swap), OUTWARD)
+    tok_mid2 = send(after(tok_swap, tok_mid), MID_SWAP)
+    cot_in = send(after(cotangent, tok_swap, tok_mid), INWARD)
+    weight_table = doubled(after(weight_table, tok_swap, tok_mid), 4)
+    rows1 = pair(after(tok_swap, tok_mid))
+    out1, kept1 = forward(rows1)
+
+    tok_out3 = send(after(tok_mid2, tok_out2), OUTWARD)
+    cot_mid = send(after(cotangent, tok_mid2, tok_out2, cot_in), MID_SWAP)
+    rows2 = pair(jnp.where(inner, tok_mid, tok_out2))
+    out2, kept2 = forward(rows2)
+
+    cot_out = send(after(cotangent, tok_out3, cot_mid), OUTWARD)
+    cot_mid2 = send(after(cot_in, tok_out3, cot_mid), MID_SWAP)
+    rows3 = pair(jnp.where(inner, tok_mid2, tok_out3))
+    out3, kept3 = forward(rows3)
+
+    weights = [w[:, None] for w in stage_weights(weight_table, inner, me)]
+
+    def chip_part(layer_output, w):
+        part = (w * layer_output.astype(jnp.float32)).astype(jnp.bfloat16)
+        return add_rounded(part[:tok_rows], send(part[tok_rows:], SIBLING))
+
+    part3 = chip_part(out3, weights[3])
+    third_in = send(part3, INWARD)
+    part2 = chip_part(out2, weights[2])
+    part1 = chip_part(out1, weights[1])
+    part0 = chip_part(out0, weights[0])
+
+    cot_out2 = send(after(cot_mid, cot_out), OUTWARD)
+    third_mid = send(after(add_rounded(part3, third_in), cot_mid2), MID_SWAP)
+    second_in = send(after(part2, third_in), INWARD)
+    cot_out3 = send(after(cot_mid2, cot_out2), OUTWARD)
+    second_mid = send(after(add_rounded(part2, second_in), third_mid), MID_SWAP)
+    first_swap = send(after(add_rounded(part1, third_mid), second_in, cot_out3), ALL_SWAP)
+    mixed = add_rounded(part0, first_swap, second_mid)
+
+    cot_stages = [
+        pair(after(cotangent, tok_swap)),
+        pair(jnp.where(inner, cot_in, cot_out)),
+        pair(jnp.where(inner, cot_mid, cot_out2)),
+        pair(jnp.where(inner, cot_mid2, cot_out3)),
+    ]
+    row_stages = [rows0, rows1, rows2, rows3]
+    saved = [kept0, kept1, kept2, kept3]
     grad_a, grad_b = 0.0, 0.0
     for rows, cot, w, kept in zip(row_stages, cot_stages, weights, saved):
         scaled = (w * cot.astype(jnp.float32)).astype(jnp.bfloat16)
-        more_a, more_b = expert_backward(rows, scaled, down_weight[0], adapter_up_maps[0], kept)
+        more_a, more_b = expert_backward(rows, scaled, down, adapt_b, kept)
         grad_a, grad_b = grad_a + more_a, grad_b + more_b
     grad_a, grad_b = group_sum(grad_a, grad_b)
     return mixed, grad_a[None], grad_b[None]

time: 180 us -> 163 us (0.906)
  waiting for transfers between devices: 79.5 us -> 65.4 us
  other arithmetic: 8.92 us -> 5.35 us
    ppermute x30 -> x31, waiting for transfers between devices: 66.4 us -> 56 us  [send(): return lax.ppermute(array, 'expert', pairs)]
    ppermute x6, waiting for transfers between devices: 13.1 us -> 9.45 us  [swap_sum(): other = lax.ppermute(rounded.astype(jnp.bfloat16), 'dp', pairs)]
    ppermute x30 -> x31, starting transfers between devices: 44.2 us -> 43.6 us  [send(): return lax.ppermute(array, 'expert', pairs)]
  transfers between devices with their start and end apart: 36 -> 37, of which waited for: 11 -> 14; matrix products, arithmetic and copies ran while one was open for 23% -> 26% of each run, Pallas kernels for 0% -> 0%
where the time goes in v3:
time: 163 us
  waiting for transfers between devices  65.4 us (40%)
  starting transfers between devices  51.9 us (32%)
  matrix products  32.3 us (20%)
  local copies, waits for them, and re-layouts  6.33 us (4%)
  other arithmetic  5.35 us (3%)
    ppermute x31, waiting for transfers between devices, send(): return lax.ppermute(array, 'expert', pairs)  56 us
    ppermute x31, starting transfers between devices, send(): return lax.ppermute(array, 'expert', pairs)  43.6 us
    dot_general x4, matrix products, expert_apply_forward(): jnp.dot(rows_in, gate_up, preferred_element_type=jnp.float32)  10.3 us
    ppermute x6, waiting for transfers between devices, swap_sum(): other = lax.ppermute(rounded.astype(jnp.bfloat16), 'dp', pairs)  9.45 us
    ppermute x6, starting transfers between devices, swap_sum(): other = lax.ppermute(rounded.astype(jnp.bfloat16), 'dp', pairs)  8.26 us
    dot_general x4, matrix products, expert_backward(): lax.dot_general(scaled, down, (((1,), (1,)), ((), ())), preferred_element...  5.25 us
    dot_general x4, matrix products, expert_apply_forward(): jnp.dot(hidden, down, preferred_element_type=jnp.float32)  4.22 us
    dot_general x4, matrix products, expert_apply_forward(): jnp.dot(rows_in, adapt_a, preferred_element_type=jnp.float32)  3.32 us
  transfers between devices with their start and end apart: 37, of which 14 were waited for; matrix products, arithmetic and copies ran while one was open for 26% of the time, Pallas kernels for 0%

profile of v3, /device:TPU:0, one launch (start us, length us, event | category | flops | bytes accessed | tf_op | source)
XLA Modules:
  0.0 162.7 jit_solution(13308895208248527358)
XLA Ops:
  2.3 5.3 %collective-permute-start.3 = (bf16[128,2048]{1,0:T(8,128)(2,1)}, bf16[128,2048]{1,0:T(8,128)(2,1)}, u32[]{:S(2)}, u32[]{:S(2)}) collective-permute-start(bf16[128,2048]{1,0:T(8,128)(2,1)} %param.10), channel_id=1, source_target_pairs={{0,2},{1,3},{2,0},{3,1},{4,6},{5,7},{6,4},{7,5},{8,10},{9,11},{10,... | collective-permute-start | bytes 1572872 | tf_op jit(solution)/shard_map/ppermute | solution.py:208
  7.5 1.9 %constant_dynamic-update-slice_fusion.1 = bf16[256,2048]{1,0:T(8,128)(2,1)} fusion(bf16[128,2048]{1,0:T(8,128)(2,1)} %param.10), kind=kLoop, calls=%fused_computation.240 | loop fusion | bytes 1048576
  9.4 10.0 %collective-permute-done.3 = bf16[128,2048]{1,0:T(8,128)(2,1)} collective-permute-done((bf16[128,2048]{1,0:T(8,128)(2,1)}, bf16[128,2048]{1,0:T(8,128)(2,1)}, u32[]{:S(2)}, u32[]{:S(2)}) %collective-permute-start.3) | collective-permute-done | bytes 524320 | tf_op jit(solution)/shard_map/ppermute | solution.py:208
  20.9 1.9 %constant_dynamic-update-slice_fusion = bf16[256,2048]{1,0:T(8,128)(2,1)} fusion(bf16[256,2048]{1,0:T(8,128)(2,1)} %constant_dynamic-update-slice_fusion.1, bf16[128,2048]{1,0:T(8,128)(2,1)} %collective-permute-done), kind=kLoop, calls=%fused_computation.239 | loop fusion | bytes 1048576 | tf_op jit(solution)/shard_map/concatenate | solution.py:277
  23.0 1.8 %convolution_convert_fusion.3 = bf16[256,128]{0,1:T(8,128)(2,1)S(1)} fusion(bf16[256,2048]{1,0:T(8,128)(2,1)} %constant_dynamic-update-slice_fusion, bf16[1,2048,128]{2,1,0:T(8,128)(2,1)} %param.18), kind=kOutput, calls=%fused_computation.74 | convolution fusion | flops 134250496 | bytes 1638400 | tf_op jit(solution)/shard_map/dot_general | solution.py:31
  26.1 4.9 %fusion.6 = f32[256,1536]{1,0:T(8,128)S(1)} fusion(bf16[256,2048]{1,0:T(8,128)(2,1)} %constant_dynamic-update-slice_fusion, bf16[1,2048,1536]{2,1,0:T(8,128)(2,1)} %param.16), kind=kOutput, calls=%fused_computation.6 | convolution fusion | flops 1610612736 | bytes 8912896 | tf_op jit(solution)/shard_map/dot_general | solution.py:34
  31.4 2.8 %collective-permute-start.2 = (f32[16,128]{1,0:T(8,128)S(1)}, f32[16,128]{1,0:T(8,128)S(1)}, u32[]{:S(2)}, u32[]{:S(2)}) collective-permute-start(f32[16,128]{1,0:T(8,128)S(1)} %pad_maximum_fusion.9), channel_id=1, source_target_pairs={{0,2},{1,3},{2,0},{3,1},{4,6},{5,7},{6,4},{7,5},{8,10},{9,11},{10,... | collective-permute-start | bytes 24584 | tf_op jit(solution)/shard_map/ppermute | solution.py:208
  35.8 3.0 %collective-permute-start.5 = (f32[32,128]{1,0:T(8,128)S(1)}, f32[32,128]{1,0:T(8,128)S(1)}, u32[]{:S(2)}, u32[]{:S(2)}) collective-permute-start(f32[32,128]{1,0:T(8,128)S(1)} %pad_maximum_fusion.8), channel_id=1, source_target_pairs={{0,4},{1,5},{2,6},{3,7},{4,0},{5,1},{6,2},{7,3},{8,12},{9,13},{10,... | collective-permute-start | bytes 49160 | tf_op jit(solution)/shard_map/ppermute | solution.py:208
  41.2 4.6 %collective-permute-start.15 = (bf16[128,2048]{1,0:T(8,128)(2,1)S(1)}, bf16[128,2048]{1,0:T(8,128)(2,1)S(1)}, u32[]{:S(2)}, u32[]{:S(2)}) collective-permute-start(bf16[128,2048]{1,0:T(8,128)(2,1)S(1)} %copy-done.7), channel_id=1, source_target_pairs={{0,2},{1,3},{6,4},{7,5},{8,10},{9,11},{14,12},{15,13},{16,18},{17,... | collective-permute-start | bytes 1572872 | tf_op jit(solution)/shard_map/ppermute | solution.py:208
  51.4 1.8 %fusion.4 = f32[256,1536]{1,0:T(8,128)S(1)} fusion(bf16[256,2048]{1,0:T(8,128)(2,1)S(1)} %constant_dynamic-update-slice_fusion.2, bf16[1,2048,1536]{2,1,0:T(8,128)(2,1)S(1)} %bitcast.168), kind=kOutput, calls=%fused_computation.4 | convolution fusion | flops 1610612736 | bytes 8912896 | tf_op jit(solution)/shard_map/dot_general | solution.py:34
  59.3 11.7 %collective-permute-done.11 = bf16[128,2048]{1,0:T(8,128)(2,1)S(1)} collective-permute-done((bf16[128,2048]{1,0:T(8,128)(2,1)}, bf16[128,2048]{1,0:T(8,128)(2,1)S(1)}, u32[]{:S(2)}, u32[]{:S(2)}) %collective-permute-start.11) | collective-permute-done | bytes 524320 | tf_op jit(solution)/shard_map/ppermute | solution.py:208
  73.0 1.8 %fusion = f32[256,1536]{1,0:T(8,128)S(1)} fusion(bf16[1,2048,1536]{2,1,0:T(8,128)(2,1)S(1)} %bitcast.168, bf16[128,2048]{1,0:T(8,128)(2,1)S(1)} %collective-permute-done.19, bf16[128,2048]{1,0:T(8,128)(2,1)S(1)} %broadcast_select_fusion.3), kind=kOutput, calls=%fused_computation | convolution fusion | flops 1612709888 | bytes 8912896 | tf_op jit(solution)/shard_map/dot_general | solution.py:34
  77.2 10.6 %collective-permute-done.22 = bf16[128,2048]{1,0:T(8,128)(2,1)S(1)} collective-permute-done((bf16[128,2048]{1,0:T(8,128)(2,1)S(1)}, bf16[128,2048]{1,0:T(8,128)(2,1)S(1)}, u32[]{:S(2)}, u32[]{:S(2)}) %collective-permute-start.22) | collective-permute-done | bytes 524320 | tf_op jit(solution)/shard_map/ppermute | solution.py:208
  89.8 1.8 %fusion.2 = f32[256,1536]{1,0:T(8,128)S(1)} fusion(bf16[1,2048,1536]{2,1,0:T(8,128)(2,1)S(1)} %bitcast.168, bf16[128,2048]{1,0:T(8,128)(2,1)S(1)} %collective-permute-done.12, bf16[128,2048]{1,0:T(8,128)(2,1)S(1)} %broadcast_select_fusion.4), kind=kOutput, calls=%fused_computation.2 | convolution fusion | flops 1612709888 | bytes 8912896 | tf_op jit(solution)/shard_map/dot_general | solution.py:34
  94.1 9.9 %collective-permute-done.23 = bf16[128,2048]{1,0:T(8,128)(2,1)S(1)} collective-permute-done((bf16[128,2048]{1,0:T(8,128)(2,1)S(1)}, bf16[128,2048]{1,0:T(8,128)(2,1)S(1)}, u32[]{:S(2)}, u32[]{:S(2)}) %collective-permute-start.23) | collective-permute-done | bytes 524320 | tf_op jit(solution)/shard_map/ppermute | solution.py:208
  107.6 4.6 %collective-permute-start.14 = (bf16[128,2048]{1,0:T(8,128)(2,1)S(1)}, bf16[128,2048]{1,0:T(8,128)(2,1)S(1)}, u32[]{:S(2)}, u32[]{:S(2)}) collective-permute-start(bf16[128,2048]{1,0:T(8,128)(2,1)S(1)} %add_convert_fusion.5), channel_id=1, source_target_pairs={{0,2},{1,3},{6,4},{7,5},{8,10},{9,11},{14,12},{15,13},{16,18},{17,... | collective-permute-start | bytes 1572872 | tf_op jit(solution)/shard_map/ppermute | solution.py:208
  112.9 6.5 %collective-permute-done.24 = bf16[128,2048]{1,0:T(8,128)(2,1)S(1)} collective-permute-done((bf16[128,2048]{1,0:T(8,128)(2,1)S(1)}, bf16[128,2048]{1,0:T(8,128)(2,1)S(1)}, u32[]{:S(2)}, u32[]{:S(2)}) %collective-permute-start.24) | collective-permute-done | bytes 524320 | tf_op jit(solution)/shard_map/ppermute | solution.py:208
  121.2 2.8 %collective-permute-done.14 = bf16[128,2048]{1,0:T(8,128)(2,1)S(1)} collective-permute-done((bf16[128,2048]{1,0:T(8,128)(2,1)S(1)}, bf16[128,2048]{1,0:T(8,128)(2,1)S(1)}, u32[]{:S(2)}, u32[]{:S(2)}) %collective-permute-start.14) | collective-permute-done | bytes 524320 | tf_op jit(solution)/shard_map/ppermute | solution.py:208
  125.0 6.1 %collective-permute-start.21 = (bf16[128,2048]{1,0:T(8,128)(2,1)S(1)}, bf16[128,2048]{1,0:T(8,128)(2,1)S(1)}, u32[]{:S(2)}, u32[]{:S(2)}) collective-permute-start(bf16[128,2048]{1,0:T(8,128)(2,1)S(1)} %add_convert_fusion.2), channel_id=1, source_target_pairs={{0,2},{1,3},{6,4},{7,5},{8,10},{9,11},{14,12},{15,13},{16,18},{17,... | collective-permute-start | bytes 1572872 | tf_op jit(solution)/shard_map/ppermute | solution.py:208
  134.8 1.8 %fusion.73 = f32[2048,128]{1,0:T(8,128)S(1)} fusion(f32[2048,128]{1,0:T(8,128)S(1)} %fusion.112, f32[2048,128]{1,0:T(8,128)S(1)} %fusion.111, f32[2048,128]{1,0:T(8,128)S(1)} %fusion.150, bf16[256,2048]{1,0:T(8,128)(2,1)} %constant_dynamic-update-slice_fusion, f32[256,64]{0,1:T(8,128)S(1)} %fusion.130, f32[256,64]{0,1:T(8,128)S(1)} %fusion.142), kind=kOutput, calls=%fused_computation.42 | convolution fusion | flops 135102464 | bytes 5373952 | tf_op jit(solution)/shard_map/dot_general | solution.py:85
  141.9 2.5 %collective-permute-start.25 = (bf16[128,2048]{1,0:T(8,128)(2,1)S(1)}, bf16[128,2048]{1,0:T(8,128)(2,1)S(1)}, u32[]{:S(2)}, u32[]{:S(2)}) collective-permute-start(bf16[128,2048]{1,0:T(8,128)(2,1)S(1)} %add_convert_fusion.3), channel_id=1, source_target_pairs={{0,2},{1,3},{2,0},{3,1},{4,6},{5,7},{6,4},{7,5},{8,10},{9,11},{10,... | collective-permute-start | bytes 1572872 | tf_op jit(solution)/shard_map/ppermute | solution.py:208
  147.7 3.8 %collective-permute-done.34 = bf16[640,128]{1,0:T(8,128)(2,1)S(1)} collective-permute-done((bf16[640,128]{1,0:T(8,128)(2,1)S(1)}, bf16[640,128]{1,0:T(8,128)(2,1)S(1)}, u32[]{:S(2)}, u32[]{:S(2)}) %collective-permute-start.34) | collective-permute-done | bytes 163872 | tf_op jit(solution)/shard_map/ppermute | solution.py:242
  154.8 2.4 %collective-permute-done.36 = bf16[2,64,768]{2,1,0:T(8,128)(2,1)S(1)} collective-permute-done((bf16[2,64,768]{2,1,0:T(8,128)(2,1)S(1)}, bf16[2,64,768]{2,1,0:T(8,128)(2,1)S(1)}, u32[]{:S(2)}, u32[]{:S(2)}) %collective-permute-start.36) | collective-permute-done | bytes 196640 | tf_op jit(solution)/shard_map/ppermute | solution.py:242
  159.1 2.4 %collective-permute-done.32 = bf16[1408,128]{1,0:T(8,128)(2,1)S(1)} collective-permute-done((bf16[1408,128]{1,0:T(8,128)(2,1)S(1)}, bf16[1408,128]{1,0:T(8,128)(2,1)S(1)}, u32[]{:S(2)}, u32[]{:S(2)}) %collective-permute-start.32) | collective-permute-done | bytes 360480 | tf_op jit(solution)/shard_map/ppermute | solution.py:242
  (158 shorter events, 54.6 us)
Async XLA Ops:
  2.3 17.2 %collective-permute-start.3 = (bf16[128,2048]{1,0:T(8,128)(2,1)}, bf16[128,2048]{1,0:T(8,128)(2,1)}, u32[]{:S(2)}, u32[]{:S(2)}) collective-permute-start(bf16[128,2048]{1,0:T(8,128)(2,1)} %param.10), channel_id=1, source_target_pairs={{0,2},{1,3},{2,0},{3,1},{4,6},{5,7},{6,4},{7,5},{8,10},{9,11},{10,... | collective-permute-start | bytes 1572872 | tf_op jit(solution)/shard_map/ppermute | solution.py:208
  7.5 13.4 %collective-permute-start = (bf16[128,2048]{1,0:T(8,128)(2,1)}, bf16[128,2048]{1,0:T(8,128)(2,1)}, u32[]{:S(2)}, u32[]{:S(2)}) collective-permute-start(bf16[128,2048]{1,0:T(8,128)(2,1)} %param.10), channel_id=1, source_target_pairs={{0,1},{1,0},{2,3},{3,2},{4,5},{5,4},{6,7},{7,6},{8,9},{9,8},{10,11... | collective-permute-start | bytes 1572872 | tf_op jit(solution)/shard_map/ppermute | solution.py:208
  19.5 33.7 %collective-permute-start.9 = (bf16[128,2048]{1,0:T(8,128)(2,1)}, bf16[128,2048]{1,0:T(8,128)(2,1)}, u32[]{:S(2)}, u32[]{:S(2)}) collective-permute-start(bf16[128,2048]{1,0:T(8,128)(2,1)} %collective-permute-done.3), channel_id=1, source_target_pairs={{2,4},{3,5},{4,2},{5,3},{10,12},{11,13},{12,10},{13,11},{18,20},{1... | collective-permute-start | bytes 1572872 | tf_op jit(solution)/shard_map/ppermute | solution.py:208
  20.9 28.8 %collective-permute-start.7 = (bf16[128,2048]{1,0:T(8,128)(2,1)}, bf16[128,2048]{1,0:T(8,128)(2,1)}, u32[]{:S(2)}, u32[]{:S(2)}) collective-permute-start(bf16[128,2048]{1,0:T(8,128)(2,1)} %collective-permute-done.3), channel_id=1, source_target_pairs={{0,1},{1,0},{2,3},{3,2},{4,5},{5,4},{6,7},{7,6},{8,9},{9,8},{10,11... | collective-permute-start | bytes 1572872 | tf_op jit(solution)/shard_map/ppermute | solution.py:208
  39.9 14.5 %collective-permute-start.10 = (bf16[128,2048]{1,0:T(8,128)(2,1)}, bf16[128,2048]{1,0:T(8,128)(2,1)S(1)}, u32[]{:S(2)}, u32[]{:S(2)}) collective-permute-start(bf16[128,2048]{1,0:T(8,128)(2,1)} %collective-permute-done.4), channel_id=1, source_target_pairs={{2,0},{3,1},{4,6},{5,7},{10,8},{11,9},{12,14},{13,15},{18,16},{19,... | collective-permute-start | bytes 1572872 | tf_op jit(solution)/shard_map/ppermute | solution.py:208
  41.2 15.3 %collective-permute-start.15 = (bf16[128,2048]{1,0:T(8,128)(2,1)S(1)}, bf16[128,2048]{1,0:T(8,128)(2,1)S(1)}, u32[]{:S(2)}, u32[]{:S(2)}) collective-permute-start(bf16[128,2048]{1,0:T(8,128)(2,1)S(1)} %copy-done.7), channel_id=1, source_target_pairs={{0,2},{1,3},{6,4},{7,5},{8,10},{9,11},{14,12},{15,13},{16,18},{17,... | collective-permute-start | bytes 1572872 | tf_op jit(solution)/shard_map/ppermute | solution.py:208
  47.8 110.2 %collective-permute-start.6 = (bf16[128,2048]{1,0:T(8,128)(2,1)S(1)}, bf16[128,2048]{1,0:T(8,128)(2,1)S(1)}, u32[]{:S(2)}, u32[]{:S(2)}) collective-permute-start(bf16[128,2048]{1,0:T(8,128)(2,1)S(1)} %slice.163), channel_id=1, source_target_pairs={{0,1},{1,0},{2,3},{3,2},{4,5},{5,4},{6,7},{7,6},{8,9},{9,8},{10,11... | collective-permute-start | bytes 1572872 | tf_op jit(solution)/shard_map/ppermute | solution.py:208
  54.5 18.0 %collective-permute-start.19 = (bf16[128,2048]{1,0:T(8,128)(2,1)S(1)}, bf16[128,2048]{1,0:T(8,128)(2,1)S(1)}, u32[]{:S(2)}, u32[]{:S(2)}) collective-permute-start(bf16[128,2048]{1,0:T(8,128)(2,1)S(1)} %broadcast_select_fusion.3), channel_id=1, source_target_pairs={{0,1},{1,0},{2,3},{3,2},{4,5},{5,4},{6,7},{7,6},{8,9},{9,8},{10,11... | collective-permute-start | bytes 1572872 | tf_op jit(solution)/shard_map/ppermute | solution.py:208
  54.6 16.4 %collective-permute-start.11 = (bf16[128,2048]{1,0:T(8,128)(2,1)}, bf16[128,2048]{1,0:T(8,128)(2,1)S(1)}, u32[]{:S(2)}, u32[]{:S(2)}) collective-permute-start(bf16[128,2048]{1,0:T(8,128)(2,1)} %collective-permute-done.9), channel_id=1, source_target_pairs={{2,0},{3,1},{4,6},{5,7},{10,8},{11,9},{12,14},{13,15},{18,16},{19,... | collective-permute-start | bytes 1572872 | tf_op jit(solution)/shard_map/ppermute | solution.py:208
  56.5 14.7 %collective-permute-start.16 = (bf16[128,2048]{1,0:T(8,128)(2,1)S(1)}, bf16[128,2048]{1,0:T(8,128)(2,1)S(1)}, u32[]{:S(2)}, u32[]{:S(2)}) collective-permute-start(bf16[128,2048]{1,0:T(8,128)(2,1)S(1)} %copy-done.7), channel_id=1, source_target_pairs={{2,4},{3,5},{4,2},{5,3},{10,12},{11,13},{12,10},{13,11},{18,20},{1... | collective-permute-start | bytes 1572872 | tf_op jit(solution)/shard_map/ppermute | solution.py:208
  58.8 79.6 %collective-permute-start.8 = (bf16[128,2048]{1,0:T(8,128)(2,1)S(1)}, bf16[128,2048]{1,0:T(8,128)(2,1)S(1)}, u32[]{:S(2)}, u32[]{:S(2)}) collective-permute-start(bf16[128,2048]{1,0:T(8,128)(2,1)S(1)} %slice.169), channel_id=1, source_target_pairs={{0,1},{1,0},{2,3},{3,2},{4,5},{5,4},{6,7},{7,6},{8,9},{9,8},{10,11... | collective-permute-start | bytes 1572872 | tf_op jit(solution)/shard_map/ppermute | solution.py:208
  71.1 16.7 %collective-permute-start.12 = (bf16[128,2048]{1,0:T(8,128)(2,1)S(1)}, bf16[128,2048]{1,0:T(8,128)(2,1)S(1)}, u32[]{:S(2)}, u32[]{:S(2)}) collective-permute-start(bf16[128,2048]{1,0:T(8,128)(2,1)S(1)} %broadcast_select_fusion.4), channel_id=1, source_target_pairs={{0,1},{1,0},{2,3},{3,2},{4,5},{5,4},{6,7},{7,6},{8,9},{9,8},{10,11... | collective-permute-start | bytes 1572872 | tf_op jit(solution)/shard_map/ppermute | solution.py:208
  71.2 16.6 %collective-permute-start.22 = (bf16[128,2048]{1,0:T(8,128)(2,1)S(1)}, bf16[128,2048]{1,0:T(8,128)(2,1)S(1)}, u32[]{:S(2)}, u32[]{:S(2)}) collective-permute-start(bf16[128,2048]{1,0:T(8,128)(2,1)S(1)} %copy-done.7), channel_id=1, source_target_pairs={{2,0},{3,1},{4,6},{5,7},{10,8},{11,9},{12,14},{13,15},{18,16},{19,... | collective-permute-start | bytes 1572872 | tf_op jit(solution)/shard_map/ppermute | solution.py:208
  75.4 18.7 %collective-permute-start.17 = (bf16[128,2048]{1,0:T(8,128)(2,1)S(1)}, bf16[128,2048]{1,0:T(8,128)(2,1)S(1)}, u32[]{:S(2)}, u32[]{:S(2)}) collective-permute-start(bf16[128,2048]{1,0:T(8,128)(2,1)S(1)} %collective-permute-done.15), channel_id=1, source_target_pairs={{2,4},{3,5},{4,2},{5,3},{10,12},{11,13},{12,10},{13,11},{18,20},{1... | collective-permute-start | bytes 1572872 | tf_op jit(solution)/shard_map/ppermute | solution.py:208
  87.8 16.2 %collective-permute-start.23 = (bf16[128,2048]{1,0:T(8,128)(2,1)S(1)}, bf16[128,2048]{1,0:T(8,128)(2,1)S(1)}, u32[]{:S(2)}, u32[]{:S(2)}) collective-permute-start(bf16[128,2048]{1,0:T(8,128)(2,1)S(1)} %collective-permute-done.16), channel_id=1, source_target_pairs={{2,0},{3,1},{4,6},{5,7},{10,8},{11,9},{12,14},{13,15},{18,16},{19,... | collective-permute-start | bytes 1572872 | tf_op jit(solution)/shard_map/ppermute | solution.py:208
  91.9 13.4 %collective-permute-start.28 = (bf16[128,2048]{1,0:T(8,128)(2,1)S(1)}, bf16[128,2048]{1,0:T(8,128)(2,1)S(1)}, u32[]{:S(2)}, u32[]{:S(2)}) collective-permute-start(bf16[128,2048]{1,0:T(8,128)(2,1)S(1)} %broadcast_select_fusion.2), channel_id=1, source_target_pairs={{0,1},{1,0},{2,3},{3,2},{4,5},{5,4},{6,7},{7,6},{8,9},{9,8},{10,11... | collective-permute-start | bytes 1572872 | tf_op jit(solution)/shard_map/ppermute | solution.py:208
  104.0 15.4 %collective-permute-start.24 = (bf16[128,2048]{1,0:T(8,128)(2,1)S(1)}, bf16[128,2048]{1,0:T(8,128)(2,1)S(1)}, u32[]{:S(2)}, u32[]{:S(2)}) collective-permute-start(bf16[128,2048]{1,0:T(8,128)(2,1)S(1)} %collective-permute-done.17), channel_id=1, source_target_pairs={{2,0},{3,1},{4,6},{5,7},{10,8},{11,9},{12,14},{13,15},{18,16},{19,... | collective-permute-start | bytes 1572872 | tf_op jit(solution)/shard_map/ppermute | solution.py:208
  105.4 14.2 %collective-permute-start.29 = (bf16[128,2048]{1,0:T(8,128)(2,1)S(1)}, bf16[128,2048]{1,0:T(8,128)(2,1)S(1)}, u32[]{:S(2)}, u32[]{:S(2)}) collective-permute-start(bf16[128,2048]{1,0:T(8,128)(2,1)S(1)} %broadcast_select_fusion.1), channel_id=1, source_target_pairs={{0,1},{1,0},{2,3},{3,2},{4,5},{5,4},{6,7},{7,6},{8,9},{9,8},{10,11... | collective-permute-start | bytes 1572872 | tf_op jit(solution)/shard_map/ppermute | solution.py:208
  107.6 16.4 %collective-permute-start.14 = (bf16[128,2048]{1,0:T(8,128)(2,1)S(1)}, bf16[128,2048]{1,0:T(8,128)(2,1)S(1)}, u32[]{:S(2)}, u32[]{:S(2)}) collective-permute-start(bf16[128,2048]{1,0:T(8,128)(2,1)S(1)} %add_convert_fusion.5), channel_id=1, source_target_pairs={{0,2},{1,3},{6,4},{7,5},{8,10},{9,11},{14,12},{15,13},{16,18},{17,... | collective-permute-start | bytes 1572872 | tf_op jit(solution)/shard_map/ppermute | solution.py:208
  124.3 14.6 %collective-permute-start.18 = (bf16[128,2048]{1,0:T(8,128)(2,1)S(1)}, bf16[128,2048]{1,0:T(8,128)(2,1)S(1)}, u32[]{:S(2)}, u32[]{:S(2)}) collective-permute-start(bf16[128,2048]{1,0:T(8,128)(2,1)S(1)} %add_convert_fusion.4), channel_id=1, source_target_pairs={{2,4},{3,5},{4,2},{5,3},{10,12},{11,13},{12,10},{13,11},{18,20},{1... | collective-permute-start | bytes 1572872 | tf_op jit(solution)/shard_map/ppermute | solution.py:208
  125.0 16.8 %collective-permute-start.21 = (bf16[128,2048]{1,0:T(8,128)(2,1)S(1)}, bf16[128,2048]{1,0:T(8,128)(2,1)S(1)}, u32[]{:S(2)}, u32[]{:S(2)}) collective-permute-start(bf16[128,2048]{1,0:T(8,128)(2,1)S(1)} %add_convert_fusion.2), channel_id=1, source_target_pairs={{0,2},{1,3},{6,4},{7,5},{8,10},{9,11},{14,12},{15,13},{16,18},{17,... | collective-permute-start | bytes 1572872 | tf_op jit(solution)/shard_map/ppermute | solution.py:208
  138.9 14.1 %collective-permute-start.31 = (bf16[1408,128]{1,0:T(8,128)(2,1)S(1)}, bf16[1408,128]{1,0:T(8,128)(2,1)S(1)}, u32[]{:S(2)}, u32[]{:S(2)}) collective-permute-start(bf16[1408,128]{1,0:T(8,128)(2,1)S(1)} %fusion.102), channel_id=1, source_target_pairs={{0,8},{8,0},{16,24},{24,16},{1,9},{9,1},{17,25},{25,17},{2,10},{10... | collective-permute-start | bytes 1081352 | tf_op jit(solution)/shard_map/ppermute | solution.py:242
  141.9 16.0 %collective-permute-start.25 = (bf16[128,2048]{1,0:T(8,128)(2,1)S(1)}, bf16[128,2048]{1,0:T(8,128)(2,1)S(1)}, u32[]{:S(2)}, u32[]{:S(2)}) collective-permute-start(bf16[128,2048]{1,0:T(8,128)(2,1)S(1)} %add_convert_fusion.3), channel_id=1, source_target_pairs={{0,2},{1,3},{2,0},{3,1},{4,6},{5,7},{6,4},{7,5},{8,10},{9,11},{10,... | collective-permute-start | bytes 1572872 | tf_op jit(solution)/shard_map/ppermute | solution.py:208
  144.5 13.5 %collective-permute-start.26 = (bf16[128,2048]{1,0:T(8,128)(2,1)S(1)}, bf16[128,2048]{1,0:T(8,128)(2,1)S(1)}, u32[]{:S(2)}, u32[]{:S(2)}) collective-permute-start(bf16[128,2048]{1,0:T(8,128)(2,1)S(1)} %add_convert_fusion.1), channel_id=1, source_target_pairs={{2,4},{3,5},{4,2},{5,3},{10,12},{11,13},{12,10},{13,11},{18,20},{1... | collective-permute-start | bytes 1572872 | tf_op jit(solution)/shard_map/ppermute | solution.py:208
  (23 other events, 253.5 us)

commit v4 on v3

--- a/solution.py
+++ b/solution.py
@@ -181,16 +181,27 @@
     return (mixed, grad_a, grad_b)
 
 
+def count_before(flags):
+    length = flags.shape[0]
+    earlier = jnp.tril(jnp.ones((length, length), jnp.bfloat16), -1)
+    return jnp.dot(earlier, flags.astype(jnp.bfloat16), preferred_element_type=jnp.float32)
+
+
 def dense_route_weights(routing, weights, choice, table, capacity):
-    holds = (routing[:, :, None] == table[None, None, :]).astype(jnp.int32)
-    copies = jnp.sum(holds, axis=2)
+    slot_total = table.shape[0]
+    experts, choice, weights = routing.T, choice.T, weights.T
+    holds = [(experts == table[s]).astype(jnp.int32) for s in range(slot_total)]
+    copies = sum(holds)
     wanted = choice % copies
-    before = jnp.cumsum(holds, axis=2) - holds
-    picked = holds * (before == wanted[:, :, None]).astype(jnp.int32)
-    taken = jnp.sum(picked, axis=1)
-    rank = jnp.cumsum(taken, axis=0) - taken
-    route_weight = jnp.sum(picked.astype(jnp.float32) * weights[:, :, None], axis=1)
-    return jnp.where(rank < capacity, route_weight, 0.0)
+    before = jnp.zeros_like(experts)
+    taken, route_weight = [], []
+    for hold in holds:
+        picked = (hold == 1) & (before == wanted)
+        before = before + hold
+        taken.append(jnp.any(picked, axis=0))
+        route_weight.append(jnp.sum(jnp.where(picked, weights, 0.0), axis=0))
+    rank = count_before(jnp.stack(taken, axis=1)).T
+    return jnp.where(rank < capacity, jnp.stack(route_weight), 0.0)
 
 
 def z_pairs(*moves):
@@ -208,8 +219,8 @@
     return lax.ppermute(array, "expert", pairs)
 
 
-def after(array, *earlier):
-    return lax.optimization_barrier((array,) + earlier)[0]
+def fence(*arrays):
+    return lax.optimization_barrier(arrays)
 
 
 def add_rounded(*terms):
@@ -279,70 +290,79 @@
     def forward(rows):
         return expert_apply_forward(rows, gate_up, down, adapt_a, adapt_b)
 
+    def chip_part(layer_output, w):
+        part = (w * layer_output.astype(jnp.float32)).astype(jnp.bfloat16)
+        return add_rounded(part[:tok_rows], send(part[tok_rows:], SIBLING))
+
+    def backward(rows, cot, w, kept):
+        scaled = (w * cot.astype(jnp.float32)).astype(jnp.bfloat16)
+        return expert_backward(rows, scaled, down, adapt_b, kept)
+
     tok_swap = send(tokens, ALL_SWAP)
     tok_mid = send(tokens, MID_SWAP)
     rows0 = pair(tokens)
-    weight_table = dense_route_weights(
-        after(routing, rows0),
-        router_route_weights,
-        route_replica_choice,
-        device_expert_table,
-        capacity,
-    ).T
-    weight_table = doubled(doubled(weight_table, 1), 2)
+    table = dense_route_weights(
+        routing, router_route_weights, route_replica_choice, device_expert_table, capacity
+    )
+    table = doubled(table, 1)
     out0, kept0 = forward(rows0)
-
-    tok_out2 = send(after(tok_mid, tok_swap), OUTWARD)
-    tok_mid2 = send(after(tok_swap, tok_mid), MID_SWAP)
-    cot_in = send(after(cotangent, tok_swap, tok_mid), INWARD)
-    weight_table = doubled(after(weight_table, tok_swap, tok_mid), 4)
-    rows1 = pair(after(tok_swap, tok_mid))
+    tok_swap, tok_mid, table, out0 = fence(tok_swap, tok_mid, table, out0)
+
+    tok_out2 = send(tok_mid, OUTWARD)
+    tok_mid2 = send(tok_swap, MID_SWAP)
+    cot_in = send(cotangent, INWARD)
+    table = doubled(table, 2)
+    rows1 = pair(tok_swap)
     out1, kept1 = forward(rows1)
-
-    tok_out3 = send(after(tok_mid2, tok_out2), OUTWARD)
-    cot_mid = send(after(cotangent, tok_mid2, tok_out2, cot_in), MID_SWAP)
+    tok_mid, tok_out2, tok_mid2, cot_in, table, out1, cotangent = fence(
+        tok_mid, tok_out2, tok_mid2, cot_in, table, out1, cotangent
+    )
+
+    tok_out3 = send(tok_mid2, OUTWARD)
+    cot_mid = send(cotangent, MID_SWAP)
+    table = doubled(table, 4)
     rows2 = pair(jnp.where(inner, tok_mid, tok_out2))
     out2, kept2 = forward(rows2)
-
-    cot_out = send(after(cotangent, tok_out3, cot_mid), OUTWARD)
-    cot_mid2 = send(after(cot_in, tok_out3, cot_mid), MID_SWAP)
+    tok_mid2, tok_out3, cot_in, cot_mid, table, out2, cotangent = fence(
+        tok_mid2, tok_out3, cot_in, cot_mid, table, out2, cotangent
+    )
+
+    cot_out = send(cotangent, OUTWARD)
+    cot_mid2 = send(cot_in, MID_SWAP)
     rows3 = pair(jnp.where(inner, tok_mid2, tok_out3))
+    weights = [w[:, None] for w in stage_weights(table, inner, me)]
     out3, kept3 = forward(rows3)
-
-    weights = [w[:, None] for w in stage_weights(weight_table, inner, me)]
-
-    def chip_part(layer_output, w):
-        part = (w * layer_output.astype(jnp.float32)).astype(jnp.bfloat16)
-        return add_rounded(part[:tok_rows], send(part[tok_rows:], SIBLING))
-
     part3 = chip_part(out3, weights[3])
+    part2 = chip_part(out2, weights[2])
+    cot_in, cot_out, cot_mid, cot_mid2, part2, part3, out0, out1, cotangent = fence(
+        cot_in, cot_out, cot_mid, cot_mid2, part2, part3, out0, out1, cotangent
+    )
+
+    cot_out2 = send(cot_mid, OUTWARD)
     third_in = send(part3, INWARD)
-    part2 = chip_part(out2, weights[2])
     part1 = chip_part(out1, weights[1])
     part0 = chip_part(out0, weights[0])
-
-    cot_out2 = send(after(cot_mid, cot_out), OUTWARD)
-    third_mid = send(after(add_rounded(part3, third_in), cot_mid2), MID_SWAP)
-    second_in = send(after(part2, third_in), INWARD)
-    cot_out3 = send(after(cot_mid2, cot_out2), OUTWARD)
-    second_mid = send(after(add_rounded(part2, second_in), third_mid), MID_SWAP)
-    first_swap = send(after(add_rounded(part1, third_mid), second_in, cot_out3), ALL_SWAP)
+    first_a, first_b = backward(rows0, pair(cotangent), weights[0], kept0)
+    more_a, more_b = backward(rows1, pair(jnp.where(inner, cot_in, cot_out)), weights[1], kept1)
+    grad_a, grad_b = first_a + more_a, first_b + more_b
+    cot_mid, cot_mid2, cot_out2, third_in, part0, part1, part2, part3, grad_a, grad_b = fence(
+        cot_mid, cot_mid2, cot_out2, third_in, part0, part1, part2, part3, grad_a, grad_b
+    )
+
+    cot_out3 = send(cot_mid2, OUTWARD)
+    third_mid = send(add_rounded(part3, third_in), MID_SWAP)
+    second_in = send(part2, INWARD)
+    more_a, more_b = backward(rows2, pair(jnp.where(inner, cot_mid, cot_out2)), weights[2], kept2)
+    grad_a, grad_b = grad_a + more_a, grad_b + more_b
+    cot_mid2, cot_out3, third_mid, second_in, part0, part1, part2, grad_a, grad_b = fence(
+        cot_mid2, cot_out3, third_mid, second_in, part0, part1, part2, grad_a, grad_b
+    )
+
+    first_swap = send(add_rounded(part1, third_mid), ALL_SWAP)
+    second_mid = send(add_rounded(part2, second_in), MID_SWAP)
+    more_a, more_b = backward(rows3, pair(jnp.where(inner, cot_mid2, cot_out3)), weights[3], kept3)
+    grad_a, grad_b = group_sum(grad_a + more_a, grad_b + more_b)
     mixed = add_rounded(part0, first_swap, second_mid)
-
-    cot_stages = [
-        pair(after(cotangent, tok_swap)),
-        pair(jnp.where(inner, cot_in, cot_out)),
-        pair(jnp.where(inner, cot_mid, cot_out2)),
-        pair(jnp.where(inner, cot_mid2, cot_out3)),
-    ]
-    row_stages = [rows0, rows1, rows2, rows3]
-    saved = [kept0, kept1, kept2, kept3]
-    grad_a, grad_b = 0.0, 0.0
-    for rows, cot, w, kept in zip(row_stages, cot_stages, weights, saved):
-        scaled = (w * cot.astype(jnp.float32)).astype(jnp.bfloat16)
-        more_a, more_b = expert_backward(rows, scaled, down, adapt_b, kept)
-        grad_a, grad_b = grad_a + more_a, grad_b + more_b
-    grad_a, grad_b = group_sum(grad_a, grad_b)
     return mixed, grad_a[None], grad_b[None]
 
 

time: 163 us -> 169 us (1.037); the launches traced: 163 us -> 167 us
  waiting for transfers between devices: 65.4 us -> 52.3 us
  matrix products: 32.3 us -> 41.2 us
  other arithmetic: 5.35 us -> 13.2 us
    ppermute x31, waiting for transfers between devices: 56 us -> 45 us  [send(): return lax.ppermute(array, 'expert', pairs)]
    dot_general x4, matrix products: 10.3 us -> 16.3 us  [expert_apply_forward(): jnp.dot(rows_in, gate_up, preferred_element_type=jnp.float32)]
    reduce_or x0 -> x2, other arithmetic: none -> 5.95 us  [dense_route_weights(): taken.append(jnp.any(picked, axis=0))]
    ppermute x6, waiting for transfers between devices: 9.45 us -> 7.24 us  [swap_sum(): other = lax.ppermute(rounded.astype(jnp.bfloat16), 'dp', pairs)]
    dot_general x4, matrix products: 4.22 us -> 6.15 us  [expert_apply_forward(): jnp.dot(hidden, down, preferred_element_type=jnp.float32)]
  transfers between devices with their start and end apart: 37 -> 37, of which waited for: 14 -> 12; matrix products, arithmetic and copies ran while one was open for 26% -> 35% of each run, Pallas kernels for 0% -> 0%
where the time goes in v4:
time: 169 us; the launch traced here: 167 us
  starting transfers between devices  52.3 us (31%)
  waiting for transfers between devices  52.3 us (31%)
  matrix products  41.2 us (24%)
  other arithmetic  13.2 us (8%)
  local copies, waits for them, and re-layouts  6.37 us (4%)
    ppermute x31, waiting for transfers between devices, send(): return lax.ppermute(array, 'expert', pairs)  45 us
    ppermute x31, starting transfers between devices, send(): return lax.ppermute(array, 'expert', pairs)  44.8 us
    dot_general x4, matrix products, expert_apply_forward(): jnp.dot(rows_in, gate_up, preferred_element_type=jnp.float32)  16.3 us
    ppermute x6, starting transfers between devices, swap_sum(): other = lax.ppermute(rounded.astype(jnp.bfloat16), 'dp', pairs)  7.47 us
    ppermute x6, waiting for transfers between devices, swap_sum(): other = lax.ppermute(rounded.astype(jnp.bfloat16), 'dp', pairs)  7.24 us
    dot_general x4, matrix products, expert_apply_forward(): jnp.dot(hidden, down, preferred_element_type=jnp.float32)  6.15 us
    dot_general x4, matrix products, expert_backward(): lax.dot_general(scaled, down, (((1,), (1,)), ((), ())), preferred_element...  6.04 us
    reduce_or x2, other arithmetic, dense_route_weights(): taken.append(jnp.any(picked, axis=0))  5.95 us
  transfers between devices with their start and end apart: 37, of which 12 were waited for; matrix products, arithmetic and copies ran while one was open for 35% of the time, Pallas kernels for 0%

profile of v4, /device:TPU:0, one launch (start us, length us, event | category | flops | bytes accessed | tf_op | source)
XLA Modules:
  0.0 167.0 jit_solution(7680127247770231980)
XLA Ops:
  1.2 2.7 %collective-permute-start = (bf16[128,2048]{1,0:T(8,128)(2,1)}, bf16[128,2048]{1,0:T(8,128)(2,1)}, u32[]{:S(2)}, u32[]{:S(2)}) collective-permute-start(bf16[128,2048]{1,0:T(8,128)(2,1)} %param.10), channel_id=1, source_target_pairs={{0,2},{1,3},{2,0},{3,1},{4,6},{5,7},{6,4},{7,5},{8,10},{9,11},{10,... | collective-permute-start | bytes 1572872 | tf_op jit(solution)/shard_map/ppermute | solution.py:219
  6.9 5.9 %fusion.207 = (pred[128]{0:T(512)(128)(4,1)S(1)}, pred[8,128]{1,0:T(8,128)(4,1)S(1)}, s32[8,128]{1,0:T(8,128)S(1)}, pred[128,8]{0,1:T(8,128)(4,1)S(1)}, pred[128...) fusion(s32[128,8]{0,1:T(8,128)} %param.14, ...), kind=kLoop, calls=%fused_computation.318 | loop fusion | flops 37760 | bytes 20640 | tf_op jit(solution)/shard_map/reduce_or | solution.py:201
  16.7 4.6 %fusion.6 = f32[256,1536]{1,0:T(8,128)S(1)} fusion(bf16[256,2048]{1,0:T(8,128)(2,1)S(1)} %constant_dynamic-update-slice_fusion, bf16[1,2048,1536]{2,1,0:T(8,128)(2,1)} %param.16), kind=kOutput, calls=%fused_computation.6 | convolution fusion | flops 1610612736 | bytes 8912896 | tf_op jit(solution)/shard_map/dot_general | solution.py:34
  22.0 2.0 %fusion.24 = bf16[256,2048]{1,0:T(8,128)(2,1)} fusion(bf16[1,768,2048]{2,1,0:T(8,128)(2,1)S(1)} %copy-done, f32[256,768]{1,0:T(8,128)S(1)} %slice_add_fusion.6, f32[256,768]{1,0:T(8,128)S(1)} %slice_add_fusion.7), kind=kOutput, calls=%fused_computation.24 | convolution fusion | flops 807010304 | bytes 5767168 | tf_op jit(solution)/shard_map/dot_general | solution.py:46
  24.4 6.3 %collective-permute-start.6 = (bf16[128,2048]{1,0:T(8,128)(2,1)}, bf16[128,2048]{1,0:T(8,128)(2,1)}, u32[]{:S(2)}, u32[]{:S(2)}) collective-permute-start(bf16[128,2048]{1,0:T(8,128)(2,1)} %param.11), channel_id=1, source_target_pairs={{0,2},{1,3},{6,4},{7,5},{8,10},{9,11},{14,12},{15,13},{16,18},{17,... | collective-permute-start | bytes 1572872 | tf_op jit(solution)/shard_map/ppermute | solution.py:219
  34.7 7.1 %collective-permute-done.7 = f32[16,128]{1,0:T(8,128)S(1)} collective-permute-done((f32[16,128]{1,0:T(8,128)S(1)}, f32[16,128]{1,0:T(8,128)S(1)}, u32[]{:S(2)}, u32[]{:S(2)}) %collective-permute-start.7) | collective-permute-done | bytes 8224 | tf_op jit(solution)/shard_map/ppermute | solution.py:219
  42.9 5.0 %fusion.4 = f32[256,1536]{1,0:T(8,128)S(1)} fusion(bf16[256,2048]{1,0:T(8,128)(2,1)S(1)} %constant_dynamic-update-slice_fusion.2, bf16[1,2048,1536]{2,1,0:T(8,128)(2,1)} %param.16), kind=kOutput, calls=%fused_computation.4 | convolution fusion | flops 1610612736 | bytes 8912896 | tf_op jit(solution)/shard_map/dot_general | solution.py:34
  48.9 2.0 %fusion.27 = bf16[256,2048]{1,0:T(8,128)(2,1)} fusion(bf16[1,768,2048]{2,1,0:T(8,128)(2,1)S(1)} %copy-done, f32[256,768]{1,0:T(8,128)S(1)} %slice_add_fusion.4, f32[256,768]{1,0:T(8,128)S(1)} %slice_add_fusion.5), kind=kOutput, calls=%fused_computation.25 | convolution fusion | flops 807010304 | bytes 5767168 | tf_op jit(solution)/shard_map/dot_general | solution.py:46
  51.9 3.1 %collective-permute-start.11 = (f32[32,128]{1,0:T(8,128)S(1)}, f32[32,128]{1,0:T(8,128)S(1)}, u32[]{:S(2)}, u32[]{:S(2)}) collective-permute-start(f32[32,128]{1,0:T(8,128)S(1)} %pad_maximum_fusion.9), channel_id=1, source_target_pairs={{0,4},{1,5},{2,6},{3,7},{4,0},{5,1},{6,2},{7,3},{8,12},{9,13},{10,... | collective-permute-start | bytes 49160 | tf_op jit(solution)/shard_map/ppermute | solution.py:219
  57.2 1.8 %convolution_convert_fusion.1 = bf16[256,128]{0,1:T(8,128)(2,1)S(1)} fusion(bf16[1,2048,128]{2,1,0:T(8,128)(2,1)} %param.18, bf16[128,2048]{1,0:T(8,128)(2,1)} %collective-permute-done.12, bf16[128,2048]{1,0:T(8,128)(2,1)} %broadcast_select_fusion.4), kind=kOutput, calls=%fused_computation.64 | convolution fusion | flops 136347648 | bytes 1638400 | tf_op jit(solution)/shard_map/dot_general | solution.py:31
  59.0 4.9 %fusion.2 = f32[256,1536]{1,0:T(8,128)S(1)} fusion(bf16[1,2048,1536]{2,1,0:T(8,128)(2,1)} %param.16, bf16[128,2048]{1,0:T(8,128)(2,1)} %collective-permute-done.12, bf16[128,2048]{1,0:T(8,128)(2,1)} %broadcast_select_fusion.4), kind=kOutput, calls=%fused_computation.2 | convolution fusion | flops 1612709888 | bytes 8912896 | tf_op jit(solution)/shard_map/dot_general | solution.py:34
  65.6 6.2 %collective-permute-done.9 = bf16[128,2048]{1,0:T(8,128)(2,1)S(1)} collective-permute-done((bf16[128,2048]{1,0:T(8,128)(2,1)}, bf16[128,2048]{1,0:T(8,128)(2,1)S(1)}, u32[]{:S(2)}, u32[]{:S(2)}) %collective-permute-start.9) | collective-permute-done | bytes 524320 | tf_op jit(solution)/shard_map/ppermute | solution.py:219
  74.4 1.8 %fusion = f32[256,1536]{1,0:T(8,128)S(1)} fusion(bf16[1,2048,1536]{2,1,0:T(8,128)(2,1)S(1)} %bitcast.408, bf16[128,2048]{1,0:T(8,128)(2,1)S(1)} %collective-permute-done.16, bf16[128,2048]{1,0:T(8,128)(2,1)S(1)} %broadcast_select_fusion.3), kind=kOutput, calls=%fused_computation | convolution fusion | flops 1612709888 | bytes 8912896 | tf_op jit(solution)/shard_map/dot_general | solution.py:34
  80.6 13.8 %collective-permute-done.13 = bf16[128,2048]{1,0:T(8,128)(2,1)S(1)} collective-permute-done((bf16[128,2048]{1,0:T(8,128)(2,1)}, bf16[128,2048]{1,0:T(8,128)(2,1)S(1)}, u32[]{:S(2)}, u32[]{:S(2)}) %collective-permute-start.13) | collective-permute-done | bytes 524320 | tf_op jit(solution)/shard_map/ppermute | solution.py:219
  97.6 7.1 %collective-permute-start.19 = (bf16[128,2048]{1,0:T(8,128)(2,1)S(1)}, bf16[128,2048]{1,0:T(8,128)(2,1)S(1)}, u32[]{:S(2)}, u32[]{:S(2)}) collective-permute-start(bf16[128,2048]{1,0:T(8,128)(2,1)S(1)} %add_convert_fusion.6), channel_id=1, source_target_pairs={{0,2},{1,3},{6,4},{7,5},{8,10},{9,11},{14,12},{15,13},{16,18},{17,... | collective-permute-start | bytes 1572872 | tf_op jit(solution)/shard_map/ppermute | solution.py:219
  104.7 2.3 %multiply_convert_fusion.18 = (bf16[256,768]{1,0:T(8,128)(2,1)S(1)}, bf16[256,768]{1,0:T(8,128)(2,1)S(1)}) fusion(f32[256,768]{1,0:T(8,128)S(1)} %copy-done.12, f32[256,768]{1,0:T(8,128)S(1)} %copy-done.14, bf16[1,768,2048]{2,1,0:T(8,128)(2,1)S(1)} %copy-done, bf16[128,2048]{1,0:T(8,128)(2,1)S(1)} %collective-permute-done.22, ...), kind=kOutput, calls=%fused_computation.111 | convolution fusion | flops 811008000 | bytes 6554624 | tf_op jit(solution)/shard_map/dot_general | solution.py:56
  111.7 3.1 %collective-permute-done.18 = bf16[128,2048]{1,0:T(8,128)(2,1)S(1)} collective-permute-done((bf16[128,2048]{1,0:T(8,128)(2,1)S(1)}, bf16[128,2048]{1,0:T(8,128)(2,1)S(1)}, u32[]{:S(2)}, u32[]{:S(2)}) %collective-permute-start.18) | collective-permute-done | bytes 524320 | tf_op jit(solution)/shard_map/ppermute | solution.py:219
  118.3 7.4 %collective-permute-start.26 = (bf16[128,2048]{1,0:T(8,128)(2,1)S(1)}, bf16[128,2048]{1,0:T(8,128)(2,1)S(1)}, u32[]{:S(2)}, u32[]{:S(2)}) collective-permute-start(bf16[128,2048]{1,0:T(8,128)(2,1)S(1)} %add_convert_fusion.7), channel_id=1, source_target_pairs={{0,2},{1,3},{6,4},{7,5},{8,10},{9,11},{14,12},{15,13},{16,18},{17,... | collective-permute-start | bytes 1572872 | tf_op jit(solution)/shard_map/ppermute | solution.py:219
  127.5 1.7 %fusion.82 = f32[2048,128]{1,0:T(8,128)S(1)} fusion(bf16[128,2048]{1,0:T(8,128)(2,1)} %collective-permute-done.12, bf16[128,2048]{1,0:T(8,128)(2,1)} %broadcast_select_fusion.4, f32[256,64]{1,0:T(8,128)S(1)} %fusion.96, f32[256,64]{1,0:T(8,128)S(1)} %fusion.108), kind=kOutput, calls=%fused_computation.148 | convolution fusion | flops 136413184 | bytes 2228224 | tf_op jit(solution)/shard_map/dot_general | solution.py:85
  129.8 6.2 %collective-permute-done.24 = bf16[128,2048]{1,0:T(8,128)(2,1)S(1)} collective-permute-done((bf16[128,2048]{1,0:T(8,128)(2,1)S(1)}, bf16[128,2048]{1,0:T(8,128)(2,1)S(1)}, u32[]{:S(2)}, u32[]{:S(2)}) %collective-permute-start.24) | collective-permute-done | bytes 524320 | tf_op jit(solution)/shard_map/ppermute | solution.py:219
  137.5 2.5 %collective-permute-start.28 = (bf16[128,2048]{1,0:T(8,128)(2,1)S(1)}, bf16[128,2048]{1,0:T(8,128)(2,1)S(1)}, u32[]{:S(2)}, u32[]{:S(2)}) collective-permute-start(bf16[128,2048]{1,0:T(8,128)(2,1)S(1)} %add_convert_fusion.2), channel_id=1, source_target_pairs={{0,2},{1,3},{2,0},{3,1},{4,6},{5,7},{6,4},{7,5},{8,10},{9,11},{10,... | collective-permute-start | bytes 1572872 | tf_op jit(solution)/shard_map/ppermute | solution.py:219
  147.5 5.1 %collective-permute-done.28 = bf16[128,2048]{1,0:T(8,128)(2,1)S(1)} collective-permute-done((bf16[128,2048]{1,0:T(8,128)(2,1)S(1)}, bf16[128,2048]{1,0:T(8,128)(2,1)S(1)}, u32[]{:S(2)}, u32[]{:S(2)}) %collective-permute-start.28) | collective-permute-done | bytes 524320 | tf_op jit(solution)/shard_map/ppermute | solution.py:219
  157.7 3.2 %collective-permute-done.34 = bf16[640,128]{1,0:T(8,128)(2,1)S(1)} collective-permute-done((bf16[640,128]{1,0:T(8,128)(2,1)S(1)}, bf16[640,128]{1,0:T(8,128)(2,1)S(1)}, u32[]{:S(2)}, u32[]{:S(2)}) %collective-permute-start.34) | collective-permute-done | bytes 163872 | tf_op jit(solution)/shard_map/ppermute | solution.py:253
  161.0 3.0 %collective-permute-done.36 = bf16[2,64,768]{2,1,0:T(8,128)(2,1)S(1)} collective-permute-done((bf16[2,64,768]{2,1,0:T(8,128)(2,1)S(1)}, bf16[2,64,768]{2,1,0:T(8,128)(2,1)S(1)}, u32[]{:S(2)}, u32[]{:S(2)}) %collective-permute-start.36) | collective-permute-done | bytes 196640 | tf_op jit(solution)/shard_map/ppermute | solution.py:253
  (187 shorter events, 56.4 us)
Async XLA Ops:
  0.6 14.5 %collective-permute-start.3 = (bf16[128,2048]{1,0:T(8,128)(2,1)}, bf16[128,2048]{1,0:T(8,128)(2,1)}, u32[]{:S(2)}, u32[]{:S(2)}) collective-permute-start(bf16[128,2048]{1,0:T(8,128)(2,1)} %param.10), channel_id=1, source_target_pairs={{0,1},{1,0},{2,3},{3,2},{4,5},{5,4},{6,7},{7,6},{8,9},{9,8},{10,11... | collective-permute-start | bytes 1572872 | tf_op jit(solution)/shard_map/ppermute | solution.py:219
  1.2 22.9 %collective-permute-start = (bf16[128,2048]{1,0:T(8,128)(2,1)}, bf16[128,2048]{1,0:T(8,128)(2,1)}, u32[]{:S(2)}, u32[]{:S(2)}) collective-permute-start(bf16[128,2048]{1,0:T(8,128)(2,1)} %param.10), channel_id=1, source_target_pairs={{0,2},{1,3},{2,0},{3,1},{4,6},{5,7},{6,4},{7,5},{8,10},{9,11},{10,... | collective-permute-start | bytes 1572872 | tf_op jit(solution)/shard_map/ppermute | solution.py:219
  3.8 20.2 %collective-permute-start.1 = (bf16[128,2048]{1,0:T(8,128)(2,1)}, bf16[128,2048]{1,0:T(8,128)(2,1)}, u32[]{:S(2)}, u32[]{:S(2)}) collective-permute-start(bf16[128,2048]{1,0:T(8,128)(2,1)} %param.10), channel_id=1, source_target_pairs={{2,4},{3,5},{4,2},{5,3},{10,12},{11,13},{12,10},{13,11},{18,20},{1... | collective-permute-start | bytes 1572872 | tf_op jit(solution)/shard_map/ppermute | solution.py:219
  24.0 17.7 %collective-permute-start.8 = (bf16[128,2048]{1,0:T(8,128)(2,1)}, bf16[128,2048]{1,0:T(8,128)(2,1)}, u32[]{:S(2)}, u32[]{:S(2)}) collective-permute-start(bf16[128,2048]{1,0:T(8,128)(2,1)} %collective-permute-done), channel_id=1, source_target_pairs={{0,1},{1,0},{2,3},{3,2},{4,5},{5,4},{6,7},{7,6},{8,9},{9,8},{10,11... | collective-permute-start | bytes 1572872 | tf_op jit(solution)/shard_map/ppermute | solution.py:219
  24.4 26.5 %collective-permute-start.6 = (bf16[128,2048]{1,0:T(8,128)(2,1)}, bf16[128,2048]{1,0:T(8,128)(2,1)}, u32[]{:S(2)}, u32[]{:S(2)}) collective-permute-start(bf16[128,2048]{1,0:T(8,128)(2,1)} %param.11), channel_id=1, source_target_pairs={{0,2},{1,3},{6,4},{7,5},{8,10},{9,11},{14,12},{15,13},{16,18},{17,... | collective-permute-start | bytes 1572872 | tf_op jit(solution)/shard_map/ppermute | solution.py:219
  30.8 11.0 %collective-permute-start.7 = (f32[16,128]{1,0:T(8,128)S(1)}, f32[16,128]{1,0:T(8,128)S(1)}, u32[]{:S(2)}, u32[]{:S(2)}) collective-permute-start(f32[16,128]{1,0:T(8,128)S(1)} %pad_maximum_fusion.10), channel_id=1, source_target_pairs={{0,2},{1,3},{2,0},{3,1},{4,6},{5,7},{6,4},{7,5},{8,10},{9,11},{10,... | collective-permute-start | bytes 24584 | tf_op jit(solution)/shard_map/ppermute | solution.py:219
  31.9 19.1 %collective-permute-start.5 = (bf16[128,2048]{1,0:T(8,128)(2,1)}, bf16[128,2048]{1,0:T(8,128)(2,1)}, u32[]{:S(2)}, u32[]{:S(2)}) collective-permute-start(bf16[128,2048]{1,0:T(8,128)(2,1)} %collective-permute-done), channel_id=1, source_target_pairs={{2,4},{3,5},{4,2},{5,3},{10,12},{11,13},{12,10},{13,11},{18,20},{1... | collective-permute-start | bytes 1572872 | tf_op jit(solution)/shard_map/ppermute | solution.py:219
  33.4 17.6 %collective-permute-start.4 = (bf16[128,2048]{1,0:T(8,128)(2,1)}, bf16[128,2048]{1,0:T(8,128)(2,1)S(1)}, u32[]{:S(2)}, u32[]{:S(2)}) collective-permute-start(bf16[128,2048]{1,0:T(8,128)(2,1)} %collective-permute-done.1), channel_id=1, source_target_pairs={{2,0},{3,1},{4,6},{5,7},{10,8},{11,9},{12,14},{13,15},{18,16},{19,... | collective-permute-start | bytes 1572872 | tf_op jit(solution)/shard_map/ppermute | solution.py:219
  55.0 10.6 %collective-permute-start.10 = (bf16[128,2048]{1,0:T(8,128)(2,1)}, bf16[128,2048]{1,0:T(8,128)(2,1)S(1)}, u32[]{:S(2)}, u32[]{:S(2)}) collective-permute-start(bf16[128,2048]{1,0:T(8,128)(2,1)} %param.11), channel_id=1, source_target_pairs={{2,4},{3,5},{4,2},{5,3},{10,12},{11,13},{12,10},{13,11},{18,20},{1... | collective-permute-start | bytes 1572872 | tf_op jit(solution)/shard_map/ppermute | solution.py:219
  55.6 16.2 %collective-permute-start.9 = (bf16[128,2048]{1,0:T(8,128)(2,1)}, bf16[128,2048]{1,0:T(8,128)(2,1)S(1)}, u32[]{:S(2)}, u32[]{:S(2)}) collective-permute-start(bf16[128,2048]{1,0:T(8,128)(2,1)} %collective-permute-done.5), channel_id=1, source_target_pairs={{2,0},{3,1},{4,6},{5,7},{10,8},{11,9},{12,14},{13,15},{18,16},{19,... | collective-permute-start | bytes 1572872 | tf_op jit(solution)/shard_map/ppermute | solution.py:219
  78.1 16.3 %collective-permute-start.13 = (bf16[128,2048]{1,0:T(8,128)(2,1)}, bf16[128,2048]{1,0:T(8,128)(2,1)S(1)}, u32[]{:S(2)}, u32[]{:S(2)}) collective-permute-start(bf16[128,2048]{1,0:T(8,128)(2,1)} %param.11), channel_id=1, source_target_pairs={{2,0},{3,1},{4,6},{5,7},{10,8},{11,9},{12,14},{13,15},{18,16},{19,... | collective-permute-start | bytes 1572872 | tf_op jit(solution)/shard_map/ppermute | solution.py:219
  79.5 14.9 %collective-permute-start.14 = (bf16[128,2048]{1,0:T(8,128)(2,1)}, bf16[128,2048]{1,0:T(8,128)(2,1)S(1)}, u32[]{:S(2)}, u32[]{:S(2)}) collective-permute-start(bf16[128,2048]{1,0:T(8,128)(2,1)} %collective-permute-done.6), channel_id=1, source_target_pairs={{2,4},{3,5},{4,2},{5,3},{10,12},{11,13},{12,10},{13,11},{18,20},{1... | collective-permute-start | bytes 1572872 | tf_op jit(solution)/shard_map/ppermute | solution.py:219
  94.5 13.0 %collective-permute-start.23 = (bf16[128,2048]{1,0:T(8,128)(2,1)S(1)}, bf16[128,2048]{1,0:T(8,128)(2,1)S(1)}, u32[]{:S(2)}, u32[]{:S(2)}) collective-permute-start(bf16[128,2048]{1,0:T(8,128)(2,1)S(1)} %broadcast_select_fusion.2), channel_id=1, source_target_pairs={{0,1},{1,0},{2,3},{3,2},{4,5},{5,4},{6,7},{7,6},{8,9},{9,8},{10,11... | collective-permute-start | bytes 1572872 | tf_op jit(solution)/shard_map/ppermute | solution.py:219
  95.4 16.0 %collective-permute-start.21 = (bf16[128,2048]{1,0:T(8,128)(2,1)S(1)}, bf16[128,2048]{1,0:T(8,128)(2,1)S(1)}, u32[]{:S(2)}, u32[]{:S(2)}) collective-permute-start(bf16[128,2048]{1,0:T(8,128)(2,1)S(1)} %slice.213), channel_id=1, source_target_pairs={{0,1},{1,0},{2,3},{3,2},{4,5},{5,4},{6,7},{7,6},{8,9},{9,8},{10,11... | collective-permute-start | bytes 1572872 | tf_op jit(solution)/shard_map/ppermute | solution.py:219
  95.8 15.7 %collective-permute-start.20 = (bf16[128,2048]{1,0:T(8,128)(2,1)S(1)}, bf16[128,2048]{1,0:T(8,128)(2,1)S(1)}, u32[]{:S(2)}, u32[]{:S(2)}) collective-permute-start(bf16[128,2048]{1,0:T(8,128)(2,1)S(1)} %slice.211), channel_id=1, source_target_pairs={{0,1},{1,0},{2,3},{3,2},{4,5},{5,4},{6,7},{7,6},{8,9},{9,8},{10,11... | collective-permute-start | bytes 1572872 | tf_op jit(solution)/shard_map/ppermute | solution.py:219
  96.3 18.5 %collective-permute-start.18 = (bf16[128,2048]{1,0:T(8,128)(2,1)S(1)}, bf16[128,2048]{1,0:T(8,128)(2,1)S(1)}, u32[]{:S(2)}, u32[]{:S(2)}) collective-permute-start(bf16[128,2048]{1,0:T(8,128)(2,1)S(1)} %collective-permute-done.10), channel_id=1, source_target_pairs={{2,0},{3,1},{4,6},{5,7},{10,8},{11,9},{12,14},{13,15},{18,16},{19,... | collective-permute-start | bytes 1572872 | tf_op jit(solution)/shard_map/ppermute | solution.py:219
  97.6 18.4 %collective-permute-start.19 = (bf16[128,2048]{1,0:T(8,128)(2,1)S(1)}, bf16[128,2048]{1,0:T(8,128)(2,1)S(1)}, u32[]{:S(2)}, u32[]{:S(2)}) collective-permute-start(bf16[128,2048]{1,0:T(8,128)(2,1)S(1)} %add_convert_fusion.6), channel_id=1, source_target_pairs={{0,2},{1,3},{6,4},{7,5},{8,10},{9,11},{14,12},{15,13},{16,18},{17,... | collective-permute-start | bytes 1572872 | tf_op jit(solution)/shard_map/ppermute | solution.py:219
  116.3 13.5 %collective-permute-start.25 = (bf16[128,2048]{1,0:T(8,128)(2,1)S(1)}, bf16[128,2048]{1,0:T(8,128)(2,1)S(1)}, u32[]{:S(2)}, u32[]{:S(2)}) collective-permute-start(bf16[128,2048]{1,0:T(8,128)(2,1)S(1)} %add_convert_fusion.3), channel_id=1, source_target_pairs={{2,4},{3,5},{4,2},{5,3},{10,12},{11,13},{12,10},{13,11},{18,20},{1... | collective-permute-start | bytes 1572872 | tf_op jit(solution)/shard_map/ppermute | solution.py:219
  117.0 19.0 %collective-permute-start.24 = (bf16[128,2048]{1,0:T(8,128)(2,1)S(1)}, bf16[128,2048]{1,0:T(8,128)(2,1)S(1)}, u32[]{:S(2)}, u32[]{:S(2)}) collective-permute-start(bf16[128,2048]{1,0:T(8,128)(2,1)S(1)} %collective-permute-done.14), channel_id=1, source_target_pairs={{2,0},{3,1},{4,6},{5,7},{10,8},{11,9},{12,14},{13,15},{18,16},{19,... | collective-permute-start | bytes 1572872 | tf_op jit(solution)/shard_map/ppermute | solution.py:219
  118.3 18.9 %collective-permute-start.26 = (bf16[128,2048]{1,0:T(8,128)(2,1)S(1)}, bf16[128,2048]{1,0:T(8,128)(2,1)S(1)}, u32[]{:S(2)}, u32[]{:S(2)}) collective-permute-start(bf16[128,2048]{1,0:T(8,128)(2,1)S(1)} %add_convert_fusion.7), channel_id=1, source_target_pairs={{0,2},{1,3},{6,4},{7,5},{8,10},{9,11},{14,12},{15,13},{16,18},{17,... | collective-permute-start | bytes 1572872 | tf_op jit(solution)/shard_map/ppermute | solution.py:219
  137.5 15.1 %collective-permute-start.28 = (bf16[128,2048]{1,0:T(8,128)(2,1)S(1)}, bf16[128,2048]{1,0:T(8,128)(2,1)S(1)}, u32[]{:S(2)}, u32[]{:S(2)}) collective-permute-start(bf16[128,2048]{1,0:T(8,128)(2,1)S(1)} %add_convert_fusion.2), channel_id=1, source_target_pairs={{0,2},{1,3},{2,0},{3,1},{4,6},{5,7},{6,4},{7,5},{8,10},{9,11},{10,... | collective-permute-start | bytes 1572872 | tf_op jit(solution)/shard_map/ppermute | solution.py:219
  140.2 12.5 %collective-permute-start.29 = (bf16[128,2048]{1,0:T(8,128)(2,1)S(1)}, bf16[128,2048]{1,0:T(8,128)(2,1)S(1)}, u32[]{:S(2)}, u32[]{:S(2)}) collective-permute-start(bf16[128,2048]{1,0:T(8,128)(2,1)S(1)} %add_convert_fusion.1), channel_id=1, source_target_pairs={{2,4},{3,5},{4,2},{5,3},{10,12},{11,13},{12,10},{13,11},{18,20},{1... | collective-permute-start | bytes 1572872 | tf_op jit(solution)/shard_map/ppermute | solution.py:219
  143.1 12.2 %collective-permute-start.35 = (bf16[2,64,768]{2,1,0:T(8,128)(2,1)S(1)}, bf16[2,64,768]{2,1,0:T(8,128)(2,1)S(1)}, u32[]{:S(2)}, u32[]{:S(2)}) collective-permute-start(bf16[2,64,768]{2,1,0:T(8,128)(2,1)S(1)} %fusion.206), channel_id=1, source_target_pairs={{0,16},{8,24},{16,0},{24,8},{1,17},{9,25},{17,1},{25,9},{2,18},{10... | collective-permute-start | bytes 589832 | tf_op jit(solution)/shard_map/ppermute | solution.py:253
  145.4 10.6 %collective-permute-start.31 = (bf16[1408,128]{1,0:T(8,128)(2,1)S(1)}, bf16[1408,128]{1,0:T(8,128)(2,1)S(1)}, u32[]{:S(2)}, u32[]{:S(2)}) collective-permute-start(bf16[1408,128]{1,0:T(8,128)(2,1)S(1)} %fusion.74), channel_id=1, source_target_pairs={{0,8},{8,0},{16,24},{24,16},{1,9},{9,1},{17,25},{25,17},{2,10},{10... | collective-permute-start | bytes 1081352 | tf_op jit(solution)/shard_map/ppermute | solution.py:253
  (34 other events, 230.3 us)

commit v5 on v1

--- a/solution.py
+++ b/solution.py
@@ -1,6 +1,10 @@
+import functools
+
 import jax
 import jax.numpy as jnp
 from jax import lax
+from jax.experimental import pallas as pl
+from jax.experimental.pallas import tpu as pltpu
 from jax.sharding import PartitionSpec as P
 
 ADAPTER_SCALE = 0.5
@@ -181,16 +185,270 @@
     return (mixed, grad_a, grad_b)
 
 
+def dot(a, b, a_dim=1, b_dim=0):
+    return lax.dot_general(
+        a, b, (((a_dim,), (b_dim,)), ((), ())), preferred_element_type=jnp.float32
+    )
+
+
+def first_half(shape):
+    return lax.broadcasted_iota(jnp.int32, shape, 1) < shape[1] // 2
+
+
+def halves(low):
+    gate = first_half(low.shape)
+    zero = jnp.zeros_like(low)
+    return jnp.where(gate, low, zero), jnp.where(gate, zero, low)
+
+
+def column(row):
+    return jnp.transpose(jnp.broadcast_to(row, (row.shape[1], row.shape[1])))[:, :1]
+
+
+def weights_kernel(capacity, table_ref, expert_ref, choice_ref, weight_ref, out_ref):
+    slot_total, tok_rows = out_ref.shape
+    experts, weights = expert_ref[...], weight_ref[...]
+    holds = [experts == table_ref[s] for s in range(slot_total)]
+    counts = [hold.astype(jnp.float32) for hold in holds]
+    copies = sum(counts)
+    choice = choice_ref[...].astype(jnp.float32)
+    wanted = choice - copies * jnp.floor((choice + 0.5) / copies)
+    before = jnp.zeros_like(copies)
+    taken, route_weight = [], []
+    for hold, count in zip(holds, counts):
+        picked = jnp.where(hold & (before == wanted), 1.0, 0.0)
+        before = before + count
+        taken.append(jnp.sum(picked, axis=0, keepdims=True))
+        route_weight.append(jnp.sum(picked * weights, axis=0, keepdims=True))
+    shape = (tok_rows, tok_rows)
+    earlier = lax.broadcasted_iota(jnp.int32, shape, 0) < lax.broadcasted_iota(jnp.int32, shape, 1)
+    rank = dot(
+        jnp.concatenate(taken).astype(jnp.bfloat16),
+        jnp.where(earlier, 1.0, 0.0).astype(jnp.bfloat16),
+    )
+    out_ref[...] = jnp.where(rank < capacity, jnp.concatenate(route_weight), 0.0)
+
+
 def dense_route_weights(routing, weights, choice, table, capacity):
-    holds = (routing[:, :, None] == table[None, None, :]).astype(jnp.int32)
-    copies = jnp.sum(holds, axis=2)
-    wanted = choice % copies
-    before = jnp.cumsum(holds, axis=2) - holds
-    picked = holds * (before == wanted[:, :, None]).astype(jnp.int32)
-    taken = jnp.sum(picked, axis=1)
-    rank = jnp.cumsum(taken, axis=0) - taken
-    route_weight = jnp.sum(picked.astype(jnp.float32) * weights[:, :, None], axis=1)
-    return jnp.where(rank < capacity, route_weight, 0.0)
+    vmem = pl.BlockSpec(memory_space=pltpu.VMEM)
+    return pl.pallas_call(
+        functools.partial(weights_kernel, capacity),
+        out_shape=jax.ShapeDtypeStruct((table.shape[0], routing.shape[0]), jnp.float32),
+        in_specs=[pl.BlockSpec(memory_space=pltpu.SMEM), vmem, vmem, vmem],
+        out_specs=vmem,
+    )(table, routing.T, choice.T, weights.T)
+
+
+def forward_kernel(
+    mine_ref, other_ref, w_ref, adapt_a_ref, gate_ref, up_ref, adapt_b_ref, down_ref,
+    low_ref, active_ref, slope_ref, part_mine_ref, part_other_ref, rows_ref, total_ref,
+):
+    step = pl.program_id(0)
+    half = mine_ref.shape[0]
+
+    @pl.when(step == 0)
+    def _():
+        rows_ref[:half] = mine_ref[...]
+        rows_ref[half:] = other_ref[...]
+        low_ref[...] = dot(rows_ref[...], adapt_a_ref[...]).astype(jnp.bfloat16)
+
+    rows = rows_ref[...]
+    low_gate, low_up = halves(low_ref[...])
+    gate = dot(rows, gate_ref[...]) + ADAPTER_SCALE * dot(low_gate, adapt_b_ref[...])
+    up = dot(rows, up_ref[...]) + ADAPTER_SCALE * dot(low_up, adapt_b_ref[...])
+    sigmoid_gate = jax.nn.sigmoid(gate)
+    active = gate * sigmoid_gate
+    active_ref[...] = active
+    slope_ref[...] = up * (sigmoid_gate * (1.0 + gate * (1.0 - sigmoid_gate)))
+    hidden = (active * up).astype(jnp.bfloat16)
+    more = dot(hidden, down_ref[...])
+
+    @pl.when(step == 0)
+    def _():
+        total_ref[...] = more
+
+    @pl.when(step > 0)
+    def _():
+        total_ref[...] += more
+
+    @pl.when(step == pl.num_programs(0) - 1)
+    def _():
+        out = total_ref[...].astype(jnp.bfloat16).astype(jnp.float32)
+        part_mine_ref[...] = (column(w_ref[0:1]) * out[:half]).astype(jnp.bfloat16)
+        part_other_ref[...] = (column(w_ref[1:2]) * out[half:]).astype(jnp.bfloat16)
+
+
+def whole(shape):
+    return pl.BlockSpec(shape, lambda j: (0,) * len(shape))
+
+
+def columns(rows, width, start=0):
+    return pl.BlockSpec((rows, width), lambda j: (0, start + j))
+
+
+def forward_stage(mine, other, w, gate_up, down, adapt_a, adapt_b, chunk=256):
+    half, features = mine.shape
+    hidden_width = down.shape[0]
+    both, ranks = 2 * half, adapt_a.shape[1]
+    steps = hidden_width // chunk
+    saved = jax.ShapeDtypeStruct((both, hidden_width), jnp.float32)
+    part = jax.ShapeDtypeStruct((half, features), jnp.bfloat16)
+    return pl.pallas_call(
+        forward_kernel,
+        grid=(steps,),
+        out_shape=(jax.ShapeDtypeStruct((both, ranks), jnp.bfloat16), saved, saved, part, part),
+        in_specs=[
+            whole((half, features)),
+            whole((half, features)),
+            whole((2, half)),
+            whole((features, ranks)),
+            columns(features, chunk),
+            columns(features, chunk, steps),
+            columns(ranks, chunk),
+            pl.BlockSpec((chunk, features), lambda j: (j, 0)),
+        ],
+        out_specs=(
+            whole((both, ranks)),
+            columns(both, chunk),
+            columns(both, chunk),
+            whole((half, features)),
+            whole((half, features)),
+        ),
+        scratch_shapes=[
+            pltpu.VMEM((both, features), jnp.bfloat16),
+            pltpu.VMEM((both, features), jnp.float32),
+        ],
+        compiler_params=pltpu.CompilerParams(vmem_limit_bytes=28 * 2**20),
+        cost_estimate=pl.CostEstimate(flops=10**6, bytes_accessed=10**4, transcendentals=0),
+    )(mine, other, w, adapt_a, gate_up, gate_up, adapt_b, down)
+
+
+def backward_kernel(
+    cot_mine_ref, cot_other_ref, w_ref, mine_ref, other_ref, low_ref, active_ref, slope_ref,
+    adapt_b_ref, down_ref, grad_a_ref, grad_b_ref, sum_a_ref, sum_b_ref, scaled_ref, back_ref,
+):
+    step = pl.program_id(0)
+    half = mine_ref.shape[0]
+
+    @pl.when(step == 0)
+    def _():
+        mine = column(w_ref[0:1]) * cot_mine_ref[...].astype(jnp.float32)
+        other = column(w_ref[1:2]) * cot_other_ref[...].astype(jnp.float32)
+        scaled_ref[:half] = mine.astype(jnp.bfloat16)
+        scaled_ref[half:] = other.astype(jnp.bfloat16)
+        back_ref[...] = jnp.zeros_like(back_ref)
+
+    back = dot(scaled_ref[...], down_ref[...], 1, 1)
+    up_grad = (back * active_ref[...]).astype(jnp.bfloat16)
+    gate_grad = (back * slope_ref[...]).astype(jnp.bfloat16)
+    low_gate, low_up = halves(low_ref[...])
+    sum_b_ref[...] = grad_b_ref[...] + ADAPTER_SCALE * (
+        dot(low_gate, gate_grad, 0, 0) + dot(low_up, up_grad, 0, 0)
+    )
+    gate_back = dot(gate_grad, adapt_b_ref[...], 1, 1)
+    up_back = dot(up_grad, adapt_b_ref[...], 1, 1)
+    back_ref[...] += jnp.where(first_half(gate_back.shape), gate_back, up_back)
+
+    @pl.when(step == pl.num_programs(0) - 1)
+    def _():
+        low_grad = (ADAPTER_SCALE * back_ref[...]).astype(jnp.bfloat16)
+        sum_a_ref[...] = (
+            grad_a_ref[...]
+            + dot(mine_ref[...], low_grad[:half], 0, 0)
+            + dot(other_ref[...], low_grad[half:], 0, 0)
+        )
+
+
+def backward_stage(cots, w, rows, saved, down, adapt_b, grads, chunk=256):
+    low, active, slope = saved
+    half, features = rows[0].shape
+    hidden_width = down.shape[0]
+    both, ranks = low.shape
+    block = whole((half, features))
+    grad_a = whole((features, ranks))
+    grad_b = columns(ranks, chunk)
+    return pl.pallas_call(
+        backward_kernel,
+        grid=(hidden_width // chunk,),
+        out_shape=(
+            jax.ShapeDtypeStruct((features, ranks), jnp.float32),
+            jax.ShapeDtypeStruct((ranks, hidden_width), jnp.float32),
+        ),
+        in_specs=[
+            block,
+            block,
+            whole((2, half)),
+            block,
+            block,
+            whole((both, ranks)),
+            columns(both, chunk),
+            columns(both, chunk),
+            columns(ranks, chunk),
+            pl.BlockSpec((chunk, features), lambda j: (j, 0)),
+            grad_a,
+            grad_b,
+        ],
+        out_specs=(grad_a, grad_b),
+        scratch_shapes=[
+            pltpu.VMEM((both, features), jnp.bfloat16),
+            pltpu.VMEM((both, ranks), jnp.float32),
+        ],
+        compiler_params=pltpu.CompilerParams(vmem_limit_bytes=28 * 2**20),
+        cost_estimate=pl.CostEstimate(flops=10**6, bytes_accessed=10**4, transcendentals=0),
+    )(*cots, w, *rows, low, active, slope, adapt_b, down, *grads)
+
+
+def z_pairs(*moves):
+    return [(2 * a + core, 2 * b + core) for a, b in moves for core in (0, 1)]
+
+
+ALL_SWAP = z_pairs((0, 1), (1, 0), (2, 3), (3, 2))
+MID_SWAP = z_pairs((1, 2), (2, 1))
+SIBLING = [(e, e ^ 1) for e in range(8)]
+
+
+def send(array, pairs):
+    return lax.ppermute(array, "expert", pairs)
+
+
+def fence(*arrays):
+    return lax.optimization_barrier(arrays)
+
+
+def add_rounded(*terms):
+    total = terms[0].astype(jnp.float32)
+    for term in terms[1:]:
+        total = total + term.astype(jnp.float32)
+    return total.astype(jnp.bfloat16)
+
+
+def sibling(block):
+    return send(block, SIBLING)
+
+
+def exchanged(weight_table, bit):
+    return send(weight_table, [(e, e ^ bit) for e in range(8)])
+
+
+def near_weights(weight_tables, me):
+    tables = weight_tables.reshape(-1, 8, weight_tables.shape[1])
+    return lax.dynamic_index_in_dim(tables, me, axis=1, keepdims=False)
+
+
+def swap_sum(array, bit):
+    rounded = lax.reduce_precision(array, 8, 7)
+    pairs = [(d, d ^ bit) for d in range(4)]
+    other = lax.ppermute(rounded.astype(jnp.bfloat16), "dp", pairs)
+    return rounded + other.astype(jnp.float32)
+
+
+def group_sum(grad_a, grad_b):
+    rows, rank = grad_a.shape
+    low_rows = (grad_a.size + grad_b.size) // 2 // rank // 16 * 16
+    x_first = swap_sum(swap_sum(grad_a[:low_rows], 1), 2)
+    y_first = swap_sum(swap_sum(grad_a[low_rows:], 2), 1)
+    sum_b = swap_sum(swap_sum(grad_b, 2), 1)
+    return jnp.concatenate([x_first, y_first]), sum_b
 
 
 def dense_body(
@@ -208,26 +466,103 @@
     slot_total = lax.axis_size("expert")
     capacity = tokens.shape[0] * routing.shape[1] // slot_total
     me = lax.axis_index("expert")
-    weight_table = dense_route_weights(
+    chip = me // 2
+    inner = (chip == 1) | (chip == 2)
+    gate_up, down = gate_up_weight[0], down_weight[0]
+    adapt_a = adapter_down_maps[0]
+    adapt_b = adapter_up_maps[0].reshape(adapt_a.shape[1], -1)
+
+    def forward(mine, other, w):
+        low, active, slope, part_mine, part_other = forward_stage(
+            mine, other, w, gate_up, down, adapt_a, adapt_b
+        )
+        return (low, active, slope), part_mine, part_other
+
+    def backward(cots, w, rows, saved, grads):
+        return backward_stage(cots, w, rows, saved, down, adapt_b, grads)
+
+    tok_swap = send(tokens, ALL_SWAP)
+    tok_mid = send(tokens, MID_SWAP)
+    tok_twin = sibling(tokens)
+    table = dense_route_weights(
         routing, router_route_weights, route_replica_choice, device_expert_table, capacity
     )
-    rows = lax.all_gather(tokens, "expert", tiled=True)
-    weight_all = lax.all_gather(weight_table, "expert", tiled=True)
-    w = lax.dynamic_slice_in_dim(weight_all, me, 1, axis=1)
-    cot = lax.all_gather(cotangent, "expert", tiled=True)
-    layer_output, saved = expert_apply_forward(
-        rows, gate_up_weight[0], down_weight[0], adapter_down_maps[0], adapter_up_maps[0]
-    )
-    part = (w * layer_output.astype(jnp.float32)).astype(jnp.bfloat16)
-    mixed = lax.psum_scatter(part, "expert", scatter_dimension=0, tiled=True)
-    scaled = (w * cot.astype(jnp.float32)).astype(jnp.bfloat16)
-    grad_a, grad_b = expert_backward(rows, scaled, down_weight[0], adapter_up_maps[0], saved)
-    grad_a, grad_b = lax.psum((grad_a, grad_b), "dp")
-    return mixed, grad_a[None], grad_b[None]
+    table = jnp.concatenate([table, exchanged(table, 1)])
+    tok_swap, tok_mid, tok_twin, table = fence(tok_swap, tok_mid, tok_twin, table)
+
+    tok_out2 = send(tok_mid, ALL_SWAP)
+    tok_mid2 = send(tok_swap, MID_SWAP)
+    swap_twin = sibling(tok_swap)
+    more_table = exchanged(table, 2)
+    weights0 = near_weights(table, me)
+    saved0, part0, away0 = forward(tokens, tok_twin, weights0)
+    tok_mid, tok_out2, tok_mid2, swap_twin, more_table, part0, away0, cotangent = fence(
+        tok_mid, tok_out2, tok_mid2, swap_twin, more_table, part0, away0, cotangent
+    )
+
+    tok_out3 = send(tok_mid2, ALL_SWAP)
+    cot_mid = send(cotangent, MID_SWAP)
+    tok_second = jnp.where(inner, tok_mid, tok_out2)
+    second_twin = sibling(tok_second)
+    weights1 = near_weights(more_table, me)
+    far_table = exchanged(jnp.concatenate([table, more_table]), 4)
+    saved1, part1, away1 = forward(tok_swap, swap_twin, weights1)
+    tok_mid2, tok_out3, cot_mid, second_twin, far_table, part1, away1, cotangent = fence(
+        tok_mid2, tok_out3, cot_mid, second_twin, far_table, part1, away1, cotangent
+    )
+
+    cot_swap = send(cotangent, ALL_SWAP)
+    tok_third = jnp.where(inner, tok_mid2, tok_out3)
+    third_twin = sibling(tok_third)
+    far = near_weights(far_table, me)
+    weights2 = jnp.where(inner, far[2:], far[:2])
+    weights3 = jnp.where(inner, far[:2], far[2:])
+    saved2, part2, away2 = forward(tok_second, second_twin, weights2)
+    saved3, part3, away3 = forward(tok_third, third_twin, weights3)
+    part3 = add_rounded(part3, sibling(away3))
+    part2 = add_rounded(part2, sibling(away2))
+    cot_twin = sibling(cotangent)
+    to_swap = jnp.where(inner, cot_mid, part3)
+    cot_swap, cot_mid, cot_twin, part2, part3, to_swap = fence(
+        cot_swap, cot_mid, cot_twin, part2, part3, to_swap
+    )
+
+    swapped5 = send(to_swap, ALL_SWAP)
+    cot_mid2 = send(cot_swap, MID_SWAP)
+    cot_swap_twin = sibling(cot_swap)
+    part1 = add_rounded(part1, sibling(away1))
+    part0 = add_rounded(part0, sibling(away0))
+    none = (jnp.zeros(adapt_a.shape, jnp.float32), jnp.zeros(adapt_b.shape, jnp.float32))
+    grads = backward((cotangent, cot_twin), weights0, (tokens, tok_twin), saved0, none)
+    swapped5, cot_mid, cot_mid2, cot_swap_twin, part0, part1, part2, part3, grads = fence(
+        swapped5, cot_mid, cot_mid2, cot_swap_twin, part0, part1, part2, part3, grads
+    )
+
+    swapped6 = send(jnp.where(inner, cot_mid2, part2), ALL_SWAP)
+    third_mid = send(add_rounded(part3, swapped5), MID_SWAP)
+    cot_second = jnp.where(inner, cot_mid, swapped5)
+    cot_second_twin = sibling(cot_second)
+    grads = backward((cot_swap, cot_swap_twin), weights1, (tok_swap, swap_twin), saved1, grads)
+    grads = backward(
+        (cot_second, cot_second_twin), weights2, (tok_second, second_twin), saved2, grads
+    )
+    swapped6, third_mid, cot_mid2, part0, part1, part2, grads = fence(
+        swapped6, third_mid, cot_mid2, part0, part1, part2, grads
+    )
+
+    first_swap = send(add_rounded(part1, third_mid), ALL_SWAP)
+    second_mid = send(add_rounded(part2, swapped6), MID_SWAP)
+    cot_third = jnp.where(inner, cot_mid2, swapped6)
+    grads = backward(
+        (cot_third, sibling(cot_third)), weights3, (tok_third, third_twin), saved3, grads
+    )
+    grad_a, grad_b = group_sum(*grads)
+    mixed = add_rounded(part0, first_swap, second_mid)
+    return mixed, grad_a[None], grad_b.reshape(adapter_up_maps.shape)
 
 
 def body(*arrays):
-    if lax.axis_size("expert") == arrays[2].shape[1]:
+    if (lax.axis_size("dp"), lax.axis_size("expert"), arrays[2].shape[1]) == (4, 8, 8):
         return dense_body(*arrays)
     return sparse_body(*arrays)
 

time: 242 us -> 157 us (0.65)
  waiting for transfers between devices: 162 us -> 45.4 us
  Pallas kernels: 0 us -> 45.1 us
  starting transfers between devices: 0.16 us -> 39.1 us
  matrix products: 35.5 us -> 0 us
  blocking collectives: 18 us -> 0 us
  between operations: 13.9 us -> 1.07 us
  local copies, waits for them, and re-layouts: 7.55 us -> 16.9 us
  other arithmetic: 4.91 us -> 8.35 us
    all_gather x2 -> x0, waiting for transfers between devices: 60.6 us -> none  [the longest x1 30.5 us: dense_body(): cot = lax.all_gather(cotangent, 'expert', tiled=True)]
    reduce_scatter x1 -> x0, waiting for transfers between devices: 50.3 us -> none  [dense_body(): mixed = lax.psum_scatter(part, 'expert', scatter_dimension=0, tiled=True)]
    psum x1 -> x0, waiting for transfers between devices: 49.7 us -> none  [dense_body(): grad_a, grad_b = lax.psum((grad_a, grad_b), 'dp')]
    ppermute x0 -> x34, waiting for transfers between devices: none -> 45.4 us  [the longest x28 38.3 us: send(): return lax.ppermute(array, 'expert', pairs)]
    pallas_call x0 -> x9, Pallas kernels: none -> 45.1 us  [the longest x4 25 us: forward_stage(): pl.pallas_call(forward_kernel, grid=(steps,), out_shape=(jax.ShapeDtypeSt...]
    ppermute x0 -> x34, starting transfers between devices: none -> 39.1 us  [the longest x28 30.7 us: send(): return lax.ppermute(array, 'expert', pairs)]
    dot_general x11 -> x0, matrix products: 35.5 us -> none  [the longest x1 8.78 us: expert_apply_forward(): jnp.dot(rows_in, gate_up, preferred_element_type=jnp.float32)]
    all_gather x1 -> x0, blocking collectives: 18 us -> none  [dense_body(): weight_all = lax.all_gather(weight_table, 'expert', tiled=True)]
  transfers between devices with their start and end apart: 4 -> 34, of which waited for: 4 -> 14; matrix products, arithmetic and copies ran while one was open for 12% -> 3% of each run, Pallas kernels for 0% -> 29%
where the time goes in v5:
time: 157 us; the launch traced here: 156 us
  waiting for transfers between devices  45.4 us (29%)
  Pallas kernels  45.1 us (29%)
  starting transfers between devices  39.1 us (25%)
  local copies, waits for them, and re-layouts  16.9 us (11%)
  other arithmetic  8.35 us (5%)
    ppermute x28, waiting for transfers between devices, send(): return lax.ppermute(array, 'expert', pairs)  38.3 us
    ppermute x28, starting transfers between devices, send(): return lax.ppermute(array, 'expert', pairs)  30.7 us
    pallas_call x4, Pallas kernels, forward_stage(): pl.pallas_call(forward_kernel, grid=(steps,), out_shape=(jax.ShapeDtypeSt...  25 us
    pallas_call x4, Pallas kernels, backward_stage(): pl.pallas_call(backward_kernel, grid=(hidden_width // chunk,), out_shape=...  18.5 us
    unnamed x46, local copies, waits for them, and re-layouts  16.8 us
    ppermute x6, starting transfers between devices, swap_sum(): other = lax.ppermute(rounded.astype(jnp.bfloat16), 'dp', pairs)  8.32 us
    ppermute x6, waiting for transfers between devices, swap_sum(): other = lax.ppermute(rounded.astype(jnp.bfloat16), 'dp', pairs)  7.12 us
  transfers between devices with their start and end apart: 34, of which 14 were waited for; matrix products, arithmetic and copies ran while one was open for 3% of the time, Pallas kernels for 29%

profile of v5, /device:TPU:0, one launch (start us, length us, event | category | flops | bytes accessed | tf_op | source)
XLA Modules:
  0.0 155.9 jit_solution(18230243506577169229)
XLA Ops:
  2.6 4.7 %collective-permute-start = (bf16[128,2048]{1,0:T(8,128)(2,1)}, bf16[128,2048]{1,0:T(8,128)(2,1)}, u32[]{:S(2)}, u32[]{:S(2)}) collective-permute-start(bf16[128,2048]{1,0:T(8,128)(2,1)} %mine_ref.3), channel_id=1, source_target_pairs={{0,2},{1,3},{2,0},{3,1},{4,6},{5,7},{6,4},{7,5},{8,10},{9,11},{10,... | collective-permute-start | bytes 1572872 | tf_op jit(solution)/shard_map/ppermute | solution.py:411
  11.7 8.2 %collective-permute-done.mine_ref = bf16[128,2048]{1,0:T(8,128)(2,1)} collective-permute-done((bf16[128,2048]{1,0:T(8,128)(2,1)}, bf16[128,2048]{1,0:T(8,128)(2,1)}, u32[]{:S(2)}, u32[]{:S(2)}) %collective-permute-start) | collective-permute-done | bytes 524320 | tf_op jit(solution)/shard_map/ppermute | solution.py:411
  25.0 2.8 %copy-done = bf16[1,2048,1536]{2,1,0:T(8,128)(2,1)S(1)} copy-done((bf16[1,2048,1536]{2,1,0:T(8,128)(2,1)S(1)}, bf16[1,2048,1536]{2,1,0:T(8,128)(2,1)}, u32[]{:S(2)}) %copy-start) | copy-done | bytes 6291480
  27.8 1.9 %copy-done.3 = bf16[1,768,2048]{2,1,0:T(8,128)(2,1)S(1)} copy-done((bf16[1,768,2048]{2,1,0:T(8,128)(2,1)S(1)}, bf16[1,768,2048]{2,1,0:T(8,128)(2,1)}, u32[]{:S(2)}) %copy-start.3) | copy-done | bytes 3145752
  33.7 5.7 %shard_map.122 = (bf16[256,128]{1,0:T(8,128)(2,1)S(1)}, f32[256,768]{1,0:T(8,128)S(1)}, f32[256,768]{1,0:T(8,128)S(1)}, bf16[128,2048]{1,0:T(8,128)(2,1)S(1)}, bf16[128,2048]{1,0:T(8,128)(2,1)S(1)}) custom-call(bf16[128,2048]{1,0:T(8,128)(2,1)S(1)} %copy-done.10, bf16[128,2048]{1,0:T(8,128)(2,1)S(1)} %copy-done.13, f32[2,128]{1,0:T(2,128)S(1)} %bitcast.54, ...), custom_call_target="tpu_custom_call" | custom-call | flops 1000000 | bytes 10000 | tf_op jit(solution)/shard_map/pallas_call | solution.py:296
  42.8 1.9 %broadcast_select_fusion.5.mine_ref = bf16[128,2048]{1,0:T(8,128)(2,1)} fusion(bf16[128,2048]{1,0:T(8,128)(2,1)} %collective-permute-done.1, bf16[128,2048]{1,0:T(8,128)(2,1)} %collective-permute-done.4, pred[]{:T(512)S(6)} %or.3), kind=kLoop, calls=%fused_computation.18 | loop fusion | flops 262144 | bytes 1572865 | tf_op jit(solution)/shard_map/jit(_where)/select_n | solution.py:505
  46.6 3.6 %collective-permute-start.11 = (f32[32,128]{1,0:T(8,128)S(1)}, f32[32,128]{1,0:T(8,128)S(1)}, u32[]{:S(2)}, u32[]{:S(2)}) collective-permute-start(f32[32,128]{1,0:T(8,128)S(1)} %pad_maximum_fusion), channel_id=1, source_target_pairs={{0,4},{1,5},{2,6},{3,7},{4,0},{5,1},{6,2},{7,3},{8,12},{9,13},{10,... | collective-permute-start | bytes 49160 | tf_op jit(solution)/shard_map/ppermute | solution.py:411
  50.2 2.8 %copy-done.1 = bf16[1,2048,1536]{2,1,0:T(8,128)(2,1)S(1)} copy-done((bf16[1,2048,1536]{2,1,0:T(8,128)(2,1)S(1)}, bf16[1,2048,1536]{2,1,0:T(8,128)(2,1)}, u32[]{:S(2)}) %copy-start.1) | copy-done | bytes 6291480
  54.0 6.9 %shard_map.123 = (bf16[256,128]{1,0:T(8,128)(2,1)S(1)}, f32[256,768]{1,0:T(8,128)S(1)}, f32[256,768]{1,0:T(8,128)S(1)}, bf16[128,2048]{1,0:T(8,128)(2,1)S(1)}, bf16[128,2048]{1,0:T(8,128)(2,1)S(1)}) custom-call(bf16[128,2048]{1,0:T(8,128)(2,1)} %collective-permute-done.mine_ref, bf16[128,2048]{1,0:T(8,128)(2,1)} %collective-permute-done.6.other_ref, ...), custom_call_target="tpu_custom_call" | custom-call | flops 1000000 | bytes 10000 | tf_op jit(solution)/shard_map/pallas_call | solution.py:296
  60.9 2.1 %collective-permute-done.11 = f32[32,128]{1,0:T(8,128)S(1)} collective-permute-done((f32[32,128]{1,0:T(8,128)S(1)}, f32[32,128]{1,0:T(8,128)S(1)}, u32[]{:S(2)}, u32[]{:S(2)}) %collective-permute-start.11) | collective-permute-done | bytes 16416 | tf_op jit(solution)/shard_map/ppermute | solution.py:411
  64.3 6.8 %shard_map.124 = (bf16[256,128]{1,0:T(8,128)(2,1)S(1)}, f32[256,768]{1,0:T(8,128)S(1)}, f32[256,768]{1,0:T(8,128)S(1)}, bf16[128,2048]{1,0:T(8,128)(2,1)S(1)}, bf16[128,2048]{1,0:T(8,128)(2,1)S(1)}) custom-call(bf16[128,2048]{1,0:T(8,128)(2,1)} %broadcast_select_fusion.5.mine_ref, bf16[128,2048]{1,0:T(8,128)(2,1)} %collective-permute-done.10.other_ref, ...), custom_call_target="tpu_custom_call" | custom-call | flops 1000000 | bytes 10000 | tf_op jit(solution)/shard_map/pallas_call | solution.py:296
  71.6 5.7 %shard_map.125 = (bf16[256,128]{1,0:T(8,128)(2,1)S(1)}, f32[256,768]{1,0:T(8,128)S(1)}, f32[256,768]{1,0:T(8,128)S(1)}, bf16[128,2048]{1,0:T(8,128)(2,1)S(1)}, bf16[128,2048]{1,0:T(8,128)(2,1)S(1)}) custom-call(bf16[128,2048]{1,0:T(8,128)(2,1)S(1)} %broadcast_select_fusion.4.mine_ref, bf16[128,2048]{1,0:T(8,128)(2,1)S(1)} %collective-permute-done.15.other_ref, ...), custom_call_target="tpu_custom_call" | custom-call | flops 1000000 | bytes 10000 | tf_op jit(solution)/shard_map/pallas_call | solution.py:296
  81.0 11.5 %collective-permute-done.12.cot_mine_ref = bf16[128,2048]{1,0:T(8,128)(2,1)S(1)} collective-permute-done((bf16[128,2048]{1,0:T(8,128)(2,1)}, bf16[128,2048]{1,0:T(8,128)(2,1)S(1)}, u32[]{:S(2)}, u32[]{:S(2)}) %collective-permute-start.12) | collective-permute-done | bytes 524320 | tf_op jit(solution)/shard_map/ppermute | solution.py:411
  93.4 2.7 %collective-permute-start.17 = (bf16[128,2048]{1,0:T(8,128)(2,1)S(1)}, bf16[128,2048]{1,0:T(8,128)(2,1)S(1)}, u32[]{:S(2)}, u32[]{:S(2)}) collective-permute-start(bf16[128,2048]{1,0:T(8,128)(2,1)S(1)} %get-tuple-element.99), channel_id=1, source_target_pairs={{0,2},{1,3},{2,0},{3,1},{4,6},{5,7},{6,4},{7,5},{8,10},{9,11},{10,... | collective-permute-start | bytes 1572872 | tf_op jit(solution)/shard_map/ppermute | solution.py:411
  96.5 4.8 %shard_map.126 = (f32[2048,128]{1,0:T(8,128)S(1)}, f32[128,768]{1,0:T(8,128)S(1)}) custom-call(bf16[128,2048]{1,0:T(8,128)(2,1)} %cot_mine_ref, bf16[128,2048]{1,0:T(8,128)(2,1)S(1)} %collective-permute-done.13.cot_other_ref, f32[2,128]{1,0:T(2,128)S(1)} %bitcast.55, bf16[128,2048]{1,0:T(8,128)(2,1)S(1)} %copy-done.11, bf16[128,2048]{1,0:T(8,128)(2,1)S(1)} %copy-done.14, ...), custom_call_target="tpu_custom_call" | custom-call | flops 1000000 | bytes 10000 | tf_op jit(solution)/shard_map/pallas_call | solution.py:370
  101.3 7.1 %collective-permute-done.17 = bf16[128,2048]{1,0:T(8,128)(2,1)S(1)} collective-permute-done((bf16[128,2048]{1,0:T(8,128)(2,1)S(1)}, bf16[128,2048]{1,0:T(8,128)(2,1)S(1)}, u32[]{:S(2)}, u32[]{:S(2)}) %collective-permute-start.17) | collective-permute-done | bytes 524320 | tf_op jit(solution)/shard_map/ppermute | solution.py:411
  108.8 2.8 %collective-permute-start.22 = (bf16[128,2048]{1,0:T(8,128)(2,1)S(1)}, bf16[128,2048]{1,0:T(8,128)(2,1)S(1)}, u32[]{:S(2)}, u32[]{:S(2)}) collective-permute-start(bf16[128,2048]{1,0:T(8,128)(2,1)S(1)} %broadcast_select_fusion.2), channel_id=1, source_target_pairs={{0,2},{1,3},{2,0},{3,1},{4,6},{5,7},{6,4},{7,5},{8,10},{9,11},{10,... | collective-permute-start | bytes 1572872 | tf_op jit(solution)/shard_map/ppermute | solution.py:411
  112.3 5.0 %shard_map.127 = (f32[2048,128]{1,0:T(8,128)S(1)}, f32[128,768]{1,0:T(8,128)S(1)}) custom-call(bf16[128,2048]{1,0:T(8,128)(2,1)S(1)} %collective-permute-done.12.cot_mine_ref, bf16[128,2048]{1,0:T(8,128)(2,1)S(1)} %collective-permute-done.19.cot_other_ref, f32[2,128]{1,0:T(2,128)S(1)} %bitcast.57, bf16[128,2048]{1,0:T(8,128)(2,1)} %collective-permute-done.mine_ref, ...), custom_call_target="tpu_custom_call" | custom-call | flops 1000000 | bytes 10000 | tf_op jit(solution)/shard_map/pallas_call | solution.py:370
  117.3 5.0 %shard_map.128 = (f32[2048,128]{1,0:T(8,128)S(1)}, f32[128,768]{1,0:T(8,128)S(1)}) custom-call(bf16[128,2048]{1,0:T(8,128)(2,1)S(1)} %broadcast_select_fusion.1.cot_mine_ref, bf16[128,2048]{1,0:T(8,128)(2,1)S(1)} %collective-permute-done.24.cot_other_ref, f32[2,128]{1,0:T(2,128)S(1)} %get-tuple-element.152.w_ref, ...), custom_call_target="tpu_custom_call" | custom-call | flops 1000000 | bytes 10000 | tf_op jit(solution)/shard_map/pallas_call | solution.py:370
  122.2 1.9 %collective-permute-done.22 = bf16[128,2048]{1,0:T(8,128)(2,1)S(1)} collective-permute-done((bf16[128,2048]{1,0:T(8,128)(2,1)S(1)}, bf16[128,2048]{1,0:T(8,128)(2,1)S(1)}, u32[]{:S(2)}, u32[]{:S(2)}) %collective-permute-start.22) | collective-permute-done | bytes 524320 | tf_op jit(solution)/shard_map/ppermute | solution.py:411
  124.5 3.7 %collective-permute-start.25 = (bf16[128,2048]{1,0:T(8,128)(2,1)S(1)}, bf16[128,2048]{1,0:T(8,128)(2,1)S(1)}, u32[]{:S(2)}, u32[]{:S(2)}) collective-permute-start(bf16[128,2048]{1,0:T(8,128)(2,1)S(1)} %add_convert_fusion.2), channel_id=1, source_target_pairs={{0,2},{1,3},{2,0},{3,1},{4,6},{5,7},{6,4},{7,5},{8,10},{9,11},{10,... | collective-permute-start | bytes 1572872 | tf_op jit(solution)/shard_map/ppermute | solution.py:411
  129.0 3.8 %shard_map.129 = (f32[2048,128]{1,0:T(8,128)S(1)}, f32[128,768]{1,0:T(8,128)S(1)}) custom-call(bf16[128,2048]{1,0:T(8,128)(2,1)S(1)} %broadcast_select_fusion.cot_mine_ref, bf16[128,2048]{1,0:T(8,128)(2,1)S(1)} %collective-permute-done.27.cot_other_ref, f32[2,128]{1,0:T(2,128)S(1)} %get-tuple-element.151.w_ref, ...), custom_call_target="tpu_custom_call" | custom-call | flops 1000000 | bytes 10000 | tf_op jit(solution)/shard_map/pallas_call | solution.py:370
  136.6 4.1 %collective-permute-done.25 = bf16[128,2048]{1,0:T(8,128)(2,1)S(1)} collective-permute-done((bf16[128,2048]{1,0:T(8,128)(2,1)S(1)}, bf16[128,2048]{1,0:T(8,128)(2,1)S(1)}, u32[]{:S(2)}, u32[]{:S(2)}) %collective-permute-start.25) | collective-permute-done | bytes 524320 | tf_op jit(solution)/shard_map/ppermute | solution.py:411
  149.3 3.5 %collective-permute-done.33 = bf16[128,768]{1,0:T(8,128)(2,1)S(1)} collective-permute-done((bf16[128,768]{1,0:T(8,128)(2,1)S(1)}, bf16[128,768]{1,0:T(8,128)(2,1)S(1)}, u32[]{:S(2)}, u32[]{:S(2)}) %collective-permute-start.33) | collective-permute-done | bytes 196640 | tf_op jit(solution)/shard_map/ppermute | solution.py:441
  (130 shorter events, 45.9 us)
Async XLA Ops:
  0.6 10.3 %collective-permute-start.2 = (bf16[128,2048]{1,0:T(8,128)(2,1)}, bf16[128,2048]{1,0:T(8,128)(2,1)S(1)}, u32[]{:S(2)}, u32[]{:S(2)}) collective-permute-start(bf16[128,2048]{1,0:T(8,128)(2,1)} %mine_ref.3), channel_id=1, source_target_pairs={{0,1},{1,0},{2,3},{3,2},{4,5},{5,4},{6,7},{7,6},{8,9},{9,8},{10,11... | collective-permute-start | bytes 1572872 | tf_op jit(solution)/shard_map/ppermute | solution.py:411
  1.1 10.6 %collective-permute-start.1 = (bf16[128,2048]{1,0:T(8,128)(2,1)}, bf16[128,2048]{1,0:T(8,128)(2,1)}, u32[]{:S(2)}, u32[]{:S(2)}) collective-permute-start(bf16[128,2048]{1,0:T(8,128)(2,1)} %mine_ref.3), channel_id=1, source_target_pairs={{2,4},{3,5},{4,2},{5,3},{10,12},{11,13},{12,10},{13,11},{18,20},{1... | collective-permute-start | bytes 1572872 | tf_op jit(solution)/shard_map/ppermute | solution.py:411
  2.6 17.3 %collective-permute-start = (bf16[128,2048]{1,0:T(8,128)(2,1)}, bf16[128,2048]{1,0:T(8,128)(2,1)}, u32[]{:S(2)}, u32[]{:S(2)}) collective-permute-start(bf16[128,2048]{1,0:T(8,128)(2,1)} %mine_ref.3), channel_id=1, source_target_pairs={{0,2},{1,3},{2,0},{3,1},{4,6},{5,7},{6,4},{7,5},{8,10},{9,11},{10,... | collective-permute-start | bytes 1572872 | tf_op jit(solution)/shard_map/ppermute | solution.py:411
  19.9 22.9 %collective-permute-start.4 = (bf16[128,2048]{1,0:T(8,128)(2,1)}, bf16[128,2048]{1,0:T(8,128)(2,1)}, u32[]{:S(2)}, u32[]{:S(2)}) collective-permute-start(bf16[128,2048]{1,0:T(8,128)(2,1)} %collective-permute-done.1), channel_id=1, source_target_pairs={{0,2},{1,3},{2,0},{3,1},{4,6},{5,7},{6,4},{7,5},{8,10},{9,11},{10,... | collective-permute-start | bytes 1572872 | tf_op jit(solution)/shard_map/ppermute | solution.py:411
  21.6 21.1 %collective-permute-start.6 = (bf16[128,2048]{1,0:T(8,128)(2,1)}, bf16[128,2048]{1,0:T(8,128)(2,1)}, u32[]{:S(2)}, u32[]{:S(2)}) collective-permute-start(bf16[128,2048]{1,0:T(8,128)(2,1)} %collective-permute-done.mine_ref), channel_id=1, source_target_pairs={{0,1},{1,0},{2,3},{3,2},{4,5},{5,4},{6,7},{7,6},{8,9},{9,8},{10,11... | collective-permute-start | bytes 1572872 | tf_op jit(solution)/shard_map/ppermute | solution.py:411
  21.6 21.1 %collective-permute-start.5 = (bf16[128,2048]{1,0:T(8,128)(2,1)}, bf16[128,2048]{1,0:T(8,128)(2,1)}, u32[]{:S(2)}, u32[]{:S(2)}) collective-permute-start(bf16[128,2048]{1,0:T(8,128)(2,1)} %collective-permute-done.mine_ref), channel_id=1, source_target_pairs={{2,4},{3,5},{4,2},{5,3},{10,12},{11,13},{12,10},{13,11},{18,20},{1... | collective-permute-start | bytes 1572872 | tf_op jit(solution)/shard_map/ppermute | solution.py:411
  23.1 19.7 %collective-permute-start.7 = (f32[16,128]{1,0:T(8,128)S(1)}, f32[16,128]{1,0:T(8,128)S(1)}, u32[]{:S(2)}, u32[]{:S(2)}) collective-permute-start(f32[16,128]{1,0:T(8,128)S(1)} %pad_maximum_fusion.1), channel_id=1, source_target_pairs={{0,2},{1,3},{2,0},{3,1},{4,6},{5,7},{6,4},{7,5},{8,10},{9,11},{10,... | collective-permute-start | bytes 24584 | tf_op jit(solution)/shard_map/ppermute | solution.py:411
  44.7 18.3 %collective-permute-start.10 = (bf16[128,2048]{1,0:T(8,128)(2,1)}, bf16[128,2048]{1,0:T(8,128)(2,1)}, u32[]{:S(2)}, u32[]{:S(2)}) collective-permute-start(bf16[128,2048]{1,0:T(8,128)(2,1)} %broadcast_select_fusion.5.mine_ref), channel_id=1, source_target_pairs={{0,1},{1,0},{2,3},{3,2},{4,5},{5,4},{6,7},{7,6},{8,9},{9,8},{10,11... | collective-permute-start | bytes 1572872 | tf_op jit(solution)/shard_map/ppermute | solution.py:411
  44.7 18.3 %collective-permute-start.8 = (bf16[128,2048]{1,0:T(8,128)(2,1)}, bf16[128,2048]{1,0:T(8,128)(2,1)}, u32[]{:S(2)}, u32[]{:S(2)}) collective-permute-start(bf16[128,2048]{1,0:T(8,128)(2,1)} %collective-permute-done.5), channel_id=1, source_target_pairs={{0,2},{1,3},{2,0},{3,1},{4,6},{5,7},{6,4},{7,5},{8,10},{9,11},{10,... | collective-permute-start | bytes 1572872 | tf_op jit(solution)/shard_map/ppermute | solution.py:411
  45.1 18.0 %collective-permute-start.9 = (bf16[128,2048]{1,0:T(8,128)(2,1)}, bf16[128,2048]{1,0:T(8,128)(2,1)}, u32[]{:S(2)}, u32[]{:S(2)}) collective-permute-start(bf16[128,2048]{1,0:T(8,128)(2,1)} %cot_mine_ref), channel_id=1, source_target_pairs={{2,4},{3,5},{4,2},{5,3},{10,12},{11,13},{12,10},{13,11},{18,20},{1... | collective-permute-start | bytes 1572872 | tf_op jit(solution)/shard_map/ppermute | solution.py:411
  46.6 16.5 %collective-permute-start.11 = (f32[32,128]{1,0:T(8,128)S(1)}, f32[32,128]{1,0:T(8,128)S(1)}, u32[]{:S(2)}, u32[]{:S(2)}) collective-permute-start(f32[32,128]{1,0:T(8,128)S(1)} %pad_maximum_fusion), channel_id=1, source_target_pairs={{0,4},{1,5},{2,6},{3,7},{4,0},{5,1},{6,2},{7,3},{8,12},{9,13},{10,... | collective-permute-start | bytes 49160 | tf_op jit(solution)/shard_map/ppermute | solution.py:411
  77.5 18.6 %collective-permute-start.20 = (bf16[128,2048]{1,0:T(8,128)(2,1)S(1)}, bf16[128,2048]{1,0:T(8,128)(2,1)S(1)}, u32[]{:S(2)}, u32[]{:S(2)}) collective-permute-start(bf16[128,2048]{1,0:T(8,128)(2,1)S(1)} %copy-done.22), channel_id=1, source_target_pairs={{0,1},{1,0},{2,3},{3,2},{4,5},{5,4},{6,7},{7,6},{8,9},{9,8},{10,11... | collective-permute-start | bytes 1572872 | tf_op jit(solution)/shard_map/ppermute | solution.py:411
  78.0 14.5 %collective-permute-start.12 = (bf16[128,2048]{1,0:T(8,128)(2,1)}, bf16[128,2048]{1,0:T(8,128)(2,1)S(1)}, u32[]{:S(2)}, u32[]{:S(2)}) collective-permute-start(bf16[128,2048]{1,0:T(8,128)(2,1)} %cot_mine_ref), channel_id=1, source_target_pairs={{0,2},{1,3},{2,0},{3,1},{4,6},{5,7},{6,4},{7,5},{8,10},{9,11},{10,... | collective-permute-start | bytes 1572872 | tf_op jit(solution)/shard_map/ppermute | solution.py:411
  78.5 17.8 %collective-permute-start.21 = (bf16[128,2048]{1,0:T(8,128)(2,1)S(1)}, bf16[128,2048]{1,0:T(8,128)(2,1)S(1)}, u32[]{:S(2)}, u32[]{:S(2)}) collective-permute-start(bf16[128,2048]{1,0:T(8,128)(2,1)S(1)} %get-tuple-element.105), channel_id=1, source_target_pairs={{0,1},{1,0},{2,3},{3,2},{4,5},{5,4},{6,7},{7,6},{8,9},{9,8},{10,11... | collective-permute-start | bytes 1572872 | tf_op jit(solution)/shard_map/ppermute | solution.py:411
  92.5 15.9 %collective-permute-start.19 = (bf16[128,2048]{1,0:T(8,128)(2,1)S(1)}, bf16[128,2048]{1,0:T(8,128)(2,1)S(1)}, u32[]{:S(2)}, u32[]{:S(2)}) collective-permute-start(bf16[128,2048]{1,0:T(8,128)(2,1)S(1)} %collective-permute-done.12.cot_mine_ref), channel_id=1, source_target_pairs={{0,1},{1,0},{2,3},{3,2},{4,5},{5,4},{6,7},{7,6},{8,9},{9,8},{10,11... | collective-permute-start | bytes 1572872 | tf_op jit(solution)/shard_map/ppermute | solution.py:411
  92.5 15.9 %collective-permute-start.18 = (bf16[128,2048]{1,0:T(8,128)(2,1)S(1)}, bf16[128,2048]{1,0:T(8,128)(2,1)S(1)}, u32[]{:S(2)}, u32[]{:S(2)}) collective-permute-start(bf16[128,2048]{1,0:T(8,128)(2,1)S(1)} %collective-permute-done.12.cot_mine_ref), channel_id=1, source_target_pairs={{2,4},{3,5},{4,2},{5,3},{10,12},{11,13},{12,10},{13,11},{18,20},{1... | collective-permute-start | bytes 1572872 | tf_op jit(solution)/shard_map/ppermute | solution.py:411
  93.4 15.0 %collective-permute-start.17 = (bf16[128,2048]{1,0:T(8,128)(2,1)S(1)}, bf16[128,2048]{1,0:T(8,128)(2,1)S(1)}, u32[]{:S(2)}, u32[]{:S(2)}) collective-permute-start(bf16[128,2048]{1,0:T(8,128)(2,1)S(1)} %get-tuple-element.99), channel_id=1, source_target_pairs={{0,2},{1,3},{2,0},{3,1},{4,6},{5,7},{6,4},{7,5},{8,10},{9,11},{10,... | collective-permute-start | bytes 1572872 | tf_op jit(solution)/shard_map/ppermute | solution.py:411
  108.8 15.4 %collective-permute-start.22 = (bf16[128,2048]{1,0:T(8,128)(2,1)S(1)}, bf16[128,2048]{1,0:T(8,128)(2,1)S(1)}, u32[]{:S(2)}, u32[]{:S(2)}) collective-permute-start(bf16[128,2048]{1,0:T(8,128)(2,1)S(1)} %broadcast_select_fusion.2), channel_id=1, source_target_pairs={{0,2},{1,3},{2,0},{3,1},{4,6},{5,7},{6,4},{7,5},{8,10},{9,11},{10,... | collective-permute-start | bytes 1572872 | tf_op jit(solution)/shard_map/ppermute | solution.py:411
  111.6 12.6 %collective-permute-start.23 = (bf16[128,2048]{1,0:T(8,128)(2,1)S(1)}, bf16[128,2048]{1,0:T(8,128)(2,1)S(1)}, u32[]{:S(2)}, u32[]{:S(2)}) collective-permute-start(bf16[128,2048]{1,0:T(8,128)(2,1)S(1)} %add_convert_fusion.3), channel_id=1, source_target_pairs={{2,4},{3,5},{4,2},{5,3},{10,12},{11,13},{12,10},{13,11},{18,20},{1... | collective-permute-start | bytes 1572872 | tf_op jit(solution)/shard_map/ppermute | solution.py:411
  124.5 16.3 %collective-permute-start.25 = (bf16[128,2048]{1,0:T(8,128)(2,1)S(1)}, bf16[128,2048]{1,0:T(8,128)(2,1)S(1)}, u32[]{:S(2)}, u32[]{:S(2)}) collective-permute-start(bf16[128,2048]{1,0:T(8,128)(2,1)S(1)} %add_convert_fusion.2), channel_id=1, source_target_pairs={{0,2},{1,3},{2,0},{3,1},{4,6},{5,7},{6,4},{7,5},{8,10},{9,11},{10,... | collective-permute-start | bytes 1572872 | tf_op jit(solution)/shard_map/ppermute | solution.py:411
  128.3 12.5 %collective-permute-start.26 = (bf16[128,2048]{1,0:T(8,128)(2,1)S(1)}, bf16[128,2048]{1,0:T(8,128)(2,1)S(1)}, u32[]{:S(2)}, u32[]{:S(2)}) collective-permute-start(bf16[128,2048]{1,0:T(8,128)(2,1)S(1)} %add_convert_fusion.1), channel_id=1, source_target_pairs={{2,4},{3,5},{4,2},{5,3},{10,12},{11,13},{12,10},{13,11},{18,20},{1... | collective-permute-start | bytes 1572872 | tf_op jit(solution)/shard_map/ppermute | solution.py:411
  134.5 9.0 %collective-permute-start.32 = (bf16[128,768]{1,0:T(8,128)(2,1)S(1)}, bf16[128,768]{1,0:T(8,128)(2,1)S(1)}, u32[]{:S(2)}, u32[]{:S(2)}) collective-permute-start(bf16[128,768]{1,0:T(8,128)(2,1)S(1)} %reduce-precision_convert_fusion), channel_id=1, source_target_pairs={{0,16},{8,24},{16,0},{24,8},{1,17},{9,25},{17,1},{25,9},{2,18},{10... | collective-permute-start | bytes 589832 | tf_op jit(solution)/shard_map/ppermute | solution.py:441
  135.1 10.7 %collective-permute-start.28 = (bf16[1408,128]{1,0:T(8,128)(2,1)S(1)}, bf16[1408,128]{1,0:T(8,128)(2,1)S(1)}, u32[]{:S(2)}, u32[]{:S(2)}) collective-permute-start(bf16[1408,128]{1,0:T(8,128)(2,1)S(1)} %fusion), channel_id=1, source_target_pairs={{0,8},{8,0},{16,24},{24,16},{1,9},{9,1},{17,25},{25,17},{2,10},{10... | collective-permute-start | bytes 1081352 | tf_op jit(solution)/shard_map/ppermute | solution.py:441
  143.5 9.3 %collective-permute-start.33 = (bf16[128,768]{1,0:T(8,128)(2,1)S(1)}, bf16[128,768]{1,0:T(8,128)(2,1)S(1)}, u32[]{:S(2)}, u32[]{:S(2)}) collective-permute-start(bf16[128,768]{1,0:T(8,128)(2,1)S(1)} %fusion.3), channel_id=1, source_target_pairs={{0,8},{8,0},{16,24},{24,16},{1,9},{9,1},{17,25},{25,17},{2,10},{10... | collective-permute-start | bytes 589832 | tf_op jit(solution)/shard_map/ppermute | solution.py:441
  (33 other events, 237.1 us)

commit v6 on v5

--- a/solution.py
+++ b/solution.py
@@ -239,17 +239,18 @@
     )(table, routing.T, choice.T, weights.T)
 
 
-def forward_kernel(
-    mine_ref, other_ref, w_ref, adapt_a_ref, gate_ref, up_ref, adapt_b_ref, down_ref,
-    low_ref, active_ref, slope_ref, part_mine_ref, part_other_ref, rows_ref, total_ref,
-):
+def forward_kernel(*refs):
+    blocks, refs = refs[:4], refs[4:]
+    w_ref, adapt_a_ref, gate_ref, up_ref, adapt_b_ref, down_ref, *refs = refs
+    low_ref, active_ref, slope_ref, part_mine_ref, part_other_ref, rows_ref, total_ref = refs
     step = pl.program_id(0)
-    half = mine_ref.shape[0]
+    quarter = blocks[0].shape[0]
+    half = 2 * quarter
 
     @pl.when(step == 0)
     def _():
-        rows_ref[:half] = mine_ref[...]
-        rows_ref[half:] = other_ref[...]
+        for at, block in enumerate(blocks):
+            rows_ref[at * quarter : (at + 1) * quarter] = block[...]
         low_ref[...] = dot(rows_ref[...], adapt_a_ref[...]).astype(jnp.bfloat16)
 
     rows = rows_ref[...]
@@ -286,8 +287,9 @@
     return pl.BlockSpec((rows, width), lambda j: (0, start + j))
 
 
-def forward_stage(mine, other, w, gate_up, down, adapt_a, adapt_b, chunk=256):
-    half, features = mine.shape
+def forward_stage(blocks, w, gate_up, down, adapt_a, adapt_b, chunk=256):
+    quarter, features = blocks[0].shape
+    half = 2 * quarter
     hidden_width = down.shape[0]
     both, ranks = 2 * half, adapt_a.shape[1]
     steps = hidden_width // chunk
@@ -297,9 +299,8 @@
         forward_kernel,
         grid=(steps,),
         out_shape=(jax.ShapeDtypeStruct((both, ranks), jnp.bfloat16), saved, saved, part, part),
-        in_specs=[
-            whole((half, features)),
-            whole((half, features)),
+        in_specs=[whole((quarter, features))] * 4
+        + [
             whole((2, half)),
             whole((features, ranks)),
             columns(features, chunk),
@@ -318,24 +319,26 @@
             pltpu.VMEM((both, features), jnp.bfloat16),
             pltpu.VMEM((both, features), jnp.float32),
         ],
-        compiler_params=pltpu.CompilerParams(vmem_limit_bytes=28 * 2**20),
+        compiler_params=pltpu.CompilerParams(vmem_limit_bytes=60 * 2**20),
         cost_estimate=pl.CostEstimate(flops=10**6, bytes_accessed=10**4, transcendentals=0),
-    )(mine, other, w, adapt_a, gate_up, gate_up, adapt_b, down)
-
-
-def backward_kernel(
-    cot_mine_ref, cot_other_ref, w_ref, mine_ref, other_ref, low_ref, active_ref, slope_ref,
-    adapt_b_ref, down_ref, grad_a_ref, grad_b_ref, sum_a_ref, sum_b_ref, scaled_ref, back_ref,
-):
+    )(*blocks, w, adapt_a, gate_up, gate_up, adapt_b, down)
+
+
+def backward_kernel(*refs):
+    cots, blocks, refs = refs[:4], refs[4:8], refs[8:]
+    w_ref, low_ref, active_ref, slope_ref, adapt_b_ref, down_ref, *refs = refs
+    grad_a_ref, grad_b_ref, sum_a_ref, sum_b_ref, scaled_ref, rows_ref, back_ref = refs
     step = pl.program_id(0)
-    half = mine_ref.shape[0]
+    quarter = blocks[0].shape[0]
 
     @pl.when(step == 0)
     def _():
-        mine = column(w_ref[0:1]) * cot_mine_ref[...].astype(jnp.float32)
-        other = column(w_ref[1:2]) * cot_other_ref[...].astype(jnp.float32)
-        scaled_ref[:half] = mine.astype(jnp.bfloat16)
-        scaled_ref[half:] = other.astype(jnp.bfloat16)
+        w = [column(w_ref[0:1]), column(w_ref[1:2])]
+        for at, (cot, block) in enumerate(zip(cots, blocks)):
+            rows = slice(at * quarter, (at + 1) * quarter)
+            w_rows = w[at // 2][at % 2 * quarter : (at % 2 + 1) * quarter]
+            scaled_ref[rows] = (w_rows * cot[...].astype(jnp.float32)).astype(jnp.bfloat16)
+            rows_ref[rows] = block[...]
         back_ref[...] = jnp.zeros_like(back_ref)
 
     back = dot(scaled_ref[...], down_ref[...], 1, 1)
@@ -352,19 +355,14 @@
     @pl.when(step == pl.num_programs(0) - 1)
     def _():
         low_grad = (ADAPTER_SCALE * back_ref[...]).astype(jnp.bfloat16)
-        sum_a_ref[...] = (
-            grad_a_ref[...]
-            + dot(mine_ref[...], low_grad[:half], 0, 0)
-            + dot(other_ref[...], low_grad[half:], 0, 0)
-        )
-
-
-def backward_stage(cots, w, rows, saved, down, adapt_b, grads, chunk=256):
+        sum_a_ref[...] = grad_a_ref[...] + dot(rows_ref[...], low_grad, 0, 0)
+
+
+def backward_stage(cots, w, blocks, saved, down, adapt_b, grads, chunk=256):
     low, active, slope = saved
-    half, features = rows[0].shape
+    quarter, features = blocks[0].shape
     hidden_width = down.shape[0]
     both, ranks = low.shape
-    block = whole((half, features))
     grad_a = whole((features, ranks))
     grad_b = columns(ranks, chunk)
     return pl.pallas_call(
@@ -374,12 +372,9 @@
             jax.ShapeDtypeStruct((features, ranks), jnp.float32),
             jax.ShapeDtypeStruct((ranks, hidden_width), jnp.float32),
         ),
-        in_specs=[
-            block,
-            block,
-            whole((2, half)),
-            block,
-            block,
+        in_specs=[whole((quarter, features))] * 8
+        + [
+            whole((2, 2 * quarter)),
             whole((both, ranks)),
             columns(both, chunk),
             columns(both, chunk),
@@ -391,11 +386,12 @@
         out_specs=(grad_a, grad_b),
         scratch_shapes=[
             pltpu.VMEM((both, features), jnp.bfloat16),
+            pltpu.VMEM((both, features), jnp.bfloat16),
             pltpu.VMEM((both, ranks), jnp.float32),
         ],
-        compiler_params=pltpu.CompilerParams(vmem_limit_bytes=28 * 2**20),
+        compiler_params=pltpu.CompilerParams(vmem_limit_bytes=60 * 2**20),
         cost_estimate=pl.CostEstimate(flops=10**6, bytes_accessed=10**4, transcendentals=0),
-    )(*cots, w, *rows, low, active, slope, adapt_b, down, *grads)
+    )(*cots, *blocks, w, low, active, slope, adapt_b, down, *grads)
 
 
 def z_pairs(*moves):
@@ -472,92 +468,123 @@
     adapt_a = adapter_down_maps[0]
     adapt_b = adapter_up_maps[0].reshape(adapt_a.shape[1], -1)
 
-    def forward(mine, other, w):
-        low, active, slope, part_mine, part_other = forward_stage(
-            mine, other, w, gate_up, down, adapt_a, adapt_b
+    def forward(mine, twin, w):
+        low, active, slope, part, away = forward_stage(
+            (*mine, *twin), w, gate_up, down, adapt_a, adapt_b
         )
-        return (low, active, slope), part_mine, part_other
-
-    def backward(cots, w, rows, saved, grads):
-        return backward_stage(cots, w, rows, saved, down, adapt_b, grads)
-
-    tok_swap = send(tokens, ALL_SWAP)
-    tok_mid = send(tokens, MID_SWAP)
-    tok_twin = sibling(tokens)
+        return (low, active, slope), part, away
+
+    def backward(mine, twin, w, rows, saved, grads):
+        return backward_stage((*mine, *twin), w, rows, saved, down, adapt_b, grads)
+
+    def in_halves(block):
+        rows = block.shape[0] // 2
+        return block[:rows], block[rows:]
+
+    def twins(halves_of):
+        return [sibling(half) for half in halves_of]
+
+    def chip_part(part, away):
+        got = sibling(away)
+        return [add_rounded(*both) for both in zip(in_halves(part), in_halves(got))]
+
+    def pick(inside, outside):
+        return jnp.where(inner, inside, outside)
+
+    tok_a, tok_b = in_halves(tokens)
+    cot_a, cot_b = in_halves(cotangent)
+    swap_a, mid_a = send(tok_a, ALL_SWAP), send(tok_a, MID_SWAP)
+    swap_b, mid_b = send(tok_b, ALL_SWAP), send(tok_b, MID_SWAP)
+    rows0 = (tok_a, tok_b, *twins((tok_a, tok_b)))
     table = dense_route_weights(
         routing, router_route_weights, route_replica_choice, device_expert_table, capacity
     )
     table = jnp.concatenate([table, exchanged(table, 1)])
-    tok_swap, tok_mid, tok_twin, table = fence(tok_swap, tok_mid, tok_twin, table)
-
-    tok_out2 = send(tok_mid, ALL_SWAP)
-    tok_mid2 = send(tok_swap, MID_SWAP)
-    swap_twin = sibling(tok_swap)
+    weights0 = near_weights(table, me)
+    saved0, part0, away0 = forward(rows0[:2], rows0[2:], weights0)
+
+    swap_a, mid_a, part0, away0, table = fence(swap_a, mid_a, part0, away0, table)
+    out2_a, mid2_a = send(mid_a, ALL_SWAP), send(swap_a, MID_SWAP)
+    swap_b, mid_b, swap_a, table = fence(swap_b, mid_b, swap_a, table)
+    out2_b, mid2_b = send(mid_b, ALL_SWAP), send(swap_b, MID_SWAP)
+    rows1 = (swap_a, swap_b, *twins((swap_a, swap_b)))
     more_table = exchanged(table, 2)
-    weights0 = near_weights(table, me)
-    saved0, part0, away0 = forward(tokens, tok_twin, weights0)
-    tok_mid, tok_out2, tok_mid2, swap_twin, more_table, part0, away0, cotangent = fence(
-        tok_mid, tok_out2, tok_mid2, swap_twin, more_table, part0, away0, cotangent
-    )
-
-    tok_out3 = send(tok_mid2, ALL_SWAP)
-    cot_mid = send(cotangent, MID_SWAP)
-    tok_second = jnp.where(inner, tok_mid, tok_out2)
-    second_twin = sibling(tok_second)
     weights1 = near_weights(more_table, me)
-    far_table = exchanged(jnp.concatenate([table, more_table]), 4)
-    saved1, part1, away1 = forward(tok_swap, swap_twin, weights1)
-    tok_mid2, tok_out3, cot_mid, second_twin, far_table, part1, away1, cotangent = fence(
-        tok_mid2, tok_out3, cot_mid, second_twin, far_table, part1, away1, cotangent
-    )
-
-    cot_swap = send(cotangent, ALL_SWAP)
-    tok_third = jnp.where(inner, tok_mid2, tok_out3)
-    third_twin = sibling(tok_third)
-    far = near_weights(far_table, me)
-    weights2 = jnp.where(inner, far[2:], far[:2])
-    weights3 = jnp.where(inner, far[:2], far[2:])
-    saved2, part2, away2 = forward(tok_second, second_twin, weights2)
-    saved3, part3, away3 = forward(tok_third, third_twin, weights3)
-    part3 = add_rounded(part3, sibling(away3))
-    part2 = add_rounded(part2, sibling(away2))
-    cot_twin = sibling(cotangent)
-    to_swap = jnp.where(inner, cot_mid, part3)
-    cot_swap, cot_mid, cot_twin, part2, part3, to_swap = fence(
-        cot_swap, cot_mid, cot_twin, part2, part3, to_swap
-    )
-
-    swapped5 = send(to_swap, ALL_SWAP)
-    cot_mid2 = send(cot_swap, MID_SWAP)
-    cot_swap_twin = sibling(cot_swap)
-    part1 = add_rounded(part1, sibling(away1))
-    part0 = add_rounded(part0, sibling(away0))
+    saved1, part1, away1 = forward(rows1[:2], rows1[2:], weights1)
+
+    out2_a, mid2_a, mid_a, part1, away1, more_table, cot_a, cot_b = fence(
+        out2_a, mid2_a, mid_a, part1, away1, more_table, cot_a, cot_b
+    )
+    out3_a, cmid_a = send(mid2_a, ALL_SWAP), send(cot_a, MID_SWAP)
+    second_a = pick(mid_a, out2_a)
+    out2_b, mid2_b, mid_b, second_a, more_table, cot_b = fence(
+        out2_b, mid2_b, mid_b, second_a, more_table, cot_b
+    )
+    out3_b, cmid_b = send(mid2_b, ALL_SWAP), send(cot_b, MID_SWAP)
+    second_b = pick(mid_b, out2_b)
+    rows2 = (second_a, second_b, *twins((second_a, second_b)))
+    far = near_weights(exchanged(jnp.concatenate([table, more_table]), 4), me)
+    weights2, weights3 = pick(far[2:], far[:2]), pick(far[:2], far[2:])
+    saved2, part2, away2 = forward(rows2[:2], rows2[2:], weights2)
+
+    out3_a, cmid_a, mid2_a, part2, away2, cot_a, cot_b = fence(
+        out3_a, cmid_a, mid2_a, part2, away2, cot_a, cot_b
+    )
+    cswap_a = send(cot_a, ALL_SWAP)
+    third_a = pick(mid2_a, out3_a)
+    out3_b, cmid_b, mid2_b, third_a, cot_b = fence(out3_b, cmid_b, mid2_b, third_a, cot_b)
+    cswap_b = send(cot_b, ALL_SWAP)
+    third_b = pick(mid2_b, out3_b)
+    rows3 = (third_a, third_b, *twins((third_a, third_b)))
+    saved3, part3, away3 = forward(rows3[:2], rows3[2:], weights3)
+
+    cswap_a, cmid_a, part3, away3, part2, away2, cot_a, cot_b = fence(
+        cswap_a, cmid_a, part3, away3, part2, away2, cot_a, cot_b
+    )
+    cmid2_a = send(cswap_a, MID_SWAP)
+    part3_a, part3_b = chip_part(part3, away3)
+    swap5_a = send(pick(cmid_a, part3_a), ALL_SWAP)
+    cswap_b, cmid_b, part3_b, cswap_a = fence(cswap_b, cmid_b, part3_b, cswap_a)
+    swap5_b, cmid2_b = send(pick(cmid_b, part3_b), ALL_SWAP), send(cswap_b, MID_SWAP)
+    part2_a, part2_b = chip_part(part2, away2)
     none = (jnp.zeros(adapt_a.shape, jnp.float32), jnp.zeros(adapt_b.shape, jnp.float32))
-    grads = backward((cotangent, cot_twin), weights0, (tokens, tok_twin), saved0, none)
-    swapped5, cot_mid, cot_mid2, cot_swap_twin, part0, part1, part2, part3, grads = fence(
-        swapped5, cot_mid, cot_mid2, cot_swap_twin, part0, part1, part2, part3, grads
-    )
-
-    swapped6 = send(jnp.where(inner, cot_mid2, part2), ALL_SWAP)
-    third_mid = send(add_rounded(part3, swapped5), MID_SWAP)
-    cot_second = jnp.where(inner, cot_mid, swapped5)
-    cot_second_twin = sibling(cot_second)
-    grads = backward((cot_swap, cot_swap_twin), weights1, (tok_swap, swap_twin), saved1, grads)
-    grads = backward(
-        (cot_second, cot_second_twin), weights2, (tok_second, second_twin), saved2, grads
-    )
-    swapped6, third_mid, cot_mid2, part0, part1, part2, grads = fence(
-        swapped6, third_mid, cot_mid2, part0, part1, part2, grads
-    )
-
-    first_swap = send(add_rounded(part1, third_mid), ALL_SWAP)
-    second_mid = send(add_rounded(part2, swapped6), MID_SWAP)
-    cot_third = jnp.where(inner, cot_mid2, swapped6)
-    grads = backward(
-        (cot_third, sibling(cot_third)), weights3, (tok_third, third_twin), saved3, grads
-    )
+    cots0 = (cot_a, cot_b)
+    grads = backward(cots0, twins(cots0), weights0, rows0, saved0, none)
+
+    swap5_a, cmid2_a, part3_a, part2_a, part2_b, part1, away1, grads = fence(
+        swap5_a, cmid2_a, part3_a, part2_a, part2_b, part1, away1, grads
+    )
+    swap6_a = send(pick(cmid2_a, part2_a), ALL_SWAP)
+    third_mid_a = send(add_rounded(part3_a, swap5_a), MID_SWAP)
+    swap5_b, cmid2_b, part3_b, part2_b, cswap_a = fence(
+        swap5_b, cmid2_b, part3_b, part2_b, cswap_a
+    )
+    swap6_b = send(pick(cmid2_b, part2_b), ALL_SWAP)
+    third_mid_b = send(add_rounded(part3_b, swap5_b), MID_SWAP)
+    part1_a, part1_b = chip_part(part1, away1)
+    cots1 = (cswap_a, cswap_b)
+    grads = backward(cots1, twins(cots1), weights1, rows1, saved1, grads)
+    cots2 = (pick(cmid_a, swap5_a), pick(cmid_b, swap5_b))
+    grads = backward(cots2, twins(cots2), weights2, rows2, saved2, grads)
+
+    swap6_a, third_mid_a, part2_a, part1_a, part1_b, part0, away0, grads = fence(
+        swap6_a, third_mid_a, part2_a, part1_a, part1_b, part0, away0, grads
+    )
+    first_a = send(add_rounded(part1_a, third_mid_a), ALL_SWAP)
+    second_mid_a = send(add_rounded(part2_a, swap6_a), MID_SWAP)
+    cots3_a = pick(cmid2_a, swap6_a)
+    swap6_b, third_mid_b, part2_b, part1_b, cots3_a = fence(
+        swap6_b, third_mid_b, part2_b, part1_b, cots3_a
+    )
+    cots3 = (cots3_a, pick(cmid2_b, swap6_b))
+    grads = backward(cots3, twins(cots3), weights3, rows3, saved3, grads)
+    first_b = send(add_rounded(part1_b, third_mid_b), ALL_SWAP)
+    second_mid_b = send(add_rounded(part2_b, swap6_b), MID_SWAP)
     grad_a, grad_b = group_sum(*grads)
-    mixed = add_rounded(part0, first_swap, second_mid)
+    part0_a, part0_b = chip_part(part0, away0)
+    mixed_a = add_rounded(part0_a, first_a, second_mid_a)
+    mixed_b = add_rounded(part0_b, first_b, second_mid_b)
+    mixed = jnp.concatenate([mixed_a, mixed_b])
     return mixed, grad_a[None], grad_b.reshape(adapter_up_maps.shape)
 
 

time: 157 us -> 196 us (1.25)
  Pallas kernels: 45.1 us -> 72 us
  starting transfers between devices: 39.1 us -> 61.5 us
  waiting for transfers between devices: 45.4 us -> 36.8 us
  local copies, waits for them, and re-layouts: 16.9 us -> 8.38 us
  other arithmetic: 8.35 us -> 14.4 us
    ppermute x28 -> x49, starting transfers between devices: 30.7 us -> 54.2 us  [send(): return lax.ppermute(array, 'expert', pairs)]
    ppermute x28 -> x49, waiting for transfers between devices: 38.3 us -> 21.4 us  [send(): return lax.ppermute(array, 'expert', pairs)]
    pallas_call x4, Pallas kernels: 25 us -> 38.5 us  [forward_stage(): pl.pallas_call(forward_kernel, grid=(steps,), out_shape=(jax.ShapeDtypeSt...]
    pallas_call x4, Pallas kernels: 18.5 us -> 32 us  [backward_stage(): pl.pallas_call(backward_kernel, grid=(hidden_width // chunk,), out_shape=...]
    unnamed x46 -> x74, local copies, waits for them, and re-layouts: 16.8 us -> 4.31 us
    ppermute x6, waiting for transfers between devices: 7.12 us -> 15.4 us  [swap_sum(): other = lax.ppermute(rounded.astype(jnp.bfloat16), 'dp', pairs)]
    convert_element_type x6, other arithmetic: 0.27 us -> 5.42 us  [swap_sum(): other = lax.ppermute(rounded.astype(jnp.bfloat16), 'dp', pairs)]
  transfers between devices with their start and end apart: 34 -> 55, of which waited for: 14 -> 13; matrix products, arithmetic and copies ran while one was open for 3% -> 8% of each run, Pallas kernels for 29% -> 37%
where the time goes in v6:
time: 196 us; the launch traced here: 195 us
  Pallas kernels  72 us (37%)
  starting transfers between devices  61.5 us (31%)
  waiting for transfers between devices  36.8 us (19%)
  other arithmetic  14.4 us (7%)
  local copies, waits for them, and re-layouts  8.38 us (4%)
    ppermute x49, starting transfers between devices, send(): return lax.ppermute(array, 'expert', pairs)  54.2 us
    pallas_call x4, Pallas kernels, forward_stage(): pl.pallas_call(forward_kernel, grid=(steps,), out_shape=(jax.ShapeDtypeSt...  38.5 us
    pallas_call x4, Pallas kernels, backward_stage(): pl.pallas_call(backward_kernel, grid=(hidden_width // chunk,), out_shape=...  32 us
    ppermute x49, waiting for transfers between devices, send(): return lax.ppermute(array, 'expert', pairs)  21.4 us
    ppermute x6, waiting for transfers between devices, swap_sum(): other = lax.ppermute(rounded.astype(jnp.bfloat16), 'dp', pairs)  15.4 us
    ppermute x6, starting transfers between devices, swap_sum(): other = lax.ppermute(rounded.astype(jnp.bfloat16), 'dp', pairs)  7.32 us
    convert_element_type x6, other arithmetic, swap_sum(): other = lax.ppermute(rounded.astype(jnp.bfloat16), 'dp', pairs)  5.42 us
    unnamed x74, local copies, waits for them, and re-layouts  4.31 us
  transfers between devices with their start and end apart: 55, of which 13 were waited for; matrix products, arithmetic and copies ran while one was open for 8% of the time, Pallas kernels for 37%

profile of v6, /device:TPU:0, one launch (start us, length us, event | category | flops | bytes accessed | tf_op | source)
XLA Modules:
  0.0 194.6 jit_solution(9379072359502623576)
XLA Ops:
  4.3 2.6 %collective-permute-start = (bf16[64,2048]{1,0:T(8,128)(2,1)S(1)}, bf16[64,2048]{1,0:T(8,128)(2,1)S(1)}, u32[]{:S(2)}, u32[]{:S(2)}) collective-permute-start(bf16[64,2048]{1,0:T(8,128)(2,1)S(1)} %get-tuple-element.219.refs_0_.refs_4_), channel_id=1, source_target_pairs={{0,2},{1,3},{2,0},{3,1},{4,6},{5,7},{6,4},{7,5},{8,10},{9,11},{10,... | collective-permute-start | bytes 786440 | tf_op jit(solution)/shard_map/ppermute | solution.py:407
  7.6 4.4 %collective-permute-start.7 = (bf16[64,2048]{1,0:T(8,128)(2,1)S(1)}, bf16[64,2048]{1,0:T(8,128)(2,1)S(1)}, u32[]{:S(2)}, u32[]{:S(2)}) collective-permute-start(bf16[64,2048]{1,0:T(8,128)(2,1)S(1)} %get-tuple-element.220.refs_1_.refs_5_), channel_id=1, source_target_pairs={{0,2},{1,3},{2,0},{3,1},{4,6},{5,7},{6,4},{7,5},{8,10},{9,11},{10,... | collective-permute-start | bytes 786440 | tf_op jit(solution)/shard_map/ppermute | solution.py:407
  14.7 9.7 %shard_map.122 = (bf16[256,128]{1,0:T(8,128)(2,1)}, f32[256,768]{1,0:T(8,128)}, f32[256,768]{1,0:T(8,128)}, bf16[128,2048]{1,0:T(8,128)(2,1)}, bf16[128,2048]{1,0:T(8,128)(2,1)}) custom-call(bf16[64,2048]{1,0:T(8,128)(2,1)} %copy-done.2, bf16[64,2048]{1,0:T(8,128)(2,1)} %copy-done.3, bf16[64,2048]{1,0:T(8,128)(2,1)} %copy-done.12, ...), custom_call_target="tpu_custom_call" | custom-call | flops 1000000 | bytes 10000 | tf_op jit(solution)/shard_map/pallas_call | solution.py:298
  27.1 3.3 %collective-permute-start.11 = (f32[16,128]{1,0:T(8,128)S(1)}, f32[16,128]{1,0:T(8,128)S(1)}, u32[]{:S(2)}, u32[]{:S(2)}) collective-permute-start(f32[16,128]{1,0:T(8,128)S(1)} %get-tuple-element.113), channel_id=1, source_target_pairs={{0,2},{1,3},{2,0},{3,1},{4,6},{5,7},{6,4},{7,5},{8,10},{9,11},{10,... | collective-permute-start | bytes 24584 | tf_op jit(solution)/shard_map/ppermute | solution.py:407
  33.8 4.5 %collective-permute-start.14 = (bf16[64,2048]{1,0:T(8,128)(2,1)S(1)}, bf16[64,2048]{1,0:T(8,128)(2,1)S(1)}, u32[]{:S(2)}, u32[]{:S(2)}) collective-permute-start(bf16[64,2048]{1,0:T(8,128)(2,1)S(1)} %collective-permute-done.8), channel_id=1, source_target_pairs={{0,2},{1,3},{2,0},{3,1},{4,6},{5,7},{6,4},{7,5},{8,10},{9,11},{10,... | collective-permute-start | bytes 786440 | tf_op jit(solution)/shard_map/ppermute | solution.py:407
  39.0 9.6 %shard_map.123 = (bf16[256,128]{1,0:T(8,128)(2,1)}, f32[256,768]{1,0:T(8,128)}, f32[256,768]{1,0:T(8,128)}, bf16[128,2048]{1,0:T(8,128)(2,1)}, bf16[128,2048]{1,0:T(8,128)(2,1)}) custom-call(bf16[64,2048]{1,0:T(8,128)(2,1)} %copy-done.8, bf16[64,2048]{1,0:T(8,128)(2,1)} %copy-done.9, bf16[64,2048]{1,0:T(8,128)(2,1)} %copy-done.10, ...), custom_call_target="tpu_custom_call" | custom-call | flops 1000000 | bytes 10000 | tf_op jit(solution)/shard_map/pallas_call | solution.py:298
  49.6 4.7 %collective-permute-start.18 = (f32[32,128]{1,0:T(8,128)S(1)}, f32[32,128]{1,0:T(8,128)S(1)}, u32[]{:S(2)}, u32[]{:S(2)}) collective-permute-start(f32[32,128]{1,0:T(8,128)S(1)} %pad_maximum_fusion.1), channel_id=1, source_target_pairs={{0,4},{1,5},{2,6},{3,7},{4,0},{5,1},{6,2},{7,3},{8,12},{9,13},{10,... | collective-permute-start | bytes 49160 | tf_op jit(solution)/shard_map/ppermute | solution.py:407
  54.6 4.6 %collective-permute-done.18 = f32[32,128]{1,0:T(8,128)S(1)} collective-permute-done((f32[32,128]{1,0:T(8,128)S(1)}, f32[32,128]{1,0:T(8,128)S(1)}, u32[]{:S(2)}, u32[]{:S(2)}) %collective-permute-start.18) | collective-permute-done | bytes 16416 | tf_op jit(solution)/shard_map/ppermute | solution.py:407
  61.2 9.6 %shard_map.124 = (bf16[256,128]{1,0:T(8,128)(2,1)}, f32[256,768]{1,0:T(8,128)}, f32[256,768]{1,0:T(8,128)}, bf16[128,2048]{1,0:T(8,128)(2,1)}, bf16[128,2048]{1,0:T(8,128)(2,1)}) custom-call(bf16[64,2048]{1,0:T(8,128)(2,1)} %copy-done.6, bf16[64,2048]{1,0:T(8,128)(2,1)} %copy-done.7, bf16[64,2048]{1,0:T(8,128)(2,1)} %copy-done.16, ...), custom_call_target="tpu_custom_call" | custom-call | flops 1000000 | bytes 10000 | tf_op jit(solution)/shard_map/pallas_call | solution.py:298
  71.6 3.7 %collective-permute-start.19 = (bf16[64,2048]{1,0:T(8,128)(2,1)S(1)}, bf16[64,2048]{1,0:T(8,128)(2,1)S(1)}, u32[]{:S(2)}, u32[]{:S(2)}) collective-permute-start(bf16[64,2048]{1,0:T(8,128)(2,1)S(1)} %get-tuple-element.152.refs_0_), channel_id=1, source_target_pairs={{0,2},{1,3},{2,0},{3,1},{4,6},{5,7},{6,4},{7,5},{8,10},{9,11},{10,... | collective-permute-start | bytes 786440 | tf_op jit(solution)/shard_map/ppermute | solution.py:407
  76.1 9.6 %shard_map.125 = (bf16[256,128]{1,0:T(8,128)(2,1)}, f32[256,768]{1,0:T(8,128)}, f32[256,768]{1,0:T(8,128)}, bf16[128,2048]{1,0:T(8,128)(2,1)}, bf16[128,2048]{1,0:T(8,128)(2,1)}) custom-call(bf16[64,2048]{1,0:T(8,128)(2,1)} %copy-done.4, bf16[64,2048]{1,0:T(8,128)(2,1)} %copy-done.5, bf16[64,2048]{1,0:T(8,128)(2,1)} %copy-done.14, ...), custom_call_target="tpu_custom_call" | custom-call | flops 1000000 | bytes 10000 | tf_op jit(solution)/shard_map/pallas_call | solution.py:298
  91.2 8.0 %shard_map.126 = (f32[2048,128]{1,0:T(8,128)}, f32[128,768]{1,0:T(8,128)}) custom-call(bf16[64,2048]{1,0:T(8,128)(2,1)} %copy-done.19, bf16[64,2048]{1,0:T(8,128)(2,1)} %copy-done.18, bf16[64,2048]{1,0:T(8,128)(2,1)} %copy-done.32, bf16[64,2048]{1,0:T(8,128)(2,1)} %copy-done.34, bf16[64,2048]{1,0:T(8,128)(2,1)} %copy-done.2, bf16[64,2048]{1,0:T(8,128)(2,1)} %copy-done.3, ...), custom_call_target="tpu_custom_call" | custom-call | flops 1000000 | bytes 10000 | tf_op jit(solution)/shard_map/pallas_call | solution.py:368
  100.7 4.9 %collective-permute-start.25 = (bf16[64,2048]{1,0:T(8,128)(2,1)S(1)}, bf16[64,2048]{1,0:T(8,128)(2,1)S(1)}, u32[]{:S(2)}, u32[]{:S(2)}) collective-permute-start(bf16[64,2048]{1,0:T(8,128)(2,1)S(1)} %get-tuple-element.209), channel_id=1, source_target_pairs={{0,2},{1,3},{2,0},{3,1},{4,6},{5,7},{6,4},{7,5},{8,10},{9,11},{10,... | collective-permute-start | bytes 786440 | tf_op jit(solution)/shard_map/ppermute | solution.py:407
  105.9 6.8 %collective-permute-done.25 = bf16[64,2048]{1,0:T(8,128)(2,1)S(1)} collective-permute-done((bf16[64,2048]{1,0:T(8,128)(2,1)S(1)}, bf16[64,2048]{1,0:T(8,128)(2,1)S(1)}, u32[]{:S(2)}, u32[]{:S(2)}) %collective-permute-start.25) | collective-permute-done | bytes 262176 | tf_op jit(solution)/shard_map/ppermute | solution.py:407
  112.8 5.2 %collective-permute-done.34 = bf16[64,2048]{1,0:T(8,128)(2,1)S(1)} collective-permute-done((bf16[64,2048]{1,0:T(8,128)(2,1)S(1)}, bf16[64,2048]{1,0:T(8,128)(2,1)S(1)}, u32[]{:S(2)}, u32[]{:S(2)}) %collective-permute-start.34) | collective-permute-done | bytes 262176 | tf_op jit(solution)/shard_map/ppermute | solution.py:407
  123.4 8.0 %shard_map.127 = (f32[2048,128]{1,0:T(8,128)}, f32[128,768]{1,0:T(8,128)}) custom-call(bf16[64,2048]{1,0:T(8,128)(2,1)} %copy-done.29, bf16[64,2048]{1,0:T(8,128)(2,1)} %collective-permute-done.33.refs_1_, bf16[64,2048]{1,0:T(8,128)(2,1)} %copy-done.33, bf16[64,2048]{1,0:T(8,128)(2,1)} %copy-done.30, bf16[64,2048]{1,0:T(8,128)(2,1)} %copy-done.8, ...), custom_call_target="tpu_custom_call" | custom-call | flops 1000000 | bytes 10000 | tf_op jit(solution)/shard_map/pallas_call | solution.py:368
  131.4 2.5 %collective-permute-start.43 = (bf16[64,2048]{1,0:T(8,128)(2,1)}, bf16[64,2048]{1,0:T(8,128)(2,1)S(1)}, u32[]{:S(2)}, u32[]{:S(2)}) collective-permute-start(bf16[64,2048]{1,0:T(8,128)(2,1)} %broadcast_select_fusion.2), channel_id=1, source_target_pairs={{0,2},{1,3},{2,0},{3,1},{4,6},{5,7},{6,4},{7,5},{8,10},{9,11},{10,... | collective-permute-start | bytes 786440 | tf_op jit(solution)/shard_map/ppermute | solution.py:407
  135.2 8.0 %shard_map.128 = (f32[2048,128]{1,0:T(8,128)}, f32[128,768]{1,0:T(8,128)}) custom-call(bf16[64,2048]{1,0:T(8,128)(2,1)} %copy-done.20, bf16[64,2048]{1,0:T(8,128)(2,1)} %copy-done.21, bf16[64,2048]{1,0:T(8,128)(2,1)} %copy-done.31, bf16[64,2048]{1,0:T(8,128)(2,1)} %collective-permute-done.37.refs_3_, bf16[64,2048]{1,0:T(8,128)(2,1)} %copy-done.6, ...), custom_call_target="tpu_custom_call" | custom-call | flops 1000000 | bytes 10000 | tf_op jit(solution)/shard_map/pallas_call | solution.py:368
  145.2 4.1 %collective-permute-start.41 = (bf16[64,2048]{1,0:T(8,128)(2,1)S(1)}, bf16[64,2048]{1,0:T(8,128)(2,1)S(1)}, u32[]{:S(2)}, u32[]{:S(2)}) collective-permute-start(bf16[64,2048]{1,0:T(8,128)(2,1)S(1)} %add_convert_fusion.7), channel_id=1, source_target_pairs={{0,2},{1,3},{2,0},{3,1},{4,6},{5,7},{6,4},{7,5},{8,10},{9,11},{10,... | collective-permute-start | bytes 786440 | tf_op jit(solution)/shard_map/ppermute | solution.py:407
  152.6 8.0 %shard_map.129 = (f32[2048,128]{1,0:T(8,128)}, f32[128,768]{1,0:T(8,128)}) custom-call(bf16[64,2048]{1,0:T(8,128)(2,1)} %copy-done.22, bf16[64,2048]{1,0:T(8,128)(2,1)} %copy-done.23, bf16[64,2048]{1,0:T(8,128)(2,1)} %copy-done.35, bf16[64,2048]{1,0:T(8,128)(2,1)} %copy-done.36, bf16[64,2048]{1,0:T(8,128)(2,1)} %copy-done.4, bf16[64,2048]{1,0:T(8,128)(2,1)} %copy-done.5, ...), custom_call_target="tpu_custom_call" | custom-call | flops 1000000 | bytes 10000 | tf_op jit(solution)/shard_map/pallas_call | solution.py:368
  166.1 2.8 %collective-permute-done.51 = bf16[640,128]{1,0:T(8,128)(2,1)S(1)} collective-permute-done((bf16[640,128]{1,0:T(8,128)(2,1)S(1)}, bf16[640,128]{1,0:T(8,128)(2,1)S(1)}, u32[]{:S(2)}, u32[]{:S(2)}) %collective-permute-start.51) | collective-permute-done | bytes 163872 | tf_op jit(solution)/shard_map/ppermute | solution.py:437
  169.5 2.7 %collective-permute-done.53 = bf16[128,768]{1,0:T(8,128)(2,1)S(1)} collective-permute-done((bf16[128,768]{1,0:T(8,128)(2,1)S(1)}, bf16[128,768]{1,0:T(8,128)(2,1)S(1)}, u32[]{:S(2)}, u32[]{:S(2)}) %collective-permute-start.53) | collective-permute-done | bytes 196640 | tf_op jit(solution)/shard_map/ppermute | solution.py:437
  180.9 4.9 %collective-permute-done.49 = bf16[1408,128]{1,0:T(8,128)(2,1)S(1)} collective-permute-done((bf16[1408,128]{1,0:T(8,128)(2,1)S(1)}, bf16[1408,128]{1,0:T(8,128)(2,1)S(1)}, u32[]{:S(2)}, u32[]{:S(2)}) %collective-permute-start.49) | collective-permute-done | bytes 360480 | tf_op jit(solution)/shard_map/ppermute | solution.py:437
  189.4 2.3 %collective-permute-done.54 = bf16[128,768]{1,0:T(8,128)(2,1)S(1)} collective-permute-done((bf16[128,768]{1,0:T(8,128)(2,1)S(1)}, bf16[128,768]{1,0:T(8,128)(2,1)S(1)}, u32[]{:S(2)}, u32[]{:S(2)}) %collective-permute-start.54) | collective-permute-done | bytes 196640 | tf_op jit(solution)/shard_map/ppermute | solution.py:437
  (212 shorter events, 58.5 us)
Async XLA Ops:
  4.3 20.1 %collective-permute-start = (bf16[64,2048]{1,0:T(8,128)(2,1)S(1)}, bf16[64,2048]{1,0:T(8,128)(2,1)S(1)}, u32[]{:S(2)}, u32[]{:S(2)}) collective-permute-start(bf16[64,2048]{1,0:T(8,128)(2,1)S(1)} %get-tuple-element.219.refs_0_.refs_4_), channel_id=1, source_target_pairs={{0,2},{1,3},{2,0},{3,1},{4,6},{5,7},{6,4},{7,5},{8,10},{9,11},{10,... | collective-permute-start | bytes 786440 | tf_op jit(solution)/shard_map/ppermute | solution.py:407
  6.9 17.5 %collective-permute-start.1 = (bf16[64,2048]{1,0:T(8,128)(2,1)S(1)}, bf16[64,2048]{1,0:T(8,128)(2,1)S(1)}, u32[]{:S(2)}, u32[]{:S(2)}) collective-permute-start(bf16[64,2048]{1,0:T(8,128)(2,1)S(1)} %get-tuple-element.219.refs_0_.refs_4_), channel_id=1, source_target_pairs={{2,4},{3,5},{4,2},{5,3},{10,12},{11,13},{12,10},{13,11},{18,20},{1... | collective-permute-start | bytes 786440 | tf_op jit(solution)/shard_map/ppermute | solution.py:407
  7.6 18.9 %collective-permute-start.7 = (bf16[64,2048]{1,0:T(8,128)(2,1)S(1)}, bf16[64,2048]{1,0:T(8,128)(2,1)S(1)}, u32[]{:S(2)}, u32[]{:S(2)}) collective-permute-start(bf16[64,2048]{1,0:T(8,128)(2,1)S(1)} %get-tuple-element.220.refs_1_.refs_5_), channel_id=1, source_target_pairs={{0,2},{1,3},{2,0},{3,1},{4,6},{5,7},{6,4},{7,5},{8,10},{9,11},{10,... | collective-permute-start | bytes 786440 | tf_op jit(solution)/shard_map/ppermute | solution.py:407
  12.0 14.5 %collective-permute-start.8 = (bf16[64,2048]{1,0:T(8,128)(2,1)S(1)}, bf16[64,2048]{1,0:T(8,128)(2,1)S(1)}, u32[]{:S(2)}, u32[]{:S(2)}) collective-permute-start(bf16[64,2048]{1,0:T(8,128)(2,1)S(1)} %get-tuple-element.220.refs_1_.refs_5_), channel_id=1, source_target_pairs={{2,4},{3,5},{4,2},{5,3},{10,12},{11,13},{12,10},{13,11},{18,20},{1... | collective-permute-start | bytes 786440 | tf_op jit(solution)/shard_map/ppermute | solution.py:407
  24.5 24.2 %collective-permute-start.5 = (bf16[64,2048]{1,0:T(8,128)(2,1)S(1)}, bf16[64,2048]{1,0:T(8,128)(2,1)S(1)}, u32[]{:S(2)}, u32[]{:S(2)}) collective-permute-start(bf16[64,2048]{1,0:T(8,128)(2,1)S(1)} %collective-permute-done.1), channel_id=1, source_target_pairs={{0,2},{1,3},{2,0},{3,1},{4,6},{5,7},{6,4},{7,5},{8,10},{9,11},{10,... | collective-permute-start | bytes 786440 | tf_op jit(solution)/shard_map/ppermute | solution.py:407
  25.8 22.8 %collective-permute-start.6 = (bf16[64,2048]{1,0:T(8,128)(2,1)S(1)}, bf16[64,2048]{1,0:T(8,128)(2,1)S(1)}, u32[]{:S(2)}, u32[]{:S(2)}) collective-permute-start(bf16[64,2048]{1,0:T(8,128)(2,1)S(1)} %collective-permute-done.refs_0_.refs_4_), channel_id=1, source_target_pairs={{2,4},{3,5},{4,2},{5,3},{10,12},{11,13},{12,10},{13,11},{18,20},{1... | collective-permute-start | bytes 786440 | tf_op jit(solution)/shard_map/ppermute | solution.py:407
  32.5 17.0 %collective-permute-start.15 = (bf16[64,2048]{1,0:T(8,128)(2,1)S(1)}, bf16[64,2048]{1,0:T(8,128)(2,1)S(1)}, u32[]{:S(2)}, u32[]{:S(2)}) collective-permute-start(bf16[64,2048]{1,0:T(8,128)(2,1)S(1)} %collective-permute-done.7.refs_1_.refs_5_), channel_id=1, source_target_pairs={{2,4},{3,5},{4,2},{5,3},{10,12},{11,13},{12,10},{13,11},{18,20},{1... | collective-permute-start | bytes 786440 | tf_op jit(solution)/shard_map/ppermute | solution.py:407
  33.8 15.8 %collective-permute-start.14 = (bf16[64,2048]{1,0:T(8,128)(2,1)S(1)}, bf16[64,2048]{1,0:T(8,128)(2,1)S(1)}, u32[]{:S(2)}, u32[]{:S(2)}) collective-permute-start(bf16[64,2048]{1,0:T(8,128)(2,1)S(1)} %collective-permute-done.8), channel_id=1, source_target_pairs={{0,2},{1,3},{2,0},{3,1},{4,6},{5,7},{6,4},{7,5},{8,10},{9,11},{10,... | collective-permute-start | bytes 786440 | tf_op jit(solution)/shard_map/ppermute | solution.py:407
  48.6 22.1 %collective-permute-start.12 = (bf16[64,2048]{1,0:T(8,128)(2,1)S(1)}, bf16[64,2048]{1,0:T(8,128)(2,1)S(1)}, u32[]{:S(2)}, u32[]{:S(2)}) collective-permute-start(bf16[64,2048]{1,0:T(8,128)(2,1)S(1)} %collective-permute-done.6), channel_id=1, source_target_pairs={{0,2},{1,3},{2,0},{3,1},{4,6},{5,7},{6,4},{7,5},{8,10},{9,11},{10,... | collective-permute-start | bytes 786440 | tf_op jit(solution)/shard_map/ppermute | solution.py:407
  48.8 22.0 %collective-permute-start.13 = (bf16[64,2048]{1,0:T(8,128)(2,1)S(1)}, bf16[64,2048]{1,0:T(8,128)(2,1)S(1)}, u32[]{:S(2)}, u32[]{:S(2)}) collective-permute-start(bf16[64,2048]{1,0:T(8,128)(2,1)S(1)} %get-tuple-element.152.refs_0_), channel_id=1, source_target_pairs={{2,4},{3,5},{4,2},{5,3},{10,12},{11,13},{12,10},{13,11},{18,20},{1... | collective-permute-start | bytes 786440 | tf_op jit(solution)/shard_map/ppermute | solution.py:407
  87.8 18.2 %collective-permute-start.26 = (bf16[64,2048]{1,0:T(8,128)(2,1)S(1)}, bf16[64,2048]{1,0:T(8,128)(2,1)S(1)}, u32[]{:S(2)}, u32[]{:S(2)}) collective-permute-start(bf16[64,2048]{1,0:T(8,128)(2,1)S(1)} %collective-permute-done.19.refs_0_), channel_id=1, source_target_pairs={{2,4},{3,5},{4,2},{5,3},{10,12},{11,13},{12,10},{13,11},{18,20},{1... | collective-permute-start | bytes 786440 | tf_op jit(solution)/shard_map/ppermute | solution.py:407
  88.6 17.0 %collective-permute-start.27 = (bf16[128,2048]{1,0:T(8,128)(2,1)}, bf16[128,2048]{1,0:T(8,128)(2,1)S(1)}, u32[]{:S(2)}, u32[]{:S(2)}) collective-permute-start(bf16[128,2048]{1,0:T(8,128)(2,1)} %get-tuple-element.149), channel_id=1, source_target_pairs={{0,1},{1,0},{2,3},{3,2},{4,5},{5,4},{6,7},{7,6},{8,9},{9,8},{10,11... | collective-permute-start | bytes 1572872 | tf_op jit(solution)/shard_map/ppermute | solution.py:407
  99.3 18.7 %collective-permute-start.35 = (bf16[64,2048]{1,0:T(8,128)(2,1)}, bf16[64,2048]{1,0:T(8,128)(2,1)S(1)}, u32[]{:S(2)}, u32[]{:S(2)}) collective-permute-start(bf16[64,2048]{1,0:T(8,128)(2,1)} %collective-permute-done.33.refs_1_), channel_id=1, source_target_pairs={{2,4},{3,5},{4,2},{5,3},{10,12},{11,13},{12,10},{13,11},{18,20},{1... | collective-permute-start | bytes 786440 | tf_op jit(solution)/shard_map/ppermute | solution.py:407
  100.0 20.2 %collective-permute-start.39 = (bf16[64,2048]{1,0:T(8,128)(2,1)}, bf16[64,2048]{1,0:T(8,128)(2,1)S(1)}, u32[]{:S(2)}, u32[]{:S(2)}) collective-permute-start(bf16[64,2048]{1,0:T(8,128)(2,1)} %collective-permute-done.33.refs_1_), channel_id=1, source_target_pairs={{0,1},{1,0},{2,3},{3,2},{4,5},{5,4},{6,7},{7,6},{8,9},{9,8},{10,11... | collective-permute-start | bytes 786440 | tf_op jit(solution)/shard_map/ppermute | solution.py:407
  112.7 30.5 %collective-permute-start.32 = (bf16[128,2048]{1,0:T(8,128)(2,1)}, bf16[128,2048]{1,0:T(8,128)(2,1)S(1)}, u32[]{:S(2)}, u32[]{:S(2)}) collective-permute-start(bf16[128,2048]{1,0:T(8,128)(2,1)} %get-tuple-element.164), channel_id=1, source_target_pairs={{0,1},{1,0},{2,3},{3,2},{4,5},{5,4},{6,7},{7,6},{8,9},{9,8},{10,11... | collective-permute-start | bytes 1572872 | tf_op jit(solution)/shard_map/ppermute | solution.py:407
  118.2 15.7 %collective-permute-start.37 = (bf16[64,2048]{1,0:T(8,128)(2,1)S(1)}, bf16[64,2048]{1,0:T(8,128)(2,1)}, u32[]{:S(2)}, u32[]{:S(2)}) collective-permute-start(bf16[64,2048]{1,0:T(8,128)(2,1)S(1)} %broadcast_select_fusion.3.refs_1_), channel_id=1, source_target_pairs={{0,1},{1,0},{2,3},{3,2},{4,5},{5,4},{6,7},{7,6},{8,9},{9,8},{10,11... | collective-permute-start | bytes 786440 | tf_op jit(solution)/shard_map/ppermute | solution.py:407
  120.3 23.1 %collective-permute-start.30 = (bf16[64,2048]{1,0:T(8,128)(2,1)}, bf16[64,2048]{1,0:T(8,128)(2,1)S(1)}, u32[]{:S(2)}, u32[]{:S(2)}) collective-permute-start(bf16[64,2048]{1,0:T(8,128)(2,1)} %broadcast_select_fusion.6), channel_id=1, source_target_pairs={{0,2},{1,3},{2,0},{3,1},{4,6},{5,7},{6,4},{7,5},{8,10},{9,11},{10,... | collective-permute-start | bytes 786440 | tf_op jit(solution)/shard_map/ppermute | solution.py:407
  122.0 21.4 %collective-permute-start.31 = (bf16[64,2048]{1,0:T(8,128)(2,1)S(1)}, bf16[64,2048]{1,0:T(8,128)(2,1)}, u32[]{:S(2)}, u32[]{:S(2)}) collective-permute-start(bf16[64,2048]{1,0:T(8,128)(2,1)S(1)} %add_convert_fusion.12), channel_id=1, source_target_pairs={{2,4},{3,5},{4,2},{5,3},{10,12},{11,13},{12,10},{13,11},{18,20},{1... | collective-permute-start | bytes 786440 | tf_op jit(solution)/shard_map/ppermute | solution.py:407
  131.4 17.9 %collective-permute-start.43 = (bf16[64,2048]{1,0:T(8,128)(2,1)}, bf16[64,2048]{1,0:T(8,128)(2,1)S(1)}, u32[]{:S(2)}, u32[]{:S(2)}) collective-permute-start(bf16[64,2048]{1,0:T(8,128)(2,1)} %broadcast_select_fusion.2), channel_id=1, source_target_pairs={{0,2},{1,3},{2,0},{3,1},{4,6},{5,7},{6,4},{7,5},{8,10},{9,11},{10,... | collective-permute-start | bytes 786440 | tf_op jit(solution)/shard_map/ppermute | solution.py:407
  133.9 15.4 %collective-permute-start.44 = (bf16[64,2048]{1,0:T(8,128)(2,1)S(1)}, bf16[64,2048]{1,0:T(8,128)(2,1)}, u32[]{:S(2)}, u32[]{:S(2)}) collective-permute-start(bf16[64,2048]{1,0:T(8,128)(2,1)S(1)} %add_convert_fusion.3), channel_id=1, source_target_pairs={{2,4},{3,5},{4,2},{5,3},{10,12},{11,13},{12,10},{13,11},{18,20},{1... | collective-permute-start | bytes 786440 | tf_op jit(solution)/shard_map/ppermute | solution.py:407
  143.5 31.0 %collective-permute-start.42 = (bf16[64,2048]{1,0:T(8,128)(2,1)S(1)}, bf16[64,2048]{1,0:T(8,128)(2,1)S(1)}, u32[]{:S(2)}, u32[]{:S(2)}) collective-permute-start(bf16[64,2048]{1,0:T(8,128)(2,1)S(1)} %add_convert_fusion.6), channel_id=1, source_target_pairs={{2,4},{3,5},{4,2},{5,3},{10,12},{11,13},{12,10},{13,11},{18,20},{1... | collective-permute-start | bytes 786440 | tf_op jit(solution)/shard_map/ppermute | solution.py:407
  145.2 30.8 %collective-permute-start.41 = (bf16[64,2048]{1,0:T(8,128)(2,1)S(1)}, bf16[64,2048]{1,0:T(8,128)(2,1)S(1)}, u32[]{:S(2)}, u32[]{:S(2)}) collective-permute-start(bf16[64,2048]{1,0:T(8,128)(2,1)S(1)} %add_convert_fusion.7), channel_id=1, source_target_pairs={{0,2},{1,3},{2,0},{3,1},{4,6},{5,7},{6,4},{7,5},{8,10},{9,11},{10,... | collective-permute-start | bytes 786440 | tf_op jit(solution)/shard_map/ppermute | solution.py:407
  149.2 30.6 %collective-permute-start.40 = (bf16[128,2048]{1,0:T(8,128)(2,1)}, bf16[128,2048]{1,0:T(8,128)(2,1)S(1)}, u32[]{:S(2)}, u32[]{:S(2)}) collective-permute-start(bf16[128,2048]{1,0:T(8,128)(2,1)} %get-tuple-element.188), channel_id=1, source_target_pairs={{0,1},{1,0},{2,3},{3,2},{4,5},{5,4},{6,7},{7,6},{8,9},{9,8},{10,11... | collective-permute-start | bytes 1572872 | tf_op jit(solution)/shard_map/ppermute | solution.py:407
  176.5 15.2 %collective-permute-start.54 = (bf16[128,768]{1,0:T(8,128)(2,1)S(1)}, bf16[128,768]{1,0:T(8,128)(2,1)S(1)}, u32[]{:S(2)}, u32[]{:S(2)}) collective-permute-start(bf16[128,768]{1,0:T(8,128)(2,1)S(1)} %fusion.3), channel_id=1, source_target_pairs={{0,8},{8,0},{16,24},{24,16},{1,9},{9,1},{17,25},{25,17},{2,10},{10... | collective-permute-start | bytes 589832 | tf_op jit(solution)/shard_map/ppermute | solution.py:437
  (68 other events, 694.8 us)

commit v7 on v6

--- a/solution.py
+++ b/solution.py
@@ -239,159 +239,114 @@
     )(table, routing.T, choice.T, weights.T)
 
 
-def forward_kernel(*refs):
-    blocks, refs = refs[:4], refs[4:]
-    w_ref, adapt_a_ref, gate_ref, up_ref, adapt_b_ref, down_ref, *refs = refs
+def load_blocks(rows_ref, blocks):
+    rows = blocks[0].shape[0]
+    for at, block in enumerate(blocks):
+        rows_ref[at * rows : (at + 1) * rows] = block[...]
+
+
+def forward_kernel(n_blocks, chunk, *refs):
+    blocks, refs = refs[:n_blocks], refs[n_blocks:]
+    w_ref, adapt_a_ref, gate_up_ref, adapt_b_ref, down_ref, *refs = refs
     low_ref, active_ref, slope_ref, part_mine_ref, part_other_ref, rows_ref, total_ref = refs
-    step = pl.program_id(0)
-    quarter = blocks[0].shape[0]
-    half = 2 * quarter
-
-    @pl.when(step == 0)
-    def _():
-        for at, block in enumerate(blocks):
-            rows_ref[at * quarter : (at + 1) * quarter] = block[...]
-        low_ref[...] = dot(rows_ref[...], adapt_a_ref[...]).astype(jnp.bfloat16)
-
+    half = part_mine_ref.shape[0]
+    hidden_width = down_ref.shape[0]
+    load_blocks(rows_ref, blocks)
     rows = rows_ref[...]
-    low_gate, low_up = halves(low_ref[...])
-    gate = dot(rows, gate_ref[...]) + ADAPTER_SCALE * dot(low_gate, adapt_b_ref[...])
-    up = dot(rows, up_ref[...]) + ADAPTER_SCALE * dot(low_up, adapt_b_ref[...])
-    sigmoid_gate = jax.nn.sigmoid(gate)
-    active = gate * sigmoid_gate
-    active_ref[...] = active
-    slope_ref[...] = up * (sigmoid_gate * (1.0 + gate * (1.0 - sigmoid_gate)))
-    hidden = (active * up).astype(jnp.bfloat16)
-    more = dot(hidden, down_ref[...])
-
-    @pl.when(step == 0)
-    def _():
-        total_ref[...] = more
-
-    @pl.when(step > 0)
-    def _():
-        total_ref[...] += more
-
-    @pl.when(step == pl.num_programs(0) - 1)
-    def _():
-        out = total_ref[...].astype(jnp.bfloat16).astype(jnp.float32)
-        part_mine_ref[...] = (column(w_ref[0:1]) * out[:half]).astype(jnp.bfloat16)
-        part_other_ref[...] = (column(w_ref[1:2]) * out[half:]).astype(jnp.bfloat16)
-
-
-def whole(shape):
-    return pl.BlockSpec(shape, lambda j: (0,) * len(shape))
-
-
-def columns(rows, width, start=0):
-    return pl.BlockSpec((rows, width), lambda j: (0, start + j))
+    low = dot(rows, adapt_a_ref[...]).astype(jnp.bfloat16)
+    low_ref[...] = low
+    low_gate, low_up = halves(low)
+    for start in range(0, hidden_width, chunk):
+        here = slice(start, start + chunk)
+        there = slice(hidden_width + start, hidden_width + start + chunk)
+        adapt_b = adapt_b_ref[:, here]
+        gate = dot(rows, gate_up_ref[:, here]) + ADAPTER_SCALE * dot(low_gate, adapt_b)
+        up = dot(rows, gate_up_ref[:, there]) + ADAPTER_SCALE * dot(low_up, adapt_b)
+        sigmoid_gate = jax.nn.sigmoid(gate)
+        active = gate * sigmoid_gate
+        active_ref[:, here] = active
+        slope_ref[:, here] = up * (sigmoid_gate * (1.0 + gate * (1.0 - sigmoid_gate)))
+        more = dot((active * up).astype(jnp.bfloat16), down_ref[here])
+        if start == 0:
+            total_ref[...] = more
+        else:
+            total_ref[...] += more
+    out = total_ref[...].astype(jnp.bfloat16).astype(jnp.float32)
+    part_mine_ref[...] = (column(w_ref[0:1]) * out[:half]).astype(jnp.bfloat16)
+    part_other_ref[...] = (column(w_ref[1:2]) * out[half:]).astype(jnp.bfloat16)
+
+
+VMEM = pl.BlockSpec(memory_space=pltpu.VMEM)
 
 
 def forward_stage(blocks, w, gate_up, down, adapt_a, adapt_b, chunk=256):
-    quarter, features = blocks[0].shape
-    half = 2 * quarter
-    hidden_width = down.shape[0]
-    both, ranks = 2 * half, adapt_a.shape[1]
-    steps = hidden_width // chunk
-    saved = jax.ShapeDtypeStruct((both, hidden_width), jnp.float32)
-    part = jax.ShapeDtypeStruct((half, features), jnp.bfloat16)
+    features = blocks[0].shape[1]
+    both = len(blocks) * blocks[0].shape[0]
+    saved = jax.ShapeDtypeStruct((both, down.shape[0]), jnp.float32)
+    part = jax.ShapeDtypeStruct((both // 2, features), jnp.bfloat16)
+    low = jax.ShapeDtypeStruct((both, adapt_a.shape[1]), jnp.bfloat16)
     return pl.pallas_call(
-        forward_kernel,
-        grid=(steps,),
-        out_shape=(jax.ShapeDtypeStruct((both, ranks), jnp.bfloat16), saved, saved, part, part),
-        in_specs=[whole((quarter, features))] * 4
-        + [
-            whole((2, half)),
-            whole((features, ranks)),
-            columns(features, chunk),
-            columns(features, chunk, steps),
-            columns(ranks, chunk),
-            pl.BlockSpec((chunk, features), lambda j: (j, 0)),
-        ],
-        out_specs=(
-            whole((both, ranks)),
-            columns(both, chunk),
-            columns(both, chunk),
-            whole((half, features)),
-            whole((half, features)),
-        ),
+        functools.partial(forward_kernel, len(blocks), chunk),
+        out_shape=(low, saved, saved, part, part),
+        in_specs=[VMEM] * (len(blocks) + 5),
+        out_specs=(VMEM,) * 5,
         scratch_shapes=[
             pltpu.VMEM((both, features), jnp.bfloat16),
             pltpu.VMEM((both, features), jnp.float32),
         ],
-        compiler_params=pltpu.CompilerParams(vmem_limit_bytes=60 * 2**20),
+        compiler_params=pltpu.CompilerParams(vmem_limit_bytes=16 * 2**20),
         cost_estimate=pl.CostEstimate(flops=10**6, bytes_accessed=10**4, transcendentals=0),
-    )(*blocks, w, adapt_a, gate_up, gate_up, adapt_b, down)
-
-
-def backward_kernel(*refs):
-    cots, blocks, refs = refs[:4], refs[4:8], refs[8:]
+    )(*blocks, w, adapt_a, gate_up, adapt_b, down)
+
+
+def backward_kernel(n_blocks, chunk, adds, *refs):
+    cots, blocks, refs = refs[:n_blocks], refs[n_blocks : 2 * n_blocks], refs[2 * n_blocks :]
     w_ref, low_ref, active_ref, slope_ref, adapt_b_ref, down_ref, *refs = refs
-    grad_a_ref, grad_b_ref, sum_a_ref, sum_b_ref, scaled_ref, rows_ref, back_ref = refs
-    step = pl.program_id(0)
-    quarter = blocks[0].shape[0]
-
-    @pl.when(step == 0)
-    def _():
-        w = [column(w_ref[0:1]), column(w_ref[1:2])]
-        for at, (cot, block) in enumerate(zip(cots, blocks)):
-            rows = slice(at * quarter, (at + 1) * quarter)
-            w_rows = w[at // 2][at % 2 * quarter : (at % 2 + 1) * quarter]
-            scaled_ref[rows] = (w_rows * cot[...].astype(jnp.float32)).astype(jnp.bfloat16)
-            rows_ref[rows] = block[...]
-        back_ref[...] = jnp.zeros_like(back_ref)
-
-    back = dot(scaled_ref[...], down_ref[...], 1, 1)
-    up_grad = (back * active_ref[...]).astype(jnp.bfloat16)
-    gate_grad = (back * slope_ref[...]).astype(jnp.bfloat16)
+    *grads, sum_a_ref, sum_b_ref, scaled_ref, rows_ref = refs
+    rows = blocks[0].shape[0]
+    load_blocks(rows_ref, blocks)
+    w = jnp.concatenate([column(w_ref[0:1]), column(w_ref[1:2])])
+    for at, cot in enumerate(cots):
+        here = slice(at * rows, (at + 1) * rows)
+        scaled_ref[here] = (w[here] * cot[...].astype(jnp.float32)).astype(jnp.bfloat16)
+    scaled = scaled_ref[...]
     low_gate, low_up = halves(low_ref[...])
-    sum_b_ref[...] = grad_b_ref[...] + ADAPTER_SCALE * (
-        dot(low_gate, gate_grad, 0, 0) + dot(low_up, up_grad, 0, 0)
-    )
-    gate_back = dot(gate_grad, adapt_b_ref[...], 1, 1)
-    up_back = dot(up_grad, adapt_b_ref[...], 1, 1)
-    back_ref[...] += jnp.where(first_half(gate_back.shape), gate_back, up_back)
-
-    @pl.when(step == pl.num_programs(0) - 1)
-    def _():
-        low_grad = (ADAPTER_SCALE * back_ref[...]).astype(jnp.bfloat16)
-        sum_a_ref[...] = grad_a_ref[...] + dot(rows_ref[...], low_grad, 0, 0)
-
-
-def backward_stage(cots, w, blocks, saved, down, adapt_b, grads, chunk=256):
+    low_back = 0.0
+    for start in range(0, down_ref.shape[0], chunk):
+        here = slice(start, start + chunk)
+        adapt_b = adapt_b_ref[:, here]
+        back = dot(scaled, down_ref[here], 1, 1)
+        up_grad = (back * active_ref[:, here]).astype(jnp.bfloat16)
+        gate_grad = (back * slope_ref[:, here]).astype(jnp.bfloat16)
+        sum_b = ADAPTER_SCALE * (dot(low_gate, gate_grad, 0, 0) + dot(low_up, up_grad, 0, 0))
+        sum_b_ref[:, here] = sum_b + grads[1][:, here] if adds else sum_b
+        gate_back, up_back = dot(gate_grad, adapt_b, 1, 1), dot(up_grad, adapt_b, 1, 1)
+        low_back = low_back + jnp.where(first_half(gate_back.shape), gate_back, up_back)
+    low_grad = (ADAPTER_SCALE * low_back).astype(jnp.bfloat16)
+    sum_a = dot(rows_ref[...], low_grad, 0, 0)
+    sum_a_ref[...] = sum_a + grads[0][...] if adds else sum_a
+
+
+def backward_stage(cots, w, blocks, saved, down, adapt_b, grads=(), chunk=256):
     low, active, slope = saved
-    quarter, features = blocks[0].shape
-    hidden_width = down.shape[0]
+    features = blocks[0].shape[1]
     both, ranks = low.shape
-    grad_a = whole((features, ranks))
-    grad_b = columns(ranks, chunk)
+    operands = (*cots, *blocks, w, low, active, slope, adapt_b, down, *grads)
     return pl.pallas_call(
-        backward_kernel,
-        grid=(hidden_width // chunk,),
+        functools.partial(backward_kernel, len(blocks), chunk, len(grads) > 0),
         out_shape=(
             jax.ShapeDtypeStruct((features, ranks), jnp.float32),
-            jax.ShapeDtypeStruct((ranks, hidden_width), jnp.float32),
+            jax.ShapeDtypeStruct((ranks, down.shape[0]), jnp.float32),
         ),
-        in_specs=[whole((quarter, features))] * 8
-        + [
-            whole((2, 2 * quarter)),
-            whole((both, ranks)),
-            columns(both, chunk),
-            columns(both, chunk),
-            columns(ranks, chunk),
-            pl.BlockSpec((chunk, features), lambda j: (j, 0)),
-            grad_a,
-            grad_b,
-        ],
-        out_specs=(grad_a, grad_b),
+        in_specs=[VMEM] * len(operands),
+        out_specs=(VMEM, VMEM),
         scratch_shapes=[
             pltpu.VMEM((both, features), jnp.bfloat16),
             pltpu.VMEM((both, features), jnp.bfloat16),
-            pltpu.VMEM((both, ranks), jnp.float32),
         ],
-        compiler_params=pltpu.CompilerParams(vmem_limit_bytes=60 * 2**20),
+        compiler_params=pltpu.CompilerParams(vmem_limit_bytes=16 * 2**20),
         cost_estimate=pl.CostEstimate(flops=10**6, bytes_accessed=10**4, transcendentals=0),
-    )(*cots, *blocks, w, low, active, slope, adapt_b, down, *grads)
+    )(*operands)
 
 
 def z_pairs(*moves):
@@ -547,9 +502,8 @@
     cswap_b, cmid_b, part3_b, cswap_a = fence(cswap_b, cmid_b, part3_b, cswap_a)
     swap5_b, cmid2_b = send(pick(cmid_b, part3_b), ALL_SWAP), send(cswap_b, MID_SWAP)
     part2_a, part2_b = chip_part(part2, away2)
-    none = (jnp.zeros(adapt_a.shape, jnp.float32), jnp.zeros(adapt_b.shape, jnp.float32))
     cots0 = (cot_a, cot_b)
-    grads = backward(cots0, twins(cots0), weights0, rows0, saved0, none)
+    grads = backward(cots0, twins(cots0), weights0, rows0, saved0, ())
 
     swap5_a, cmid2_a, part3_a, part2_a, part2_b, part1, away1, grads = fence(
         swap5_a, cmid2_a, part3_a, part2_a, part2_b, part1, away1, grads

time: 196 us -> 171 us (0.87)
  Pallas kernels: 72 us -> 34 us
  local copies, waits for them, and re-layouts: 8.38 us -> 25.5 us
  other arithmetic: 14.4 us -> 6.44 us
  waiting for transfers between devices: 36.8 us -> 41 us
    pallas_call x8, Pallas kernels: 70.5 us -> 32.5 us  [the longest x4 17.5 us: forward_stage(): pl.pallas_call(functools.partial(forward_kernel, len(blocks), chunk), out...]
    unnamed x74 -> x56, local copies, waits for them, and re-layouts: 4.31 us -> 22.8 us
    convert_element_type x6, other arithmetic: 5.42 us -> 0.28 us  [swap_sum(): other = lax.ppermute(rounded.astype(jnp.bfloat16), 'dp', pairs)]
    ppermute x49, waiting for transfers between devices: 21.4 us -> 24.9 us  [send(): return lax.ppermute(array, 'expert', pairs)]
  transfers between devices with their start and end apart: 55 -> 55, of which waited for: 13 -> 14; matrix products, arithmetic and copies ran while one was open for 8% -> 4% of each run, Pallas kernels for 37% -> 20%
where the time goes in v7:
time: 171 us; the launch traced here: 170 us
  starting transfers between devices  61.8 us (36%)
  waiting for transfers between devices  41 us (24%)
  Pallas kernels  34 us (20%)
  local copies, waits for them, and re-layouts  25.5 us (15%)
  other arithmetic  6.44 us (4%)
    ppermute x49, starting transfers between devices, send(): return lax.ppermute(array, 'expert', pairs)  54.4 us
    ppermute x49, waiting for transfers between devices, send(): return lax.ppermute(array, 'expert', pairs)  24.9 us
    unnamed x56, local copies, waits for them, and re-layouts  22.8 us
    pallas_call x4, Pallas kernels, forward_stage(): pl.pallas_call(functools.partial(forward_kernel, len(blocks), chunk), out...  17.5 us
    ppermute x6, waiting for transfers between devices, swap_sum(): other = lax.ppermute(rounded.astype(jnp.bfloat16), 'dp', pairs)  16.1 us
    pallas_call x4, Pallas kernels, backward_stage(): pl.pallas_call(functools.partial(backward_kernel, len(blocks), chunk, len...  14.9 us
    ppermute x6, starting transfers between devices, swap_sum(): other = lax.ppermute(rounded.astype(jnp.bfloat16), 'dp', pairs)  7.33 us
  transfers between devices with their start and end apart: 55, of which 14 were waited for; matrix products, arithmetic and copies ran while one was open for 4% of the time, Pallas kernels for 20%

profile of v7, /device:TPU:0, one launch (start us, length us, event | category | flops | bytes accessed | tf_op | source)
XLA Modules:
  0.0 170.1 jit_solution(7892077525897722313)
XLA Ops:
  9.0 3.8 %collective-permute-start.7 = (bf16[64,2048]{1,0:T(8,128)(2,1)}, bf16[64,2048]{1,0:T(8,128)(2,1)}, u32[]{:S(2)}, u32[]{:S(2)}) collective-permute-start(bf16[64,2048]{1,0:T(8,128)(2,1)} %get-tuple-element.220.refs_1_.refs_5_), channel_id=1, source_target_pairs={{0,2},{1,3},{2,0},{3,1},{4,6},{5,7},{6,4},{7,5},{8,10},{9,11},{10,... | collective-permute-start | bytes 786440 | tf_op jit(solution)/shard_map/ppermute | solution.py:362
  18.1 2.8 %copy-done.2 = bf16[1,2048,1536]{2,1,0:T(8,128)(2,1)S(1)} copy-done((bf16[1,2048,1536]{2,1,0:T(8,128)(2,1)S(1)}, bf16[1,2048,1536]{2,1,0:T(8,128)(2,1)}, u32[]{:S(2)}) %copy-start.2) | copy-done | bytes 6291480
  24.8 4.9 %shard_map.122 = (bf16[256,128]{1,0:T(8,128)(2,1)S(1)}, f32[256,768]{1,0:T(8,128)S(1)}, f32[256,768]{1,0:T(8,128)S(1)}, bf16[128,2048]{1,0:T(8,128)(2,1)S(1)}, bf16[128,2048]{1,0:T(8,128)(2,1)S(1)}) custom-call(bf16[64,2048]{1,0:T(8,128)(2,1)} %get-tuple-element.219.refs_0_.refs_4_, bf16[64,2048]{1,0:T(8,128)(2,1)} %get-tuple-element.220.refs_1_.refs_5_, ...), custom_call_target="tpu_custom_call" | custom-call | flops 1000000 | bytes 10000 | tf_op jit(solution)/shard_map/pallas_call | solution.py:288
  42.1 3.9 %collective-permute-start.14 = (bf16[64,2048]{1,0:T(8,128)(2,1)}, bf16[64,2048]{1,0:T(8,128)(2,1)S(1)}, u32[]{:S(2)}, u32[]{:S(2)}) collective-permute-start(bf16[64,2048]{1,0:T(8,128)(2,1)} %collective-permute-done.8), channel_id=1, source_target_pairs={{0,2},{1,3},{2,0},{3,1},{4,6},{5,7},{6,4},{7,5},{8,10},{9,11},{10,... | collective-permute-start | bytes 786440 | tf_op jit(solution)/shard_map/ppermute | solution.py:362
  49.8 5.1 %shard_map.123 = (bf16[256,128]{1,0:T(8,128)(2,1)S(1)}, f32[256,768]{1,0:T(8,128)S(1)}, f32[256,768]{1,0:T(8,128)S(1)}, bf16[128,2048]{1,0:T(8,128)(2,1)S(1)}, bf16[128,2048]{1,0:T(8,128)(2,1)S(1)}) custom-call(bf16[64,2048]{1,0:T(8,128)(2,1)} %collective-permute-done.refs_0_.refs_4_, bf16[64,2048]{1,0:T(8,128)(2,1)} %collective-permute-done.7.refs_1_.refs_5_, ...), custom_call_target="tpu_custom_call" | custom-call | flops 1000000 | bytes 10000 | tf_op jit(solution)/shard_map/pallas_call | solution.py:288
  56.8 4.7 %collective-permute-start.18 = (f32[32,128]{1,0:T(8,128)S(1)}, f32[32,128]{1,0:T(8,128)S(1)}, u32[]{:S(2)}, u32[]{:S(2)}) collective-permute-start(f32[32,128]{1,0:T(8,128)S(1)} %pad_maximum_fusion.1), channel_id=1, source_target_pairs={{0,4},{1,5},{2,6},{3,7},{4,0},{5,1},{6,2},{7,3},{8,12},{9,13},{10,... | collective-permute-start | bytes 49160 | tf_op jit(solution)/shard_map/ppermute | solution.py:362
  61.8 3.6 %collective-permute-done.18 = f32[32,128]{1,0:T(8,128)S(1)} collective-permute-done((f32[32,128]{1,0:T(8,128)S(1)}, f32[32,128]{1,0:T(8,128)S(1)}, u32[]{:S(2)}, u32[]{:S(2)}) %collective-permute-start.18) | collective-permute-done | bytes 16416 | tf_op jit(solution)/shard_map/ppermute | solution.py:362
  66.3 2.8 %copy-done.4 = bf16[1,2048,1536]{2,1,0:T(8,128)(2,1)S(1)} copy-done((bf16[1,2048,1536]{2,1,0:T(8,128)(2,1)S(1)}, bf16[1,2048,1536]{2,1,0:T(8,128)(2,1)}, u32[]{:S(2)}) %copy-start.4) | copy-done | bytes 6291480
  69.1 3.8 %shard_map.124 = (bf16[256,128]{1,0:T(8,128)(2,1)S(1)}, f32[256,768]{1,0:T(8,128)S(1)}, f32[256,768]{1,0:T(8,128)S(1)}, bf16[128,2048]{1,0:T(8,128)(2,1)S(1)}, bf16[128,2048]{1,0:T(8,128)(2,1)S(1)}) custom-call(bf16[64,2048]{1,0:T(8,128)(2,1)S(1)} %broadcast_select_fusion.11.refs_0_.refs_4_, bf16[64,2048]{1,0:T(8,128)(2,1)S(1)} %broadcast_select_fusion.10.refs_1_.refs_5_, ...), custom_call_target="tpu_custom_call" | custom-call | flops 1000000 | bytes 10000 | tf_op jit(solution)/shard_map/pallas_call | solution.py:288
  73.7 4.4 %collective-permute-start.19 = (bf16[64,2048]{1,0:T(8,128)(2,1)S(1)}, bf16[64,2048]{1,0:T(8,128)(2,1)S(1)}, u32[]{:S(2)}, u32[]{:S(2)}) collective-permute-start(bf16[64,2048]{1,0:T(8,128)(2,1)S(1)} %copy-done.18), channel_id=1, source_target_pairs={{0,2},{1,3},{2,0},{3,1},{4,6},{5,7},{6,4},{7,5},{8,10},{9,11},{10,... | collective-permute-start | bytes 786440 | tf_op jit(solution)/shard_map/ppermute | solution.py:362
  78.1 2.8 %copy-done.5 = bf16[1,2048,1536]{2,1,0:T(8,128)(2,1)S(1)} copy-done((bf16[1,2048,1536]{2,1,0:T(8,128)(2,1)S(1)}, bf16[1,2048,1536]{2,1,0:T(8,128)(2,1)}, u32[]{:S(2)}) %copy-start.5) | copy-done | bytes 6291480
  80.9 3.8 %shard_map.125 = (bf16[256,128]{1,0:T(8,128)(2,1)S(1)}, f32[256,768]{1,0:T(8,128)S(1)}, f32[256,768]{1,0:T(8,128)S(1)}, bf16[128,2048]{1,0:T(8,128)(2,1)S(1)}, bf16[128,2048]{1,0:T(8,128)(2,1)S(1)}) custom-call(bf16[64,2048]{1,0:T(8,128)(2,1)S(1)} %broadcast_select_fusion.9.refs_0_.refs_4_, bf16[64,2048]{1,0:T(8,128)(2,1)S(1)} %broadcast_select_fusion.8.refs_1_.refs_5_, ...), custom_call_target="tpu_custom_call" | custom-call | flops 1000000 | bytes 10000 | tf_op jit(solution)/shard_map/pallas_call | solution.py:288
  87.9 4.2 %shard_map.126 = (f32[2048,128]{1,0:T(8,128)S(1)}, f32[128,768]{1,0:T(8,128)S(1)}) custom-call(bf16[64,2048]{1,0:T(8,128)(2,1)S(1)} %copy-done.18, bf16[64,2048]{1,0:T(8,128)(2,1)S(1)} %copy-done.17, bf16[64,2048]{1,0:T(8,128)(2,1)S(1)} %collective-permute-done.28.refs_2_, bf16[64,2048]{1,0:T(8,128)(2,1)S(1)} %collective-permute-done.29.refs_3_, ...), custom_call_target="tpu_custom_call" | custom-call | flops 1000000 | bytes 10000 | tf_op jit(solution)/shard_map/pallas_call | solution.py:335
  94.9 4.8 %collective-permute-start.25 = (bf16[64,2048]{1,0:T(8,128)(2,1)S(1)}, bf16[64,2048]{1,0:T(8,128)(2,1)S(1)}, u32[]{:S(2)}, u32[]{:S(2)}) collective-permute-start(bf16[64,2048]{1,0:T(8,128)(2,1)S(1)} %get-tuple-element.209), channel_id=1, source_target_pairs={{0,2},{1,3},{2,0},{3,1},{4,6},{5,7},{6,4},{7,5},{8,10},{9,11},{10,... | collective-permute-start | bytes 786440 | tf_op jit(solution)/shard_map/ppermute | solution.py:362
  100.0 6.9 %collective-permute-done.25 = bf16[64,2048]{1,0:T(8,128)(2,1)S(1)} collective-permute-done((bf16[64,2048]{1,0:T(8,128)(2,1)S(1)}, bf16[64,2048]{1,0:T(8,128)(2,1)S(1)}, u32[]{:S(2)}, u32[]{:S(2)}) %collective-permute-start.25) | collective-permute-done | bytes 262176 | tf_op jit(solution)/shard_map/ppermute | solution.py:362
  107.0 5.3 %collective-permute-done.34 = bf16[64,2048]{1,0:T(8,128)(2,1)S(1)} collective-permute-done((bf16[64,2048]{1,0:T(8,128)(2,1)S(1)}, bf16[64,2048]{1,0:T(8,128)(2,1)S(1)}, u32[]{:S(2)}, u32[]{:S(2)}) %collective-permute-start.34) | collective-permute-done | bytes 262176 | tf_op jit(solution)/shard_map/ppermute | solution.py:362
  115.8 4.4 %shard_map.127 = (f32[2048,128]{1,0:T(8,128)S(1)}, f32[128,768]{1,0:T(8,128)S(1)}) custom-call(bf16[64,2048]{1,0:T(8,128)(2,1)S(1)} %collective-permute-done.19.refs_0_, bf16[64,2048]{1,0:T(8,128)(2,1)S(1)} %collective-permute-done.33.refs_1_, bf16[64,2048]{1,0:T(8,128)(2,1)S(1)} %collective-permute-done.38.refs_2_, ...), custom_call_target="tpu_custom_call" | custom-call | flops 1000000 | bytes 10000 | tf_op jit(solution)/shard_map/pallas_call | solution.py:335
  120.2 2.9 %collective-permute-start.43 = (bf16[64,2048]{1,0:T(8,128)(2,1)S(1)}, bf16[64,2048]{1,0:T(8,128)(2,1)S(1)}, u32[]{:S(2)}, u32[]{:S(2)}) collective-permute-start(bf16[64,2048]{1,0:T(8,128)(2,1)S(1)} %broadcast_select_fusion.2), channel_id=1, source_target_pairs={{0,2},{1,3},{2,0},{3,1},{4,6},{5,7},{6,4},{7,5},{8,10},{9,11},{10,... | collective-permute-start | bytes 786440 | tf_op jit(solution)/shard_map/ppermute | solution.py:362
  123.8 3.2 %shard_map.128 = (f32[2048,128]{1,0:T(8,128)S(1)}, f32[128,768]{1,0:T(8,128)S(1)}) custom-call(bf16[64,2048]{1,0:T(8,128)(2,1)S(1)} %broadcast_select_fusion.5.refs_0_, bf16[64,2048]{1,0:T(8,128)(2,1)S(1)} %broadcast_select_fusion.3.refs_1_, bf16[64,2048]{1,0:T(8,128)(2,1)S(1)} %collective-permute-done.36.refs_2_, ...), custom_call_target="tpu_custom_call" | custom-call | flops 1000000 | bytes 10000 | tf_op jit(solution)/shard_map/pallas_call | solution.py:335
  128.0 4.7 %collective-permute-start.41 = (bf16[64,2048]{1,0:T(8,128)(2,1)S(1)}, bf16[64,2048]{1,0:T(8,128)(2,1)S(1)}, u32[]{:S(2)}, u32[]{:S(2)}) collective-permute-start(bf16[64,2048]{1,0:T(8,128)(2,1)S(1)} %add_convert_fusion.7), channel_id=1, source_target_pairs={{0,2},{1,3},{2,0},{3,1},{4,6},{5,7},{6,4},{7,5},{8,10},{9,11},{10,... | collective-permute-start | bytes 786440 | tf_op jit(solution)/shard_map/ppermute | solution.py:362
  135.4 3.2 %shard_map.129 = (f32[2048,128]{1,0:T(8,128)S(1)}, f32[128,768]{1,0:T(8,128)S(1)}) custom-call(bf16[64,2048]{1,0:T(8,128)(2,1)S(1)} %broadcast_select_fusion.1.refs_0_, bf16[64,2048]{1,0:T(8,128)(2,1)S(1)} %broadcast_select_fusion.refs_1_, bf16[64,2048]{1,0:T(8,128)(2,1)S(1)} %collective-permute-done.47.refs_2_, ...), custom_call_target="tpu_custom_call" | custom-call | flops 1000000 | bytes 10000 | tf_op jit(solution)/shard_map/pallas_call | solution.py:335
  140.8 4.9 %collective-permute-done.51 = bf16[640,128]{1,0:T(8,128)(2,1)S(1)} collective-permute-done((bf16[640,128]{1,0:T(8,128)(2,1)S(1)}, bf16[640,128]{1,0:T(8,128)(2,1)S(1)}, u32[]{:S(2)}, u32[]{:S(2)}) %collective-permute-start.51) | collective-permute-done | bytes 163872 | tf_op jit(solution)/shard_map/ppermute | solution.py:392
  153.4 3.2 %collective-permute-done.45 = bf16[64,2048]{1,0:T(8,128)(2,1)S(1)} collective-permute-done((bf16[64,2048]{1,0:T(8,128)(2,1)S(1)}, bf16[64,2048]{1,0:T(8,128)(2,1)S(1)}, u32[]{:S(2)}, u32[]{:S(2)}) %collective-permute-start.45) | collective-permute-done | bytes 262176 | tf_op jit(solution)/shard_map/ppermute | solution.py:362
  157.8 3.5 %collective-permute-done.49 = bf16[1408,128]{1,0:T(8,128)(2,1)S(1)} collective-permute-done((bf16[1408,128]{1,0:T(8,128)(2,1)S(1)}, bf16[1408,128]{1,0:T(8,128)(2,1)S(1)}, u32[]{:S(2)}, u32[]{:S(2)}) %collective-permute-start.49) | collective-permute-done | bytes 360480 | tf_op jit(solution)/shard_map/ppermute | solution.py:392
  (192 shorter events, 71.4 us)
Async XLA Ops:
  5.1 28.0 %collective-permute-start = (bf16[64,2048]{1,0:T(8,128)(2,1)}, bf16[64,2048]{1,0:T(8,128)(2,1)}, u32[]{:S(2)}, u32[]{:S(2)}) collective-permute-start(bf16[64,2048]{1,0:T(8,128)(2,1)} %get-tuple-element.219.refs_0_.refs_4_), channel_id=1, source_target_pairs={{0,2},{1,3},{2,0},{3,1},{4,6},{5,7},{6,4},{7,5},{8,10},{9,11},{10,... | collective-permute-start | bytes 786440 | tf_op jit(solution)/shard_map/ppermute | solution.py:362
  7.6 25.4 %collective-permute-start.1 = (bf16[64,2048]{1,0:T(8,128)(2,1)}, bf16[64,2048]{1,0:T(8,128)(2,1)}, u32[]{:S(2)}, u32[]{:S(2)}) collective-permute-start(bf16[64,2048]{1,0:T(8,128)(2,1)} %get-tuple-element.219.refs_0_.refs_4_), channel_id=1, source_target_pairs={{2,4},{3,5},{4,2},{5,3},{10,12},{11,13},{12,10},{13,11},{18,20},{1... | collective-permute-start | bytes 786440 | tf_op jit(solution)/shard_map/ppermute | solution.py:362
  9.0 26.1 %collective-permute-start.7 = (bf16[64,2048]{1,0:T(8,128)(2,1)}, bf16[64,2048]{1,0:T(8,128)(2,1)}, u32[]{:S(2)}, u32[]{:S(2)}) collective-permute-start(bf16[64,2048]{1,0:T(8,128)(2,1)} %get-tuple-element.220.refs_1_.refs_5_), channel_id=1, source_target_pairs={{0,2},{1,3},{2,0},{3,1},{4,6},{5,7},{6,4},{7,5},{8,10},{9,11},{10,... | collective-permute-start | bytes 786440 | tf_op jit(solution)/shard_map/ppermute | solution.py:362
  13.5 21.6 %collective-permute-start.8 = (bf16[64,2048]{1,0:T(8,128)(2,1)}, bf16[64,2048]{1,0:T(8,128)(2,1)}, u32[]{:S(2)}, u32[]{:S(2)}) collective-permute-start(bf16[64,2048]{1,0:T(8,128)(2,1)} %get-tuple-element.220.refs_1_.refs_5_), channel_id=1, source_target_pairs={{2,4},{3,5},{4,2},{5,3},{10,12},{11,13},{12,10},{13,11},{18,20},{1... | collective-permute-start | bytes 786440 | tf_op jit(solution)/shard_map/ppermute | solution.py:362
  33.1 21.8 %collective-permute-start.5 = (bf16[64,2048]{1,0:T(8,128)(2,1)}, bf16[64,2048]{1,0:T(8,128)(2,1)}, u32[]{:S(2)}, u32[]{:S(2)}) collective-permute-start(bf16[64,2048]{1,0:T(8,128)(2,1)} %collective-permute-done.1), channel_id=1, source_target_pairs={{0,2},{1,3},{2,0},{3,1},{4,6},{5,7},{6,4},{7,5},{8,10},{9,11},{10,... | collective-permute-start | bytes 786440 | tf_op jit(solution)/shard_map/ppermute | solution.py:362
  33.7 21.2 %collective-permute-start.6 = (bf16[64,2048]{1,0:T(8,128)(2,1)}, bf16[64,2048]{1,0:T(8,128)(2,1)}, u32[]{:S(2)}, u32[]{:S(2)}) collective-permute-start(bf16[64,2048]{1,0:T(8,128)(2,1)} %collective-permute-done.refs_0_.refs_4_), channel_id=1, source_target_pairs={{2,4},{3,5},{4,2},{5,3},{10,12},{11,13},{12,10},{13,11},{18,20},{1... | collective-permute-start | bytes 786440 | tf_op jit(solution)/shard_map/ppermute | solution.py:362
  41.4 15.3 %collective-permute-start.15 = (bf16[64,2048]{1,0:T(8,128)(2,1)}, bf16[64,2048]{1,0:T(8,128)(2,1)S(1)}, u32[]{:S(2)}, u32[]{:S(2)}) collective-permute-start(bf16[64,2048]{1,0:T(8,128)(2,1)} %collective-permute-done.7.refs_1_.refs_5_), channel_id=1, source_target_pairs={{2,4},{3,5},{4,2},{5,3},{10,12},{11,13},{12,10},{13,11},{18,20},{1... | collective-permute-start | bytes 786440 | tf_op jit(solution)/shard_map/ppermute | solution.py:362
  42.1 14.6 %collective-permute-start.14 = (bf16[64,2048]{1,0:T(8,128)(2,1)}, bf16[64,2048]{1,0:T(8,128)(2,1)S(1)}, u32[]{:S(2)}, u32[]{:S(2)}) collective-permute-start(bf16[64,2048]{1,0:T(8,128)(2,1)} %collective-permute-done.8), channel_id=1, source_target_pairs={{0,2},{1,3},{2,0},{3,1},{4,6},{5,7},{6,4},{7,5},{8,10},{9,11},{10,... | collective-permute-start | bytes 786440 | tf_op jit(solution)/shard_map/ppermute | solution.py:362
  54.9 18.0 %collective-permute-start.12 = (bf16[64,2048]{1,0:T(8,128)(2,1)}, bf16[64,2048]{1,0:T(8,128)(2,1)S(1)}, u32[]{:S(2)}, u32[]{:S(2)}) collective-permute-start(bf16[64,2048]{1,0:T(8,128)(2,1)} %collective-permute-done.6), channel_id=1, source_target_pairs={{0,2},{1,3},{2,0},{3,1},{4,6},{5,7},{6,4},{7,5},{8,10},{9,11},{10,... | collective-permute-start | bytes 786440 | tf_op jit(solution)/shard_map/ppermute | solution.py:362
  55.0 17.9 %collective-permute-start.13 = (bf16[64,2048]{1,0:T(8,128)(2,1)S(1)}, bf16[64,2048]{1,0:T(8,128)(2,1)S(1)}, u32[]{:S(2)}, u32[]{:S(2)}) collective-permute-start(bf16[64,2048]{1,0:T(8,128)(2,1)S(1)} %copy-done.18), channel_id=1, source_target_pairs={{2,4},{3,5},{4,2},{5,3},{10,12},{11,13},{12,10},{13,11},{18,20},{1... | collective-permute-start | bytes 786440 | tf_op jit(solution)/shard_map/ppermute | solution.py:362
  86.9 13.1 %collective-permute-start.26 = (bf16[64,2048]{1,0:T(8,128)(2,1)S(1)}, bf16[64,2048]{1,0:T(8,128)(2,1)S(1)}, u32[]{:S(2)}, u32[]{:S(2)}) collective-permute-start(bf16[64,2048]{1,0:T(8,128)(2,1)S(1)} %collective-permute-done.19.refs_0_), channel_id=1, source_target_pairs={{2,4},{3,5},{4,2},{5,3},{10,12},{11,13},{12,10},{13,11},{18,20},{1... | collective-permute-start | bytes 786440 | tf_op jit(solution)/shard_map/ppermute | solution.py:362
  87.6 12.1 %collective-permute-start.27 = (bf16[128,2048]{1,0:T(8,128)(2,1)S(1)}, bf16[128,2048]{1,0:T(8,128)(2,1)S(1)}, u32[]{:S(2)}, u32[]{:S(2)}) collective-permute-start(bf16[128,2048]{1,0:T(8,128)(2,1)S(1)} %get-tuple-element.149), channel_id=1, source_target_pairs={{0,1},{1,0},{2,3},{3,2},{4,5},{5,4},{6,7},{7,6},{8,9},{9,8},{10,11... | collective-permute-start | bytes 1572872 | tf_op jit(solution)/shard_map/ppermute | solution.py:362
  94.0 18.3 %collective-permute-start.35 = (bf16[64,2048]{1,0:T(8,128)(2,1)S(1)}, bf16[64,2048]{1,0:T(8,128)(2,1)S(1)}, u32[]{:S(2)}, u32[]{:S(2)}) collective-permute-start(bf16[64,2048]{1,0:T(8,128)(2,1)S(1)} %collective-permute-done.33.refs_1_), channel_id=1, source_target_pairs={{2,4},{3,5},{4,2},{5,3},{10,12},{11,13},{12,10},{13,11},{18,20},{1... | collective-permute-start | bytes 786440 | tf_op jit(solution)/shard_map/ppermute | solution.py:362
  94.7 18.4 %collective-permute-start.39 = (bf16[64,2048]{1,0:T(8,128)(2,1)S(1)}, bf16[64,2048]{1,0:T(8,128)(2,1)S(1)}, u32[]{:S(2)}, u32[]{:S(2)}) collective-permute-start(bf16[64,2048]{1,0:T(8,128)(2,1)S(1)} %collective-permute-done.33.refs_1_), channel_id=1, source_target_pairs={{0,1},{1,0},{2,3},{3,2},{4,5},{5,4},{6,7},{7,6},{8,9},{9,8},{10,11... | collective-permute-start | bytes 786440 | tf_op jit(solution)/shard_map/ppermute | solution.py:362
  99.8 12.5 %collective-permute-start.34 = (bf16[64,2048]{1,0:T(8,128)(2,1)S(1)}, bf16[64,2048]{1,0:T(8,128)(2,1)S(1)}, u32[]{:S(2)}, u32[]{:S(2)}) collective-permute-start(bf16[64,2048]{1,0:T(8,128)(2,1)S(1)} %broadcast_select_fusion.4), channel_id=1, source_target_pairs={{0,2},{1,3},{2,0},{3,1},{4,6},{5,7},{6,4},{7,5},{8,10},{9,11},{10,... | collective-permute-start | bytes 786440 | tf_op jit(solution)/shard_map/ppermute | solution.py:362
  106.9 20.2 %collective-permute-start.32 = (bf16[128,2048]{1,0:T(8,128)(2,1)S(1)}, bf16[128,2048]{1,0:T(8,128)(2,1)S(1)}, u32[]{:S(2)}, u32[]{:S(2)}) collective-permute-start(bf16[128,2048]{1,0:T(8,128)(2,1)S(1)} %get-tuple-element.164), channel_id=1, source_target_pairs={{0,1},{1,0},{2,3},{3,2},{4,5},{5,4},{6,7},{7,6},{8,9},{9,8},{10,11... | collective-permute-start | bytes 1572872 | tf_op jit(solution)/shard_map/ppermute | solution.py:362
  113.1 14.0 %collective-permute-start.30 = (bf16[64,2048]{1,0:T(8,128)(2,1)S(1)}, bf16[64,2048]{1,0:T(8,128)(2,1)S(1)}, u32[]{:S(2)}, u32[]{:S(2)}) collective-permute-start(bf16[64,2048]{1,0:T(8,128)(2,1)S(1)} %broadcast_select_fusion.6), channel_id=1, source_target_pairs={{0,2},{1,3},{2,0},{3,1},{4,6},{5,7},{6,4},{7,5},{8,10},{9,11},{10,... | collective-permute-start | bytes 786440 | tf_op jit(solution)/shard_map/ppermute | solution.py:362
  114.9 12.2 %collective-permute-start.31 = (bf16[64,2048]{1,0:T(8,128)(2,1)S(1)}, bf16[64,2048]{1,0:T(8,128)(2,1)S(1)}, u32[]{:S(2)}, u32[]{:S(2)}) collective-permute-start(bf16[64,2048]{1,0:T(8,128)(2,1)S(1)} %add_convert_fusion.12), channel_id=1, source_target_pairs={{2,4},{3,5},{4,2},{5,3},{10,12},{11,13},{12,10},{13,11},{18,20},{1... | collective-permute-start | bytes 786440 | tf_op jit(solution)/shard_map/ppermute | solution.py:362
  120.2 12.5 %collective-permute-start.43 = (bf16[64,2048]{1,0:T(8,128)(2,1)S(1)}, bf16[64,2048]{1,0:T(8,128)(2,1)S(1)}, u32[]{:S(2)}, u32[]{:S(2)}) collective-permute-start(bf16[64,2048]{1,0:T(8,128)(2,1)S(1)} %broadcast_select_fusion.2), channel_id=1, source_target_pairs={{0,2},{1,3},{2,0},{3,1},{4,6},{5,7},{6,4},{7,5},{8,10},{9,11},{10,... | collective-permute-start | bytes 786440 | tf_op jit(solution)/shard_map/ppermute | solution.py:362
  127.2 22.6 %collective-permute-start.42 = (bf16[64,2048]{1,0:T(8,128)(2,1)S(1)}, bf16[64,2048]{1,0:T(8,128)(2,1)S(1)}, u32[]{:S(2)}, u32[]{:S(2)}) collective-permute-start(bf16[64,2048]{1,0:T(8,128)(2,1)S(1)} %add_convert_fusion.6), channel_id=1, source_target_pairs={{2,4},{3,5},{4,2},{5,3},{10,12},{11,13},{12,10},{13,11},{18,20},{1... | collective-permute-start | bytes 786440 | tf_op jit(solution)/shard_map/ppermute | solution.py:362
  128.0 23.4 %collective-permute-start.41 = (bf16[64,2048]{1,0:T(8,128)(2,1)S(1)}, bf16[64,2048]{1,0:T(8,128)(2,1)S(1)}, u32[]{:S(2)}, u32[]{:S(2)}) collective-permute-start(bf16[64,2048]{1,0:T(8,128)(2,1)S(1)} %add_convert_fusion.7), channel_id=1, source_target_pairs={{0,2},{1,3},{2,0},{3,1},{4,6},{5,7},{6,4},{7,5},{8,10},{9,11},{10,... | collective-permute-start | bytes 786440 | tf_op jit(solution)/shard_map/ppermute | solution.py:362
  132.7 23.9 %collective-permute-start.40 = (bf16[128,2048]{1,0:T(8,128)(2,1)S(1)}, bf16[128,2048]{1,0:T(8,128)(2,1)S(1)}, u32[]{:S(2)}, u32[]{:S(2)}) collective-permute-start(bf16[128,2048]{1,0:T(8,128)(2,1)S(1)} %copy-done.26), channel_id=1, source_target_pairs={{0,1},{1,0},{2,3},{3,2},{4,5},{5,4},{6,7},{7,6},{8,9},{9,8},{10,11... | collective-permute-start | bytes 1572872 | tf_op jit(solution)/shard_map/ppermute | solution.py:362
  151.4 13.1 %collective-permute-start.52 = (bf16[640,128]{1,0:T(8,128)(2,1)S(1)}, bf16[640,128]{1,0:T(8,128)(2,1)S(1)}, u32[]{:S(2)}, u32[]{:S(2)}) collective-permute-start(bf16[640,128]{1,0:T(8,128)(2,1)S(1)} %fusion.4), channel_id=1, source_target_pairs={{0,8},{8,0},{16,24},{24,16},{1,9},{9,1},{17,25},{25,17},{2,10},{10... | collective-permute-start | bytes 491528 | tf_op jit(solution)/shard_map/ppermute | solution.py:392
  151.9 14.7 %collective-permute-start.54 = (bf16[128,768]{1,0:T(8,128)(2,1)S(1)}, bf16[128,768]{1,0:T(8,128)(2,1)S(1)}, u32[]{:S(2)}, u32[]{:S(2)}) collective-permute-start(bf16[128,768]{1,0:T(8,128)(2,1)S(1)} %fusion.3), channel_id=1, source_target_pairs={{0,8},{8,0},{16,24},{24,16},{1,9},{9,1},{17,25},{25,17},{2,10},{10... | collective-permute-start | bytes 589832 | tf_op jit(solution)/shard_map/ppermute | solution.py:392
  (59 other events, 464.1 us)

commit v8 on v0

--- a/solution.py
+++ b/solution.py
@@ -1,6 +1,10 @@
+import functools
+
 import jax
 import jax.numpy as jnp
 from jax import lax
+from jax.experimental import pallas as pl
+from jax.experimental.pallas import tpu as pltpu
 from jax.sharding import PartitionSpec as P
 
 ADAPTER_SCALE = 0.5
@@ -88,7 +92,7 @@
     return (grad_adapt_a, jnp.stack([gate_up_map_gradient, up_map_gradient]))
 
 
-def body(
+def sparse_body(
     tokens,
     cotangent,
     routing,
@@ -179,6 +183,456 @@
     grad_a = summed_a.reshape(grad_adapt_a.shape)[None]
     grad_b = summed_b.reshape(grad_adapt_b.shape)[None]
     return (mixed, grad_a, grad_b)
+
+
+def dot(a, b, a_dim=1, b_dim=0):
+    return lax.dot_general(
+        a, b, (((a_dim,), (b_dim,)), ((), ())), preferred_element_type=jnp.float32
+    )
+
+
+def first_half(shape):
+    return lax.broadcasted_iota(jnp.int32, shape, 1) < shape[1] // 2
+
+
+def halves(low):
+    gate = first_half(low.shape)
+    zero = jnp.zeros_like(low)
+    return jnp.where(gate, low, zero), jnp.where(gate, zero, low)
+
+
+def split_weights(table):
+    parts = []
+    for _ in range(3):
+        part = table.astype(jnp.bfloat16).astype(jnp.float32)
+        parts.append(part)
+        table = table - part
+    slot_total, tok_rows = table.shape
+    parts.append(jnp.zeros((tok_rows - 3 * slot_total, tok_rows), jnp.float32))
+    return jnp.transpose(jnp.concatenate(parts)).astype(jnp.bfloat16)
+
+
+def joined_weight(extra, slot, slot_total):
+    lane = lax.broadcasted_iota(jnp.int32, extra.shape, 1)
+    mine = lane == slot
+    for part in range(1, 3):
+        mine = mine | (lane == slot + part * slot_total)
+    chosen = jnp.where(mine, extra.astype(jnp.float32), 0.0)
+    return jnp.sum(chosen, axis=1, keepdims=True)
+
+
+def tagged_kernel(
+    capacity, table_ref, expert_ref, choice_ref, weight_ref, tokens_ref, out_ref, extra_ref, sems
+):
+    slot_total = table_ref.shape[0]
+    tok_rows, features = tokens_ref.shape
+    rows = pltpu.make_async_copy(tokens_ref, out_ref.at[:, :features], sems.at[0])
+    rows.start()
+    experts, weights = expert_ref[...], weight_ref[...]
+    holds = [experts == table_ref[s] for s in range(slot_total)]
+    counts = [hold.astype(jnp.float32) for hold in holds]
+    copies = sum(counts)
+    choice = choice_ref[...].astype(jnp.float32)
+    wanted = choice - copies * jnp.floor((choice + 0.5) / copies)
+    before = jnp.zeros_like(copies)
+    taken, route_weight = [], []
+    for hold, count in zip(holds, counts):
+        picked = jnp.where(hold & (before == wanted), 1.0, 0.0)
+        before = before + count
+        taken.append(jnp.sum(picked, axis=0, keepdims=True))
+        route_weight.append(jnp.sum(picked * weights, axis=0, keepdims=True))
+    shape = (tok_rows, tok_rows)
+    earlier = lax.broadcasted_iota(jnp.int32, shape, 0) < lax.broadcasted_iota(jnp.int32, shape, 1)
+    rank = dot(
+        jnp.concatenate(taken).astype(jnp.bfloat16),
+        jnp.where(earlier, 1.0, 0.0).astype(jnp.bfloat16),
+    )
+    table = jnp.where(rank < capacity, jnp.concatenate(route_weight), 0.0)
+    extra_ref[...] = split_weights(table)
+    extra = pltpu.make_async_copy(extra_ref, out_ref.at[:, features:], sems.at[1])
+    extra.start()
+    rows.wait()
+    extra.wait()
+
+
+VMEM = pl.BlockSpec(memory_space=pltpu.VMEM)
+SMEM = pl.BlockSpec(memory_space=pltpu.SMEM)
+ANY = pl.BlockSpec(memory_space=pl.ANY)
+EXTRA = 128
+
+
+def tagged_tokens(tokens, routing, weights, choice, table, capacity):
+    tok_rows, features = tokens.shape
+    return pl.pallas_call(
+        functools.partial(tagged_kernel, capacity),
+        out_shape=jax.ShapeDtypeStruct((tok_rows, features + EXTRA), tokens.dtype),
+        in_specs=[SMEM, VMEM, VMEM, VMEM, ANY],
+        out_specs=ANY,
+        scratch_shapes=[
+            pltpu.VMEM((tok_rows, EXTRA), jnp.bfloat16),
+            pltpu.SemaphoreType.DMA((2,)),
+        ],
+    )(table, routing.T, choice.T, weights.T, tokens)
+
+
+class Copies:
+    def __init__(self, sems):
+        self.sems, self.used = sems, 0
+
+    def start(self, source, target):
+        copy = pltpu.make_async_copy(source, target, self.sems.at[self.used])
+        self.used += 1
+        copy.start()
+        return copy
+
+
+def wait_all(copies):
+    for copy in copies:
+        copy.wait()
+
+
+def chunks_of(width, chunk):
+    return [slice(start, start + chunk) for start in range(0, width, chunk)]
+
+
+def forward_kernel(
+    chunk, slot_ref, mine_hbm, other_hbm, adapt_a_hbm, gate_up_hbm, adapt_b_hbm, down_hbm,
+    low_hbm, active_hbm, slope_hbm, part_mine_hbm, part_other_hbm,
+    rows_ref, extra_ref, adapt_a_ref, gate_up_ref, adapt_b_ref, down_ref,
+    low_ref, active_ref, slope_ref, part_ref, total_ref, sems,
+):
+    copies = Copies(sems)
+    half, features = mine_hbm.shape[0], rows_ref.shape[1]
+    hidden_width = down_ref.shape[0]
+    here_of = chunks_of(hidden_width, chunk)
+    there_of = [slice(here.start + hidden_width, here.stop + hidden_width) for here in here_of]
+    fetch_rows, fetch_extra = [], []
+    for at, block in enumerate((mine_hbm, other_hbm)):
+        to = pl.ds(at * half, half)
+        fetch_rows.append(copies.start(block.at[:, :features], rows_ref.at[to]))
+        fetch_extra.append(copies.start(block.at[:, features:], extra_ref.at[to]))
+    fetch_rows.append(copies.start(adapt_a_hbm, adapt_a_ref))
+    fetch_chunk = []
+    for at, (here, there) in enumerate(zip(here_of, there_of)):
+        moves = [copies.start(adapt_b_hbm, adapt_b_ref)] if at == 0 else []
+        for cols in (here, there):
+            moves.append(copies.start(gate_up_hbm.at[:, cols], gate_up_ref.at[:, cols]))
+        moves.append(copies.start(down_hbm.at[here], down_ref.at[here]))
+        fetch_chunk.append(moves)
+    stores = []
+    wait_all(fetch_rows)
+    rows = rows_ref[...]
+    low = dot(rows, adapt_a_ref[...]).astype(jnp.bfloat16)
+    low_ref[...] = low
+    stores.append(copies.start(low_ref, low_hbm))
+    low_gate, low_up = halves(low)
+    for here, there, moves in zip(here_of, there_of, fetch_chunk):
+        wait_all(moves)
+        adapt_b = adapt_b_ref[:, here]
+        gate = dot(rows, gate_up_ref[:, here]) + ADAPTER_SCALE * dot(low_gate, adapt_b)
+        up = dot(rows, gate_up_ref[:, there]) + ADAPTER_SCALE * dot(low_up, adapt_b)
+        sigmoid_gate = jax.nn.sigmoid(gate)
+        active = gate * sigmoid_gate
+        active_ref[:, here] = active
+        slope_ref[:, here] = up * (sigmoid_gate * (1.0 + gate * (1.0 - sigmoid_gate)))
+        stores.append(copies.start(active_ref.at[:, here], active_hbm.at[:, here]))
+        stores.append(copies.start(slope_ref.at[:, here], slope_hbm.at[:, here]))
+        more = dot((active * up).astype(jnp.bfloat16), down_ref[here])
+        if here.start == 0:
+            total_ref[...] = more
+        else:
+            total_ref[...] += more
+    wait_all(fetch_extra)
+    w = joined_weight(extra_ref[...], slot_ref[0], slot_ref[1])
+    out = total_ref[...].astype(jnp.bfloat16).astype(jnp.float32)
+    part_ref[...] = (w * out).astype(jnp.bfloat16)
+    stores.append(copies.start(part_ref.at[half:], part_other_hbm))
+    stores.append(copies.start(part_ref.at[:half], part_mine_hbm))
+    wait_all(stores)
+
+
+def forward_stage(slot, mine, other, gate_up, down, adapt_a, adapt_b, chunk=256):
+    hidden_width, features = down.shape
+    half, both, ranks = mine.shape[0], 2 * mine.shape[0], adapt_a.shape[1]
+    bf16, f32 = jnp.bfloat16, jnp.float32
+    steps = hidden_width // chunk
+    return pl.pallas_call(
+        functools.partial(forward_kernel, chunk),
+        out_shape=(
+            jax.ShapeDtypeStruct((both, ranks), bf16),
+            jax.ShapeDtypeStruct((both, hidden_width), f32),
+            jax.ShapeDtypeStruct((both, hidden_width), f32),
+            jax.ShapeDtypeStruct((half, features), bf16),
+            jax.ShapeDtypeStruct((half, features), bf16),
+        ),
+        in_specs=[SMEM] + [ANY] * 6,
+        out_specs=(ANY,) * 5,
+        scratch_shapes=[
+            pltpu.VMEM((both, features), bf16),
+            pltpu.VMEM((both, EXTRA), bf16),
+            pltpu.VMEM(adapt_a.shape, bf16),
+            pltpu.VMEM(gate_up.shape, bf16),
+            pltpu.VMEM(adapt_b.shape, bf16),
+            pltpu.VMEM(down.shape, bf16),
+            pltpu.VMEM((both, ranks), bf16),
+            pltpu.VMEM((both, hidden_width), f32),
+            pltpu.VMEM((both, hidden_width), f32),
+            pltpu.VMEM((both, features), bf16),
+            pltpu.VMEM((both, features), f32),
+            pltpu.SemaphoreType.DMA((9 + 5 * steps,)),
+        ],
+        compiler_params=pltpu.CompilerParams(vmem_limit_bytes=60 * 2**20),
+        cost_estimate=pl.CostEstimate(flops=10**6, bytes_accessed=10**4, transcendentals=0),
+    )(slot, mine, other, adapt_a, gate_up, adapt_b, down)
+
+
+def backward_kernel(chunk, adds, last, *refs):
+    slot_ref, cot_mine, cot_other, mine_hbm, other_hbm, *refs = refs
+    low_hbm, active_hbm, slope_hbm, adapt_b_hbm, down_hbm, *refs = refs
+    grads_hbm, refs = refs[: 2 * adds], refs[2 * adds :]
+    outs, refs = refs[: 2 + last], refs[2 + last :]
+    cot_ref, scaled_ref, rows_ref, extra_ref, low_ref, active_ref, slope_ref, *refs = refs
+    adapt_b_ref, down_ref, grad_a_ref, grad_b_ref, out_a_ref, out_b_ref, sems = refs
+    copies = Copies(sems)
+    half, features = cot_mine.shape
+    here_of = chunks_of(down_ref.shape[0], chunk)
+    first, fetch_rows, fetch_grads = [], [], []
+    for at, cot in enumerate((cot_mine, cot_other)):
+        first.append(copies.start(cot, cot_ref.at[pl.ds(at * half, half)]))
+    for at, block in enumerate((mine_hbm, other_hbm)):
+        first.append(copies.start(block.at[:, features:], extra_ref.at[pl.ds(at * half, half)]))
+    first.append(copies.start(low_hbm, low_ref))
+    first.append(copies.start(adapt_b_hbm, adapt_b_ref))
+    fetch_chunk = [
+        (
+            copies.start(down_hbm.at[here], down_ref.at[here]),
+            copies.start(active_hbm.at[:, here], active_ref.at[:, here]),
+            copies.start(slope_hbm.at[:, here], slope_ref.at[:, here]),
+        )
+        for here in here_of
+    ]
+    for at, block in enumerate((mine_hbm, other_hbm)):
+        to = rows_ref.at[pl.ds(at * half, half)]
+        fetch_rows.append(copies.start(block.at[:, :features], to))
+    for grad_hbm, grad_ref in zip(grads_hbm, (grad_a_ref, grad_b_ref)):
+        fetch_grads.append(copies.start(grad_hbm, grad_ref))
+    wait_all(first)
+    w = joined_weight(extra_ref[...], slot_ref[0], slot_ref[1])
+    scaled_ref[...] = (w * cot_ref[...].astype(jnp.float32)).astype(jnp.bfloat16)
+    scaled = scaled_ref[...]
+    low_gate, low_up = halves(low_ref[...])
+    low_back = 0.0
+    sums_b = []
+    for here, moves in zip(here_of, fetch_chunk):
+        wait_all(moves)
+        adapt_b = adapt_b_ref[:, here]
+        back = dot(scaled, down_ref[here], 1, 1)
+        up_grad = (back * active_ref[:, here]).astype(jnp.bfloat16)
+        gate_grad = (back * slope_ref[:, here]).astype(jnp.bfloat16)
+        sum_b = dot(low_gate, gate_grad, 0, 0) + dot(low_up, up_grad, 0, 0)
+        sums_b.append(ADAPTER_SCALE * sum_b)
+        gate_back, up_back = dot(gate_grad, adapt_b, 1, 1), dot(up_grad, adapt_b, 1, 1)
+        low_back = low_back + jnp.where(first_half(gate_back.shape), gate_back, up_back)
+    wait_all(fetch_grads)
+    for here, sum_b in zip(here_of, sums_b):
+        total = sum_b + grad_b_ref[:, here] if adds else sum_b
+        out_b_ref[:, here] = total.astype(out_b_ref.dtype)
+    stores = [copies.start(out_b_ref, outs[-1])]
+    low_grad = (ADAPTER_SCALE * low_back).astype(jnp.bfloat16)
+    wait_all(fetch_rows)
+    sum_a = dot(rows_ref[...], low_grad, 0, 0)
+    total = sum_a + grad_a_ref[...] if adds else sum_a
+    out_a_ref[...] = total.astype(out_a_ref.dtype)
+    at = 0
+    for out in outs[:-1]:
+        stores.append(copies.start(out_a_ref.at[pl.ds(at, out.shape[0])], out))
+        at += out.shape[0]
+    wait_all(stores)
+
+
+def backward_stage(slot, cots, blocks, saved, down, adapt_b, grads=(), cut=None, chunk=256):
+    low, active, slope = saved
+    hidden_width, features = down.shape
+    both, ranks = low.shape
+    bf16, f32 = jnp.bfloat16, jnp.float32
+    out_dtype = f32 if cut is None else bf16
+    rows_of = [features] if cut is None else [cut, features - cut]
+    outs = [(rows, ranks) for rows in rows_of] + [(ranks, hidden_width)]
+    operands = (*cots, *blocks, low, active, slope, adapt_b, down, *grads)
+    steps = hidden_width // chunk
+    return pl.pallas_call(
+        functools.partial(backward_kernel, chunk, len(grads) // 2, int(cut is not None)),
+        out_shape=tuple(jax.ShapeDtypeStruct(shape, out_dtype) for shape in outs),
+        in_specs=[SMEM] + [ANY] * len(operands),
+        out_specs=(ANY,) * len(outs),
+        scratch_shapes=[
+            pltpu.VMEM((both, features), bf16),
+            pltpu.VMEM((both, features), bf16),
+            pltpu.VMEM((both, features), bf16),
+            pltpu.VMEM((both, EXTRA), bf16),
+            pltpu.VMEM(low.shape, bf16),
+            pltpu.VMEM(active.shape, f32),
+            pltpu.VMEM(slope.shape, f32),
+            pltpu.VMEM(adapt_b.shape, bf16),
+            pltpu.VMEM(down.shape, bf16),
+            pltpu.VMEM((features, ranks), f32),
+            pltpu.VMEM((ranks, hidden_width), f32),
+            pltpu.VMEM((features, ranks), out_dtype),
+            pltpu.VMEM((ranks, hidden_width), out_dtype),
+            pltpu.SemaphoreType.DMA((13 + 3 * steps,)),
+        ],
+        compiler_params=pltpu.CompilerParams(vmem_limit_bytes=60 * 2**20),
+        cost_estimate=pl.CostEstimate(flops=10**6, bytes_accessed=10**4, transcendentals=0),
+    )(slot, *operands)
+
+
+def z_pairs(*moves):
+    return [(2 * a + core, 2 * b + core) for a, b in moves for core in (0, 1)]
+
+
+ALL_SWAP = z_pairs((0, 1), (1, 0), (2, 3), (3, 2))
+MID_SWAP = z_pairs((1, 2), (2, 1))
+SIBLING = [(e, e ^ 1) for e in range(8)]
+
+
+def send(array, pairs):
+    return lax.ppermute(array, "expert", pairs)
+
+
+def fence(*arrays):
+    return lax.optimization_barrier(arrays)
+
+
+def add_rounded(*terms):
+    total = terms[0].astype(jnp.float32)
+    for term in terms[1:]:
+        total = total + term.astype(jnp.float32)
+    return total.astype(jnp.bfloat16)
+
+
+def sibling(block):
+    return send(block, SIBLING)
+
+
+def dp_swap(array, bit):
+    return lax.ppermute(array, "dp", [(d, d ^ bit) for d in range(4)])
+
+
+def rounded_sum(one, other):
+    return lax.reduce_precision(one.astype(jnp.float32) + other.astype(jnp.float32), 8, 7)
+
+
+def group_sum(x_first, *y_first):
+    totals = []
+    for array, bits in ((x_first, (1, 2)), *((array, (2, 1)) for array in y_first)):
+        pair = rounded_sum(array, dp_swap(array, bits[0]))
+        totals.append(pair + dp_swap(pair.astype(jnp.bfloat16), bits[1]).astype(jnp.float32))
+    return totals
+
+
+def dense_body(
+    tokens,
+    cotangent,
+    routing,
+    router_route_weights,
+    route_replica_choice,
+    device_expert_table,
+    gate_up_weight,
+    down_weight,
+    adapter_down_maps,
+    adapter_up_maps,
+):
+    slot_total = lax.axis_size("expert")
+    capacity = tokens.shape[0] * routing.shape[1] // slot_total
+    me = lax.axis_index("expert")
+    chip = me // 2
+    inner = (chip == 1) | (chip == 2)
+    gate_up, down = gate_up_weight[0], down_weight[0]
+    adapt_a = adapter_down_maps[0]
+    adapt_b = adapter_up_maps[0].reshape(adapt_a.shape[1], -1)
+
+    slot = jnp.stack([me, jnp.int32(slot_total)])
+
+    def forward(mine, twin):
+        *saved, part, away = forward_stage(slot, mine, twin, gate_up, down, adapt_a, adapt_b)
+        return saved, part, away
+
+    def backward(cots, rows, saved, grads=(), cut=None):
+        return backward_stage(slot, cots, rows, saved, down, adapt_b, grads, cut)
+
+    def pick(inside, outside):
+        return jnp.where(inner, inside, outside)
+
+    tokens = tagged_tokens(
+        tokens, routing, router_route_weights, route_replica_choice, device_expert_table, capacity
+    )
+    tok_swap = send(tokens, ALL_SWAP)
+    tok_mid = send(tokens, MID_SWAP)
+    rows0 = (tokens, sibling(tokens))
+    saved0, part0, away0 = forward(*rows0)
+    tok_swap, tok_mid, part0, away0, cotangent = fence(tok_swap, tok_mid, part0, away0, cotangent)
+
+    tok_out2 = send(tok_mid, ALL_SWAP)
+    tok_mid2 = send(tok_swap, MID_SWAP)
+    rows1 = (tok_swap, sibling(tok_swap))
+    saved1, part1, away1 = forward(*rows1)
+    tok_mid, tok_out2, tok_mid2, part1, away1, cotangent = fence(
+        tok_mid, tok_out2, tok_mid2, part1, away1, cotangent
+    )
+
+    tok_out3 = send(tok_mid2, ALL_SWAP)
+    cot_mid = send(cotangent, MID_SWAP)
+    tok_second = pick(tok_mid, tok_out2)
+    rows2 = (tok_second, sibling(tok_second))
+    saved2, part2, away2 = forward(*rows2)
+    tok_mid2, tok_out3, cot_mid, part2, away2, cotangent = fence(
+        tok_mid2, tok_out3, cot_mid, part2, away2, cotangent
+    )
+
+    cot_swap = send(cotangent, ALL_SWAP)
+    tok_third = pick(tok_mid2, tok_out3)
+    rows3 = (tok_third, sibling(tok_third))
+    saved3, part3, away3 = forward(*rows3)
+    cot_swap, cot_mid, part0, away0, part1, away1, part2, away2, part3, away3, cotangent = fence(
+        cot_swap, cot_mid, part0, away0, part1, away1, part2, away2, part3, away3, cotangent
+    )
+
+    cot_out2 = send(cot_mid, ALL_SWAP)
+    cot_mid2 = send(cot_swap, MID_SWAP)
+    grads = backward((cotangent, sibling(cotangent)), rows0, saved0)
+    part3 = add_rounded(part3, sibling(away3))
+    cot_mid, cot_out2, cot_mid2, cot_swap, part2, away2, part3, grads = fence(
+        cot_mid, cot_out2, cot_mid2, cot_swap, part2, away2, part3, grads
+    )
+
+    swap6 = send(pick(cot_mid2, part3), ALL_SWAP)
+    grads = backward((cot_swap, sibling(cot_swap)), rows1, saved1, grads)
+    cot_second = pick(cot_mid, cot_out2)
+    grads = backward((cot_second, sibling(cot_second)), rows2, saved2, grads)
+    part2 = add_rounded(part2, sibling(away2))
+    swap6, cot_mid2, part0, away0, part1, away1, part2, part3, grads = fence(
+        swap6, cot_mid2, part0, away0, part1, away1, part2, part3, grads
+    )
+
+    second_in = send(part2, ALL_SWAP)
+    third_mid = send(add_rounded(part3, swap6), MID_SWAP)
+    cot_third = pick(cot_mid2, swap6)
+    cut = (adapt_a.size + adapt_b.size) // 2 // adapt_a.shape[1] // 16 * 16
+    grads = backward((cot_third, sibling(cot_third)), rows3, saved3, grads, cut)
+    grad_a_top, grad_a_rest, grad_b = group_sum(*grads)
+    part1 = add_rounded(part1, sibling(away1))
+    part0 = add_rounded(part0, sibling(away0))
+    first_swap = send(add_rounded(part1, third_mid), ALL_SWAP)
+    second_mid = send(add_rounded(part2, second_in), MID_SWAP)
+    mixed = add_rounded(part0, first_swap, second_mid)
+    grad_a = jnp.concatenate([grad_a_top, grad_a_rest])
+    return mixed, grad_a[None], grad_b.reshape(adapter_up_maps.shape)
+
+
+def body(*arrays):
+    if (lax.axis_size("dp"), lax.axis_size("expert"), arrays[2].shape[1]) == (4, 8, 8):
+        return dense_body(*arrays)
+    return sparse_body(*arrays)
 
 
 def solution(mesh):

time: 547 us -> 168 us (0.31)
  waiting for transfers between devices: 275 us -> 26.3 us
  blocking collectives: 117 us -> 0 us
  Pallas kernels: 0 us -> 80.6 us
  local copies, waits for them, and re-layouts: 52.7 us -> 6.51 us
  matrix products: 43.3 us -> 0 us
  starting transfers between devices: 21.5 us -> 41.2 us
  between operations: 14.3 us -> 1.13 us
  other arithmetic: 21.7 us -> 11.9 us
    all_to_all x5 -> x0, waiting for transfers between devices: 218 us -> none  [the longest x1 87.8 us: body(): lax.all_to_all(layer_output.reshape(slot_total, capacity, model_feature_w...]
    all_to_all x2 -> x0, blocking collectives: 117 us -> none  [the longest x1 100 us: body(): lax.all_to_all(rows_out, 'expert', split_axis=0, concat_axis=0, tiled=True)]
    pallas_call x0 -> x9, Pallas kernels: none -> 80.6 us  [the longest x4 33.1 us: forward_stage(): pl.pallas_call(functools.partial(forward_kernel, chunk), out_shape=(jax.S...]
    psum x1 -> x0, waiting for transfers between devices: 57.9 us -> none  [body(): piece_a, piece_b = lax.psum((piece_a, piece_b), 'dp')]
    dot_general x15 -> x0, matrix products: 43.3 us -> none  [the longest x1 10.4 us: expert_apply_forward(): jnp.dot(rows_in, gate_up, preferred_element_type=jnp.float32)]
    ppermute x0 -> x32, starting transfers between devices: none -> 41.2 us  [the longest x26 32.9 us: send(): return lax.ppermute(array, 'expert', pairs)]
    gather x4 -> x0, local copies, waits for them, and re-layouts: 36.1 us -> none  [the longest x1 11.7 us: body(): picked_rows = returned[jnp.minimum(dest_index, slot_total * capacity - 1)]]
    ppermute x0 -> x32, waiting for transfers between devices: none -> 26.3 us  [the longest x26 16.8 us: send(): return lax.ppermute(array, 'expert', pairs)]
  transfers between devices with their start and end apart: 6 -> 32, of which waited for: 6 -> 9; matrix products, arithmetic and copies ran while one was open for 7% -> 6% of each run, Pallas kernels for 0% -> 37%
where the time goes in v8:
time: 168 us
  Pallas kernels  80.6 us (48%)
  starting transfers between devices  41.2 us (25%)
  waiting for transfers between devices  26.3 us (16%)
  other arithmetic  11.9 us (7%)
  local copies, waits for them, and re-layouts  6.51 us (4%)
    pallas_call x4, Pallas kernels, forward_stage(): pl.pallas_call(functools.partial(forward_kernel, chunk), out_shape=(jax.S...  33.1 us
    ppermute x26, starting transfers between devices, send(): return lax.ppermute(array, 'expert', pairs)  32.9 us
    pallas_call x4, Pallas kernels, backward_stage(): pl.pallas_call(functools.partial(backward_kernel, chunk, len(grads) // 2,...  29.6 us
    pallas_call x1, Pallas kernels, tagged_tokens(): pl.pallas_call(functools.partial(tagged_kernel, capacity), out_shape=jax....  17.8 us
    ppermute x26, waiting for transfers between devices, send(): return lax.ppermute(array, 'expert', pairs)  16.8 us
    ppermute x6, waiting for transfers between devices, dp_swap(): return lax.ppermute(array, 'dp', [(d, d ^ bit) for d in range(4)])  9.51 us
    ppermute x6, starting transfers between devices, dp_swap(): return lax.ppermute(array, 'dp', [(d, d ^ bit) for d in range(4)])  8.23 us
    unnamed x46, local copies, waits for them, and re-layouts  6.51 us
  transfers between devices with their start and end apart: 32, of which 9 were waited for; matrix products, arithmetic and copies ran while one was open for 6% of the time, Pallas kernels for 37%

profile of v8, /device:TPU:0, one launch (start us, length us, event | category | flops | bytes accessed | tf_op | source)
XLA Modules:
  0.0 167.6 jit_solution(11215223468851942531)
XLA Ops:
  0.6 17.8 %shard_map.121.mine_hbm.refs_3_ = bf16[128,2176]{1,0:T(8,128)(2,1)} custom-call(s32[8]{0:T(128)} %table_ref.1, s32[8,128]{1,0:T(8,128)} %bitcast.36, s32[8,128]{1,0:T(8,128)} %bitcast.37, f32[8,128]{1,0:T(8,128)} %bitcast.38, bf16[128,2048]{1,0:T(8,128)(2,1)} %tokens_ref.1), custom_call_target="tpu_custom_call" | custom-call | tf_op jit(solution)/shard_map/pallas_call | solution.py:266
  19.0 2.6 %collective-permute-start = (bf16[128,2176]{1,0:T(8,128)(2,1)}, bf16[128,2176]{1,0:T(8,128)(2,1)S(1)}, u32[]{:S(2)}, u32[]{:S(2)}) collective-permute-start(bf16[128,2176]{1,0:T(8,128)(2,1)} %shard_map.121.mine_hbm.refs_3_), channel_id=1, source_target_pairs={{0,2},{1,3},{2,0},{3,1},{4,6},{5,7},{6,4},{7,5},{8,10},{9,11},{10,... | collective-permute-start | bytes 1671176 | tf_op jit(solution)/shard_map/ppermute | solution.py:499
  23.7 8.3 %shard_map.122 = (bf16[256,128]{1,0:T(8,128)(2,1)}, f32[256,768]{1,0:T(8,128)}, f32[256,768]{1,0:T(8,128)}, bf16[128,2048]{1,0:T(8,128)(2,1)}, bf16[128,2048]{1,0:T(8,128)(2,1)}) custom-call(s32[2]{0:T(128)} %pad_add_fusion.slot_ref.refs_0_, bf16[128,2176]{1,0:T(8,128)(2,1)} %shard_map.121.mine_hbm.refs_3_, bf16[128,2176]{1,0:T(8,128)(2,1)} %copy-done.2, ...), custom_call_target="tpu_custom_call" | custom-call | flops 1000000 | bytes 10000 | tf_op jit(solution)/shard_map/pallas_call | solution.py:359
  32.0 3.0 %collective-permute-done.mine_hbm.refs_3_ = bf16[128,2176]{1,0:T(8,128)(2,1)S(1)} collective-permute-done((bf16[128,2176]{1,0:T(8,128)(2,1)}, bf16[128,2176]{1,0:T(8,128)(2,1)S(1)}, u32[]{:S(2)}, u32[]{:S(2)}) %collective-permute-start) | collective-permute-done | bytes 557088 | tf_op jit(solution)/shard_map/ppermute | solution.py:499
  35.8 7.8 %collective-permute-start.3 = (bf16[128,2176]{1,0:T(8,128)(2,1)S(1)}, bf16[128,2176]{1,0:T(8,128)(2,1)S(1)}, u32[]{:S(2)}, u32[]{:S(2)}) collective-permute-start(bf16[128,2176]{1,0:T(8,128)(2,1)S(1)} %collective-permute-done.1), channel_id=1, source_target_pairs={{0,2},{1,3},{2,0},{3,1},{4,6},{5,7},{6,4},{7,5},{8,10},{9,11},{10,... | collective-permute-start | bytes 1671176 | tf_op jit(solution)/shard_map/ppermute | solution.py:499
  44.3 8.3 %shard_map.123 = (bf16[256,128]{1,0:T(8,128)(2,1)}, f32[256,768]{1,0:T(8,128)}, f32[256,768]{1,0:T(8,128)}, bf16[128,2048]{1,0:T(8,128)(2,1)}, bf16[128,2048]{1,0:T(8,128)(2,1)}) custom-call(s32[2]{0:T(128)} %pad_add_fusion.slot_ref.refs_0_, bf16[128,2176]{1,0:T(8,128)(2,1)} %copy-done.3, bf16[128,2176]{1,0:T(8,128)(2,1)} %copy-done.4, ...), custom_call_target="tpu_custom_call" | custom-call | flops 1000000 | bytes 10000 | tf_op jit(solution)/shard_map/pallas_call | solution.py:359
  52.6 3.9 %collective-permute-done.3 = bf16[128,2176]{1,0:T(8,128)(2,1)S(1)} collective-permute-done((bf16[128,2176]{1,0:T(8,128)(2,1)S(1)}, bf16[128,2176]{1,0:T(8,128)(2,1)S(1)}, u32[]{:S(2)}, u32[]{:S(2)}) %collective-permute-start.3) | collective-permute-done | bytes 557088 | tf_op jit(solution)/shard_map/ppermute | solution.py:499
  56.7 1.8 %collective-permute-start.6 = (bf16[128,2176]{1,0:T(8,128)(2,1)S(1)}, bf16[128,2176]{1,0:T(8,128)(2,1)S(1)}, u32[]{:S(2)}, u32[]{:S(2)}) collective-permute-start(bf16[128,2176]{1,0:T(8,128)(2,1)S(1)} %collective-permute-done.4), channel_id=1, source_target_pairs={{0,2},{1,3},{2,0},{3,1},{4,6},{5,7},{6,4},{7,5},{8,10},{9,11},{10,... | collective-permute-start | bytes 1671176 | tf_op jit(solution)/shard_map/ppermute | solution.py:499
  60.3 8.2 %shard_map.124 = (bf16[256,128]{1,0:T(8,128)(2,1)}, f32[256,768]{1,0:T(8,128)}, f32[256,768]{1,0:T(8,128)}, bf16[128,2048]{1,0:T(8,128)(2,1)}, bf16[128,2048]{1,0:T(8,128)(2,1)}) custom-call(s32[2]{0:T(128)} %pad_add_fusion.slot_ref.refs_0_, bf16[128,2176]{1,0:T(8,128)(2,1)} %copy-done.1, bf16[128,2176]{1,0:T(8,128)(2,1)} %copy-done.6, ...), custom_call_target="tpu_custom_call" | custom-call | flops 1000000 | bytes 10000 | tf_op jit(solution)/shard_map/pallas_call | solution.py:359
  68.5 3.2 %collective-permute-done.6 = bf16[128,2176]{1,0:T(8,128)(2,1)S(1)} collective-permute-done((bf16[128,2176]{1,0:T(8,128)(2,1)S(1)}, bf16[128,2176]{1,0:T(8,128)(2,1)S(1)}, u32[]{:S(2)}, u32[]{:S(2)}) %collective-permute-start.6) | collective-permute-done | bytes 557088 | tf_op jit(solution)/shard_map/ppermute | solution.py:499
  71.9 3.0 %collective-permute-start.9 = (bf16[128,2048]{1,0:T(8,128)(2,1)S(1)}, bf16[128,2048]{1,0:T(8,128)(2,1)S(1)}, u32[]{:S(2)}, u32[]{:S(2)}) collective-permute-start(bf16[128,2048]{1,0:T(8,128)(2,1)S(1)} %copy-done.12), channel_id=1, source_target_pairs={{0,2},{1,3},{2,0},{3,1},{4,6},{5,7},{6,4},{7,5},{8,10},{9,11},{10,... | collective-permute-start | bytes 1572872 | tf_op jit(solution)/shard_map/ppermute | solution.py:499
  75.7 8.3 %shard_map.125 = (bf16[256,128]{1,0:T(8,128)(2,1)}, f32[256,768]{1,0:T(8,128)}, f32[256,768]{1,0:T(8,128)}, bf16[128,2048]{1,0:T(8,128)(2,1)}, bf16[128,2048]{1,0:T(8,128)(2,1)}) custom-call(s32[2]{0:T(128)} %pad_add_fusion.slot_ref.refs_0_, bf16[128,2176]{1,0:T(8,128)(2,1)} %copy-done, bf16[128,2176]{1,0:T(8,128)(2,1)} %copy-done.5, ...), custom_call_target="tpu_custom_call" | custom-call | flops 1000000 | bytes 10000 | tf_op jit(solution)/shard_map/pallas_call | solution.py:359
  84.0 3.4 %collective-permute-done.9.refs_1_ = bf16[128,2048]{1,0:T(8,128)(2,1)S(1)} collective-permute-done((bf16[128,2048]{1,0:T(8,128)(2,1)S(1)}, bf16[128,2048]{1,0:T(8,128)(2,1)S(1)}, u32[]{:S(2)}, u32[]{:S(2)}) %collective-permute-start.9) | collective-permute-done | bytes 524320 | tf_op jit(solution)/shard_map/ppermute | solution.py:499
  87.9 1.8 %collective-permute-start.11 = (bf16[128,2048]{1,0:T(8,128)(2,1)}, bf16[128,2048]{1,0:T(8,128)(2,1)}, u32[]{:S(2)}, u32[]{:S(2)}) collective-permute-start(bf16[128,2048]{1,0:T(8,128)(2,1)} %copy-done.21), channel_id=1, source_target_pairs={{0,2},{1,3},{2,0},{3,1},{4,6},{5,7},{6,4},{7,5},{8,10},{9,11},{10,... | collective-permute-start | bytes 1572872 | tf_op jit(solution)/shard_map/ppermute | solution.py:499
  91.4 7.4 %shard_map.126 = (f32[2048,128]{1,0:T(8,128)}, f32[128,768]{1,0:T(8,128)}) custom-call(s32[2]{0:T(128)} %pad_add_fusion.slot_ref.refs_0_, bf16[128,2048]{1,0:T(8,128)(2,1)} %refs_1_, bf16[128,2048]{1,0:T(8,128)(2,1)} %copy-done.13, bf16[128,2176]{1,0:T(8,128)(2,1)} %shard_map.121.mine_hbm.refs_3_, bf16[128,2176]{1,0:T(8,128)(2,1)} %copy-done.2, ...), custom_call_target="tpu_custom_call" | custom-call | flops 1000000 | bytes 10000 | tf_op jit(solution)/shard_map/pallas_call | solution.py:463
  99.0 3.2 %collective-permute-done.11 = bf16[128,2048]{1,0:T(8,128)(2,1)} collective-permute-done((bf16[128,2048]{1,0:T(8,128)(2,1)}, bf16[128,2048]{1,0:T(8,128)(2,1)}, u32[]{:S(2)}, u32[]{:S(2)}) %collective-permute-start.11) | collective-permute-done | bytes 524320 | tf_op jit(solution)/shard_map/ppermute | solution.py:499
  104.8 2.3 %collective-permute-start.15 = (bf16[128,2048]{1,0:T(8,128)(2,1)}, bf16[128,2048]{1,0:T(8,128)(2,1)S(1)}, u32[]{:S(2)}, u32[]{:S(2)}) collective-permute-start(bf16[128,2048]{1,0:T(8,128)(2,1)} %broadcast_select_fusion.4), channel_id=1, source_target_pairs={{0,2},{1,3},{2,0},{3,1},{4,6},{5,7},{6,4},{7,5},{8,10},{9,11},{10,... | collective-permute-start | bytes 1572872 | tf_op jit(solution)/shard_map/ppermute | solution.py:499
  107.9 7.5 %shard_map.127 = (f32[2048,128]{1,0:T(8,128)}, f32[128,768]{1,0:T(8,128)}) custom-call(s32[2]{0:T(128)} %pad_add_fusion.slot_ref.refs_0_, bf16[128,2048]{1,0:T(8,128)(2,1)} %copy-done.16, bf16[128,2048]{1,0:T(8,128)(2,1)} %copy-done.20, bf16[128,2176]{1,0:T(8,128)(2,1)} %copy-done.3, bf16[128,2176]{1,0:T(8,128)(2,1)} %copy-done.4, ...), custom_call_target="tpu_custom_call" | custom-call | flops 1000000 | bytes 10000 | tf_op jit(solution)/shard_map/pallas_call | solution.py:463
  116.2 7.4 %shard_map.128 = (f32[2048,128]{1,0:T(8,128)}, f32[128,768]{1,0:T(8,128)}) custom-call(s32[2]{0:T(128)} %pad_add_fusion.slot_ref.refs_0_, bf16[128,2048]{1,0:T(8,128)(2,1)} %copy-done.7, bf16[128,2048]{1,0:T(8,128)(2,1)} %copy-done.18, bf16[128,2176]{1,0:T(8,128)(2,1)} %copy-done.1, bf16[128,2176]{1,0:T(8,128)(2,1)} %copy-done.6, ...), custom_call_target="tpu_custom_call" | custom-call | flops 1000000 | bytes 10000 | tf_op jit(solution)/shard_map/pallas_call | solution.py:463
  128.1 7.4 %shard_map.129 = (bf16[1408,128]{1,0:T(8,128)(2,1)}, bf16[640,128]{1,0:T(8,128)(2,1)}, bf16[128,768]{1,0:T(8,128)(2,1)}) custom-call(s32[2]{0:T(128)} %pad_add_fusion.slot_ref.refs_0_, bf16[128,2048]{1,0:T(8,128)(2,1)} %copy-done.8, bf16[128,2048]{1,0:T(8,128)(2,1)} %copy-done.19, bf16[128,2176]{1,0:T(8,128)(2,1)} %copy-done, bf16[128,2176]{1,0:T(8,128)(2,1)} %copy-done.5, ...), custom_call_target="tpu_custom_call" | custom-call | flops 1000000 | bytes 10000 | tf_op jit(solution)/shard_map/pallas_call | solution.py:463
  140.7 4.7 %collective-permute-start.22 = (bf16[128,2048]{1,0:T(8,128)(2,1)S(1)}, bf16[128,2048]{1,0:T(8,128)(2,1)S(1)}, u32[]{:S(2)}, u32[]{:S(2)}) collective-permute-start(bf16[128,2048]{1,0:T(8,128)(2,1)S(1)} %add_convert_fusion.2), channel_id=1, source_target_pairs={{0,2},{1,3},{2,0},{3,1},{4,6},{5,7},{6,4},{7,5},{8,10},{9,11},{10,... | collective-permute-start | bytes 1572872 | tf_op jit(solution)/shard_map/ppermute | solution.py:499
  150.7 3.1 %collective-permute-done.29 = bf16[640,128]{1,0:T(8,128)(2,1)S(1)} collective-permute-done((bf16[640,128]{1,0:T(8,128)(2,1)S(1)}, bf16[640,128]{1,0:T(8,128)(2,1)S(1)}, u32[]{:S(2)}, u32[]{:S(2)}) %collective-permute-start.29) | collective-permute-done | bytes 163872 | tf_op jit(solution)/shard_map/ppermute | solution.py:518
  153.9 1.6 collective-permute-start.31
  161.5 4.9 %collective-permute-done.27 = bf16[1408,128]{1,0:T(8,128)(2,1)S(1)} collective-permute-done((bf16[1408,128]{1,0:T(8,128)(2,1)S(1)}, bf16[1408,128]{1,0:T(8,128)(2,1)S(1)}, u32[]{:S(2)}, u32[]{:S(2)}) %collective-permute-start.27) | collective-permute-done | bytes 360480 | tf_op jit(solution)/shard_map/ppermute | solution.py:518
  (114 shorter events, 35.5 us)
Async XLA Ops:
  19.0 16.1 %collective-permute-start = (bf16[128,2176]{1,0:T(8,128)(2,1)}, bf16[128,2176]{1,0:T(8,128)(2,1)S(1)}, u32[]{:S(2)}, u32[]{:S(2)}) collective-permute-start(bf16[128,2176]{1,0:T(8,128)(2,1)} %shard_map.121.mine_hbm.refs_3_), channel_id=1, source_target_pairs={{0,2},{1,3},{2,0},{3,1},{4,6},{5,7},{6,4},{7,5},{8,10},{9,11},{10,... | collective-permute-start | bytes 1671176 | tf_op jit(solution)/shard_map/ppermute | solution.py:499
  21.6 13.4 %collective-permute-start.1 = (bf16[128,2176]{1,0:T(8,128)(2,1)}, bf16[128,2176]{1,0:T(8,128)(2,1)S(1)}, u32[]{:S(2)}, u32[]{:S(2)}) collective-permute-start(bf16[128,2176]{1,0:T(8,128)(2,1)} %shard_map.121.mine_hbm.refs_3_), channel_id=1, source_target_pairs={{2,4},{3,5},{4,2},{5,3},{10,12},{11,13},{12,10},{13,11},{18,20},{1... | collective-permute-start | bytes 1671176 | tf_op jit(solution)/shard_map/ppermute | solution.py:499
  35.0 8.5 %collective-permute-start.5 = (bf16[128,2176]{1,0:T(8,128)(2,1)S(1)}, bf16[128,2176]{1,0:T(8,128)(2,1)S(1)}, u32[]{:S(2)}, u32[]{:S(2)}) collective-permute-start(bf16[128,2176]{1,0:T(8,128)(2,1)S(1)} %collective-permute-done.mine_hbm.refs_3_), channel_id=1, source_target_pairs={{0,1},{1,0},{2,3},{3,2},{4,5},{5,4},{6,7},{7,6},{8,9},{9,8},{10,11... | collective-permute-start | bytes 1671176 | tf_op jit(solution)/shard_map/ppermute | solution.py:499
  35.1 17.6 %collective-permute-start.4 = (bf16[128,2176]{1,0:T(8,128)(2,1)S(1)}, bf16[128,2176]{1,0:T(8,128)(2,1)S(1)}, u32[]{:S(2)}, u32[]{:S(2)}) collective-permute-start(bf16[128,2176]{1,0:T(8,128)(2,1)S(1)} %collective-permute-done.mine_hbm.refs_3_), channel_id=1, source_target_pairs={{2,4},{3,5},{4,2},{5,3},{10,12},{11,13},{12,10},{13,11},{18,20},{1... | collective-permute-start | bytes 1671176 | tf_op jit(solution)/shard_map/ppermute | solution.py:499
  35.8 20.8 %collective-permute-start.3 = (bf16[128,2176]{1,0:T(8,128)(2,1)S(1)}, bf16[128,2176]{1,0:T(8,128)(2,1)S(1)}, u32[]{:S(2)}, u32[]{:S(2)}) collective-permute-start(bf16[128,2176]{1,0:T(8,128)(2,1)S(1)} %collective-permute-done.1), channel_id=1, source_target_pairs={{0,2},{1,3},{2,0},{3,1},{4,6},{5,7},{6,4},{7,5},{8,10},{9,11},{10,... | collective-permute-start | bytes 1671176 | tf_op jit(solution)/shard_map/ppermute | solution.py:499
  56.7 15.0 %collective-permute-start.6 = (bf16[128,2176]{1,0:T(8,128)(2,1)S(1)}, bf16[128,2176]{1,0:T(8,128)(2,1)S(1)}, u32[]{:S(2)}, u32[]{:S(2)}) collective-permute-start(bf16[128,2176]{1,0:T(8,128)(2,1)S(1)} %collective-permute-done.4), channel_id=1, source_target_pairs={{0,2},{1,3},{2,0},{3,1},{4,6},{5,7},{6,4},{7,5},{8,10},{9,11},{10,... | collective-permute-start | bytes 1671176 | tf_op jit(solution)/shard_map/ppermute | solution.py:499
  58.5 10.0 %collective-permute-start.7 = (bf16[128,2048]{1,0:T(8,128)(2,1)S(1)}, bf16[128,2048]{1,0:T(8,128)(2,1)S(1)}, u32[]{:S(2)}, u32[]{:S(2)}) collective-permute-start(bf16[128,2048]{1,0:T(8,128)(2,1)S(1)} %copy-done.11), channel_id=1, source_target_pairs={{2,4},{3,5},{4,2},{5,3},{10,12},{11,13},{12,10},{13,11},{18,20},{1... | collective-permute-start | bytes 1572872 | tf_op jit(solution)/shard_map/ppermute | solution.py:499
  71.9 15.5 %collective-permute-start.9 = (bf16[128,2048]{1,0:T(8,128)(2,1)S(1)}, bf16[128,2048]{1,0:T(8,128)(2,1)S(1)}, u32[]{:S(2)}, u32[]{:S(2)}) collective-permute-start(bf16[128,2048]{1,0:T(8,128)(2,1)S(1)} %copy-done.12), channel_id=1, source_target_pairs={{0,2},{1,3},{2,0},{3,1},{4,6},{5,7},{6,4},{7,5},{8,10},{9,11},{10,... | collective-permute-start | bytes 1572872 | tf_op jit(solution)/shard_map/ppermute | solution.py:499
  87.4 11.4 %collective-permute-start.13 = (bf16[128,2048]{1,0:T(8,128)(2,1)}, bf16[128,2048]{1,0:T(8,128)(2,1)S(1)}, u32[]{:S(2)}, u32[]{:S(2)}) collective-permute-start(bf16[128,2048]{1,0:T(8,128)(2,1)} %get-tuple-element.109), channel_id=1, source_target_pairs={{0,1},{1,0},{2,3},{3,2},{4,5},{5,4},{6,7},{7,6},{8,9},{9,8},{10,11... | collective-permute-start | bytes 1572872 | tf_op jit(solution)/shard_map/ppermute | solution.py:499
  87.9 14.2 %collective-permute-start.11 = (bf16[128,2048]{1,0:T(8,128)(2,1)}, bf16[128,2048]{1,0:T(8,128)(2,1)}, u32[]{:S(2)}, u32[]{:S(2)}) collective-permute-start(bf16[128,2048]{1,0:T(8,128)(2,1)} %copy-done.21), channel_id=1, source_target_pairs={{0,2},{1,3},{2,0},{3,1},{4,6},{5,7},{6,4},{7,5},{8,10},{9,11},{10,... | collective-permute-start | bytes 1572872 | tf_op jit(solution)/shard_map/ppermute | solution.py:499
  89.7 12.5 %collective-permute-start.12 = (bf16[128,2048]{1,0:T(8,128)(2,1)S(1)}, bf16[128,2048]{1,0:T(8,128)(2,1)S(1)}, u32[]{:S(2)}, u32[]{:S(2)}) collective-permute-start(bf16[128,2048]{1,0:T(8,128)(2,1)S(1)} %collective-permute-done.9.refs_1_), channel_id=1, source_target_pairs={{2,4},{3,5},{4,2},{5,3},{10,12},{11,13},{12,10},{13,11},{18,20},{1... | collective-permute-start | bytes 1572872 | tf_op jit(solution)/shard_map/ppermute | solution.py:499
  103.3 12.1 %collective-permute-start.17 = (bf16[128,2048]{1,0:T(8,128)(2,1)S(1)}, bf16[128,2048]{1,0:T(8,128)(2,1)S(1)}, u32[]{:S(2)}, u32[]{:S(2)}) collective-permute-start(bf16[128,2048]{1,0:T(8,128)(2,1)S(1)} %broadcast_select_fusion.3.refs_1_), channel_id=1, source_target_pairs={{0,1},{1,0},{2,3},{3,2},{4,5},{5,4},{6,7},{7,6},{8,9},{9,8},{10,11... | collective-permute-start | bytes 1572872 | tf_op jit(solution)/shard_map/ppermute | solution.py:499
  103.9 19.7 %collective-permute-start.16 = (bf16[128,2048]{1,0:T(8,128)(2,1)}, bf16[128,2048]{1,0:T(8,128)(2,1)S(1)}, u32[]{:S(2)}, u32[]{:S(2)}) collective-permute-start(bf16[128,2048]{1,0:T(8,128)(2,1)} %get-tuple-element.123), channel_id=1, source_target_pairs={{0,1},{1,0},{2,3},{3,2},{4,5},{5,4},{6,7},{7,6},{8,9},{9,8},{10,11... | collective-permute-start | bytes 1572872 | tf_op jit(solution)/shard_map/ppermute | solution.py:499
  104.8 19.0 %collective-permute-start.15 = (bf16[128,2048]{1,0:T(8,128)(2,1)}, bf16[128,2048]{1,0:T(8,128)(2,1)S(1)}, u32[]{:S(2)}, u32[]{:S(2)}) collective-permute-start(bf16[128,2048]{1,0:T(8,128)(2,1)} %broadcast_select_fusion.4), channel_id=1, source_target_pairs={{0,2},{1,3},{2,0},{3,1},{4,6},{5,7},{6,4},{7,5},{8,10},{9,11},{10,... | collective-permute-start | bytes 1572872 | tf_op jit(solution)/shard_map/ppermute | solution.py:499
  124.2 12.9 %collective-permute-start.21 = (bf16[128,2048]{1,0:T(8,128)(2,1)S(1)}, bf16[128,2048]{1,0:T(8,128)(2,1)}, u32[]{:S(2)}, u32[]{:S(2)}) collective-permute-start(bf16[128,2048]{1,0:T(8,128)(2,1)S(1)} %add_convert_fusion.3), channel_id=1, source_target_pairs={{2,4},{3,5},{4,2},{5,3},{10,12},{11,13},{12,10},{13,11},{18,20},{1... | collective-permute-start | bytes 1572872 | tf_op jit(solution)/shard_map/ppermute | solution.py:499
  125.7 12.9 %collective-permute-start.20 = (bf16[128,2048]{1,0:T(8,128)(2,1)}, bf16[128,2048]{1,0:T(8,128)(2,1)}, u32[]{:S(2)}, u32[]{:S(2)}) collective-permute-start(bf16[128,2048]{1,0:T(8,128)(2,1)} %get-tuple-element.142), channel_id=1, source_target_pairs={{0,1},{1,0},{2,3},{3,2},{4,5},{5,4},{6,7},{7,6},{8,9},{9,8},{10,11... | collective-permute-start | bytes 1572872 | tf_op jit(solution)/shard_map/ppermute | solution.py:499
  126.0 14.6 %collective-permute-start.23 = (bf16[128,2048]{1,0:T(8,128)(2,1)S(1)}, bf16[128,2048]{1,0:T(8,128)(2,1)S(1)}, u32[]{:S(2)}, u32[]{:S(2)}) collective-permute-start(bf16[128,2048]{1,0:T(8,128)(2,1)S(1)} %add_convert_fusion.6), channel_id=1, source_target_pairs={{0,2},{1,3},{2,0},{3,1},{4,6},{5,7},{6,4},{7,5},{8,10},{9,11},{10,... | collective-permute-start | bytes 1572872 | tf_op jit(solution)/shard_map/ppermute | solution.py:499
  127.1 33.2 %collective-permute-start.19 = (bf16[128,2048]{1,0:T(8,128)(2,1)}, bf16[128,2048]{1,0:T(8,128)(2,1)S(1)}, u32[]{:S(2)}, u32[]{:S(2)}) collective-permute-start(bf16[128,2048]{1,0:T(8,128)(2,1)} %get-tuple-element.140), channel_id=1, source_target_pairs={{0,1},{1,0},{2,3},{3,2},{4,5},{5,4},{6,7},{7,6},{8,9},{9,8},{10,11... | collective-permute-start | bytes 1572872 | tf_op jit(solution)/shard_map/ppermute | solution.py:499
  135.5 12.6 %collective-permute-start.30 = (bf16[128,768]{1,0:T(8,128)(2,1)}, bf16[128,768]{1,0:T(8,128)(2,1)S(1)}, u32[]{:S(2)}, u32[]{:S(2)}) collective-permute-start(bf16[128,768]{1,0:T(8,128)(2,1)} %get-tuple-element.154), channel_id=1, source_target_pairs={{0,16},{8,24},{16,0},{24,8},{1,17},{9,25},{17,1},{25,9},{2,18},{10... | collective-permute-start | bytes 589832 | tf_op jit(solution)/shard_map/ppermute | solution.py:518
  137.1 19.4 %collective-permute-start.26 = (bf16[1408,128]{1,0:T(8,128)(2,1)}, bf16[1408,128]{1,0:T(8,128)(2,1)S(1)}, u32[]{:S(2)}, u32[]{:S(2)}) collective-permute-start(bf16[1408,128]{1,0:T(8,128)(2,1)} %get-tuple-element.152), channel_id=1, source_target_pairs={{0,8},{8,0},{16,24},{24,16},{1,9},{9,1},{17,25},{25,17},{2,10},{10... | collective-permute-start | bytes 1081352 | tf_op jit(solution)/shard_map/ppermute | solution.py:518
  138.6 7.8 %collective-permute-start.28 = (bf16[640,128]{1,0:T(8,128)(2,1)}, bf16[640,128]{1,0:T(8,128)(2,1)S(1)}, u32[]{:S(2)}, u32[]{:S(2)}) collective-permute-start(bf16[640,128]{1,0:T(8,128)(2,1)} %get-tuple-element.153), channel_id=1, source_target_pairs={{0,16},{8,24},{16,0},{24,8},{1,17},{9,25},{17,1},{25,9},{2,18},{10... | collective-permute-start | bytes 491528 | tf_op jit(solution)/shard_map/ppermute | solution.py:518
  140.7 19.7 %collective-permute-start.22 = (bf16[128,2048]{1,0:T(8,128)(2,1)S(1)}, bf16[128,2048]{1,0:T(8,128)(2,1)S(1)}, u32[]{:S(2)}, u32[]{:S(2)}) collective-permute-start(bf16[128,2048]{1,0:T(8,128)(2,1)S(1)} %add_convert_fusion.2), channel_id=1, source_target_pairs={{0,2},{1,3},{2,0},{3,1},{4,6},{5,7},{6,4},{7,5},{8,10},{9,11},{10,... | collective-permute-start | bytes 1572872 | tf_op jit(solution)/shard_map/ppermute | solution.py:499
  146.5 13.9 %collective-permute-start.24 = (bf16[128,2048]{1,0:T(8,128)(2,1)S(1)}, bf16[128,2048]{1,0:T(8,128)(2,1)S(1)}, u32[]{:S(2)}, u32[]{:S(2)}) collective-permute-start(bf16[128,2048]{1,0:T(8,128)(2,1)S(1)} %add_convert_fusion.1), channel_id=1, source_target_pairs={{2,4},{3,5},{4,2},{5,3},{10,12},{11,13},{12,10},{13,11},{18,20},{1... | collective-permute-start | bytes 1572872 | tf_op jit(solution)/shard_map/ppermute | solution.py:499
  157.6 8.9 %collective-permute-start.27 = (bf16[1408,128]{1,0:T(8,128)(2,1)S(1)}, bf16[1408,128]{1,0:T(8,128)(2,1)S(1)}, u32[]{:S(2)}, u32[]{:S(2)}) collective-permute-start(bf16[1408,128]{1,0:T(8,128)(2,1)S(1)} %fusion), channel_id=1, source_target_pairs={{0,16},{8,24},{16,0},{24,8},{1,17},{9,25},{17,1},{25,9},{2,18},{10... | collective-permute-start | bytes 1081352 | tf_op jit(solution)/shard_map/ppermute | solution.py:518
  (31 other events, 261.1 us)

commit v9 on v0

--- a/solution.py
+++ b/solution.py
@@ -1,6 +1,10 @@
+import functools
+
 import jax
 import jax.numpy as jnp
 from jax import lax
+from jax.experimental import pallas as pl
+from jax.experimental.pallas import tpu as pltpu
 from jax.sharding import PartitionSpec as P
 
 ADAPTER_SCALE = 0.5
@@ -88,7 +92,7 @@
     return (grad_adapt_a, jnp.stack([gate_up_map_gradient, up_map_gradient]))
 
 
-def body(
+def sparse_body(
     tokens,
     cotangent,
     routing,
@@ -179,6 +183,397 @@
     grad_a = summed_a.reshape(grad_adapt_a.shape)[None]
     grad_b = summed_b.reshape(grad_adapt_b.shape)[None]
     return (mixed, grad_a, grad_b)
+
+
+def dot(a, b, a_dim=1, b_dim=0):
+    return lax.dot_general(
+        a, b, (((a_dim,), (b_dim,)), ((), ())), preferred_element_type=jnp.float32
+    )
+
+
+def first_half(shape):
+    return lax.broadcasted_iota(jnp.int32, shape, 1) < shape[1] // 2
+
+
+def halves(low):
+    gate = first_half(low.shape)
+    zero = jnp.zeros_like(low)
+    return jnp.where(gate, low, zero), jnp.where(gate, zero, low)
+
+
+def split_weights(table):
+    parts = []
+    for _ in range(3):
+        part = table.astype(jnp.bfloat16).astype(jnp.float32)
+        parts.append(part)
+        table = table - part
+    slot_total, tok_rows = table.shape
+    parts.append(jnp.zeros((tok_rows - 3 * slot_total, tok_rows), jnp.float32))
+    return jnp.transpose(jnp.concatenate(parts)).astype(jnp.bfloat16)
+
+
+def joined_weight(extra, slot, slot_total):
+    lane = lax.broadcasted_iota(jnp.int32, extra.shape, 1)
+    mine = lane == slot
+    for part in range(1, 3):
+        mine = mine | (lane == slot + part * slot_total)
+    chosen = jnp.where(mine, extra.astype(jnp.float32), 0.0)
+    return jnp.sum(chosen, axis=1, keepdims=True)
+
+
+def tagged_kernel(capacity, table_ref, expert_ref, choice_ref, weight_ref, tokens_ref, out_ref):
+    slot_total = table_ref.shape[0]
+    tok_rows, features = tokens_ref.shape
+    out_ref[:, :features] = tokens_ref[...]
+    experts, weights = expert_ref[...], weight_ref[...]
+    holds = [experts == table_ref[s] for s in range(slot_total)]
+    counts = [hold.astype(jnp.float32) for hold in holds]
+    copies = sum(counts)
+    choice = choice_ref[...].astype(jnp.float32)
+    wanted = choice - copies * jnp.floor((choice + 0.5) / copies)
+    before = jnp.zeros_like(copies)
+    taken, route_weight = [], []
+    for hold, count in zip(holds, counts):
+        picked = jnp.where(hold & (before == wanted), 1.0, 0.0)
+        before = before + count
+        taken.append(jnp.sum(picked, axis=0, keepdims=True))
+        route_weight.append(jnp.sum(picked * weights, axis=0, keepdims=True))
+    shape = (tok_rows, tok_rows)
+    earlier = lax.broadcasted_iota(jnp.int32, shape, 0) < lax.broadcasted_iota(jnp.int32, shape, 1)
+    rank = dot(
+        jnp.concatenate(taken).astype(jnp.bfloat16),
+        jnp.where(earlier, 1.0, 0.0).astype(jnp.bfloat16),
+    )
+    table = jnp.where(rank < capacity, jnp.concatenate(route_weight), 0.0)
+    out_ref[:, features:] = split_weights(table)
+
+
+VMEM = pl.BlockSpec(memory_space=pltpu.VMEM)
+SMEM = pl.BlockSpec(memory_space=pltpu.SMEM)
+EXTRA = 128
+
+
+def tagged_tokens(tokens, routing, weights, choice, table, capacity):
+    tok_rows, features = tokens.shape
+    return pl.pallas_call(
+        functools.partial(tagged_kernel, capacity),
+        out_shape=jax.ShapeDtypeStruct((tok_rows, features + EXTRA), tokens.dtype),
+        in_specs=[SMEM, VMEM, VMEM, VMEM, VMEM],
+        out_specs=VMEM,
+    )(table, routing.T, choice.T, weights.T, tokens)
+
+
+def stage_call(kernel, outs, scratch, macs, operands):
+    out_shape = tuple(jax.ShapeDtypeStruct(*out) for out in outs)
+    moved = sum(array.size * array.dtype.itemsize for array in (*operands, *out_shape))
+    return pl.pallas_call(
+        kernel,
+        out_shape=out_shape,
+        in_specs=[SMEM] + [VMEM] * (len(operands) - 1),
+        out_specs=(VMEM,) * len(outs),
+        scratch_shapes=[pltpu.VMEM(*shape) for shape in scratch],
+        compiler_params=pltpu.CompilerParams(vmem_limit_bytes=16 * 2**20),
+        cost_estimate=pl.CostEstimate(flops=2 * macs, bytes_accessed=moved, transcendentals=0),
+    )(*operands)
+
+
+def forward_kernel(
+    chunk, slot_ref, mine_ref, other_ref, adapt_a_ref, gate_up_ref, adapt_b_ref, down_ref,
+    low_ref, active_ref, slope_ref, part_mine_ref, part_other_ref, rows_ref, total_ref,
+):
+    half, features = part_mine_ref.shape
+    hidden_width = down_ref.shape[0]
+    rows_ref[:half] = mine_ref[:, :features]
+    rows_ref[half:] = other_ref[:, :features]
+    rows = rows_ref[...]
+    low = dot(rows, adapt_a_ref[...]).astype(jnp.bfloat16)
+    low_ref[...] = low
+    low_gate, low_up = halves(low)
+    for start in range(0, hidden_width, chunk):
+        here = slice(start, start + chunk)
+        there = slice(hidden_width + start, hidden_width + start + chunk)
+        adapt_b = adapt_b_ref[:, here]
+        gate = dot(rows, gate_up_ref[:, here]) + ADAPTER_SCALE * dot(low_gate, adapt_b)
+        up = dot(rows, gate_up_ref[:, there]) + ADAPTER_SCALE * dot(low_up, adapt_b)
+        sigmoid_gate = jax.nn.sigmoid(gate)
+        active = gate * sigmoid_gate
+        active_ref[:, here] = active
+        slope_ref[:, here] = up * (sigmoid_gate * (1.0 + gate * (1.0 - sigmoid_gate)))
+        more = dot((active * up).astype(jnp.bfloat16), down_ref[here])
+        if start == 0:
+            total_ref[...] = more
+        else:
+            total_ref[...] += more
+    out = total_ref[...].astype(jnp.bfloat16).astype(jnp.float32)
+    for block_ref, part_ref, out in (
+        (mine_ref, part_mine_ref, out[:half]),
+        (other_ref, part_other_ref, out[half:]),
+    ):
+        w = joined_weight(block_ref[:, features:], slot_ref[0], slot_ref[1])
+        part_ref[...] = (w * out).astype(jnp.bfloat16)
+
+
+def forward_stage(slot, mine, other, gate_up, down, adapt_a, adapt_b, chunk=256):
+    hidden_width, features = down.shape
+    half, both, ranks = mine.shape[0], 2 * mine.shape[0], adapt_a.shape[1]
+    bf16, f32 = jnp.bfloat16, jnp.float32
+    saved = ((both, hidden_width), f32)
+    part = ((half, features), bf16)
+    return stage_call(
+        functools.partial(forward_kernel, chunk),
+        (((both, ranks), bf16), saved, saved, part, part),
+        [((both, features), bf16), ((both, features), f32)],
+        both * (gate_up.size + down.size + adapt_a.size),
+        (slot, mine, other, adapt_a, gate_up, adapt_b, down),
+    )
+
+
+def backward_kernel(chunk, adds, cut, *refs):
+    slot_ref, cot_mine, cot_other, mine_ref, other_ref, *refs = refs
+    low_ref, active_ref, slope_ref, adapt_b_ref, down_ref, *refs = refs
+    grads, (out_a_ref, out_b_ref, scaled_ref, rows_ref) = refs[: 2 * adds], refs[2 * adds :]
+    half, features = cot_mine.shape
+    for at, (cot_ref, block_ref) in enumerate(((cot_mine, mine_ref), (cot_other, other_ref))):
+        here = slice(at * half, (at + 1) * half)
+        w = joined_weight(block_ref[:, features:], slot_ref[0], slot_ref[1])
+        scaled_ref[here] = (w * cot_ref[...].astype(jnp.float32)).astype(jnp.bfloat16)
+        rows_ref[here] = block_ref[:, :features]
+    scaled = scaled_ref[...]
+    low_gate, low_up = halves(low_ref[...])
+    low_back = 0.0
+    for start in range(0, down_ref.shape[0], chunk):
+        here = slice(start, start + chunk)
+        adapt_b = adapt_b_ref[:, here]
+        back = dot(scaled, down_ref[here], 1, 1)
+        up_grad = (back * active_ref[:, here]).astype(jnp.bfloat16)
+        gate_grad = (back * slope_ref[:, here]).astype(jnp.bfloat16)
+        sum_b = ADAPTER_SCALE * (dot(low_gate, gate_grad, 0, 0) + dot(low_up, up_grad, 0, 0))
+        sum_b = sum_b + grads[1][:, here] if adds else sum_b
+        if cut is None:
+            out_b_ref[:, here] = sum_b
+        else:
+            ranks = sum_b.shape[0]
+            for col in range(0, chunk, ranks):
+                at = features - cut + start + col
+                out_b_ref[at : at + ranks] = sum_b[:, col : col + ranks].astype(jnp.bfloat16)
+        gate_back, up_back = dot(gate_grad, adapt_b, 1, 1), dot(up_grad, adapt_b, 1, 1)
+        low_back = low_back + jnp.where(first_half(gate_back.shape), gate_back, up_back)
+    low_grad = (ADAPTER_SCALE * low_back).astype(jnp.bfloat16)
+    sum_a = dot(rows_ref[...], low_grad, 0, 0)
+    sum_a = sum_a + grads[0][...] if adds else sum_a
+    if cut is None:
+        out_a_ref[...] = sum_a
+    else:
+        out_a_ref[...] = sum_a[:cut].astype(jnp.bfloat16)
+        out_b_ref[: features - cut] = sum_a[cut:].astype(jnp.bfloat16)
+
+
+def backward_stage(slot, cots, blocks, saved, down, adapt_b, grads=(), cut=None, chunk=256):
+    hidden_width, features = down.shape
+    both, ranks = saved[0].shape
+    bf16, f32 = jnp.bfloat16, jnp.float32
+    outs = (((features, ranks), f32), ((ranks, hidden_width), f32))
+    if cut is not None:
+        outs = (((cut, ranks), bf16), ((features - cut + hidden_width, ranks), bf16))
+    return stage_call(
+        functools.partial(backward_kernel, chunk, len(grads) // 2, cut),
+        outs,
+        [((both, features), bf16), ((both, features), bf16)],
+        both * (down.size + features * ranks + 4 * adapt_b.size),
+        (slot, *cots, *blocks, *saved, adapt_b, down, *grads),
+    )
+
+
+def pair_kernel(*refs):
+    for one_ref, other_ref, out_ref in zip(refs[:2], refs[2:4], refs[4:]):
+        total = one_ref[...].astype(jnp.float32) + other_ref[...].astype(jnp.float32)
+        out_ref[...] = total.astype(out_ref.dtype)
+
+
+def pair_sums(ones, others):
+    return pl.pallas_call(
+        pair_kernel,
+        out_shape=tuple(jax.ShapeDtypeStruct(one.shape, one.dtype) for one in ones),
+        in_specs=[VMEM] * 4,
+        out_specs=(VMEM,) * 2,
+    )(*ones, *others)
+
+
+def finish_kernel(one_x, one_y, other_x, other_y, grad_a_ref, grad_b_ref):
+    cut, ranks = one_x.shape
+    rest = grad_a_ref.shape[0] - cut
+    grad_a_ref[:cut] = one_x[...].astype(jnp.float32) + other_x[...].astype(jnp.float32)
+    total = one_y[...].astype(jnp.float32) + other_y[...].astype(jnp.float32)
+    grad_a_ref[cut:] = total[:rest]
+    for col in range(0, grad_b_ref.shape[1], ranks):
+        grad_b_ref[:, col : col + ranks] = total[rest + col : rest + col + ranks]
+
+
+def finished(ones, others, features, hidden_width):
+    ranks = ones[0].shape[1]
+    shapes = ((features, ranks), (ranks, hidden_width))
+    return pl.pallas_call(
+        finish_kernel,
+        grid=(1,),
+        out_shape=tuple(jax.ShapeDtypeStruct(shape, jnp.float32) for shape in shapes),
+        in_specs=[pl.BlockSpec(one.shape, lambda j: (0, 0)) for one in (*ones, *others)],
+        out_specs=tuple(pl.BlockSpec(shape, lambda j: (0, 0)) for shape in shapes),
+    )(*ones, *others)
+
+
+def z_pairs(*moves):
+    return [(2 * a + core, 2 * b + core) for a, b in moves for core in (0, 1)]
+
+
+ALL_SWAP = z_pairs((0, 1), (1, 0), (2, 3), (3, 2))
+MID_SWAP = z_pairs((1, 2), (2, 1))
+SIBLING = [(e, e ^ 1) for e in range(8)]
+
+
+def send(array, pairs):
+    return lax.ppermute(array, "expert", pairs)
+
+
+def fence(*arrays):
+    return lax.optimization_barrier(arrays)
+
+
+def add_rounded(*terms):
+    total = terms[0].astype(jnp.float32)
+    for term in terms[1:]:
+        total = total + term.astype(jnp.float32)
+    return total.astype(jnp.bfloat16)
+
+
+def sibling(block):
+    return send(block, SIBLING)
+
+
+def dp_swap(array, bit):
+    return lax.ppermute(array, "dp", [(d, d ^ bit) for d in range(4)])
+
+
+def group_sum(mine, features, hidden_width):
+    got = dp_swap(mine[0], 1), dp_swap(mine[1], 2)
+    pairs = pair_sums(mine, got)
+    got = dp_swap(pairs[0], 2), dp_swap(pairs[1], 1)
+    return finished(pairs, got, features, hidden_width)
+
+
+def dense_body(
+    tokens,
+    cotangent,
+    routing,
+    router_route_weights,
+    route_replica_choice,
+    device_expert_table,
+    gate_up_weight,
+    down_weight,
+    adapter_down_maps,
+    adapter_up_maps,
+):
+    slot_total = lax.axis_size("expert")
+    capacity = tokens.shape[0] * routing.shape[1] // slot_total
+    me = lax.axis_index("expert")
+    chip = me // 2
+    inner = (chip == 1) | (chip == 2)
+    gate_up, down = gate_up_weight[0], down_weight[0]
+    adapt_a = adapter_down_maps[0]
+    adapt_b = adapter_up_maps[0].reshape(adapt_a.shape[1], -1)
+
+    slot = jnp.stack([me, jnp.int32(slot_total)])
+
+    def forward(mine, twin):
+        *saved, part, away = forward_stage(slot, mine, twin, gate_up, down, adapt_a, adapt_b)
+        return saved, part, away
+
+    def backward(cots, rows, saved, grads=(), cut=None):
+        return backward_stage(slot, cots, rows, saved, down, adapt_b, grads, cut)
+
+    def pick(inside, outside):
+        return jnp.where(inner, inside, outside)
+
+    def after(array, earlier):
+        return fence(array, earlier)[0]
+
+    tokens = tagged_tokens(
+        tokens, routing, router_route_weights, route_replica_choice, device_expert_table, capacity
+    )
+    tok_swap = send(tokens, ALL_SWAP)
+    twin = sibling(tokens)
+    rows0 = (tokens, twin)
+    tok_mid = send(after(tokens, twin), MID_SWAP)
+    tok_swap, tok_mid, rows0, cotangent = fence(tok_swap, tok_mid, rows0, cotangent)
+
+    tok_out2 = send(tok_mid, ALL_SWAP)
+    twin = sibling(tok_swap)
+    rows1 = (tok_swap, twin)
+    tok_mid2 = send(after(tok_swap, twin), MID_SWAP)
+    saved0, part0, away0 = forward(*rows0)
+    tok_mid, tok_out2, tok_mid2, rows1, part0, away0, cotangent = fence(
+        tok_mid, tok_out2, tok_mid2, rows1, part0, away0, cotangent
+    )
+
+    tok_out3 = send(tok_mid2, ALL_SWAP)
+    tok_second = pick(tok_mid, tok_out2)
+    twin = sibling(tok_second)
+    rows2 = (tok_second, twin)
+    cot_mid = send(after(cotangent, twin), MID_SWAP)
+    saved1, part1, away1 = forward(*rows1)
+    tok_mid2, tok_out3, cot_mid, rows2, part1, away1, cotangent = fence(
+        tok_mid2, tok_out3, cot_mid, rows2, part1, away1, cotangent
+    )
+
+    cot_swap = send(cotangent, ALL_SWAP)
+    tok_third = pick(tok_mid2, tok_out3)
+    rows3 = (tok_third, sibling(tok_third))
+    cots0 = (cotangent, sibling(cotangent))
+    saved2, part2, away2 = forward(*rows2)
+    saved3, part3, away3 = forward(*rows3)
+    cot_swap, cot_mid, cots0, part2, away2, part3, away3 = fence(
+        cot_swap, cot_mid, cots0, part2, away2, part3, away3
+    )
+
+    cot_out2 = send(cot_mid, ALL_SWAP)
+    twin = sibling(cot_swap)
+    cots1 = (cot_swap, twin)
+    cot_mid2 = send(after(cot_swap, twin), MID_SWAP)
+    part3 = add_rounded(part3, sibling(away3))
+    grads = backward(cots0, rows0, saved0)
+    grads = backward(cots1, rows1, saved1, grads)
+    cot_mid, cot_out2, cot_mid2, part2, away2, part3, grads = fence(
+        cot_mid, cot_out2, cot_mid2, part2, away2, part3, grads
+    )
+
+    swap6 = send(pick(cot_mid2, part3), ALL_SWAP)
+    cot_second = pick(cot_mid, cot_out2)
+    cots2 = (cot_second, sibling(cot_second))
+    grads = backward(cots2, rows2, saved2, grads)
+    part2 = add_rounded(part2, sibling(away2))
+    swap6, cot_mid2, part0, away0, part1, away1, part2, part3, grads = fence(
+        swap6, cot_mid2, part0, away0, part1, away1, part2, part3, grads
+    )
+
+    second_in = send(part2, ALL_SWAP)
+    cot_third = pick(cot_mid2, swap6)
+    twin = sibling(cot_third)
+    third_mid = send(after(add_rounded(part3, swap6), twin), MID_SWAP)
+    features, hidden_width = adapt_a.shape[0], adapt_b.shape[1]
+    cut = (features + hidden_width) // 2
+    grads = backward((cot_third, twin), rows3, saved3, grads, cut)
+    grad_a, grad_b = group_sum(grads, features, hidden_width)
+    part1 = add_rounded(part1, sibling(away1))
+    part0 = add_rounded(part0, sibling(away0))
+    first_swap = send(add_rounded(part1, third_mid), ALL_SWAP)
+    second_mid = send(add_rounded(part2, second_in), MID_SWAP)
+    mixed = add_rounded(part0, first_swap, second_mid)
+    return mixed, grad_a[None], grad_b.reshape(adapter_up_maps.shape)
+
+
+def body(*arrays):
+    if (lax.axis_size("dp"), lax.axis_size("expert"), arrays[2].shape[1]) == (4, 8, 8):
+        return dense_body(*arrays)
+    return sparse_body(*arrays)
 
 
 def solution(mesh):

time: 547 us -> 154 us (0.28)
  waiting for transfers between devices: 275 us -> 52 us
  blocking collectives: 117 us -> 0 us
  local copies, waits for them, and re-layouts: 52.7 us -> 8.49 us
  matrix products: 43.3 us -> 0 us
  Pallas kernels: 0 us -> 38.6 us
  starting transfers between devices: 21.5 us -> 47.1 us
  other arithmetic: 21.7 us -> 5.96 us
  between operations: 14.3 us -> 0.96 us
    all_to_all x5 -> x0, waiting for transfers between devices: 218 us -> none  [the longest x1 87.8 us: body(): lax.all_to_all(layer_output.reshape(slot_total, capacity, model_feature_w...]
    all_to_all x2 -> x0, blocking collectives: 117 us -> none  [the longest x1 100 us: body(): lax.all_to_all(rows_out, 'expert', split_axis=0, concat_axis=0, tiled=True)]
    psum x1 -> x0, waiting for transfers between devices: 57.9 us -> none  [body(): piece_a, piece_b = lax.psum((piece_a, piece_b), 'dp')]
    ppermute x0 -> x30, waiting for transfers between devices: none -> 52 us  [the longest x26 43.1 us: send(): return lax.ppermute(array, 'expert', pairs)]
    ppermute x0 -> x30, starting transfers between devices: none -> 47.1 us  [the longest x26 41 us: send(): return lax.ppermute(array, 'expert', pairs)]
    dot_general x15 -> x0, matrix products: 43.3 us -> none  [the longest x1 10.4 us: expert_apply_forward(): jnp.dot(rows_in, gate_up, preferred_element_type=jnp.float32)]
    pallas_call x0 -> x11, Pallas kernels: none -> 38.6 us  [the longest x8 31.7 us: stage_call(): pl.pallas_call(kernel, out_shape=out_shape, in_specs=[SMEM] + [VMEM] * (l...]
    gather x4 -> x0, local copies, waits for them, and re-layouts: 36.1 us -> none  [the longest x1 11.7 us: body(): picked_rows = returned[jnp.minimum(dest_index, slot_total * capacity - 1)]]
  transfers between devices with their start and end apart: 6 -> 30, of which waited for: 6 -> 10; matrix products, arithmetic and copies ran while one was open for 7% -> 2% of each run, Pallas kernels for 0% -> 24%
where the time goes in v9:
time: 154 us; the launch traced here: 153 us
  waiting for transfers between devices  52 us (34%)
  starting transfers between devices  47.1 us (31%)
  Pallas kernels  38.6 us (25%)
  local copies, waits for them, and re-layouts  8.49 us (6%)
  other arithmetic  5.96 us (4%)
    ppermute x26, waiting for transfers between devices, send(): return lax.ppermute(array, 'expert', pairs)  43.1 us
    ppermute x26, starting transfers between devices, send(): return lax.ppermute(array, 'expert', pairs)  41 us
    pallas_call x8, Pallas kernels, stage_call(): pl.pallas_call(kernel, out_shape=out_shape, in_specs=[SMEM] + [VMEM] * (l...  31.7 us
    ppermute x4, waiting for transfers between devices, dp_swap(): return lax.ppermute(array, 'dp', [(d, d ^ bit) for d in range(4)])  8.89 us
    unnamed x30, local copies, waits for them, and re-layouts  8.49 us
    ppermute x4, starting transfers between devices, dp_swap(): return lax.ppermute(array, 'dp', [(d, d ^ bit) for d in range(4)])  6.07 us
    convert_element_type x6, other arithmetic, add_rounded(): return total.astype(jnp.bfloat16)  4.51 us
  transfers between devices with their start and end apart: 30, of which 10 were waited for; matrix products, arithmetic and copies ran while one was open for 2% of the time, Pallas kernels for 24%

profile of v9, /device:TPU:0, one launch (start us, length us, event | category | flops | bytes accessed | tf_op | source)
XLA Modules:
  0.0 153.1 jit_solution(10752928057109207137)
XLA Ops:
  3.2 2.6 %collective-permute-start = (bf16[128,2176]{1,0:T(8,128)(2,1)}, bf16[128,2176]{1,0:T(8,128)(2,1)S(1)}, u32[]{:S(2)}, u32[]{:S(2)}) collective-permute-start(bf16[128,2176]{1,0:T(8,128)(2,1)} %shard_map.121.mine_ref.refs_3_), channel_id=1, source_target_pairs={{0,2},{1,3},{2,0},{3,1},{4,6},{5,7},{6,4},{7,5},{8,10},{9,11},{10,... | collective-permute-start | bytes 1671176 | tf_op jit(solution)/shard_map/ppermute | solution.py:434
  7.3 12.0 %collective-permute-done.mine_ref.refs_3_ = bf16[128,2176]{1,0:T(8,128)(2,1)S(1)} collective-permute-done((bf16[128,2176]{1,0:T(8,128)(2,1)}, bf16[128,2176]{1,0:T(8,128)(2,1)S(1)}, u32[]{:S(2)}, u32[]{:S(2)}) %collective-permute-start) | collective-permute-done | bytes 557088 | tf_op jit(solution)/shard_map/ppermute | solution.py:434
  19.3 5.5 %collective-permute-start.3 = (bf16[128,2176]{1,0:T(8,128)(2,1)}, bf16[128,2176]{1,0:T(8,128)(2,1)}, u32[]{:S(2)}, u32[]{:S(2)}) collective-permute-start(bf16[128,2176]{1,0:T(8,128)(2,1)} %collective-permute-done.2), channel_id=1, source_target_pairs={{0,2},{1,3},{2,0},{3,1},{4,6},{5,7},{6,4},{7,5},{8,10},{9,11},{10,... | collective-permute-start | bytes 1671176 | tf_op jit(solution)/shard_map/ppermute | solution.py:434
  27.5 2.8 %copy-done.2 = bf16[1,2048,1536]{2,1,0:T(8,128)(2,1)S(1)} copy-done((bf16[1,2048,1536]{2,1,0:T(8,128)(2,1)S(1)}, bf16[1,2048,1536]{2,1,0:T(8,128)(2,1)}, u32[]{:S(2)}) %copy-start.2) | copy-done | bytes 6291480
  33.4 4.3 %shard_map.122 = (bf16[256,128]{1,0:T(8,128)(2,1)S(1)}, f32[256,768]{1,0:T(8,128)S(1)}, f32[256,768]{1,0:T(8,128)S(1)}, bf16[128,2048]{1,0:T(8,128)(2,1)S(1)}, bf16[128,2048]{1,0:T(8,128)(2,1)S(1)}) custom-call(s32[2]{0:T(128)S(1)} %pad_add_fusion.slot_ref.refs_0_, bf16[128,2176]{1,0:T(8,128)(2,1)S(1)} %copy-done.8, ...), custom_call_target="tpu_custom_call" | custom-call | flops 2550136832 | bytes 13959176 | tf_op jit(solution)/shard_map/pallas_call | solution.py:269
  39.7 5.0 %collective-permute-start.6 = (bf16[128,2176]{1,0:T(8,128)(2,1)S(1)}, bf16[128,2176]{1,0:T(8,128)(2,1)S(1)}, u32[]{:S(2)}, u32[]{:S(2)}) collective-permute-start(bf16[128,2176]{1,0:T(8,128)(2,1)S(1)} %collective-permute-done.5), channel_id=1, source_target_pairs={{0,2},{1,3},{2,0},{3,1},{4,6},{5,7},{6,4},{7,5},{8,10},{9,11},{10,... | collective-permute-start | bytes 1671176 | tf_op jit(solution)/shard_map/ppermute | solution.py:434
  45.5 4.4 %shard_map.123 = (bf16[256,128]{1,0:T(8,128)(2,1)S(1)}, f32[256,768]{1,0:T(8,128)S(1)}, f32[256,768]{1,0:T(8,128)S(1)}, bf16[128,2048]{1,0:T(8,128)(2,1)S(1)}, bf16[128,2048]{1,0:T(8,128)(2,1)S(1)}) custom-call(s32[2]{0:T(128)S(1)} %pad_add_fusion.slot_ref.refs_0_, bf16[128,2176]{1,0:T(8,128)(2,1)S(1)} %collective-permute-done.mine_ref.refs_3_, ...), custom_call_target="tpu_custom_call" | custom-call | flops 2550136832 | bytes 13959176 | tf_op jit(solution)/shard_map/pallas_call | solution.py:269
  49.9 7.9 %collective-permute-done.6 = bf16[128,2176]{1,0:T(8,128)(2,1)S(1)} collective-permute-done((bf16[128,2176]{1,0:T(8,128)(2,1)S(1)}, bf16[128,2176]{1,0:T(8,128)(2,1)S(1)}, u32[]{:S(2)}, u32[]{:S(2)}) %collective-permute-start.6) | collective-permute-done | bytes 557088 | tf_op jit(solution)/shard_map/ppermute | solution.py:434
  58.5 4.5 %collective-permute-start.9 = (bf16[128,2048]{1,0:T(8,128)(2,1)S(1)}, bf16[128,2048]{1,0:T(8,128)(2,1)S(1)}, u32[]{:S(2)}, u32[]{:S(2)}) collective-permute-start(bf16[128,2048]{1,0:T(8,128)(2,1)S(1)} %copy-done.9), channel_id=1, source_target_pairs={{0,2},{1,3},{2,0},{3,1},{4,6},{5,7},{6,4},{7,5},{8,10},{9,11},{10,... | collective-permute-start | bytes 1572872 | tf_op jit(solution)/shard_map/ppermute | solution.py:434
  63.0 4.3 %shard_map.124 = (bf16[256,128]{1,0:T(8,128)(2,1)S(1)}, f32[256,768]{1,0:T(8,128)S(1)}, f32[256,768]{1,0:T(8,128)S(1)}, bf16[128,2048]{1,0:T(8,128)(2,1)S(1)}, bf16[128,2048]{1,0:T(8,128)(2,1)S(1)}) custom-call(s32[2]{0:T(128)S(1)} %pad_add_fusion.slot_ref.refs_0_, bf16[128,2176]{1,0:T(8,128)(2,1)S(1)} %broadcast_select_fusion.1.mine_ref.refs_3_, ...), custom_call_target="tpu_custom_call" | custom-call | flops 2550136832 | bytes 13959176 | tf_op jit(solution)/shard_map/pallas_call | solution.py:269
  67.4 4.3 %shard_map.125 = (bf16[256,128]{1,0:T(8,128)(2,1)S(1)}, f32[256,768]{1,0:T(8,128)S(1)}, f32[256,768]{1,0:T(8,128)S(1)}, bf16[128,2048]{1,0:T(8,128)(2,1)S(1)}, bf16[128,2048]{1,0:T(8,128)(2,1)S(1)}) custom-call(s32[2]{0:T(128)S(1)} %pad_add_fusion.slot_ref.refs_0_, bf16[128,2176]{1,0:T(8,128)(2,1)S(1)} %broadcast_select_fusion.mine_ref.refs_3_, ...), custom_call_target="tpu_custom_call" | custom-call | flops 2550136832 | bytes 13959176 | tf_op jit(solution)/shard_map/pallas_call | solution.py:269
  71.7 3.5 %collective-permute-done.9.refs_1_ = bf16[128,2048]{1,0:T(8,128)(2,1)S(1)} collective-permute-done((bf16[128,2048]{1,0:T(8,128)(2,1)S(1)}, bf16[128,2048]{1,0:T(8,128)(2,1)S(1)}, u32[]{:S(2)}, u32[]{:S(2)}) %collective-permute-start.9) | collective-permute-done | bytes 524320 | tf_op jit(solution)/shard_map/ppermute | solution.py:434
  77.5 3.6 %shard_map.126 = (f32[2048,128]{1,0:T(8,128)S(1)}, f32[128,768]{1,0:T(8,128)S(1)}) custom-call(s32[2]{0:T(128)S(1)} %pad_add_fusion.slot_ref.refs_0_, bf16[128,2048]{1,0:T(8,128)(2,1)S(1)} %copy-done.9, bf16[128,2048]{1,0:T(8,128)(2,1)S(1)} %collective-permute-done.10.refs_2_, bf16[128,2176]{1,0:T(8,128)(2,1)S(1)} %copy-done.8, ...), custom_call_target="tpu_custom_call" | custom-call | flops 1140850688 | bytes 8585224 | tf_op jit(solution)/shard_map/pallas_call | solution.py:269
  82.0 3.6 %shard_map.127 = (f32[2048,128]{1,0:T(8,128)S(1)}, f32[128,768]{1,0:T(8,128)S(1)}) custom-call(s32[2]{0:T(128)S(1)} %pad_add_fusion.slot_ref.refs_0_, bf16[128,2048]{1,0:T(8,128)(2,1)S(1)} %collective-permute-done.9.refs_1_, bf16[128,2048]{1,0:T(8,128)(2,1)S(1)} %collective-permute-done.13.refs_2_, ...), custom_call_target="tpu_custom_call" | custom-call | flops 1140850688 | bytes 10027016 | tf_op jit(solution)/shard_map/pallas_call | solution.py:269
  85.7 3.8 %collective-permute-done.12 = bf16[128,2048]{1,0:T(8,128)(2,1)S(1)} collective-permute-done((bf16[128,2048]{1,0:T(8,128)(2,1)S(1)}, bf16[128,2048]{1,0:T(8,128)(2,1)S(1)}, u32[]{:S(2)}, u32[]{:S(2)}) %collective-permute-start.12) | collective-permute-done | bytes 524320 | tf_op jit(solution)/shard_map/ppermute | solution.py:434
  90.3 7.3 %collective-permute-start.16 = (bf16[128,2048]{1,0:T(8,128)(2,1)S(1)}, bf16[128,2048]{1,0:T(8,128)(2,1)S(1)}, u32[]{:S(2)}, u32[]{:S(2)}) collective-permute-start(bf16[128,2048]{1,0:T(8,128)(2,1)S(1)} %broadcast_select_fusion.4), channel_id=1, source_target_pairs={{0,2},{1,3},{2,0},{3,1},{4,6},{5,7},{6,4},{7,5},{8,10},{9,11},{10,... | collective-permute-start | bytes 1572872 | tf_op jit(solution)/shard_map/ppermute | solution.py:434
  97.6 3.6 %shard_map.128 = (f32[2048,128]{1,0:T(8,128)S(1)}, f32[128,768]{1,0:T(8,128)S(1)}) custom-call(s32[2]{0:T(128)S(1)} %pad_add_fusion.slot_ref.refs_0_, bf16[128,2048]{1,0:T(8,128)(2,1)S(1)} %broadcast_select_fusion.3.refs_1_, bf16[128,2048]{1,0:T(8,128)(2,1)S(1)} %collective-permute-done.18.refs_2_, ...), custom_call_target="tpu_custom_call" | custom-call | flops 1140850688 | bytes 10027016 | tf_op jit(solution)/shard_map/pallas_call | solution.py:269
  101.3 8.4 %collective-permute-done.16 = bf16[128,2048]{1,0:T(8,128)(2,1)S(1)} collective-permute-done((bf16[128,2048]{1,0:T(8,128)(2,1)S(1)}, bf16[128,2048]{1,0:T(8,128)(2,1)S(1)}, u32[]{:S(2)}, u32[]{:S(2)}) %collective-permute-start.16) | collective-permute-done | bytes 524320 | tf_op jit(solution)/shard_map/ppermute | solution.py:434
  113.0 3.6 %shard_map.129 = (bf16[1408,128]{1,0:T(8,128)(2,1)S(1)}, bf16[1408,128]{1,0:T(8,128)(2,1)S(1)}) custom-call(s32[2]{0:T(128)S(1)} %pad_add_fusion.slot_ref.refs_0_, bf16[128,2048]{1,0:T(8,128)(2,1)S(1)} %broadcast_select_fusion.2.refs_1_, bf16[128,2048]{1,0:T(8,128)(2,1)S(1)} %collective-permute-done.21.refs_2_, ...), custom_call_target="tpu_custom_call" | custom-call | flops 1140850688 | bytes 9306120 | tf_op jit(solution)/shard_map/pallas_call | solution.py:269
  118.2 6.5 %collective-permute-done.24 = bf16[128,2048]{1,0:T(8,128)(2,1)S(1)} collective-permute-done((bf16[128,2048]{1,0:T(8,128)(2,1)S(1)}, bf16[128,2048]{1,0:T(8,128)(2,1)S(1)}, u32[]{:S(2)}, u32[]{:S(2)}) %collective-permute-start.24) | collective-permute-done | bytes 524320 | tf_op jit(solution)/shard_map/ppermute | solution.py:434
  128.9 4.5 %collective-permute-start.23 = (bf16[128,2048]{1,0:T(8,128)(2,1)}, bf16[128,2048]{1,0:T(8,128)(2,1)}, u32[]{:S(2)}, u32[]{:S(2)}) collective-permute-start(bf16[128,2048]{1,0:T(8,128)(2,1)} %add_convert_fusion.2), channel_id=1, source_target_pairs={{0,2},{1,3},{2,0},{3,1},{4,6},{5,7},{6,4},{7,5},{8,10},{9,11},{10,... | collective-permute-start | bytes 1572872 | tf_op jit(solution)/shard_map/ppermute | solution.py:434
  134.8 2.3 %shard_map.130 = (bf16[1408,128]{1,0:T(8,128)(2,1)}, bf16[1408,128]{1,0:T(8,128)(2,1)}) custom-call(bf16[1408,128]{1,0:T(8,128)(2,1)} %copy-done.10, bf16[1408,128]{1,0:T(8,128)(2,1)} %copy-done.11, bf16[1408,128]{1,0:T(8,128)(2,1)} %copy-done.12, bf16[1408,128]{1,0:T(8,128)(2,1)} %collective-permute-done.27.refs_3_), custom_call_target="tpu_custom_call" | custom-call | tf_op jit(solution)/shard_map/pallas_call | solution.py:394
  140.1 6.3 %collective-permute-done.28.other_x = bf16[1408,128]{1,0:T(8,128)(2,1)S(1)} collective-permute-done((bf16[1408,128]{1,0:T(8,128)(2,1)}, bf16[1408,128]{1,0:T(8,128)(2,1)S(1)}, u32[]{:S(2)}, u32[]{:S(2)}) %collective-permute-start.28) | collective-permute-done | bytes 360480 | tf_op jit(solution)/shard_map/ppermute | solution.py:453
  148.4 2.5 %shard_map.131 = (f32[2048,128]{1,0:T(8,128)}, f32[128,768]{1,0:T(8,128)}) custom-call(bf16[1408,128]{1,0:T(8,128)(2,1)} %get-tuple-element.167.one_x, bf16[1408,128]{1,0:T(8,128)(2,1)} %get-tuple-element.168.one_y, bf16[1408,128]{1,0:T(8,128)(2,1)} %copy-done.13, bf16[1408,128]{1,0:T(8,128)(2,1)} %copy-done.14), custom_call_target="tpu_custom_call" | custom-call | tf_op jit(solution)/shard_map/pallas_call | solution.py:415
  (89 shorter events, 35.0 us)
Async XLA Ops:
  3.2 16.1 %collective-permute-start = (bf16[128,2176]{1,0:T(8,128)(2,1)}, bf16[128,2176]{1,0:T(8,128)(2,1)S(1)}, u32[]{:S(2)}, u32[]{:S(2)}) collective-permute-start(bf16[128,2176]{1,0:T(8,128)(2,1)} %shard_map.121.mine_ref.refs_3_), channel_id=1, source_target_pairs={{0,2},{1,3},{2,0},{3,1},{4,6},{5,7},{6,4},{7,5},{8,10},{9,11},{10,... | collective-permute-start | bytes 1671176 | tf_op jit(solution)/shard_map/ppermute | solution.py:434
  5.8 13.5 %collective-permute-start.2 = (bf16[128,2176]{1,0:T(8,128)(2,1)}, bf16[128,2176]{1,0:T(8,128)(2,1)}, u32[]{:S(2)}, u32[]{:S(2)}) collective-permute-start(bf16[128,2176]{1,0:T(8,128)(2,1)} %shard_map.121.mine_ref.refs_3_), channel_id=1, source_target_pairs={{2,4},{3,5},{4,2},{5,3},{10,12},{11,13},{12,10},{13,11},{18,20},{1... | collective-permute-start | bytes 1671176 | tf_op jit(solution)/shard_map/ppermute | solution.py:434
  19.3 19.1 %collective-permute-start.3 = (bf16[128,2176]{1,0:T(8,128)(2,1)}, bf16[128,2176]{1,0:T(8,128)(2,1)}, u32[]{:S(2)}, u32[]{:S(2)}) collective-permute-start(bf16[128,2176]{1,0:T(8,128)(2,1)} %collective-permute-done.2), channel_id=1, source_target_pairs={{0,2},{1,3},{2,0},{3,1},{4,6},{5,7},{6,4},{7,5},{8,10},{9,11},{10,... | collective-permute-start | bytes 1671176 | tf_op jit(solution)/shard_map/ppermute | solution.py:434
  24.9 13.6 %collective-permute-start.5 = (bf16[128,2176]{1,0:T(8,128)(2,1)S(1)}, bf16[128,2176]{1,0:T(8,128)(2,1)S(1)}, u32[]{:S(2)}, u32[]{:S(2)}) collective-permute-start(bf16[128,2176]{1,0:T(8,128)(2,1)S(1)} %collective-permute-done.mine_ref.refs_3_), channel_id=1, source_target_pairs={{2,4},{3,5},{4,2},{5,3},{10,12},{11,13},{12,10},{13,11},{18,20},{1... | collective-permute-start | bytes 1671176 | tf_op jit(solution)/shard_map/ppermute | solution.py:434
  39.7 18.2 %collective-permute-start.6 = (bf16[128,2176]{1,0:T(8,128)(2,1)S(1)}, bf16[128,2176]{1,0:T(8,128)(2,1)S(1)}, u32[]{:S(2)}, u32[]{:S(2)}) collective-permute-start(bf16[128,2176]{1,0:T(8,128)(2,1)S(1)} %collective-permute-done.5), channel_id=1, source_target_pairs={{0,2},{1,3},{2,0},{3,1},{4,6},{5,7},{6,4},{7,5},{8,10},{9,11},{10,... | collective-permute-start | bytes 1671176 | tf_op jit(solution)/shard_map/ppermute | solution.py:434
  44.6 13.2 %collective-permute-start.8 = (bf16[128,2048]{1,0:T(8,128)(2,1)S(1)}, bf16[128,2048]{1,0:T(8,128)(2,1)S(1)}, u32[]{:S(2)}, u32[]{:S(2)}) collective-permute-start(bf16[128,2048]{1,0:T(8,128)(2,1)S(1)} %copy-done.9), channel_id=1, source_target_pairs={{2,4},{3,5},{4,2},{5,3},{10,12},{11,13},{12,10},{13,11},{18,20},{1... | collective-permute-start | bytes 1572872 | tf_op jit(solution)/shard_map/ppermute | solution.py:434
  58.0 9.4 %collective-permute-start.11 = (bf16[128,2176]{1,0:T(8,128)(2,1)S(1)}, bf16[128,2176]{1,0:T(8,128)(2,1)S(1)}, u32[]{:S(2)}, u32[]{:S(2)}) collective-permute-start(bf16[128,2176]{1,0:T(8,128)(2,1)S(1)} %broadcast_select_fusion.mine_ref.refs_3_), channel_id=1, source_target_pairs={{0,1},{1,0},{2,3},{3,2},{4,5},{5,4},{6,7},{7,6},{8,9},{9,8},{10,11... | collective-permute-start | bytes 1671176 | tf_op jit(solution)/shard_map/ppermute | solution.py:434
  58.0 13.7 %collective-permute-start.10 = (bf16[128,2048]{1,0:T(8,128)(2,1)S(1)}, bf16[128,2048]{1,0:T(8,128)(2,1)S(1)}, u32[]{:S(2)}, u32[]{:S(2)}) collective-permute-start(bf16[128,2048]{1,0:T(8,128)(2,1)S(1)} %copy-done.9), channel_id=1, source_target_pairs={{0,1},{1,0},{2,3},{3,2},{4,5},{5,4},{6,7},{7,6},{8,9},{9,8},{10,11... | collective-permute-start | bytes 1572872 | tf_op jit(solution)/shard_map/ppermute | solution.py:434
  58.5 16.7 %collective-permute-start.9 = (bf16[128,2048]{1,0:T(8,128)(2,1)S(1)}, bf16[128,2048]{1,0:T(8,128)(2,1)S(1)}, u32[]{:S(2)}, u32[]{:S(2)}) collective-permute-start(bf16[128,2048]{1,0:T(8,128)(2,1)S(1)} %copy-done.9), channel_id=1, source_target_pairs={{0,2},{1,3},{2,0},{3,1},{4,6},{5,7},{6,4},{7,5},{8,10},{9,11},{10,... | collective-permute-start | bytes 1572872 | tf_op jit(solution)/shard_map/ppermute | solution.py:434
  75.2 10.4 %collective-permute-start.15 = (bf16[128,2048]{1,0:T(8,128)(2,1)S(1)}, bf16[128,2048]{1,0:T(8,128)(2,1)S(1)}, u32[]{:S(2)}, u32[]{:S(2)}) collective-permute-start(bf16[128,2048]{1,0:T(8,128)(2,1)S(1)} %get-tuple-element.121), channel_id=1, source_target_pairs={{0,1},{1,0},{2,3},{3,2},{4,5},{5,4},{6,7},{7,6},{8,9},{9,8},{10,11... | collective-permute-start | bytes 1572872 | tf_op jit(solution)/shard_map/ppermute | solution.py:434
  75.7 13.8 %collective-permute-start.12 = (bf16[128,2048]{1,0:T(8,128)(2,1)S(1)}, bf16[128,2048]{1,0:T(8,128)(2,1)S(1)}, u32[]{:S(2)}, u32[]{:S(2)}) collective-permute-start(bf16[128,2048]{1,0:T(8,128)(2,1)S(1)} %collective-permute-done.8), channel_id=1, source_target_pairs={{0,2},{1,3},{2,0},{3,1},{4,6},{5,7},{6,4},{7,5},{8,10},{9,11},{10,... | collective-permute-start | bytes 1572872 | tf_op jit(solution)/shard_map/ppermute | solution.py:434
  81.1 8.5 %collective-permute-start.14 = (bf16[128,2048]{1,0:T(8,128)(2,1)S(1)}, bf16[128,2048]{1,0:T(8,128)(2,1)S(1)}, u32[]{:S(2)}, u32[]{:S(2)}) collective-permute-start(bf16[128,2048]{1,0:T(8,128)(2,1)S(1)} %collective-permute-done.9.refs_1_), channel_id=1, source_target_pairs={{2,4},{3,5},{4,2},{5,3},{10,12},{11,13},{12,10},{13,11},{18,20},{1... | collective-permute-start | bytes 1572872 | tf_op jit(solution)/shard_map/ppermute | solution.py:434
  89.7 11.4 %collective-permute-start.17 = (bf16[128,2048]{1,0:T(8,128)(2,1)S(1)}, bf16[128,2048]{1,0:T(8,128)(2,1)S(1)}, u32[]{:S(2)}, u32[]{:S(2)}) collective-permute-start(bf16[128,2048]{1,0:T(8,128)(2,1)S(1)} %get-tuple-element.141), channel_id=1, source_target_pairs={{0,1},{1,0},{2,3},{3,2},{4,5},{5,4},{6,7},{7,6},{8,9},{9,8},{10,11... | collective-permute-start | bytes 1572872 | tf_op jit(solution)/shard_map/ppermute | solution.py:434
  90.3 19.5 %collective-permute-start.16 = (bf16[128,2048]{1,0:T(8,128)(2,1)S(1)}, bf16[128,2048]{1,0:T(8,128)(2,1)S(1)}, u32[]{:S(2)}, u32[]{:S(2)}) collective-permute-start(bf16[128,2048]{1,0:T(8,128)(2,1)S(1)} %broadcast_select_fusion.4), channel_id=1, source_target_pairs={{0,2},{1,3},{2,0},{3,1},{4,6},{5,7},{6,4},{7,5},{8,10},{9,11},{10,... | collective-permute-start | bytes 1572872 | tf_op jit(solution)/shard_map/ppermute | solution.py:434
  109.9 41.0 %collective-permute-start.19 = (bf16[128,2048]{1,0:T(8,128)(2,1)S(1)}, bf16[128,2048]{1,0:T(8,128)(2,1)S(1)}, u32[]{:S(2)}, u32[]{:S(2)}) collective-permute-start(bf16[128,2048]{1,0:T(8,128)(2,1)S(1)} %get-tuple-element.152), channel_id=1, source_target_pairs={{0,1},{1,0},{2,3},{3,2},{4,5},{5,4},{6,7},{7,6},{8,9},{9,8},{10,11... | collective-permute-start | bytes 1572872 | tf_op jit(solution)/shard_map/ppermute | solution.py:434
  110.4 16.8 %collective-permute-start.20 = (bf16[128,2048]{1,0:T(8,128)(2,1)S(1)}, bf16[128,2048]{1,0:T(8,128)(2,1)S(1)}, u32[]{:S(2)}, u32[]{:S(2)}) collective-permute-start(bf16[128,2048]{1,0:T(8,128)(2,1)S(1)} %get-tuple-element.154), channel_id=1, source_target_pairs={{0,1},{1,0},{2,3},{3,2},{4,5},{5,4},{6,7},{7,6},{8,9},{9,8},{10,11... | collective-permute-start | bytes 1572872 | tf_op jit(solution)/shard_map/ppermute | solution.py:434
  110.4 14.3 %collective-permute-start.24 = (bf16[128,2048]{1,0:T(8,128)(2,1)S(1)}, bf16[128,2048]{1,0:T(8,128)(2,1)S(1)}, u32[]{:S(2)}, u32[]{:S(2)}) collective-permute-start(bf16[128,2048]{1,0:T(8,128)(2,1)S(1)} %add_convert_fusion.6), channel_id=1, source_target_pairs={{0,2},{1,3},{2,0},{3,1},{4,6},{5,7},{6,4},{7,5},{8,10},{9,11},{10,... | collective-permute-start | bytes 1572872 | tf_op jit(solution)/shard_map/ppermute | solution.py:434
  112.3 15.5 %collective-permute-start.22 = (bf16[128,2048]{1,0:T(8,128)(2,1)S(1)}, bf16[128,2048]{1,0:T(8,128)(2,1)S(1)}, u32[]{:S(2)}, u32[]{:S(2)}) collective-permute-start(bf16[128,2048]{1,0:T(8,128)(2,1)S(1)} %add_convert_fusion.3), channel_id=1, source_target_pairs={{2,4},{3,5},{4,2},{5,3},{10,12},{11,13},{12,10},{13,11},{18,20},{1... | collective-permute-start | bytes 1572872 | tf_op jit(solution)/shard_map/ppermute | solution.py:434
  116.6 16.8 %collective-permute-start.26 = (bf16[1408,128]{1,0:T(8,128)(2,1)S(1)}, bf16[1408,128]{1,0:T(8,128)(2,1)S(1)}, u32[]{:S(2)}, u32[]{:S(2)}) collective-permute-start(bf16[1408,128]{1,0:T(8,128)(2,1)S(1)} %get-tuple-element.165.refs_0_), channel_id=1, source_target_pairs={{0,8},{8,0},{16,24},{24,16},{1,9},{9,1},{17,25},{25,17},{2,10},{10... | collective-permute-start | bytes 1081352 | tf_op jit(solution)/shard_map/ppermute | solution.py:453
  124.7 10.1 %collective-permute-start.27 = (bf16[1408,128]{1,0:T(8,128)(2,1)S(1)}, bf16[1408,128]{1,0:T(8,128)(2,1)}, u32[]{:S(2)}, u32[]{:S(2)}) collective-permute-start(bf16[1408,128]{1,0:T(8,128)(2,1)S(1)} %get-tuple-element.166.refs_1_), channel_id=1, source_target_pairs={{0,16},{8,24},{16,0},{24,8},{1,17},{9,25},{17,1},{25,9},{2,18},{10... | collective-permute-start | bytes 1081352 | tf_op jit(solution)/shard_map/ppermute | solution.py:453
  127.2 23.7 %collective-permute-start.25 = (bf16[128,2048]{1,0:T(8,128)(2,1)}, bf16[128,2048]{1,0:T(8,128)(2,1)S(1)}, u32[]{:S(2)}, u32[]{:S(2)}) collective-permute-start(bf16[128,2048]{1,0:T(8,128)(2,1)} %add_convert_fusion.1), channel_id=1, source_target_pairs={{2,4},{3,5},{4,2},{5,3},{10,12},{11,13},{12,10},{13,11},{18,20},{1... | collective-permute-start | bytes 1572872 | tf_op jit(solution)/shard_map/ppermute | solution.py:434
  128.9 22.0 %collective-permute-start.23 = (bf16[128,2048]{1,0:T(8,128)(2,1)}, bf16[128,2048]{1,0:T(8,128)(2,1)}, u32[]{:S(2)}, u32[]{:S(2)}) collective-permute-start(bf16[128,2048]{1,0:T(8,128)(2,1)} %add_convert_fusion.2), channel_id=1, source_target_pairs={{0,2},{1,3},{2,0},{3,1},{4,6},{5,7},{6,4},{7,5},{8,10},{9,11},{10,... | collective-permute-start | bytes 1572872 | tf_op jit(solution)/shard_map/ppermute | solution.py:434
  137.1 9.3 %collective-permute-start.28 = (bf16[1408,128]{1,0:T(8,128)(2,1)}, bf16[1408,128]{1,0:T(8,128)(2,1)S(1)}, u32[]{:S(2)}, u32[]{:S(2)}) collective-permute-start(bf16[1408,128]{1,0:T(8,128)(2,1)} %get-tuple-element.167.one_x), channel_id=1, source_target_pairs={{0,16},{8,24},{16,0},{24,8},{1,17},{9,25},{17,1},{25,9},{2,18},{10... | collective-permute-start | bytes 1081352 | tf_op jit(solution)/shard_map/ppermute | solution.py:453
  138.6 9.0 %collective-permute-start.29 = (bf16[1408,128]{1,0:T(8,128)(2,1)}, bf16[1408,128]{1,0:T(8,128)(2,1)S(1)}, u32[]{:S(2)}, u32[]{:S(2)}) collective-permute-start(bf16[1408,128]{1,0:T(8,128)(2,1)} %get-tuple-element.168.one_y), channel_id=1, source_target_pairs={{0,8},{8,0},{16,24},{24,16},{1,9},{9,1},{17,25},{25,17},{2,10},{10... | collective-permute-start | bytes 1081352 | tf_op jit(solution)/shard_map/ppermute | solution.py:453
  (21 other events, 146.5 us)

commit v10 on v9

--- a/solution.py
+++ b/solution.py
@@ -221,10 +221,10 @@
     return jnp.sum(chosen, axis=1, keepdims=True)
 
 
-def tagged_kernel(capacity, table_ref, expert_ref, choice_ref, weight_ref, tokens_ref, out_ref):
+def tagged_kernel(capacity, table_ref, expert_ref, choice_ref, weight_ref, tokens_ref, *out_refs):
     slot_total = table_ref.shape[0]
     tok_rows, features = tokens_ref.shape
-    out_ref[:, :features] = tokens_ref[...]
+    rows = tok_rows // len(out_refs)
     experts, weights = expert_ref[...], weight_ref[...]
     holds = [experts == table_ref[s] for s in range(slot_total)]
     counts = [hold.astype(jnp.float32) for hold in holds]
@@ -245,21 +245,27 @@
         jnp.where(earlier, 1.0, 0.0).astype(jnp.bfloat16),
     )
     table = jnp.where(rank < capacity, jnp.concatenate(route_weight), 0.0)
-    out_ref[:, features:] = split_weights(table)
+    extra = split_weights(table)
+    for at, out_ref in enumerate(out_refs):
+        here = slice(at * rows, (at + 1) * rows)
+        out_ref[:, :features] = tokens_ref[here]
+        out_ref[:, features:] = extra[here]
 
 
 VMEM = pl.BlockSpec(memory_space=pltpu.VMEM)
 SMEM = pl.BlockSpec(memory_space=pltpu.SMEM)
 EXTRA = 128
+PARTS = 2
 
 
 def tagged_tokens(tokens, routing, weights, choice, table, capacity):
     tok_rows, features = tokens.shape
+    part = jax.ShapeDtypeStruct((tok_rows // PARTS, features + EXTRA), tokens.dtype)
     return pl.pallas_call(
         functools.partial(tagged_kernel, capacity),
-        out_shape=jax.ShapeDtypeStruct((tok_rows, features + EXTRA), tokens.dtype),
+        out_shape=(part,) * PARTS,
         in_specs=[SMEM, VMEM, VMEM, VMEM, VMEM],
-        out_specs=VMEM,
+        out_specs=(VMEM,) * PARTS,
     )(table, routing.T, choice.T, weights.T, tokens)
 
 
@@ -272,20 +278,17 @@
         in_specs=[SMEM] + [VMEM] * (len(operands) - 1),
         out_specs=(VMEM,) * len(outs),
         scratch_shapes=[pltpu.VMEM(*shape) for shape in scratch],
-        compiler_params=pltpu.CompilerParams(vmem_limit_bytes=16 * 2**20),
+        compiler_params=pltpu.CompilerParams(vmem_limit_bytes=24 * 2**20),
         cost_estimate=pl.CostEstimate(flops=2 * macs, bytes_accessed=moved, transcendentals=0),
     )(*operands)
 
 
 def forward_kernel(
-    chunk, slot_ref, mine_ref, other_ref, adapt_a_ref, gate_up_ref, adapt_b_ref, down_ref,
-    low_ref, active_ref, slope_ref, part_mine_ref, part_other_ref, rows_ref, total_ref,
+    chunk, slot_ref, rows_ref, adapt_a_ref, gate_up_ref, adapt_b_ref, down_ref,
+    low_ref, active_ref, slope_ref, part_ref, total_ref,
 ):
-    half, features = part_mine_ref.shape
-    hidden_width = down_ref.shape[0]
-    rows_ref[:half] = mine_ref[:, :features]
-    rows_ref[half:] = other_ref[:, :features]
-    rows = rows_ref[...]
+    hidden_width, features = down_ref.shape
+    rows = rows_ref[:, :features]
     low = dot(rows, adapt_a_ref[...]).astype(jnp.bfloat16)
     low_ref[...] = low
     low_gate, low_up = halves(low)
@@ -305,39 +308,37 @@
         else:
             total_ref[...] += more
     out = total_ref[...].astype(jnp.bfloat16).astype(jnp.float32)
-    for block_ref, part_ref, out in (
-        (mine_ref, part_mine_ref, out[:half]),
-        (other_ref, part_other_ref, out[half:]),
-    ):
-        w = joined_weight(block_ref[:, features:], slot_ref[0], slot_ref[1])
-        part_ref[...] = (w * out).astype(jnp.bfloat16)
-
-
-def forward_stage(slot, mine, other, gate_up, down, adapt_a, adapt_b, chunk=256):
+    w = joined_weight(rows_ref[:, features:], slot_ref[0], slot_ref[1])
+    part_ref[...] = (w * out).astype(jnp.bfloat16)
+
+
+def forward_part(slot, rows, gate_up, down, adapt_a, adapt_b, chunk=256):
     hidden_width, features = down.shape
-    half, both, ranks = mine.shape[0], 2 * mine.shape[0], adapt_a.shape[1]
+    count, ranks = rows.shape[0], adapt_a.shape[1]
     bf16, f32 = jnp.bfloat16, jnp.float32
-    saved = ((both, hidden_width), f32)
-    part = ((half, features), bf16)
+    saved = ((count, hidden_width), f32)
     return stage_call(
         functools.partial(forward_kernel, chunk),
-        (((both, ranks), bf16), saved, saved, part, part),
-        [((both, features), bf16), ((both, features), f32)],
-        both * (gate_up.size + down.size + adapt_a.size),
-        (slot, mine, other, adapt_a, gate_up, adapt_b, down),
-    )
-
-
-def backward_kernel(chunk, adds, cut, *refs):
-    slot_ref, cot_mine, cot_other, mine_ref, other_ref, *refs = refs
-    low_ref, active_ref, slope_ref, adapt_b_ref, down_ref, *refs = refs
-    grads, (out_a_ref, out_b_ref, scaled_ref, rows_ref) = refs[: 2 * adds], refs[2 * adds :]
-    half, features = cot_mine.shape
-    for at, (cot_ref, block_ref) in enumerate(((cot_mine, mine_ref), (cot_other, other_ref))):
-        here = slice(at * half, (at + 1) * half)
-        w = joined_weight(block_ref[:, features:], slot_ref[0], slot_ref[1])
-        scaled_ref[here] = (w * cot_ref[...].astype(jnp.float32)).astype(jnp.bfloat16)
-        rows_ref[here] = block_ref[:, :features]
+        (((count, ranks), bf16), saved, saved, ((count, features), bf16)),
+        [((count, features), f32)],
+        count * (gate_up.size + down.size + adapt_a.size),
+        (slot, rows, adapt_a, gate_up, adapt_b, down),
+    )
+
+
+def backward_kernel(chunk, adds, cut, part, *refs):
+    slot_ref, refs = refs[0], refs[1:]
+    n_blocks = slot_ref.shape[0] - 2
+    cots, refs = refs[:n_blocks], refs[n_blocks:]
+    rows_ref, low_ref, active_ref, slope_ref, adapt_b_ref, down_ref, *refs = refs
+    grads, (out_a_ref, out_b_ref, scaled_ref) = refs[: 2 * adds], refs[2 * adds :]
+    features = cots[0].shape[1]
+    length = rows_ref.shape[0] // n_blocks
+    for at, cot_ref in enumerate(cots):
+        here = pl.ds(pl.multiple_of(slot_ref[2 + at] * length, length), length)
+        w = joined_weight(rows_ref[here, features:], slot_ref[0], slot_ref[1])
+        cot = cot_ref[part * length : (part + 1) * length].astype(jnp.float32)
+        scaled_ref[here] = (w * cot).astype(jnp.bfloat16)
     scaled = scaled_ref[...]
     low_gate, low_up = halves(low_ref[...])
     low_back = 0.0
@@ -359,7 +360,7 @@
         gate_back, up_back = dot(gate_grad, adapt_b, 1, 1), dot(up_grad, adapt_b, 1, 1)
         low_back = low_back + jnp.where(first_half(gate_back.shape), gate_back, up_back)
     low_grad = (ADAPTER_SCALE * low_back).astype(jnp.bfloat16)
-    sum_a = dot(rows_ref[...], low_grad, 0, 0)
+    sum_a = dot(rows_ref[:, :features], low_grad, 0, 0)
     sum_a = sum_a + grads[0][...] if adds else sum_a
     if cut is None:
         out_a_ref[...] = sum_a
@@ -368,19 +369,19 @@
         out_b_ref[: features - cut] = sum_a[cut:].astype(jnp.bfloat16)
 
 
-def backward_stage(slot, cots, blocks, saved, down, adapt_b, grads=(), cut=None, chunk=256):
+def backward_part(slot, part, cots, rows, saved, down, adapt_b, grads=(), cut=None, chunk=256):
     hidden_width, features = down.shape
-    both, ranks = saved[0].shape
+    count, ranks = saved[0].shape
     bf16, f32 = jnp.bfloat16, jnp.float32
     outs = (((features, ranks), f32), ((ranks, hidden_width), f32))
     if cut is not None:
         outs = (((cut, ranks), bf16), ((features - cut + hidden_width, ranks), bf16))
     return stage_call(
-        functools.partial(backward_kernel, chunk, len(grads) // 2, cut),
+        functools.partial(backward_kernel, chunk, len(grads) // 2, cut, part),
         outs,
-        [((both, features), bf16), ((both, features), bf16)],
-        both * (down.size + features * ranks + 4 * adapt_b.size),
-        (slot, *cots, *blocks, *saved, adapt_b, down, *grads),
+        [((count, features), bf16)],
+        count * (down.size + features * ranks + 4 * adapt_b.size),
+        (slot, *cots, rows, *saved, adapt_b, down, *grads),
     )
 
 
@@ -481,92 +482,54 @@
     adapt_a = adapter_down_maps[0]
     adapt_b = adapter_up_maps[0].reshape(adapt_a.shape[1], -1)
 
-    slot = jnp.stack([me, jnp.int32(slot_total)])
-
-    def forward(mine, twin):
-        *saved, part, away = forward_stage(slot, mine, twin, gate_up, down, adapt_a, adapt_b)
-        return saved, part, away
-
-    def backward(cots, rows, saved, grads=(), cut=None):
-        return backward_stage(slot, cots, rows, saved, down, adapt_b, grads, cut)
-
     def pick(inside, outside):
         return jnp.where(inner, inside, outside)
 
-    def after(array, earlier):
-        return fence(array, earlier)[0]
-
-    tokens = tagged_tokens(
+    whose = [me, me ^ 2, pick(me ^ 6, me ^ 4), pick(me ^ 4, me ^ 6)]
+    whose = [device ^ core for device in whose for core in (0, 1)]
+    slot = jnp.stack([me, jnp.int32(slot_total), *whose])
+
+    def forward(rows):
+        return forward_part(slot[:2], rows, gate_up, down, adapt_a, adapt_b)
+
+    def backward(part, *operands, **options):
+        return backward_part(slot, part, cots, *operands, down, adapt_b, **options)
+
+    parts = tagged_tokens(
         tokens, routing, router_route_weights, route_replica_choice, device_expert_table, capacity
     )
-    tok_swap = send(tokens, ALL_SWAP)
-    twin = sibling(tokens)
-    rows0 = (tokens, twin)
-    tok_mid = send(after(tokens, twin), MID_SWAP)
-    tok_swap, tok_mid, rows0, cotangent = fence(tok_swap, tok_mid, rows0, cotangent)
-
-    tok_out2 = send(tok_mid, ALL_SWAP)
-    twin = sibling(tok_swap)
-    rows1 = (tok_swap, twin)
-    tok_mid2 = send(after(tok_swap, twin), MID_SWAP)
-    saved0, part0, away0 = forward(*rows0)
-    tok_mid, tok_out2, tok_mid2, rows1, part0, away0, cotangent = fence(
-        tok_mid, tok_out2, tok_mid2, rows1, part0, away0, cotangent
-    )
-
-    tok_out3 = send(tok_mid2, ALL_SWAP)
-    tok_second = pick(tok_mid, tok_out2)
-    twin = sibling(tok_second)
-    rows2 = (tok_second, twin)
-    cot_mid = send(after(cotangent, twin), MID_SWAP)
-    saved1, part1, away1 = forward(*rows1)
-    tok_mid2, tok_out3, cot_mid, rows2, part1, away1, cotangent = fence(
-        tok_mid2, tok_out3, cot_mid, rows2, part1, away1, cotangent
-    )
+    rows = [lax.all_gather(part, "expert", tiled=True) for part in parts]
 
     cot_swap = send(cotangent, ALL_SWAP)
-    tok_third = pick(tok_mid2, tok_out3)
-    rows3 = (tok_third, sibling(tok_third))
-    cots0 = (cotangent, sibling(cotangent))
-    saved2, part2, away2 = forward(*rows2)
-    saved3, part3, away3 = forward(*rows3)
-    cot_swap, cot_mid, cots0, part2, away2, part3, away3 = fence(
-        cot_swap, cot_mid, cots0, part2, away2, part3, away3
-    )
+    cot_mid = send(cotangent, MID_SWAP)
+    twin = sibling(cotangent)
+    cot_swap, cot_mid, twin = fence(cot_swap, cot_mid, twin)
+    cots = [cotangent, twin]
 
     cot_out2 = send(cot_mid, ALL_SWAP)
-    twin = sibling(cot_swap)
-    cots1 = (cot_swap, twin)
-    cot_mid2 = send(after(cot_swap, twin), MID_SWAP)
-    part3 = add_rounded(part3, sibling(away3))
-    grads = backward(cots0, rows0, saved0)
-    grads = backward(cots1, rows1, saved1, grads)
-    cot_mid, cot_out2, cot_mid2, part2, away2, part3, grads = fence(
-        cot_mid, cot_out2, cot_mid2, part2, away2, part3, grads
-    )
-
-    swap6 = send(pick(cot_mid2, part3), ALL_SWAP)
+    cot_mid2 = send(cot_swap, MID_SWAP)
+    cots += [cot_swap, sibling(cot_swap)]
+    rows[0], twin = fence(rows[0], twin)
+    *saved0, out0 = forward(rows[0])
+    mixed0 = lax.psum_scatter(out0, "expert", scatter_dimension=0, tiled=True)
+
+    cot_mid, cot_out2, cot_mid2, out0 = fence(cot_mid, cot_out2, cot_mid2, out0)
+    cot_out3 = send(cot_mid2, ALL_SWAP)
     cot_second = pick(cot_mid, cot_out2)
-    cots2 = (cot_second, sibling(cot_second))
-    grads = backward(cots2, rows2, saved2, grads)
-    part2 = add_rounded(part2, sibling(away2))
-    swap6, cot_mid2, part0, away0, part1, away1, part2, part3, grads = fence(
-        swap6, cot_mid2, part0, away0, part1, away1, part2, part3, grads
-    )
-
-    second_in = send(part2, ALL_SWAP)
-    cot_third = pick(cot_mid2, swap6)
-    twin = sibling(cot_third)
-    third_mid = send(after(add_rounded(part3, swap6), twin), MID_SWAP)
+    cots += [cot_second, sibling(cot_second)]
+    rows[1], cot_second = fence(rows[1], cot_second)
+    *saved1, out1 = forward(rows[1])
+    cot_mid2, cot_out3, out1 = fence(cot_mid2, cot_out3, out1)
+    mixed1 = lax.psum_scatter(out1, "expert", scatter_dimension=0, tiled=True)
+
+    cot_third = pick(cot_mid2, cot_out3)
+    cots += [cot_third, sibling(cot_third)]
     features, hidden_width = adapt_a.shape[0], adapt_b.shape[1]
     cut = (features + hidden_width) // 2
-    grads = backward((cot_third, twin), rows3, saved3, grads, cut)
+    grads = backward(0, rows[0], saved0)
+    grads = backward(1, rows[1], saved1, grads=grads, cut=cut)
     grad_a, grad_b = group_sum(grads, features, hidden_width)
-    part1 = add_rounded(part1, sibling(away1))
-    part0 = add_rounded(part0, sibling(away0))
-    first_swap = send(add_rounded(part1, third_mid), ALL_SWAP)
-    second_mid = send(add_rounded(part2, second_in), MID_SWAP)
-    mixed = add_rounded(part0, first_swap, second_mid)
+    mixed = jnp.concatenate([mixed0, mixed1])
     return mixed, grad_a[None], grad_b.reshape(adapter_up_maps.shape)
 
 

time: 154 us -> 180 us (1.17)
  starting transfers between devices: 47.1 us -> 17.6 us
  local copies, waits for them, and re-layouts: 8.49 us -> 33.5 us
  waiting for transfers between devices: 52 us -> 66.9 us
  between operations: 0.96 us -> 13.9 us
  Pallas kernels: 38.6 us -> 41.3 us
    ppermute x26 -> x9, starting transfers between devices: 41 us -> 12.2 us  [send(): return lax.ppermute(array, 'expert', pairs)]
    unnamed x30 -> x74, local copies, waits for them, and re-layouts: 8.49 us -> 33.4 us
    ppermute x4, waiting for transfers between devices: 8.89 us -> 17 us  [dp_swap(): return lax.ppermute(array, 'dp', [(d, d ^ bit) for d in range(4)])]
    all_gather x0 -> x2, waiting for transfers between devices: none -> 5.71 us  [dense_body(): rows = [lax.all_gather(part, 'expert', tiled=True) for part in parts]]
    convert_element_type x6 -> x0, other arithmetic: 4.51 us -> none  [add_rounded(): return total.astype(jnp.bfloat16)]
    pallas_call x8 -> x4, Pallas kernels: 31.7 us -> 34.4 us  [stage_call(): pl.pallas_call(kernel, out_shape=out_shape, in_specs=[SMEM] + [VMEM] * (l...]
    select_n x5 -> x2, other arithmetic: 1.38 us -> 3.82 us  [pick(): return jnp.where(inner, inside, outside)]
    concatenate x0 -> x1, other arithmetic: none -> 1.87 us  [dense_body(): mixed = jnp.concatenate([mixed0, mixed1])]
  transfers between devices with their start and end apart: 30 -> 17, of which waited for: 10 -> 10; matrix products, arithmetic and copies ran while one was open for 2% -> 2% of each run, Pallas kernels for 24% -> 22%
where the time goes in v10:
time: 180 us; the launch traced here: 179 us
  waiting for transfers between devices  66.9 us (37%)
  Pallas kernels  41.3 us (23%)
  local copies, waits for them, and re-layouts  33.5 us (19%)
  starting transfers between devices  17.6 us (10%)
  between operations  13.9 us (8%)
  other arithmetic  5.76 us (3%)
    ppermute x9, waiting for transfers between devices, send(): return lax.ppermute(array, 'expert', pairs)  43.5 us
    pallas_call x4, Pallas kernels, stage_call(): pl.pallas_call(kernel, out_shape=out_shape, in_specs=[SMEM] + [VMEM] * (l...  34.4 us
    unnamed x74, local copies, waits for them, and re-layouts  33.4 us
    ppermute x4, waiting for transfers between devices, dp_swap(): return lax.ppermute(array, 'dp', [(d, d ^ bit) for d in range(4)])  17 us
    ppermute x9, starting transfers between devices, send(): return lax.ppermute(array, 'expert', pairs)  12.2 us
    all_gather x2, waiting for transfers between devices, dense_body(): rows = [lax.all_gather(part, 'expert', tiled=True) for part in parts]  5.71 us
    ppermute x4, starting transfers between devices, dp_swap(): return lax.ppermute(array, 'dp', [(d, d ^ bit) for d in range(4)])  5.3 us
    select_n x2, other arithmetic, pick(): return jnp.where(inner, inside, outside)  3.82 us
  transfers between devices with their start and end apart: 17, of which 10 were waited for; matrix products, arithmetic and copies ran while one was open for 2% of the time, Pallas kernels for 22%

profile of v10, /device:TPU:0, one launch (start us, length us, event | category | flops | bytes accessed | tf_op | source)
XLA Modules:
  0.0 179.1 jit_solution(1420132285911216847)
XLA Ops:
  7.2 2.1 %shard_map.121 = (bf16[64,2176]{1,0:T(8,128)(2,1)}, bf16[64,2176]{1,0:T(8,128)(2,1)}) custom-call(s32[8]{0:T(128)} %table_ref.1, s32[8,128]{1,0:T(8,128)} %bitcast.29, s32[8,128]{1,0:T(8,128)} %bitcast.30, f32[8,128]{1,0:T(8,128)} %bitcast.31, bf16[128,2048]{1,0:T(8,128)(2,1)} %tokens_ref.1), custom_call_target="tpu_custom_call" | custom-call | tf_op jit(solution)/shard_map/pallas_call | solution.py:264
  11.4 5.5 %collective-permute-start = (bf16[128,2048]{1,0:T(8,128)(2,1)}, bf16[128,2048]{1,0:T(8,128)(2,1)S(1)}, u32[]{:S(2)}, u32[]{:S(2)}) collective-permute-start(bf16[128,2048]{1,0:T(8,128)(2,1)} %refs_1_.3), channel_id=1, source_target_pairs={{0,2},{1,3},{2,0},{3,1},{4,6},{5,7},{6,4},{7,5},{8,10},{9,11},{10,... | collective-permute-start | bytes 1572872 | tf_op jit(solution)/shard_map/ppermute | solution.py:435
  17.7 25.4 %collective-permute-done.refs_3_ = bf16[128,2048]{1,0:T(8,128)(2,1)S(1)} collective-permute-done((bf16[128,2048]{1,0:T(8,128)(2,1)}, bf16[128,2048]{1,0:T(8,128)(2,1)S(1)}, u32[]{:S(2)}, u32[]{:S(2)}) %collective-permute-start) | collective-permute-done | bytes 524320 | tf_op jit(solution)/shard_map/ppermute | solution.py:435
  43.1 5.7 %all-gather.3.cloned.1.call-done.rows_ref.refs_9_ = bf16[512,2176]{1,0:T(8,128)(2,1)} async-done(((bf16[64,2176]{1,0:T(8,128)(2,1)}), bf16[512,2176]{1,0:T(8,128)(2,1)}) %all-gather.3.cloned.1.call-update) | async-done | bytes 2228240 | tf_op jit(solution)/shard_map/all_gather | solution.py:501
  48.9 1.9 %copy-done = bf16[1,768,2048]{2,1,0:T(8,128)(2,1)S(1)} copy-done((bf16[1,768,2048]{2,1,0:T(8,128)(2,1)S(1)}, bf16[1,768,2048]{2,1,0:T(8,128)(2,1)}, u32[]{:S(2)}) %copy-start) | copy-done | bytes 3145752
  50.7 1.6 copy-done.3
  53.3 2.8 %copy-done.28 = bf16[1,2048,1536]{2,1,0:T(8,128)(2,1)S(1)} copy-done((bf16[1,2048,1536]{2,1,0:T(8,128)(2,1)S(1)}, bf16[1,2048,1536]{2,1,0:T(8,128)(2,1)}, u32[]{:S(2)}) %copy-start.28) | copy-done | bytes 6291480
  57.1 9.6 %shard_map.122 = (bf16[512,128]{1,0:T(8,128)(2,1)S(1)}, f32[512,768]{1,0:T(8,128)S(1)}, f32[512,768]{1,0:T(8,128)S(1)}, bf16[512,2048]{1,0:T(8,128)(2,1)S(1)}) custom-call(s32[2]{0:T(128)S(1)} %pad_add_fusion.slot_ref, bf16[512,2176]{1,0:T(8,128)(2,1)S(1)} %copy-done.3, bf16[2048,128]{1,0:T(8,128)(2,1)S(1)} %bitcast.27, bf16[2048,1536]{1,0:T(8,128)(2,1)S(1)} %bitcast.25, ...), custom_call_target="tpu_custom_call" | custom-call | flops 5100273664 | bytes 17760264 | tf_op jit(solution)/shard_map/pallas_call | solution.py:275
  70.5 1.8 collective-permute-start.3
  73.7 15.8 %collective-permute-done.3 = bf16[128,2048]{1,0:T(8,128)(2,1)} collective-permute-done((bf16[128,2048]{1,0:T(8,128)(2,1)}, bf16[128,2048]{1,0:T(8,128)(2,1)}, u32[]{:S(2)}, u32[]{:S(2)}) %collective-permute-start.3) | collective-permute-done | bytes 524320 | tf_op jit(solution)/shard_map/ppermute | solution.py:435
  89.5 1.6 collective-permute-start.5
  91.2 1.9 %broadcast_select_fusion.1.refs_5_ = bf16[128,2048]{1,0:T(8,128)(2,1)} fusion(bf16[128,2048]{1,0:T(8,128)(2,1)} %copy-done.32, bf16[128,2048]{1,0:T(8,128)(2,1)} %collective-permute-done.3, pred[]{:T(512)S(6)} %or.3), kind=kLoop, calls=%fused_computation.2 | loop fusion | flops 262144 | bytes 1572865 | tf_op jit(solution)/shard_map/jit(_where)/select_n | solution.py:486
  93.1 1.6 copy-done.5
  94.7 2.8 %copy-done.29 = bf16[1,2048,1536]{2,1,0:T(8,128)(2,1)S(1)} copy-done((bf16[1,2048,1536]{2,1,0:T(8,128)(2,1)S(1)}, bf16[1,2048,1536]{2,1,0:T(8,128)(2,1)}, u32[]{:S(2)}) %copy-start.29) | copy-done | bytes 6291480
  98.6 9.6 %shard_map.123 = (bf16[512,128]{1,0:T(8,128)(2,1)S(1)}, f32[512,768]{1,0:T(8,128)S(1)}, f32[512,768]{1,0:T(8,128)S(1)}, bf16[512,2048]{1,0:T(8,128)(2,1)S(1)}) custom-call(s32[2]{0:T(128)S(1)} %pad_add_fusion.slot_ref, bf16[512,2176]{1,0:T(8,128)(2,1)S(1)} %copy-done.5, bf16[2048,128]{1,0:T(8,128)(2,1)S(1)} %bitcast.28, bf16[2048,1536]{1,0:T(8,128)(2,1)S(1)} %bitcast.26, ...), custom_call_target="tpu_custom_call" | custom-call | flops 5100273664 | bytes 17760264 | tf_op jit(solution)/shard_map/pallas_call | solution.py:275
  113.3 1.9 %broadcast_select_fusion.refs_7_ = bf16[128,2048]{1,0:T(8,128)(2,1)} fusion(bf16[128,2048]{1,0:T(8,128)(2,1)} %collective-permute-done.4, bf16[128,2048]{1,0:T(8,128)(2,1)} %collective-permute-done.5, pred[]{:T(512)S(6)} %or.3), kind=kLoop, calls=%fused_computation.1 | loop fusion | flops 262144 | bytes 1572865 | tf_op jit(solution)/shard_map/jit(_where)/select_n | solution.py:486
  118.5 1.6 copy-done.4
  126.1 7.6 %shard_map.124 = (f32[2048,128]{1,0:T(8,128)S(1)}, f32[128,768]{1,0:T(8,128)S(1)}) custom-call(s32[10]{0:T(128)S(1)} %stack.39.refs_0_, bf16[128,2048]{1,0:T(8,128)(2,1)S(1)} %copy-done.7, bf16[128,2048]{1,0:T(8,128)(2,1)S(1)} %copy-done.9, bf16[128,2048]{1,0:T(8,128)(2,1)S(1)} %copy-done.11, bf16[128,2048]{1,0:T(8,128)(2,1)} %collective-permute-done.6.refs_4_, ...), custom_call_target="tpu_custom_call" | custom-call | flops 2281701376 | bytes 14483496 | tf_op jit(solution)/shard_map/pallas_call | solution.py:275
  133.8 7.6 %shard_map.125 = (bf16[1408,128]{1,0:T(8,128)(2,1)S(1)}, bf16[1408,128]{1,0:T(8,128)(2,1)S(1)}) custom-call(s32[10]{0:T(128)S(1)} %stack.39.refs_0_, bf16[128,2048]{1,0:T(8,128)(2,1)S(1)} %copy-done.7, bf16[128,2048]{1,0:T(8,128)(2,1)S(1)} %copy-done.9, bf16[128,2048]{1,0:T(8,128)(2,1)S(1)} %copy-done.11, bf16[128,2048]{1,0:T(8,128)(2,1)} %collective-permute-done.6.refs_4_, ...), custom_call_target="tpu_custom_call" | custom-call | flops 2281701376 | bytes 15204392 | tf_op jit(solution)/shard_map/pallas_call | solution.py:275
  144.9 7.6 %collective-permute-done.9.refs_2_ = bf16[1408,128]{1,0:T(8,128)(2,1)S(1)} collective-permute-done((bf16[1408,128]{1,0:T(8,128)(2,1)S(1)}, bf16[1408,128]{1,0:T(8,128)(2,1)S(1)}, u32[]{:S(2)}, u32[]{:S(2)}) %collective-permute-start.9) | collective-permute-done | bytes 360480 | tf_op jit(solution)/shard_map/ppermute | solution.py:454
  154.4 2.3 %shard_map.126 = (bf16[1408,128]{1,0:T(8,128)(2,1)}, bf16[1408,128]{1,0:T(8,128)(2,1)}) custom-call(bf16[1408,128]{1,0:T(8,128)(2,1)} %copy-done.24, bf16[1408,128]{1,0:T(8,128)(2,1)} %copy-done.25, bf16[1408,128]{1,0:T(8,128)(2,1)} %copy-done.33, bf16[1408,128]{1,0:T(8,128)(2,1)} %copy-done.35), custom_call_target="tpu_custom_call" | custom-call | tf_op jit(solution)/shard_map/pallas_call | solution.py:395
  159.1 7.1 %collective-permute-done.11.other_x = bf16[1408,128]{1,0:T(8,128)(2,1)S(1)} collective-permute-done((bf16[1408,128]{1,0:T(8,128)(2,1)}, bf16[1408,128]{1,0:T(8,128)(2,1)S(1)}, u32[]{:S(2)}, u32[]{:S(2)}) %collective-permute-start.11) | collective-permute-done | bytes 360480 | tf_op jit(solution)/shard_map/ppermute | solution.py:454
  168.2 2.5 %shard_map.127 = (f32[2048,128]{1,0:T(8,128)}, f32[128,768]{1,0:T(8,128)}) custom-call(bf16[1408,128]{1,0:T(8,128)(2,1)} %get-tuple-element.57.one_x, bf16[1408,128]{1,0:T(8,128)(2,1)} %get-tuple-element.58.one_y, bf16[1408,128]{1,0:T(8,128)(2,1)} %copy-done.34, bf16[1408,128]{1,0:T(8,128)(2,1)} %copy-done.36), custom_call_target="tpu_custom_call" | custom-call | tf_op jit(solution)/shard_map/pallas_call | solution.py:416
  170.7 1.9 %pad_maximum_fusion = bf16[128,2048]{1,0:T(8,128)(2,1)} fusion(bf16[64,2048]{1,0:T(8,128)(2,1)} %reduce-scatter.5.cloned.1.call-done, bf16[64,2048]{1,0:T(8,128)(2,1)} %reduce-scatter.3.cloned.1.call-done), kind=kLoop, calls=%fused_computation | loop fusion | flops 1048576 | bytes 1048576 | tf_op jit(solution)/shard_map/concatenate | solution.py:532
  (100 shorter events, 35.3 us)
Async XLA Ops:
  7.2 41.7 %all-gather.3.cloned.1.call-start = ((), (), s32[]{:S(2)}) async-start(), calls=%async_computation.2 | async-start | bytes 2506752 | tf_op jit(solution)/shard_map/all_gather | solution.py:501
  9.4 83.7 %all-gather.5.cloned.1.call-start = ((), (), s32[]{:S(2)}) async-start(), calls=%async_computation.4 | async-start | bytes 2506752 | tf_op jit(solution)/shard_map/all_gather | solution.py:501
  10.1 160.6 %reduce-scatter.3.cloned.1.call-start = ((), (), s32[]{:S(2)}) async-start(), calls=%async_computation.3 | async-start | bytes 2359296 | tf_op jit(solution)/shard_map/reduce_scatter | solution.py:514
  10.2 6.7 %collective-permute-start.2 = (bf16[128,2048]{1,0:T(8,128)(2,1)}, bf16[128,2048]{1,0:T(8,128)(2,1)S(1)}, u32[]{:S(2)}, u32[]{:S(2)}) collective-permute-start(bf16[128,2048]{1,0:T(8,128)(2,1)} %refs_1_.3), channel_id=1, source_target_pairs={{0,1},{1,0},{2,3},{3,2},{4,5},{5,4},{6,7},{7,6},{8,9},{9,8},{10,11... | collective-permute-start | bytes 1572872 | tf_op jit(solution)/shard_map/ppermute | solution.py:435
  10.7 7.0 %collective-permute-start.1 = (bf16[128,2048]{1,0:T(8,128)(2,1)}, bf16[128,2048]{1,0:T(8,128)(2,1)S(1)}, u32[]{:S(2)}, u32[]{:S(2)}) collective-permute-start(bf16[128,2048]{1,0:T(8,128)(2,1)} %refs_1_.3), channel_id=1, source_target_pairs={{2,4},{3,5},{4,2},{5,3},{10,12},{11,13},{12,10},{13,11},{18,20},{1... | collective-permute-start | bytes 1572872 | tf_op jit(solution)/shard_map/ppermute | solution.py:435
  11.4 31.8 %collective-permute-start = (bf16[128,2048]{1,0:T(8,128)(2,1)}, bf16[128,2048]{1,0:T(8,128)(2,1)S(1)}, u32[]{:S(2)}, u32[]{:S(2)}) collective-permute-start(bf16[128,2048]{1,0:T(8,128)(2,1)} %refs_1_.3), channel_id=1, source_target_pairs={{0,2},{1,3},{2,0},{3,1},{4,6},{5,7},{6,4},{7,5},{8,10},{9,11},{10,... | collective-permute-start | bytes 1572872 | tf_op jit(solution)/shard_map/ppermute | solution.py:435
  17.7 31.1 %copy-start.32 = (bf16[128,2048]{1,0:T(8,128)(2,1)}, bf16[128,2048]{1,0:T(8,128)(2,1)S(1)}, u32[]{:S(2)}) copy-start(bf16[128,2048]{1,0:T(8,128)(2,1)S(1)} %collective-permute-done.1) | copy-start | bytes 1572868
  70.4 22.7 %copy-start.1 = (bf16[1,768,2048]{2,1,0:T(8,128)(2,1)S(1)}, bf16[1,768,2048]{2,1,0:T(8,128)(2,1)}, u32[]{:S(2)}) copy-start(bf16[1,768,2048]{2,1,0:T(8,128)(2,1)} %param.17) | copy-start | bytes 9437188
  70.4 22.7 %copy-start.23 = (bf16[1,2,64,768]{3,2,1,0:T(8,128)(2,1)S(1)}, bf16[1,2,64,768]{3,2,1,0:T(8,128)(2,1)}, u32[]{:S(2)}) copy-start(bf16[1,2,64,768]{3,2,1,0:T(8,128)(2,1)} %param.19) | copy-start | bytes 589828
  70.4 100.3 %reduce-scatter.5.cloned.1.call-start = ((), (), s32[]{:S(2)}) async-start(), calls=%async_computation.5 | async-start | bytes 2359296 | tf_op jit(solution)/shard_map/reduce_scatter | solution.py:523
  70.5 19.0 %collective-permute-start.3 = (bf16[128,2048]{1,0:T(8,128)(2,1)}, bf16[128,2048]{1,0:T(8,128)(2,1)}, u32[]{:S(2)}, u32[]{:S(2)}) collective-permute-start(bf16[128,2048]{1,0:T(8,128)(2,1)} %copy-done.32), channel_id=1, source_target_pairs={{0,2},{1,3},{2,0},{3,1},{4,6},{5,7},{6,4},{7,5},{8,10},{9,11},{10,... | collective-permute-start | bytes 1572872 | tf_op jit(solution)/shard_map/ppermute | solution.py:435
  72.2 17.3 %collective-permute-start.4 = (bf16[128,2048]{1,0:T(8,128)(2,1)}, bf16[128,2048]{1,0:T(8,128)(2,1)}, u32[]{:S(2)}, u32[]{:S(2)}) collective-permute-start(bf16[128,2048]{1,0:T(8,128)(2,1)} %copy-done.10), channel_id=1, source_target_pairs={{2,4},{3,5},{4,2},{5,3},{10,12},{11,13},{12,10},{13,11},{18,20},{1... | collective-permute-start | bytes 1572872 | tf_op jit(solution)/shard_map/ppermute | solution.py:435
  89.5 23.2 %collective-permute-start.5 = (bf16[128,2048]{1,0:T(8,128)(2,1)}, bf16[128,2048]{1,0:T(8,128)(2,1)}, u32[]{:S(2)}, u32[]{:S(2)}) collective-permute-start(bf16[128,2048]{1,0:T(8,128)(2,1)} %collective-permute-done.4), channel_id=1, source_target_pairs={{0,2},{1,3},{2,0},{3,1},{4,6},{5,7},{6,4},{7,5},{8,10},{9,11},{10,... | collective-permute-start | bytes 1572872 | tf_op jit(solution)/shard_map/ppermute | solution.py:435
  112.7 2.6 %collective-permute-start.6 = (bf16[128,2048]{1,0:T(8,128)(2,1)}, bf16[128,2048]{1,0:T(8,128)(2,1)}, u32[]{:S(2)}, u32[]{:S(2)}) collective-permute-start(bf16[128,2048]{1,0:T(8,128)(2,1)} %copy-done.10), channel_id=1, source_target_pairs={{0,1},{1,0},{2,3},{3,2},{4,5},{5,4},{6,7},{7,6},{8,9},{9,8},{10,11... | collective-permute-start | bytes 1572872 | tf_op jit(solution)/shard_map/ppermute | solution.py:435
  112.8 3.0 %collective-permute-start.7 = (bf16[128,2048]{1,0:T(8,128)(2,1)}, bf16[128,2048]{1,0:T(8,128)(2,1)}, u32[]{:S(2)}, u32[]{:S(2)}) collective-permute-start(bf16[128,2048]{1,0:T(8,128)(2,1)} %broadcast_select_fusion.1.refs_5_), channel_id=1, source_target_pairs={{0,1},{1,0},{2,3},{3,2},{4,5},{5,4},{6,7},{7,6},{8,9},{9,8},{10,11... | collective-permute-start | bytes 1572872 | tf_op jit(solution)/shard_map/ppermute | solution.py:435
  115.2 2.3 %collective-permute-start.8 = (bf16[128,2048]{1,0:T(8,128)(2,1)}, bf16[128,2048]{1,0:T(8,128)(2,1)}, u32[]{:S(2)}, u32[]{:S(2)}) collective-permute-start(bf16[128,2048]{1,0:T(8,128)(2,1)} %broadcast_select_fusion.refs_7_), channel_id=1, source_target_pairs={{0,1},{1,0},{2,3},{3,2},{4,5},{5,4},{6,7},{7,6},{8,9},{9,8},{10,11... | collective-permute-start | bytes 1572872 | tf_op jit(solution)/shard_map/ppermute | solution.py:435
  126.1 7.6 %copy-start.19 = (f32[512,768]{1,0:T(8,128)S(1)}, f32[512,768]{1,0:T(8,128)}, u32[]{:S(2)}) copy-start(f32[512,768]{1,0:T(8,128)} %copy-done.18) | copy-start | bytes 4718596
  126.1 7.6 %copy-start.21 = (f32[512,768]{1,0:T(8,128)S(1)}, f32[512,768]{1,0:T(8,128)}, u32[]{:S(2)}) copy-start(f32[512,768]{1,0:T(8,128)} %copy-done.20) | copy-start | bytes 4718596
  126.1 7.6 %copy-start.27 = (bf16[512,128]{1,0:T(8,128)(2,1)S(1)}, bf16[512,128]{1,0:T(8,128)(2,1)}, u32[]{:S(2)}) copy-start(bf16[512,128]{1,0:T(8,128)(2,1)} %copy-done.26) | copy-start | bytes 393220
  141.4 11.2 %copy-start.25 = (bf16[1408,128]{1,0:T(8,128)(2,1)}, bf16[1408,128]{1,0:T(8,128)(2,1)S(1)}, u32[]{:S(2)}) copy-start(bf16[1408,128]{1,0:T(8,128)(2,1)S(1)} %get-tuple-element.56.refs_1_) | copy-start | bytes 1081348
  142.1 10.4 %collective-permute-start.9 = (bf16[1408,128]{1,0:T(8,128)(2,1)S(1)}, bf16[1408,128]{1,0:T(8,128)(2,1)S(1)}, u32[]{:S(2)}, u32[]{:S(2)}) collective-permute-start(bf16[1408,128]{1,0:T(8,128)(2,1)S(1)} %get-tuple-element.55.refs_0_), channel_id=1, source_target_pairs={{0,8},{8,0},{16,24},{24,16},{1,9},{9,1},{17,25},{25,17},{2,10},{10... | collective-permute-start | bytes 1081352 | tf_op jit(solution)/shard_map/ppermute | solution.py:454
  143.5 10.2 %collective-permute-start.10 = (bf16[1408,128]{1,0:T(8,128)(2,1)S(1)}, bf16[1408,128]{1,0:T(8,128)(2,1)S(1)}, u32[]{:S(2)}, u32[]{:S(2)}) collective-permute-start(bf16[1408,128]{1,0:T(8,128)(2,1)S(1)} %get-tuple-element.56.refs_1_), channel_id=1, source_target_pairs={{0,16},{8,24},{16,0},{24,8},{1,17},{9,25},{17,1},{25,9},{2,18},{10... | collective-permute-start | bytes 1081352 | tf_op jit(solution)/shard_map/ppermute | solution.py:454
  156.7 9.6 %collective-permute-start.11 = (bf16[1408,128]{1,0:T(8,128)(2,1)}, bf16[1408,128]{1,0:T(8,128)(2,1)S(1)}, u32[]{:S(2)}, u32[]{:S(2)}) collective-permute-start(bf16[1408,128]{1,0:T(8,128)(2,1)} %get-tuple-element.57.one_x), channel_id=1, source_target_pairs={{0,16},{8,24},{16,0},{24,8},{1,17},{9,25},{17,1},{25,9},{2,18},{10... | collective-permute-start | bytes 1081352 | tf_op jit(solution)/shard_map/ppermute | solution.py:454
  158.1 9.3 %collective-permute-start.12 = (bf16[1408,128]{1,0:T(8,128)(2,1)}, bf16[1408,128]{1,0:T(8,128)(2,1)S(1)}, u32[]{:S(2)}, u32[]{:S(2)}) collective-permute-start(bf16[1408,128]{1,0:T(8,128)(2,1)} %get-tuple-element.58.one_y), channel_id=1, source_target_pairs={{0,8},{8,0},{16,24},{24,16},{1,9},{9,1},{17,25},{25,17},{2,10},{10... | collective-permute-start | bytes 1081352 | tf_op jit(solution)/shard_map/ppermute | solution.py:454
  (30 other events, 49.0 us)
Sparse Core Ops, SparseCore 0:
  10.2 38.5 all-gather.2
  50.5 31.3 all-gather.4
  84.1 44.6 reduce-scatter.2
  131.0 34.8 reduce-scatter.4

commit v11 on v9

--- a/solution.py
+++ b/solution.py
@@ -329,14 +329,16 @@
 
 
 def backward_kernel(chunk, adds, cut, *refs):
-    slot_ref, cot_mine, cot_other, mine_ref, other_ref, *refs = refs
+    slot_ref, cot_all_ref, mine_ref, other_ref, *refs = refs
     low_ref, active_ref, slope_ref, adapt_b_ref, down_ref, *refs = refs
     grads, (out_a_ref, out_b_ref, scaled_ref, rows_ref) = refs[: 2 * adds], refs[2 * adds :]
-    half, features = cot_mine.shape
-    for at, (cot_ref, block_ref) in enumerate(((cot_mine, mine_ref), (cot_other, other_ref))):
+    half, features = mine_ref.shape[0], cot_all_ref.shape[1]
+    for at, block_ref in enumerate((mine_ref, other_ref)):
         here = slice(at * half, (at + 1) * half)
         w = joined_weight(block_ref[:, features:], slot_ref[0], slot_ref[1])
-        scaled_ref[here] = (w * cot_ref[...].astype(jnp.float32)).astype(jnp.bfloat16)
+        whose = pl.multiple_of(slot_ref[2 + at] * half, half)
+        cot = cot_all_ref[pl.ds(whose, half)].astype(jnp.float32)
+        scaled_ref[here] = (w * cot).astype(jnp.bfloat16)
         rows_ref[here] = block_ref[:, :features]
     scaled = scaled_ref[...]
     low_gate, low_up = halves(low_ref[...])
@@ -368,7 +370,7 @@
         out_b_ref[: features - cut] = sum_a[cut:].astype(jnp.bfloat16)
 
 
-def backward_stage(slot, cots, blocks, saved, down, adapt_b, grads=(), cut=None, chunk=256):
+def backward_stage(slot, cot_all, blocks, saved, down, adapt_b, grads=(), cut=None, chunk=256):
     hidden_width, features = down.shape
     both, ranks = saved[0].shape
     bf16, f32 = jnp.bfloat16, jnp.float32
@@ -380,7 +382,7 @@
         outs,
         [((both, features), bf16), ((both, features), bf16)],
         both * (down.size + features * ranks + 4 * adapt_b.size),
-        (slot, *cots, *blocks, *saved, adapt_b, down, *grads),
+        (slot, cot_all, *blocks, *saved, adapt_b, down, *grads),
     )
 
 
@@ -451,13 +453,6 @@
 
 def dp_swap(array, bit):
     return lax.ppermute(array, "dp", [(d, d ^ bit) for d in range(4)])
-
-
-def group_sum(mine, features, hidden_width):
-    got = dp_swap(mine[0], 1), dp_swap(mine[1], 2)
-    pairs = pair_sums(mine, got)
-    got = dp_swap(pairs[0], 2), dp_swap(pairs[1], 1)
-    return finished(pairs, got, features, hidden_width)
 
 
 def dense_body(
@@ -481,21 +476,23 @@
     adapt_a = adapter_down_maps[0]
     adapt_b = adapter_up_maps[0].reshape(adapt_a.shape[1], -1)
 
-    slot = jnp.stack([me, jnp.int32(slot_total)])
-
-    def forward(mine, twin):
-        *saved, part, away = forward_stage(slot, mine, twin, gate_up, down, adapt_a, adapt_b)
-        return saved, part, away
-
-    def backward(cots, rows, saved, grads=(), cut=None):
-        return backward_stage(slot, cots, rows, saved, down, adapt_b, grads, cut)
-
     def pick(inside, outside):
         return jnp.where(inner, inside, outside)
 
     def after(array, earlier):
         return fence(array, earlier)[0]
 
+    whose = [me, me ^ 2, pick(me ^ 6, me ^ 4), pick(me ^ 4, me ^ 6)]
+    slots = [jnp.stack([me, jnp.int32(slot_total), device, device ^ 1]) for device in whose]
+
+    def forward(*blocks):
+        *saved, part, away = forward_stage(slots[0], *blocks, gate_up, down, adapt_a, adapt_b)
+        return saved, part, away
+
+    def backward(stage, rows, saved, grads=(), cut=None):
+        return backward_stage(slots[stage], cots, rows, saved, down, adapt_b, grads, cut)
+
+    cots = lax.all_gather(cotangent, "expert", tiled=True)
     tokens = tagged_tokens(
         tokens, routing, router_route_weights, route_replica_choice, device_expert_table, capacity
     )
@@ -503,69 +500,51 @@
     twin = sibling(tokens)
     rows0 = (tokens, twin)
     tok_mid = send(after(tokens, twin), MID_SWAP)
-    tok_swap, tok_mid, rows0, cotangent = fence(tok_swap, tok_mid, rows0, cotangent)
+    saved0, part0, away0 = forward(*rows0)
+    tok_swap, tok_mid, part0, away0 = fence(tok_swap, tok_mid, part0, away0)
 
     tok_out2 = send(tok_mid, ALL_SWAP)
     twin = sibling(tok_swap)
     rows1 = (tok_swap, twin)
     tok_mid2 = send(after(tok_swap, twin), MID_SWAP)
-    saved0, part0, away0 = forward(*rows0)
-    tok_mid, tok_out2, tok_mid2, rows1, part0, away0, cotangent = fence(
-        tok_mid, tok_out2, tok_mid2, rows1, part0, away0, cotangent
-    )
+    saved1, part1, away1 = forward(*rows1)
+    tok_mid, tok_out2, tok_mid2, part1, away1 = fence(tok_mid, tok_out2, tok_mid2, part1, away1)
 
     tok_out3 = send(tok_mid2, ALL_SWAP)
     tok_second = pick(tok_mid, tok_out2)
-    twin = sibling(tok_second)
-    rows2 = (tok_second, twin)
-    cot_mid = send(after(cotangent, twin), MID_SWAP)
-    saved1, part1, away1 = forward(*rows1)
-    tok_mid2, tok_out3, cot_mid, rows2, part1, away1, cotangent = fence(
-        tok_mid2, tok_out3, cot_mid, rows2, part1, away1, cotangent
-    )
-
-    cot_swap = send(cotangent, ALL_SWAP)
+    rows2 = (tok_second, sibling(tok_second))
+    saved2, part2, away2 = forward(*rows2)
+    tok_mid2, tok_out3, part2, away2, cots = fence(tok_mid2, tok_out3, part2, away2, cots)
+
     tok_third = pick(tok_mid2, tok_out3)
     rows3 = (tok_third, sibling(tok_third))
-    cots0 = (cotangent, sibling(cotangent))
-    saved2, part2, away2 = forward(*rows2)
     saved3, part3, away3 = forward(*rows3)
-    cot_swap, cot_mid, cots0, part2, away2, part3, away3 = fence(
-        cot_swap, cot_mid, cots0, part2, away2, part3, away3
-    )
-
-    cot_out2 = send(cot_mid, ALL_SWAP)
-    twin = sibling(cot_swap)
-    cots1 = (cot_swap, twin)
-    cot_mid2 = send(after(cot_swap, twin), MID_SWAP)
     part3 = add_rounded(part3, sibling(away3))
-    grads = backward(cots0, rows0, saved0)
-    grads = backward(cots1, rows1, saved1, grads)
-    cot_mid, cot_out2, cot_mid2, part2, away2, part3, grads = fence(
-        cot_mid, cot_out2, cot_mid2, part2, away2, part3, grads
-    )
-
-    swap6 = send(pick(cot_mid2, part3), ALL_SWAP)
-    cot_second = pick(cot_mid, cot_out2)
-    cots2 = (cot_second, sibling(cot_second))
-    grads = backward(cots2, rows2, saved2, grads)
+    part3, part2, away2 = fence(part3, part2, away2)
+
+    third_in = send(part3, ALL_SWAP)
     part2 = add_rounded(part2, sibling(away2))
-    swap6, cot_mid2, part0, away0, part1, away1, part2, part3, grads = fence(
-        swap6, cot_mid2, part0, away0, part1, away1, part2, part3, grads
-    )
-
-    second_in = send(part2, ALL_SWAP)
-    cot_third = pick(cot_mid2, swap6)
-    twin = sibling(cot_third)
-    third_mid = send(after(add_rounded(part3, swap6), twin), MID_SWAP)
     features, hidden_width = adapt_a.shape[0], adapt_b.shape[1]
     cut = (features + hidden_width) // 2
-    grads = backward((cot_third, twin), rows3, saved3, grads, cut)
-    grad_a, grad_b = group_sum(grads, features, hidden_width)
+    grads = backward(0, rows0, saved0)
+    grads = backward(1, rows1, saved1, grads)
+    grads = backward(2, rows2, saved2, grads)
+    grads = backward(3, rows3, saved3, grads, cut)
+    third_in, part3, part2, part1, away1, grads = fence(third_in, part3, part2, part1, away1, grads)
+
+    second_in = send(part2, ALL_SWAP)
+    third_mid = send(add_rounded(part3, third_in), MID_SWAP)
+    got = dp_swap(grads[0], 1), dp_swap(grads[1], 2)
     part1 = add_rounded(part1, sibling(away1))
     part0 = add_rounded(part0, sibling(away0))
+    second_in, third_mid, part0, part1, part2, grads, got = fence(
+        second_in, third_mid, part0, part1, part2, grads, got
+    )
     first_swap = send(add_rounded(part1, third_mid), ALL_SWAP)
     second_mid = send(add_rounded(part2, second_in), MID_SWAP)
+    pairs = pair_sums(grads, got)
+    got = dp_swap(pairs[0], 2), dp_swap(pairs[1], 1)
+    grad_a, grad_b = finished(pairs, got, features, hidden_width)
     mixed = add_rounded(part0, first_swap, second_mid)
     return mixed, grad_a[None], grad_b.reshape(adapter_up_maps.shape)
 

time: 154 us -> 193 us (1.25)
  local copies, waits for them, and re-layouts: 8.49 us -> 41.3 us
  between operations: 0.96 us -> 14.5 us
  waiting for transfers between devices: 52 us -> 40.1 us
  starting transfers between devices: 47.1 us -> 49.5 us
  Pallas kernels: 38.6 us -> 40.6 us
    unnamed x30 -> x130, local copies, waits for them, and re-layouts: 8.49 us -> 41.3 us
    ppermute x26 -> x18, waiting for transfers between devices: 43.1 us -> 23.4 us  [send(): return lax.ppermute(array, 'expert', pairs)]
    ppermute x4, waiting for transfers between devices: 8.89 us -> 16 us  [dp_swap(): return lax.ppermute(array, 'dp', [(d, d ^ bit) for d in range(4)])]
    ppermute x26 -> x18, starting transfers between devices: 41 us -> 43.4 us  [send(): return lax.ppermute(array, 'expert', pairs)]
    pallas_call x8, Pallas kernels: 31.7 us -> 33.7 us  [stage_call(): pl.pallas_call(kernel, out_shape=out_shape, in_specs=[SMEM] + [VMEM] * (l...]
    convert_element_type x6 -> x8, other arithmetic: 4.51 us -> 3.11 us  [add_rounded(): return total.astype(jnp.bfloat16)]
  transfers between devices with their start and end apart: 30 -> 23, of which waited for: 10 -> 11; matrix products, arithmetic and copies ran while one was open for 2% -> 1% of each run, Pallas kernels for 24% -> 19%
where the time goes in v11:
time: 193 us; the launch traced here: 192 us
  starting transfers between devices  49.5 us (26%)
  local copies, waits for them, and re-layouts  41.3 us (21%)
  Pallas kernels  40.6 us (21%)
  waiting for transfers between devices  40.1 us (21%)
  between operations  14.5 us (8%)
  other arithmetic  5.65 us (3%)
    ppermute x18, starting transfers between devices, send(): return lax.ppermute(array, 'expert', pairs)  43.4 us
    unnamed x130, local copies, waits for them, and re-layouts  41.3 us
    pallas_call x8, Pallas kernels, stage_call(): pl.pallas_call(kernel, out_shape=out_shape, in_specs=[SMEM] + [VMEM] * (l...  33.7 us
    ppermute x18, waiting for transfers between devices, send(): return lax.ppermute(array, 'expert', pairs)  23.4 us
    ppermute x4, waiting for transfers between devices, dp_swap(): return lax.ppermute(array, 'dp', [(d, d ^ bit) for d in range(4)])  16 us
    ppermute x4, starting transfers between devices, dp_swap(): return lax.ppermute(array, 'dp', [(d, d ^ bit) for d in range(4)])  6.05 us
  transfers between devices with their start and end apart: 23, of which 11 were waited for; matrix products, arithmetic and copies ran while one was open for 1% of the time, Pallas kernels for 19%

profile of v11, /device:TPU:0, one launch (start us, length us, event | category | flops | bytes accessed | tf_op | source)
XLA Modules:
  0.0 191.7 jit_solution(294047237244319134)
XLA Ops:
  10.5 2.6 %collective-permute-start = (bf16[128,2176]{1,0:T(8,128)(2,1)}, bf16[128,2176]{1,0:T(8,128)(2,1)}, u32[]{:S(2)}, u32[]{:S(2)}) collective-permute-start(bf16[128,2176]{1,0:T(8,128)(2,1)} %shard_map.121.mine_ref.refs_2_), channel_id=1, source_target_pairs={{0,2},{1,3},{2,0},{3,1},{4,6},{5,7},{6,4},{7,5},{8,10},{9,11},{10,... | collective-permute-start | bytes 1671176 | tf_op jit(solution)/shard_map/ppermute | solution.py:436
  17.4 3.1 %copy-done.2 = bf16[1,2048,1536]{2,1,0:T(8,128)(2,1)S(1)} copy-done((bf16[1,2048,1536]{2,1,0:T(8,128)(2,1)S(1)}, bf16[1,2048,1536]{2,1,0:T(8,128)(2,1)}, u32[]{:S(2)}) %copy-start.2) | copy-done | bytes 6291480
  24.6 4.3 %shard_map.122 = (bf16[256,128]{1,0:T(8,128)(2,1)S(1)}, f32[256,768]{1,0:T(8,128)S(1)}, f32[256,768]{1,0:T(8,128)S(1)}, bf16[128,2048]{1,0:T(8,128)(2,1)S(1)}, bf16[128,2048]{1,0:T(8,128)(2,1)S(1)}) custom-call(s32[4]{0:T(128)S(1)} %pad_add_fusion.slot_ref.refs_0_, bf16[128,2176]{1,0:T(8,128)(2,1)S(1)} %copy-done.18, bf16[128,2176]{1,0:T(8,128)(2,1)S(1)} %copy-done.21, ...), custom_call_target="tpu_custom_call" | custom-call | flops 2550136832 | bytes 13959184 | tf_op jit(solution)/shard_map/pallas_call | solution.py:269
  34.2 22.1 %collective-permute-start.3 = (bf16[128,2176]{1,0:T(8,128)(2,1)}, bf16[128,2176]{1,0:T(8,128)(2,1)}, u32[]{:S(2)}, u32[]{:S(2)}) collective-permute-start(bf16[128,2176]{1,0:T(8,128)(2,1)} %collective-permute-done.2), channel_id=1, source_target_pairs={{0,2},{1,3},{2,0},{3,1},{4,6},{5,7},{6,4},{7,5},{8,10},{9,11},{10,... | collective-permute-start | bytes 1671176 | tf_op jit(solution)/shard_map/ppermute | solution.py:436
  58.7 2.8 %copy-done.3 = bf16[1,2048,1536]{2,1,0:T(8,128)(2,1)S(1)} copy-done((bf16[1,2048,1536]{2,1,0:T(8,128)(2,1)S(1)}, bf16[1,2048,1536]{2,1,0:T(8,128)(2,1)}, u32[]{:S(2)}) %copy-start.3) | copy-done | bytes 6291480
  63.6 4.8 %shard_map.123 = (bf16[256,128]{1,0:T(8,128)(2,1)S(1)}, f32[256,768]{1,0:T(8,128)S(1)}, f32[256,768]{1,0:T(8,128)S(1)}, bf16[128,2048]{1,0:T(8,128)(2,1)S(1)}, bf16[128,2048]{1,0:T(8,128)(2,1)S(1)}) custom-call(s32[4]{0:T(128)S(1)} %pad_add_fusion.slot_ref.refs_0_, bf16[128,2176]{1,0:T(8,128)(2,1)} %collective-permute-done.mine_ref.refs_2_, ...), custom_call_target="tpu_custom_call" | custom-call | flops 2550136832 | bytes 13959184 | tf_op jit(solution)/shard_map/pallas_call | solution.py:269
  70.0 5.5 %collective-permute-done.3 = bf16[128,2176]{1,0:T(8,128)(2,1)} collective-permute-done((bf16[128,2176]{1,0:T(8,128)(2,1)}, bf16[128,2176]{1,0:T(8,128)(2,1)}, u32[]{:S(2)}, u32[]{:S(2)}) %collective-permute-start.3) | collective-permute-done | bytes 557088 | tf_op jit(solution)/shard_map/ppermute | solution.py:436
  76.8 3.1 %collective-permute-start.6 = (bf16[128,2176]{1,0:T(8,128)(2,1)}, bf16[128,2176]{1,0:T(8,128)(2,1)}, u32[]{:S(2)}, u32[]{:S(2)}) collective-permute-start(bf16[128,2176]{1,0:T(8,128)(2,1)} %collective-permute-done.5), channel_id=1, source_target_pairs={{0,2},{1,3},{2,0},{3,1},{4,6},{5,7},{6,4},{7,5},{8,10},{9,11},{10,... | collective-permute-start | bytes 1671176 | tf_op jit(solution)/shard_map/ppermute | solution.py:436
  79.9 2.8 %copy-done.4 = bf16[1,2048,1536]{2,1,0:T(8,128)(2,1)S(1)} copy-done((bf16[1,2048,1536]{2,1,0:T(8,128)(2,1)S(1)}, bf16[1,2048,1536]{2,1,0:T(8,128)(2,1)}, u32[]{:S(2)}) %copy-start.4) | copy-done | bytes 6291480
  82.7 4.3 %shard_map.124 = (bf16[256,128]{1,0:T(8,128)(2,1)S(1)}, f32[256,768]{1,0:T(8,128)S(1)}, f32[256,768]{1,0:T(8,128)S(1)}, bf16[128,2048]{1,0:T(8,128)(2,1)S(1)}, bf16[128,2048]{1,0:T(8,128)(2,1)S(1)}) custom-call(s32[4]{0:T(128)S(1)} %pad_add_fusion.slot_ref.refs_0_, bf16[128,2176]{1,0:T(8,128)(2,1)S(1)} %broadcast_select_fusion.1.mine_ref.refs_2_, ...), custom_call_target="tpu_custom_call" | custom-call | flops 2550136832 | bytes 13959184 | tf_op jit(solution)/shard_map/pallas_call | solution.py:269
  90.4 3.0 %collective-permute-done.6 = bf16[128,2176]{1,0:T(8,128)(2,1)} collective-permute-done((bf16[128,2176]{1,0:T(8,128)(2,1)}, bf16[128,2176]{1,0:T(8,128)(2,1)}, u32[]{:S(2)}, u32[]{:S(2)}) %collective-permute-start.6) | collective-permute-done | bytes 557088 | tf_op jit(solution)/shard_map/ppermute | solution.py:436
  96.6 2.8 %copy-done.5 = bf16[1,2048,1536]{2,1,0:T(8,128)(2,1)S(1)} copy-done((bf16[1,2048,1536]{2,1,0:T(8,128)(2,1)S(1)}, bf16[1,2048,1536]{2,1,0:T(8,128)(2,1)}, u32[]{:S(2)}) %copy-start.5) | copy-done | bytes 6291480
  100.4 5.0 %shard_map.125 = (bf16[256,128]{1,0:T(8,128)(2,1)S(1)}, f32[256,768]{1,0:T(8,128)S(1)}, f32[256,768]{1,0:T(8,128)S(1)}, bf16[128,2048]{1,0:T(8,128)(2,1)S(1)}, bf16[128,2048]{1,0:T(8,128)(2,1)}) custom-call(s32[4]{0:T(128)S(1)} %pad_add_fusion.slot_ref.refs_0_, bf16[128,2176]{1,0:T(8,128)(2,1)S(1)} %broadcast_select_fusion.mine_ref.refs_2_, ...), custom_call_target="tpu_custom_call" | custom-call | flops 2550136832 | bytes 13959184 | tf_op jit(solution)/shard_map/pallas_call | solution.py:269
  119.5 3.6 %shard_map.126 = (f32[2048,128]{1,0:T(8,128)S(1)}, f32[128,768]{1,0:T(8,128)S(1)}) custom-call(s32[4]{0:T(128)S(1)} %pad_add_fusion.slot_ref.refs_0_, bf16[1024,2048]{1,0:T(8,128)(2,1)S(1)} %copy-done.6, bf16[128,2176]{1,0:T(8,128)(2,1)S(1)} %copy-done.19, bf16[128,2176]{1,0:T(8,128)(2,1)S(1)} %copy-done.22, ...), custom_call_target="tpu_custom_call" | custom-call | flops 1140850688 | bytes 11730960 | tf_op jit(solution)/shard_map/pallas_call | solution.py:269
  123.2 4.5 %shard_map.127 = (f32[2048,128]{1,0:T(8,128)S(1)}, f32[128,768]{1,0:T(8,128)S(1)}) custom-call(s32[4]{0:T(128)S(1)} %pad_add_fusion.4.refs_0_, bf16[1024,2048]{1,0:T(8,128)(2,1)S(1)} %copy-done.7, bf16[128,2176]{1,0:T(8,128)(2,1)} %collective-permute-done.mine_ref.refs_2_, bf16[128,2176]{1,0:T(8,128)(2,1)S(1)} %copy-done.25, ...), custom_call_target="tpu_custom_call" | custom-call | flops 1140850688 | bytes 13172752 | tf_op jit(solution)/shard_map/pallas_call | solution.py:269
  127.7 3.6 %shard_map.128 = (f32[2048,128]{1,0:T(8,128)S(1)}, f32[128,768]{1,0:T(8,128)S(1)}) custom-call(s32[4]{0:T(128)S(1)} %pad_add_fusion.3.refs_0_, bf16[1024,2048]{1,0:T(8,128)(2,1)S(1)} %copy-done.7, bf16[128,2176]{1,0:T(8,128)(2,1)S(1)} %copy-done.15, bf16[128,2176]{1,0:T(8,128)(2,1)S(1)} %copy-done.27, bf16[256,128]{1,0:T(8,128)(2,1)S(1)} %get-tuple-element.98.refs_4_, ...), custom_call_target="tpu_custom_call" | custom-call | flops 1140850688 | bytes 13172752 | tf_op jit(solution)/shard_map/pallas_call | solution.py:269
  133.2 3.6 %shard_map.129 = (bf16[1408,128]{1,0:T(8,128)(2,1)S(1)}, bf16[1408,128]{1,0:T(8,128)(2,1)S(1)}) custom-call(s32[4]{0:T(128)S(1)} %pad_add_fusion.2.refs_0_, bf16[1024,2048]{1,0:T(8,128)(2,1)S(1)} %copy-done.7, bf16[128,2176]{1,0:T(8,128)(2,1)S(1)} %copy-done.17, bf16[128,2176]{1,0:T(8,128)(2,1)S(1)} %copy-done.29, bf16[256,128]{1,0:T(8,128)(2,1)S(1)} %copy-done.56, ...), custom_call_target="tpu_custom_call" | custom-call | flops 1140850688 | bytes 12451856 | tf_op jit(solution)/shard_map/pallas_call | solution.py:269
  137.0 8.4 %collective-permute-done.10 = bf16[128,2048]{1,0:T(8,128)(2,1)S(1)} collective-permute-done((bf16[128,2048]{1,0:T(8,128)(2,1)S(1)}, bf16[128,2048]{1,0:T(8,128)(2,1)S(1)}, u32[]{:S(2)}, u32[]{:S(2)}) %collective-permute-start.10) | collective-permute-done | bytes 524320 | tf_op jit(solution)/shard_map/ppermute | solution.py:436
  146.2 4.6 %collective-permute-start.12 = (bf16[128,2048]{1,0:T(8,128)(2,1)S(1)}, bf16[128,2048]{1,0:T(8,128)(2,1)S(1)}, u32[]{:S(2)}, u32[]{:S(2)}) collective-permute-start(bf16[128,2048]{1,0:T(8,128)(2,1)S(1)} %add_convert_fusion.6), channel_id=1, source_target_pairs={{0,2},{1,3},{2,0},{3,1},{4,6},{5,7},{6,4},{7,5},{8,10},{9,11},{10,... | collective-permute-start | bytes 1572872 | tf_op jit(solution)/shard_map/ppermute | solution.py:436
  154.1 7.2 %collective-permute-done.16.refs_2_ = bf16[1408,128]{1,0:T(8,128)(2,1)S(1)} collective-permute-done((bf16[1408,128]{1,0:T(8,128)(2,1)S(1)}, bf16[1408,128]{1,0:T(8,128)(2,1)S(1)}, u32[]{:S(2)}, u32[]{:S(2)}) %collective-permute-start.16) | collective-permute-done | bytes 360480 | tf_op jit(solution)/shard_map/ppermute | solution.py:455
  164.1 3.5 %collective-permute-start.18 = (bf16[128,2048]{1,0:T(8,128)(2,1)S(1)}, bf16[128,2048]{1,0:T(8,128)(2,1)S(1)}, u32[]{:S(2)}, u32[]{:S(2)}) collective-permute-start(bf16[128,2048]{1,0:T(8,128)(2,1)S(1)} %add_convert_fusion.2), channel_id=1, source_target_pairs={{0,2},{1,3},{2,0},{3,1},{4,6},{5,7},{6,4},{7,5},{8,10},{9,11},{10,... | collective-permute-start | bytes 1572872 | tf_op jit(solution)/shard_map/ppermute | solution.py:436
  167.6 2.3 %shard_map.130 = (bf16[1408,128]{1,0:T(8,128)(2,1)}, bf16[1408,128]{1,0:T(8,128)(2,1)}) custom-call(bf16[1408,128]{1,0:T(8,128)(2,1)} %copy-done.53, bf16[1408,128]{1,0:T(8,128)(2,1)} %copy-done.54, bf16[1408,128]{1,0:T(8,128)(2,1)} %copy-done.61, bf16[1408,128]{1,0:T(8,128)(2,1)} %copy-done.62), custom_call_target="tpu_custom_call" | custom-call | tf_op jit(solution)/shard_map/pallas_call | solution.py:396
  172.9 6.4 %collective-permute-done.20.other_x = bf16[1408,128]{1,0:T(8,128)(2,1)S(1)} collective-permute-done((bf16[1408,128]{1,0:T(8,128)(2,1)}, bf16[1408,128]{1,0:T(8,128)(2,1)S(1)}, u32[]{:S(2)}, u32[]{:S(2)}) %collective-permute-start.20) | collective-permute-done | bytes 360480 | tf_op jit(solution)/shard_map/ppermute | solution.py:455
  181.3 2.5 %shard_map.131 = (f32[2048,128]{1,0:T(8,128)}, f32[128,768]{1,0:T(8,128)}) custom-call(bf16[1408,128]{1,0:T(8,128)(2,1)} %get-tuple-element.133.one_x, bf16[1408,128]{1,0:T(8,128)(2,1)} %get-tuple-element.134.one_y, bf16[1408,128]{1,0:T(8,128)(2,1)} %copy-done.63, bf16[1408,128]{1,0:T(8,128)(2,1)} %copy-done.64), custom_call_target="tpu_custom_call" | custom-call | tf_op jit(solution)/shard_map/pallas_call | solution.py:417
  (178 shorter events, 60.9 us)
Async XLA Ops:
  7.2 86.3 %all-gather.2.cloned.1.call-start = ((), (), s32[]{:S(2)}) async-start(), calls=%async_computation | async-start | bytes 4718592 | tf_op jit(solution)/shard_map/all_gather | solution.py:495
  10.1 3.0 %collective-permute-start.1 = (bf16[128,2176]{1,0:T(8,128)(2,1)}, bf16[128,2176]{1,0:T(8,128)(2,1)S(1)}, u32[]{:S(2)}, u32[]{:S(2)}) collective-permute-start(bf16[128,2176]{1,0:T(8,128)(2,1)} %shard_map.121.mine_ref.refs_2_), channel_id=1, source_target_pairs={{0,1},{1,0},{2,3},{3,2},{4,5},{5,4},{6,7},{7,6},{8,9},{9,8},{10,11... | collective-permute-start | bytes 1671176 | tf_op jit(solution)/shard_map/ppermute | solution.py:436
  10.5 23.7 %collective-permute-start = (bf16[128,2176]{1,0:T(8,128)(2,1)}, bf16[128,2176]{1,0:T(8,128)(2,1)}, u32[]{:S(2)}, u32[]{:S(2)}) collective-permute-start(bf16[128,2176]{1,0:T(8,128)(2,1)} %shard_map.121.mine_ref.refs_2_), channel_id=1, source_target_pairs={{0,2},{1,3},{2,0},{3,1},{4,6},{5,7},{6,4},{7,5},{8,10},{9,11},{10,... | collective-permute-start | bytes 1671176 | tf_op jit(solution)/shard_map/ppermute | solution.py:436
  13.9 20.3 %collective-permute-start.2 = (bf16[128,2176]{1,0:T(8,128)(2,1)}, bf16[128,2176]{1,0:T(8,128)(2,1)}, u32[]{:S(2)}, u32[]{:S(2)}) collective-permute-start(bf16[128,2176]{1,0:T(8,128)(2,1)} %shard_map.121.mine_ref.refs_2_), channel_id=1, source_target_pairs={{2,4},{3,5},{4,2},{5,3},{10,12},{11,13},{12,10},{13,11},{18,20},{1... | collective-permute-start | bytes 1671176 | tf_op jit(solution)/shard_map/ppermute | solution.py:436
  24.6 34.1 %copy-start.9 = (bf16[1,2,64,768]{3,2,1,0:T(8,128)(2,1)S(1)}, bf16[1,2,64,768]{3,2,1,0:T(8,128)(2,1)}, u32[]{:S(2)}) copy-start(bf16[1,2,64,768]{3,2,1,0:T(8,128)(2,1)} %param.19) | copy-start | bytes 589828
  34.2 22.1 %collective-permute-start.4 = (bf16[128,2176]{1,0:T(8,128)(2,1)}, bf16[128,2176]{1,0:T(8,128)(2,1)S(1)}, u32[]{:S(2)}, u32[]{:S(2)}) collective-permute-start(bf16[128,2176]{1,0:T(8,128)(2,1)} %collective-permute-done.mine_ref.refs_2_), channel_id=1, source_target_pairs={{0,1},{1,0},{2,3},{3,2},{4,5},{5,4},{6,7},{7,6},{8,9},{9,8},{10,11... | collective-permute-start | bytes 1671176 | tf_op jit(solution)/shard_map/ppermute | solution.py:436
  34.2 41.4 %collective-permute-start.3 = (bf16[128,2176]{1,0:T(8,128)(2,1)}, bf16[128,2176]{1,0:T(8,128)(2,1)}, u32[]{:S(2)}, u32[]{:S(2)}) collective-permute-start(bf16[128,2176]{1,0:T(8,128)(2,1)} %collective-permute-done.2), channel_id=1, source_target_pairs={{0,2},{1,3},{2,0},{3,1},{4,6},{5,7},{6,4},{7,5},{8,10},{9,11},{10,... | collective-permute-start | bytes 1671176 | tf_op jit(solution)/shard_map/ppermute | solution.py:436
  57.2 18.4 %collective-permute-start.5 = (bf16[128,2176]{1,0:T(8,128)(2,1)}, bf16[128,2176]{1,0:T(8,128)(2,1)}, u32[]{:S(2)}, u32[]{:S(2)}) collective-permute-start(bf16[128,2176]{1,0:T(8,128)(2,1)} %collective-permute-done.mine_ref.refs_2_), channel_id=1, source_target_pairs={{2,4},{3,5},{4,2},{5,3},{10,12},{11,13},{12,10},{13,11},{18,20},{1... | collective-permute-start | bytes 1671176 | tf_op jit(solution)/shard_map/ppermute | solution.py:436
  76.7 3.2 %collective-permute-start.7 = (bf16[128,2176]{1,0:T(8,128)(2,1)S(1)}, bf16[128,2176]{1,0:T(8,128)(2,1)S(1)}, u32[]{:S(2)}, u32[]{:S(2)}) collective-permute-start(bf16[128,2176]{1,0:T(8,128)(2,1)S(1)} %broadcast_select_fusion.1.mine_ref.refs_2_), channel_id=1, source_target_pairs={{0,1},{1,0},{2,3},{3,2},{4,5},{5,4},{6,7},{7,6},{8,9},{9,8},{10,11... | collective-permute-start | bytes 1671176 | tf_op jit(solution)/shard_map/ppermute | solution.py:436
  76.8 16.7 %collective-permute-start.6 = (bf16[128,2176]{1,0:T(8,128)(2,1)}, bf16[128,2176]{1,0:T(8,128)(2,1)}, u32[]{:S(2)}, u32[]{:S(2)}) collective-permute-start(bf16[128,2176]{1,0:T(8,128)(2,1)} %collective-permute-done.5), channel_id=1, source_target_pairs={{0,2},{1,3},{2,0},{3,1},{4,6},{5,7},{6,4},{7,5},{8,10},{9,11},{10,... | collective-permute-start | bytes 1671176 | tf_op jit(solution)/shard_map/ppermute | solution.py:436
  94.6 2.0 %collective-permute-start.8 = (bf16[128,2176]{1,0:T(8,128)(2,1)S(1)}, bf16[128,2176]{1,0:T(8,128)(2,1)S(1)}, u32[]{:S(2)}, u32[]{:S(2)}) collective-permute-start(bf16[128,2176]{1,0:T(8,128)(2,1)S(1)} %broadcast_select_fusion.mine_ref.refs_2_), channel_id=1, source_target_pairs={{0,1},{1,0},{2,3},{3,2},{4,5},{5,4},{6,7},{7,6},{8,9},{9,8},{10,11... | collective-permute-start | bytes 1671176 | tf_op jit(solution)/shard_map/ppermute | solution.py:436
  108.7 2.3 %collective-permute-start.9 = (bf16[128,2048]{1,0:T(8,128)(2,1)}, bf16[128,2048]{1,0:T(8,128)(2,1)}, u32[]{:S(2)}, u32[]{:S(2)}) collective-permute-start(bf16[128,2048]{1,0:T(8,128)(2,1)} %get-tuple-element.86), channel_id=1, source_target_pairs={{0,1},{1,0},{2,3},{3,2},{4,5},{5,4},{6,7},{7,6},{8,9},{9,8},{10,11... | collective-permute-start | bytes 1572872 | tf_op jit(solution)/shard_map/ppermute | solution.py:436
  112.3 24.6 %collective-permute-start.11 = (bf16[128,2048]{1,0:T(8,128)(2,1)}, bf16[128,2048]{1,0:T(8,128)(2,1)S(1)}, u32[]{:S(2)}, u32[]{:S(2)}) collective-permute-start(bf16[128,2048]{1,0:T(8,128)(2,1)} %copy-done.60), channel_id=1, source_target_pairs={{0,1},{1,0},{2,3},{3,2},{4,5},{5,4},{6,7},{7,6},{8,9},{9,8},{10,11... | collective-permute-start | bytes 1572872 | tf_op jit(solution)/shard_map/ppermute | solution.py:436
  112.6 38.3 %collective-permute-start.14 = (bf16[128,2048]{1,0:T(8,128)(2,1)}, bf16[128,2048]{1,0:T(8,128)(2,1)S(1)}, u32[]{:S(2)}, u32[]{:S(2)}) collective-permute-start(bf16[128,2048]{1,0:T(8,128)(2,1)} %copy-done.57), channel_id=1, source_target_pairs={{0,1},{1,0},{2,3},{3,2},{4,5},{5,4},{6,7},{7,6},{8,9},{9,8},{10,11... | collective-permute-start | bytes 1572872 | tf_op jit(solution)/shard_map/ppermute | solution.py:436
  131.4 14.0 %collective-permute-start.10 = (bf16[128,2048]{1,0:T(8,128)(2,1)S(1)}, bf16[128,2048]{1,0:T(8,128)(2,1)S(1)}, u32[]{:S(2)}, u32[]{:S(2)}) collective-permute-start(bf16[128,2048]{1,0:T(8,128)(2,1)S(1)} %add_convert_fusion.7), channel_id=1, source_target_pairs={{0,2},{1,3},{2,0},{3,1},{4,6},{5,7},{6,4},{7,5},{8,10},{9,11},{10,... | collective-permute-start | bytes 1572872 | tf_op jit(solution)/shard_map/ppermute | solution.py:436
  145.4 8.6 %collective-permute-start.15 = (bf16[128,2048]{1,0:T(8,128)(2,1)S(1)}, bf16[128,2048]{1,0:T(8,128)(2,1)S(1)}, u32[]{:S(2)}, u32[]{:S(2)}) collective-permute-start(bf16[128,2048]{1,0:T(8,128)(2,1)S(1)} %copy-done.59), channel_id=1, source_target_pairs={{0,1},{1,0},{2,3},{3,2},{4,5},{5,4},{6,7},{7,6},{8,9},{9,8},{10,11... | collective-permute-start | bytes 1572872 | tf_op jit(solution)/shard_map/ppermute | solution.py:436
  145.5 17.0 %collective-permute-start.13 = (bf16[128,2048]{1,0:T(8,128)(2,1)S(1)}, bf16[128,2048]{1,0:T(8,128)(2,1)S(1)}, u32[]{:S(2)}, u32[]{:S(2)}) collective-permute-start(bf16[128,2048]{1,0:T(8,128)(2,1)S(1)} %add_convert_fusion.5), channel_id=1, source_target_pairs={{2,4},{3,5},{4,2},{5,3},{10,12},{11,13},{12,10},{13,11},{18,20},{1... | collective-permute-start | bytes 1572872 | tf_op jit(solution)/shard_map/ppermute | solution.py:436
  146.2 16.9 %collective-permute-start.12 = (bf16[128,2048]{1,0:T(8,128)(2,1)S(1)}, bf16[128,2048]{1,0:T(8,128)(2,1)S(1)}, u32[]{:S(2)}, u32[]{:S(2)}) collective-permute-start(bf16[128,2048]{1,0:T(8,128)(2,1)S(1)} %add_convert_fusion.6), channel_id=1, source_target_pairs={{0,2},{1,3},{2,0},{3,1},{4,6},{5,7},{6,4},{7,5},{8,10},{9,11},{10,... | collective-permute-start | bytes 1572872 | tf_op jit(solution)/shard_map/ppermute | solution.py:436
  151.0 10.3 %collective-permute-start.16 = (bf16[1408,128]{1,0:T(8,128)(2,1)S(1)}, bf16[1408,128]{1,0:T(8,128)(2,1)S(1)}, u32[]{:S(2)}, u32[]{:S(2)}) collective-permute-start(bf16[1408,128]{1,0:T(8,128)(2,1)S(1)} %get-tuple-element.129.refs_0_), channel_id=1, source_target_pairs={{0,8},{8,0},{16,24},{24,16},{1,9},{9,1},{17,25},{25,17},{2,10},{10... | collective-permute-start | bytes 1081352 | tf_op jit(solution)/shard_map/ppermute | solution.py:455
  152.5 10.0 %collective-permute-start.17 = (bf16[1408,128]{1,0:T(8,128)(2,1)S(1)}, bf16[1408,128]{1,0:T(8,128)(2,1)S(1)}, u32[]{:S(2)}, u32[]{:S(2)}) collective-permute-start(bf16[1408,128]{1,0:T(8,128)(2,1)S(1)} %get-tuple-element.130.refs_1_), channel_id=1, source_target_pairs={{0,16},{8,24},{16,0},{24,8},{1,17},{9,25},{17,1},{25,9},{2,18},{10... | collective-permute-start | bytes 1081352 | tf_op jit(solution)/shard_map/ppermute | solution.py:455
  163.3 20.5 %collective-permute-start.19 = (bf16[128,2048]{1,0:T(8,128)(2,1)S(1)}, bf16[128,2048]{1,0:T(8,128)(2,1)S(1)}, u32[]{:S(2)}, u32[]{:S(2)}) collective-permute-start(bf16[128,2048]{1,0:T(8,128)(2,1)S(1)} %add_convert_fusion.1), channel_id=1, source_target_pairs={{2,4},{3,5},{4,2},{5,3},{10,12},{11,13},{12,10},{13,11},{18,20},{1... | collective-permute-start | bytes 1572872 | tf_op jit(solution)/shard_map/ppermute | solution.py:436
  164.1 19.7 %collective-permute-start.18 = (bf16[128,2048]{1,0:T(8,128)(2,1)S(1)}, bf16[128,2048]{1,0:T(8,128)(2,1)S(1)}, u32[]{:S(2)}, u32[]{:S(2)}) collective-permute-start(bf16[128,2048]{1,0:T(8,128)(2,1)S(1)} %add_convert_fusion.2), channel_id=1, source_target_pairs={{0,2},{1,3},{2,0},{3,1},{4,6},{5,7},{6,4},{7,5},{8,10},{9,11},{10,... | collective-permute-start | bytes 1572872 | tf_op jit(solution)/shard_map/ppermute | solution.py:436
  169.9 9.4 %collective-permute-start.20 = (bf16[1408,128]{1,0:T(8,128)(2,1)}, bf16[1408,128]{1,0:T(8,128)(2,1)S(1)}, u32[]{:S(2)}, u32[]{:S(2)}) collective-permute-start(bf16[1408,128]{1,0:T(8,128)(2,1)} %get-tuple-element.133.one_x), channel_id=1, source_target_pairs={{0,16},{8,24},{16,0},{24,8},{1,17},{9,25},{17,1},{25,9},{2,18},{10... | collective-permute-start | bytes 1081352 | tf_op jit(solution)/shard_map/ppermute | solution.py:455
  171.4 9.2 %collective-permute-start.21 = (bf16[1408,128]{1,0:T(8,128)(2,1)}, bf16[1408,128]{1,0:T(8,128)(2,1)S(1)}, u32[]{:S(2)}, u32[]{:S(2)}) collective-permute-start(bf16[1408,128]{1,0:T(8,128)(2,1)} %get-tuple-element.134.one_y), channel_id=1, source_target_pairs={{0,8},{8,0},{16,24},{24,16},{1,9},{9,1},{17,25},{25,17},{2,10},{10... | collective-permute-start | bytes 1081352 | tf_op jit(solution)/shard_map/ppermute | solution.py:455
  (64 other events, 319.7 us)
Sparse Core Ops, SparseCore 0:
  9.6 59.3 all-gather.1

commit v12 on v11

--- a/solution.py
+++ b/solution.py
@@ -329,16 +329,14 @@
 
 
 def backward_kernel(chunk, adds, cut, *refs):
-    slot_ref, cot_all_ref, mine_ref, other_ref, *refs = refs
+    slot_ref, cot_mine, cot_other, mine_ref, other_ref, *refs = refs
     low_ref, active_ref, slope_ref, adapt_b_ref, down_ref, *refs = refs
     grads, (out_a_ref, out_b_ref, scaled_ref, rows_ref) = refs[: 2 * adds], refs[2 * adds :]
-    half, features = mine_ref.shape[0], cot_all_ref.shape[1]
-    for at, block_ref in enumerate((mine_ref, other_ref)):
+    half, features = cot_mine.shape
+    for at, (cot_ref, block_ref) in enumerate(((cot_mine, mine_ref), (cot_other, other_ref))):
         here = slice(at * half, (at + 1) * half)
         w = joined_weight(block_ref[:, features:], slot_ref[0], slot_ref[1])
-        whose = pl.multiple_of(slot_ref[2 + at] * half, half)
-        cot = cot_all_ref[pl.ds(whose, half)].astype(jnp.float32)
-        scaled_ref[here] = (w * cot).astype(jnp.bfloat16)
+        scaled_ref[here] = (w * cot_ref[...].astype(jnp.float32)).astype(jnp.bfloat16)
         rows_ref[here] = block_ref[:, :features]
     scaled = scaled_ref[...]
     low_gate, low_up = halves(low_ref[...])
@@ -370,7 +368,7 @@
         out_b_ref[: features - cut] = sum_a[cut:].astype(jnp.bfloat16)
 
 
-def backward_stage(slot, cot_all, blocks, saved, down, adapt_b, grads=(), cut=None, chunk=256):
+def backward_stage(slot, cots, blocks, saved, down, adapt_b, grads=(), cut=None, chunk=256):
     hidden_width, features = down.shape
     both, ranks = saved[0].shape
     bf16, f32 = jnp.bfloat16, jnp.float32
@@ -382,7 +380,7 @@
         outs,
         [((both, features), bf16), ((both, features), bf16)],
         both * (down.size + features * ranks + 4 * adapt_b.size),
-        (slot, cot_all, *blocks, *saved, adapt_b, down, *grads),
+        (slot, *cots, *blocks, *saved, adapt_b, down, *grads),
     )
 
 
@@ -423,12 +421,7 @@
     )(*ones, *others)
 
 
-def z_pairs(*moves):
-    return [(2 * a + core, 2 * b + core) for a, b in moves for core in (0, 1)]
-
-
-ALL_SWAP = z_pairs((0, 1), (1, 0), (2, 3), (3, 2))
-MID_SWAP = z_pairs((1, 2), (2, 1))
+RING = [(2 * chip + core, 2 * ((chip + 1) % 4) + core) for chip in range(4) for core in (0, 1)]
 SIBLING = [(e, e ^ 1) for e in range(8)]
 
 
@@ -470,82 +463,83 @@
     slot_total = lax.axis_size("expert")
     capacity = tokens.shape[0] * routing.shape[1] // slot_total
     me = lax.axis_index("expert")
-    chip = me // 2
-    inner = (chip == 1) | (chip == 2)
     gate_up, down = gate_up_weight[0], down_weight[0]
     adapt_a = adapter_down_maps[0]
     adapt_b = adapter_up_maps[0].reshape(adapt_a.shape[1], -1)
 
-    def pick(inside, outside):
-        return jnp.where(inner, inside, outside)
-
-    def after(array, earlier):
-        return fence(array, earlier)[0]
-
-    whose = [me, me ^ 2, pick(me ^ 6, me ^ 4), pick(me ^ 4, me ^ 6)]
-    slots = [jnp.stack([me, jnp.int32(slot_total), device, device ^ 1]) for device in whose]
-
-    def forward(*blocks):
-        *saved, part, away = forward_stage(slots[0], *blocks, gate_up, down, adapt_a, adapt_b)
+    slot = jnp.stack([me, jnp.int32(slot_total)])
+
+    def forward(mine, twin):
+        *saved, part, away = forward_stage(slot, mine, twin, gate_up, down, adapt_a, adapt_b)
         return saved, part, away
 
-    def backward(stage, rows, saved, grads=(), cut=None):
-        return backward_stage(slots[stage], cots, rows, saved, down, adapt_b, grads, cut)
-
-    cots = lax.all_gather(cotangent, "expert", tiled=True)
+    def backward(cots, rows, saved, grads=(), cut=None):
+        return backward_stage(slot, cots, rows, saved, down, adapt_b, grads, cut)
+
+    def step(block):
+        return send(block, RING)
+
     tokens = tagged_tokens(
         tokens, routing, router_route_weights, route_replica_choice, device_expert_table, capacity
     )
-    tok_swap = send(tokens, ALL_SWAP)
-    twin = sibling(tokens)
-    rows0 = (tokens, twin)
-    tok_mid = send(after(tokens, twin), MID_SWAP)
+    tok1 = step(tokens)
+    rows0 = (tokens, sibling(tokens))
+    tok1, rows0, cotangent = fence(tok1, rows0, cotangent)
+
+    tok2 = step(tok1)
+    rows1 = (tok1, sibling(tok1))
     saved0, part0, away0 = forward(*rows0)
-    tok_swap, tok_mid, part0, away0 = fence(tok_swap, tok_mid, part0, away0)
-
-    tok_out2 = send(tok_mid, ALL_SWAP)
-    twin = sibling(tok_swap)
-    rows1 = (tok_swap, twin)
-    tok_mid2 = send(after(tok_swap, twin), MID_SWAP)
+    tok2, rows1, part0, away0, cotangent = fence(tok2, rows1, part0, away0, cotangent)
+
+    tok3 = step(tok2)
+    rows2 = (tok2, sibling(tok2))
     saved1, part1, away1 = forward(*rows1)
-    tok_mid, tok_out2, tok_mid2, part1, away1 = fence(tok_mid, tok_out2, tok_mid2, part1, away1)
-
-    tok_out3 = send(tok_mid2, ALL_SWAP)
-    tok_second = pick(tok_mid, tok_out2)
-    rows2 = (tok_second, sibling(tok_second))
+    tok3, rows2, part1, away1, cotangent = fence(tok3, rows2, part1, away1, cotangent)
+
+    cot1 = step(cotangent)
+    rows3 = (tok3, sibling(tok3))
+    cots0 = (cotangent, sibling(cotangent))
     saved2, part2, away2 = forward(*rows2)
-    tok_mid2, tok_out3, part2, away2, cots = fence(tok_mid2, tok_out3, part2, away2, cots)
-
-    tok_third = pick(tok_mid2, tok_out3)
-    rows3 = (tok_third, sibling(tok_third))
+    cot1, rows3, cots0, part2, away2 = fence(cot1, rows3, cots0, part2, away2)
+
+    cot2 = step(cot1)
+    cots1 = (cot1, sibling(cot1))
     saved3, part3, away3 = forward(*rows3)
-    part3 = add_rounded(part3, sibling(away3))
-    part3, part2, away2 = fence(part3, part2, away2)
-
-    third_in = send(part3, ALL_SWAP)
+    grads = backward(cots0, rows0, saved0)
+    cot2, cots1, part1, away1, part2, away2, part3, away3, grads = fence(
+        cot2, cots1, part1, away1, part2, away2, part3, away3, grads
+    )
+
+    cot3 = step(cot2)
+    cots2 = (cot2, sibling(cot2))
+    part1 = add_rounded(part1, sibling(away1))
+    grads = backward(cots1, rows1, saved1, grads)
+    grads = backward(cots2, rows2, saved2, grads)
+    cot3, part1, part2, away2, part3, away3, grads = fence(
+        cot3, part1, part2, away2, part3, away3, grads
+    )
+
+    sum1 = step(part1)
+    cots3 = (cot3, sibling(cot3))
     part2 = add_rounded(part2, sibling(away2))
     features, hidden_width = adapt_a.shape[0], adapt_b.shape[1]
     cut = (features + hidden_width) // 2
-    grads = backward(0, rows0, saved0)
-    grads = backward(1, rows1, saved1, grads)
-    grads = backward(2, rows2, saved2, grads)
-    grads = backward(3, rows3, saved3, grads, cut)
-    third_in, part3, part2, part1, away1, grads = fence(third_in, part3, part2, part1, away1, grads)
-
-    second_in = send(part2, ALL_SWAP)
-    third_mid = send(add_rounded(part3, third_in), MID_SWAP)
+    grads = backward(cots3, rows3, saved3, grads, cut)
+    sum1, part2, part0, away0, part3, away3, grads = fence(
+        sum1, part2, part0, away0, part3, away3, grads
+    )
+
+    sum2 = step(add_rounded(part2, sum1))
     got = dp_swap(grads[0], 1), dp_swap(grads[1], 2)
-    part1 = add_rounded(part1, sibling(away1))
+    part3 = add_rounded(part3, sibling(away3))
     part0 = add_rounded(part0, sibling(away0))
-    second_in, third_mid, part0, part1, part2, grads, got = fence(
-        second_in, third_mid, part0, part1, part2, grads, got
-    )
-    first_swap = send(add_rounded(part1, third_mid), ALL_SWAP)
-    second_mid = send(add_rounded(part2, second_in), MID_SWAP)
+    sum2, part0, part3, grads, got = fence(sum2, part0, part3, grads, got)
+
+    sum3 = step(add_rounded(part3, sum2))
     pairs = pair_sums(grads, got)
     got = dp_swap(pairs[0], 2), dp_swap(pairs[1], 1)
     grad_a, grad_b = finished(pairs, got, features, hidden_width)
-    mixed = add_rounded(part0, first_swap, second_mid)
+    mixed = add_rounded(part0, sum3)
     return mixed, grad_a[None], grad_b.reshape(adapter_up_maps.shape)
 
 

time: 193 us -> 157 us (0.81)
  waiting for transfers between devices: 40.1 us -> 97.6 us
  starting transfers between devices: 49.5 us -> 8.76 us
  local copies, waits for them, and re-layouts: 41.3 us -> 8.98 us
  between operations: 14.5 us -> 0.94 us
  other arithmetic: 5.65 us -> 1.78 us
  Pallas kernels: 40.6 us -> 38.6 us
    ppermute x18 -> x21, waiting for transfers between devices: 23.4 us -> 81.2 us  [send(): return lax.ppermute(array, 'expert', pairs)]
    ppermute x18 -> x21, starting transfers between devices: 43.4 us -> 4.7 us  [send(): return lax.ppermute(array, 'expert', pairs)]
    unnamed x130 -> x32, local copies, waits for them, and re-layouts: 41.3 us -> 8.98 us
    select_n x2 -> x0, other arithmetic: 2.24 us -> none  [pick(): return jnp.where(inner, inside, outside)]
    pallas_call x8, Pallas kernels: 33.7 us -> 31.6 us  [stage_call(): pl.pallas_call(kernel, out_shape=out_shape, in_specs=[SMEM] + [VMEM] * (l...]
    ppermute x4, starting transfers between devices: 6.05 us -> 4.05 us  [dp_swap(): return lax.ppermute(array, 'dp', [(d, d ^ bit) for d in range(4)])]
  transfers between devices with their start and end apart: 23 -> 25, of which waited for: 11 -> 14; matrix products, arithmetic and copies ran while one was open for 1% -> 0% of each run, Pallas kernels for 19% -> 23%
where the time goes in v12:
time: 157 us
  waiting for transfers between devices  97.6 us (62%)
  Pallas kernels  38.6 us (25%)
  local copies, waits for them, and re-layouts  8.98 us (6%)
  starting transfers between devices  8.76 us (6%)
  other arithmetic  1.78 us (1%)
    ppermute x21, waiting for transfers between devices, send(): return lax.ppermute(array, 'expert', pairs)  81.2 us
    pallas_call x8, Pallas kernels, stage_call(): pl.pallas_call(kernel, out_shape=out_shape, in_specs=[SMEM] + [VMEM] * (l...  31.6 us
    ppermute x4, waiting for transfers between devices, dp_swap(): return lax.ppermute(array, 'dp', [(d, d ^ bit) for d in range(4)])  16.4 us
    unnamed x32, local copies, waits for them, and re-layouts  8.98 us
    ppermute x21, starting transfers between devices, send(): return lax.ppermute(array, 'expert', pairs)  4.7 us
    ppermute x4, starting transfers between devices, dp_swap(): return lax.ppermute(array, 'dp', [(d, d ^ bit) for d in range(4)])  4.05 us
  transfers between devices with their start and end apart: 25, of which 14 were waited for; matrix products, arithmetic and copies ran while one was open for 0% of the time, Pallas kernels for 23%

profile of v12, /device:TPU:0, one launch (start us, length us, event | category | flops | bytes accessed | tf_op | source)
XLA Modules:
  0.0 156.7 jit_solution(16423884096084961850)
XLA Ops:
  0.6 2.2 %shard_map.121.mine_ref.refs_3_ = bf16[128,2176]{1,0:T(8,128)(2,1)} custom-call(s32[8]{0:T(128)} %table_ref.1, s32[8,128]{1,0:T(8,128)} %bitcast.34, s32[8,128]{1,0:T(8,128)} %bitcast.35, f32[8,128]{1,0:T(8,128)} %bitcast.36, bf16[128,2048]{1,0:T(8,128)(2,1)} %tokens_ref.1), custom_call_target="tpu_custom_call" | custom-call | tf_op jit(solution)/shard_map/pallas_call | solution.py:258
  3.3 2.6 %collective-permute-start = (bf16[128,2176]{1,0:T(8,128)(2,1)}, bf16[128,2176]{1,0:T(8,128)(2,1)S(1)}, u32[]{:S(2)}, u32[]{:S(2)}) collective-permute-start(bf16[128,2176]{1,0:T(8,128)(2,1)} %shard_map.121.mine_ref.refs_3_), channel_id=1, source_target_pairs={{0,2},{1,3},{2,4},{3,5},{4,6},{5,7},{6,0},{7,1},{8,10},{9,11},{10,... | collective-permute-start | bytes 1671176 | tf_op jit(solution)/shard_map/ppermute | solution.py:429
  5.9 15.5 %collective-permute-done.mine_ref.refs_3_ = bf16[128,2176]{1,0:T(8,128)(2,1)S(1)} collective-permute-done((bf16[128,2176]{1,0:T(8,128)(2,1)}, bf16[128,2176]{1,0:T(8,128)(2,1)S(1)}, u32[]{:S(2)}, u32[]{:S(2)}) %collective-permute-start) | collective-permute-done | bytes 557088 | tf_op jit(solution)/shard_map/ppermute | solution.py:429
  21.5 1.9 %copy-done = bf16[1,768,2048]{2,1,0:T(8,128)(2,1)S(1)} copy-done((bf16[1,768,2048]{2,1,0:T(8,128)(2,1)S(1)}, bf16[1,768,2048]{2,1,0:T(8,128)(2,1)}, u32[]{:S(2)}) %copy-start) | copy-done | bytes 3145752
  23.4 2.8 %copy-done.2 = bf16[1,2048,1536]{2,1,0:T(8,128)(2,1)S(1)} copy-done((bf16[1,2048,1536]{2,1,0:T(8,128)(2,1)S(1)}, bf16[1,2048,1536]{2,1,0:T(8,128)(2,1)}, u32[]{:S(2)}) %copy-start.2) | copy-done | bytes 6291480
  29.2 4.3 %shard_map.122 = (bf16[256,128]{1,0:T(8,128)(2,1)S(1)}, f32[256,768]{1,0:T(8,128)S(1)}, f32[256,768]{1,0:T(8,128)S(1)}, bf16[128,2048]{1,0:T(8,128)(2,1)S(1)}, bf16[128,2048]{1,0:T(8,128)(2,1)S(1)}) custom-call(s32[2]{0:T(128)S(1)} %pad_add_fusion.slot_ref.refs_0_, bf16[128,2176]{1,0:T(8,128)(2,1)S(1)} %copy-done.8, ...), custom_call_target="tpu_custom_call" | custom-call | flops 2550136832 | bytes 13959176 | tf_op jit(solution)/shard_map/pallas_call | solution.py:269
  33.5 4.8 %collective-permute-done.2.mine_ref.refs_3_ = bf16[128,2176]{1,0:T(8,128)(2,1)S(1)} collective-permute-done((bf16[128,2176]{1,0:T(8,128)(2,1)S(1)}, bf16[128,2176]{1,0:T(8,128)(2,1)S(1)}, u32[]{:S(2)}, u32[]{:S(2)}) %collective-permute-start.2) | collective-permute-done | bytes 557088 | tf_op jit(solution)/shard_map/ppermute | solution.py:429
  38.3 4.3 %shard_map.123 = (bf16[256,128]{1,0:T(8,128)(2,1)S(1)}, f32[256,768]{1,0:T(8,128)S(1)}, f32[256,768]{1,0:T(8,128)S(1)}, bf16[128,2048]{1,0:T(8,128)(2,1)S(1)}, bf16[128,2048]{1,0:T(8,128)(2,1)S(1)}) custom-call(s32[2]{0:T(128)S(1)} %pad_add_fusion.slot_ref.refs_0_, bf16[128,2176]{1,0:T(8,128)(2,1)S(1)} %collective-permute-done.mine_ref.refs_3_, ...), custom_call_target="tpu_custom_call" | custom-call | flops 2550136832 | bytes 13959176 | tf_op jit(solution)/shard_map/pallas_call | solution.py:269
  42.6 12.5 %collective-permute-done.4.mine_ref.refs_3_ = bf16[128,2176]{1,0:T(8,128)(2,1)S(1)} collective-permute-done((bf16[128,2176]{1,0:T(8,128)(2,1)S(1)}, bf16[128,2176]{1,0:T(8,128)(2,1)S(1)}, u32[]{:S(2)}, u32[]{:S(2)}) %collective-permute-start.4) | collective-permute-done | bytes 557088 | tf_op jit(solution)/shard_map/ppermute | solution.py:429
  55.6 4.3 %shard_map.124 = (bf16[256,128]{1,0:T(8,128)(2,1)S(1)}, f32[256,768]{1,0:T(8,128)S(1)}, f32[256,768]{1,0:T(8,128)S(1)}, bf16[128,2048]{1,0:T(8,128)(2,1)S(1)}, bf16[128,2048]{1,0:T(8,128)(2,1)S(1)}) custom-call(s32[2]{0:T(128)S(1)} %pad_add_fusion.slot_ref.refs_0_, bf16[128,2176]{1,0:T(8,128)(2,1)S(1)} %collective-permute-done.2.mine_ref.refs_3_, ...), custom_call_target="tpu_custom_call" | custom-call | flops 2550136832 | bytes 13959176 | tf_op jit(solution)/shard_map/pallas_call | solution.py:269
  59.9 11.3 %collective-permute-done.6.refs_1_ = bf16[128,2048]{1,0:T(8,128)(2,1)S(1)} collective-permute-done((bf16[128,2048]{1,0:T(8,128)(2,1)S(1)}, bf16[128,2048]{1,0:T(8,128)(2,1)S(1)}, u32[]{:S(2)}, u32[]{:S(2)}) %collective-permute-start.6) | collective-permute-done | bytes 524320 | tf_op jit(solution)/shard_map/ppermute | solution.py:429
  71.3 3.6 %shard_map.126 = (f32[2048,128]{1,0:T(8,128)S(1)}, f32[128,768]{1,0:T(8,128)S(1)}) custom-call(s32[2]{0:T(128)S(1)} %pad_add_fusion.slot_ref.refs_0_, bf16[128,2048]{1,0:T(8,128)(2,1)S(1)} %copy-done.9, bf16[128,2048]{1,0:T(8,128)(2,1)S(1)} %collective-permute-done.8.refs_2_, bf16[128,2176]{1,0:T(8,128)(2,1)S(1)} %copy-done.8, ...), custom_call_target="tpu_custom_call" | custom-call | flops 1140850688 | bytes 8585224 | tf_op jit(solution)/shard_map/pallas_call | solution.py:269
  74.9 4.3 %shard_map.125 = (bf16[256,128]{1,0:T(8,128)(2,1)S(1)}, f32[256,768]{1,0:T(8,128)S(1)}, f32[256,768]{1,0:T(8,128)S(1)}, bf16[128,2048]{1,0:T(8,128)(2,1)S(1)}, bf16[128,2048]{1,0:T(8,128)(2,1)S(1)}) custom-call(s32[2]{0:T(128)S(1)} %pad_add_fusion.slot_ref.refs_0_, bf16[128,2176]{1,0:T(8,128)(2,1)S(1)} %collective-permute-done.4.mine_ref.refs_3_, ...), custom_call_target="tpu_custom_call" | custom-call | flops 2550136832 | bytes 13959176 | tf_op jit(solution)/shard_map/pallas_call | solution.py:269
  79.2 8.2 %collective-permute-done.9.refs_1_ = bf16[128,2048]{1,0:T(8,128)(2,1)S(1)} collective-permute-done((bf16[128,2048]{1,0:T(8,128)(2,1)S(1)}, bf16[128,2048]{1,0:T(8,128)(2,1)S(1)}, u32[]{:S(2)}, u32[]{:S(2)}) %collective-permute-start.9) | collective-permute-done | bytes 524320 | tf_op jit(solution)/shard_map/ppermute | solution.py:429
  87.9 3.6 %shard_map.127 = (f32[2048,128]{1,0:T(8,128)S(1)}, f32[128,768]{1,0:T(8,128)S(1)}) custom-call(s32[2]{0:T(128)S(1)} %pad_add_fusion.slot_ref.refs_0_, bf16[128,2048]{1,0:T(8,128)(2,1)S(1)} %collective-permute-done.6.refs_1_, bf16[128,2048]{1,0:T(8,128)(2,1)S(1)} %collective-permute-done.10.refs_2_, ...), custom_call_target="tpu_custom_call" | custom-call | flops 1140850688 | bytes 10027016 | tf_op jit(solution)/shard_map/pallas_call | solution.py:269
  91.5 3.6 %shard_map.128 = (f32[2048,128]{1,0:T(8,128)S(1)}, f32[128,768]{1,0:T(8,128)S(1)}) custom-call(s32[2]{0:T(128)S(1)} %pad_add_fusion.slot_ref.refs_0_, bf16[128,2048]{1,0:T(8,128)(2,1)S(1)} %collective-permute-done.9.refs_1_, bf16[128,2048]{1,0:T(8,128)(2,1)S(1)} %collective-permute-done.13.refs_2_, ...), custom_call_target="tpu_custom_call" | custom-call | flops 1140850688 | bytes 10027016 | tf_op jit(solution)/shard_map/pallas_call | solution.py:269
  95.2 8.3 %collective-permute-done.11.refs_1_ = bf16[128,2048]{1,0:T(8,128)(2,1)S(1)} collective-permute-done((bf16[128,2048]{1,0:T(8,128)(2,1)S(1)}, bf16[128,2048]{1,0:T(8,128)(2,1)S(1)}, u32[]{:S(2)}, u32[]{:S(2)}) %collective-permute-start.11) | collective-permute-done | bytes 524320 | tf_op jit(solution)/shard_map/ppermute | solution.py:429
  105.4 3.7 %shard_map.129 = (bf16[1408,128]{1,0:T(8,128)(2,1)S(1)}, bf16[1408,128]{1,0:T(8,128)(2,1)S(1)}) custom-call(s32[2]{0:T(128)S(1)} %pad_add_fusion.slot_ref.refs_0_, bf16[128,2048]{1,0:T(8,128)(2,1)S(1)} %collective-permute-done.11.refs_1_, bf16[128,2048]{1,0:T(8,128)(2,1)S(1)} %collective-permute-done.16.refs_2_, ...), custom_call_target="tpu_custom_call" | custom-call | flops 1140850688 | bytes 9306120 | tf_op jit(solution)/shard_map/pallas_call | solution.py:269
  109.3 10.3 %collective-permute-done.14 = bf16[128,2048]{1,0:T(8,128)(2,1)S(1)} collective-permute-done((bf16[128,2048]{1,0:T(8,128)(2,1)S(1)}, bf16[128,2048]{1,0:T(8,128)(2,1)S(1)}, u32[]{:S(2)}, u32[]{:S(2)}) %collective-permute-start.14) | collective-permute-done | bytes 524320 | tf_op jit(solution)/shard_map/ppermute | solution.py:429
  124.7 5.8 %collective-permute-done.20.refs_2_ = bf16[1408,128]{1,0:T(8,128)(2,1)S(1)} collective-permute-done((bf16[1408,128]{1,0:T(8,128)(2,1)S(1)}, bf16[1408,128]{1,0:T(8,128)(2,1)S(1)}, u32[]{:S(2)}, u32[]{:S(2)}) %collective-permute-start.20) | collective-permute-done | bytes 360480 | tf_op jit(solution)/shard_map/ppermute | solution.py:448
  131.7 7.3 %collective-permute-done.17 = bf16[128,2048]{1,0:T(8,128)(2,1)S(1)} collective-permute-done((bf16[128,2048]{1,0:T(8,128)(2,1)S(1)}, bf16[128,2048]{1,0:T(8,128)(2,1)S(1)}, u32[]{:S(2)}, u32[]{:S(2)}) %collective-permute-start.17) | collective-permute-done | bytes 524320 | tf_op jit(solution)/shard_map/ppermute | solution.py:429
  139.2 2.3 %shard_map.130 = (bf16[1408,128]{1,0:T(8,128)(2,1)}, bf16[1408,128]{1,0:T(8,128)(2,1)}) custom-call(bf16[1408,128]{1,0:T(8,128)(2,1)} %copy-done.10, bf16[1408,128]{1,0:T(8,128)(2,1)} %copy-done.11, bf16[1408,128]{1,0:T(8,128)(2,1)} %copy-done.12, bf16[1408,128]{1,0:T(8,128)(2,1)} %copy-done.13), custom_call_target="tpu_custom_call" | custom-call | tf_op jit(solution)/shard_map/pallas_call | solution.py:394
  142.6 9.2 %collective-permute-done.23.other_x = bf16[1408,128]{1,0:T(8,128)(2,1)S(1)} collective-permute-done((bf16[1408,128]{1,0:T(8,128)(2,1)}, bf16[1408,128]{1,0:T(8,128)(2,1)S(1)}, u32[]{:S(2)}, u32[]{:S(2)}) %collective-permute-start.23) | collective-permute-done | bytes 360480 | tf_op jit(solution)/shard_map/ppermute | solution.py:448
  153.2 2.5 %shard_map.131 = (f32[2048,128]{1,0:T(8,128)}, f32[128,768]{1,0:T(8,128)}) custom-call(bf16[1408,128]{1,0:T(8,128)(2,1)} %get-tuple-element.177.one_x, bf16[1408,128]{1,0:T(8,128)(2,1)} %get-tuple-element.178.one_y, bf16[1408,128]{1,0:T(8,128)(2,1)} %copy-done.14, bf16[1408,128]{1,0:T(8,128)(2,1)} %copy-done.15), custom_call_target="tpu_custom_call" | custom-call | tf_op jit(solution)/shard_map/pallas_call | solution.py:415
  (77 shorter events, 16.7 us)
Async XLA Ops:
  2.9 3.0 %collective-permute-start.1 = (bf16[128,2176]{1,0:T(8,128)(2,1)}, bf16[128,2176]{1,0:T(8,128)(2,1)S(1)}, u32[]{:S(2)}, u32[]{:S(2)}) collective-permute-start(bf16[128,2176]{1,0:T(8,128)(2,1)} %shard_map.121.mine_ref.refs_3_), channel_id=1, source_target_pairs={{0,1},{1,0},{2,3},{3,2},{4,5},{5,4},{6,7},{7,6},{8,9},{9,8},{10,11... | collective-permute-start | bytes 1671176 | tf_op jit(solution)/shard_map/ppermute | solution.py:429
  3.3 18.1 %collective-permute-start = (bf16[128,2176]{1,0:T(8,128)(2,1)}, bf16[128,2176]{1,0:T(8,128)(2,1)S(1)}, u32[]{:S(2)}, u32[]{:S(2)}) collective-permute-start(bf16[128,2176]{1,0:T(8,128)(2,1)} %shard_map.121.mine_ref.refs_3_), channel_id=1, source_target_pairs={{0,2},{1,3},{2,4},{3,5},{4,6},{5,7},{6,0},{7,1},{8,10},{9,11},{10,... | collective-permute-start | bytes 1671176 | tf_op jit(solution)/shard_map/ppermute | solution.py:429
  21.4 12.1 %collective-permute-start.3 = (bf16[128,2176]{1,0:T(8,128)(2,1)S(1)}, bf16[128,2176]{1,0:T(8,128)(2,1)S(1)}, u32[]{:S(2)}, u32[]{:S(2)}) collective-permute-start(bf16[128,2176]{1,0:T(8,128)(2,1)S(1)} %collective-permute-done.mine_ref.refs_3_), channel_id=1, source_target_pairs={{0,1},{1,0},{2,3},{3,2},{4,5},{5,4},{6,7},{7,6},{8,9},{9,8},{10,11... | collective-permute-start | bytes 1671176 | tf_op jit(solution)/shard_map/ppermute | solution.py:429
  21.4 16.8 %collective-permute-start.2 = (bf16[128,2176]{1,0:T(8,128)(2,1)S(1)}, bf16[128,2176]{1,0:T(8,128)(2,1)S(1)}, u32[]{:S(2)}, u32[]{:S(2)}) collective-permute-start(bf16[128,2176]{1,0:T(8,128)(2,1)S(1)} %collective-permute-done.mine_ref.refs_3_), channel_id=1, source_target_pairs={{0,2},{1,3},{2,4},{3,5},{4,6},{5,7},{6,0},{7,1},{8,10},{9,11},{10,... | collective-permute-start | bytes 1671176 | tf_op jit(solution)/shard_map/ppermute | solution.py:429
  38.3 4.3 %collective-permute-start.5 = (bf16[128,2176]{1,0:T(8,128)(2,1)S(1)}, bf16[128,2176]{1,0:T(8,128)(2,1)S(1)}, u32[]{:S(2)}, u32[]{:S(2)}) collective-permute-start(bf16[128,2176]{1,0:T(8,128)(2,1)S(1)} %collective-permute-done.2.mine_ref.refs_3_), channel_id=1, source_target_pairs={{0,1},{1,0},{2,3},{3,2},{4,5},{5,4},{6,7},{7,6},{8,9},{9,8},{10,11... | collective-permute-start | bytes 1671176 | tf_op jit(solution)/shard_map/ppermute | solution.py:429
  38.3 16.8 %collective-permute-start.4 = (bf16[128,2176]{1,0:T(8,128)(2,1)S(1)}, bf16[128,2176]{1,0:T(8,128)(2,1)S(1)}, u32[]{:S(2)}, u32[]{:S(2)}) collective-permute-start(bf16[128,2176]{1,0:T(8,128)(2,1)S(1)} %collective-permute-done.2.mine_ref.refs_3_), channel_id=1, source_target_pairs={{0,2},{1,3},{2,4},{3,5},{4,6},{5,7},{6,0},{7,1},{8,10},{9,11},{10,... | collective-permute-start | bytes 1671176 | tf_op jit(solution)/shard_map/ppermute | solution.py:429
  55.1 16.1 %collective-permute-start.7 = (bf16[128,2176]{1,0:T(8,128)(2,1)S(1)}, bf16[128,2176]{1,0:T(8,128)(2,1)S(1)}, u32[]{:S(2)}, u32[]{:S(2)}) collective-permute-start(bf16[128,2176]{1,0:T(8,128)(2,1)S(1)} %collective-permute-done.4.mine_ref.refs_3_), channel_id=1, source_target_pairs={{0,1},{1,0},{2,3},{3,2},{4,5},{5,4},{6,7},{7,6},{8,9},{9,8},{10,11... | collective-permute-start | bytes 1671176 | tf_op jit(solution)/shard_map/ppermute | solution.py:429
  55.1 4.8 %collective-permute-start.8 = (bf16[128,2048]{1,0:T(8,128)(2,1)S(1)}, bf16[128,2048]{1,0:T(8,128)(2,1)S(1)}, u32[]{:S(2)}, u32[]{:S(2)}) collective-permute-start(bf16[128,2048]{1,0:T(8,128)(2,1)S(1)} %copy-done.9), channel_id=1, source_target_pairs={{0,1},{1,0},{2,3},{3,2},{4,5},{5,4},{6,7},{7,6},{8,9},{9,8},{10,11... | collective-permute-start | bytes 1572872 | tf_op jit(solution)/shard_map/ppermute | solution.py:429
  55.6 15.6 %collective-permute-start.6 = (bf16[128,2048]{1,0:T(8,128)(2,1)S(1)}, bf16[128,2048]{1,0:T(8,128)(2,1)S(1)}, u32[]{:S(2)}, u32[]{:S(2)}) collective-permute-start(bf16[128,2048]{1,0:T(8,128)(2,1)S(1)} %copy-done.9), channel_id=1, source_target_pairs={{0,2},{1,3},{2,4},{3,5},{4,6},{5,7},{6,0},{7,1},{8,10},{9,11},{10,... | collective-permute-start | bytes 1572872 | tf_op jit(solution)/shard_map/ppermute | solution.py:429
  71.2 7.9 %collective-permute-start.10 = (bf16[128,2048]{1,0:T(8,128)(2,1)S(1)}, bf16[128,2048]{1,0:T(8,128)(2,1)S(1)}, u32[]{:S(2)}, u32[]{:S(2)}) collective-permute-start(bf16[128,2048]{1,0:T(8,128)(2,1)S(1)} %collective-permute-done.6.refs_1_), channel_id=1, source_target_pairs={{0,1},{1,0},{2,3},{3,2},{4,5},{5,4},{6,7},{7,6},{8,9},{9,8},{10,11... | collective-permute-start | bytes 1572872 | tf_op jit(solution)/shard_map/ppermute | solution.py:429
  71.3 16.1 %collective-permute-start.9 = (bf16[128,2048]{1,0:T(8,128)(2,1)S(1)}, bf16[128,2048]{1,0:T(8,128)(2,1)S(1)}, u32[]{:S(2)}, u32[]{:S(2)}) collective-permute-start(bf16[128,2048]{1,0:T(8,128)(2,1)S(1)} %collective-permute-done.6.refs_1_), channel_id=1, source_target_pairs={{0,2},{1,3},{2,4},{3,5},{4,6},{5,7},{6,0},{7,1},{8,10},{9,11},{10,... | collective-permute-start | bytes 1572872 | tf_op jit(solution)/shard_map/ppermute | solution.py:429
  87.4 4.1 %collective-permute-start.13 = (bf16[128,2048]{1,0:T(8,128)(2,1)S(1)}, bf16[128,2048]{1,0:T(8,128)(2,1)S(1)}, u32[]{:S(2)}, u32[]{:S(2)}) collective-permute-start(bf16[128,2048]{1,0:T(8,128)(2,1)S(1)} %collective-permute-done.9.refs_1_), channel_id=1, source_target_pairs={{0,1},{1,0},{2,3},{3,2},{4,5},{5,4},{6,7},{7,6},{8,9},{9,8},{10,11... | collective-permute-start | bytes 1572872 | tf_op jit(solution)/shard_map/ppermute | solution.py:429
  87.4 7.7 %collective-permute-start.12 = (bf16[128,2048]{1,0:T(8,128)(2,1)S(1)}, bf16[128,2048]{1,0:T(8,128)(2,1)S(1)}, u32[]{:S(2)}, u32[]{:S(2)}) collective-permute-start(bf16[128,2048]{1,0:T(8,128)(2,1)S(1)} %get-tuple-element.128), channel_id=1, source_target_pairs={{0,1},{1,0},{2,3},{3,2},{4,5},{5,4},{6,7},{7,6},{8,9},{9,8},{10,11... | collective-permute-start | bytes 1572872 | tf_op jit(solution)/shard_map/ppermute | solution.py:429
  87.9 15.6 %collective-permute-start.11 = (bf16[128,2048]{1,0:T(8,128)(2,1)S(1)}, bf16[128,2048]{1,0:T(8,128)(2,1)S(1)}, u32[]{:S(2)}, u32[]{:S(2)}) collective-permute-start(bf16[128,2048]{1,0:T(8,128)(2,1)S(1)} %collective-permute-done.9.refs_1_), channel_id=1, source_target_pairs={{0,2},{1,3},{2,4},{3,5},{4,6},{5,7},{6,0},{7,1},{8,10},{9,11},{10,... | collective-permute-start | bytes 1572872 | tf_op jit(solution)/shard_map/ppermute | solution.py:429
  103.5 5.6 %collective-permute-start.15 = (bf16[128,2048]{1,0:T(8,128)(2,1)S(1)}, bf16[128,2048]{1,0:T(8,128)(2,1)S(1)}, u32[]{:S(2)}, u32[]{:S(2)}) collective-permute-start(bf16[128,2048]{1,0:T(8,128)(2,1)S(1)} %get-tuple-element.149), channel_id=1, source_target_pairs={{0,1},{1,0},{2,3},{3,2},{4,5},{5,4},{6,7},{7,6},{8,9},{9,8},{10,11... | collective-permute-start | bytes 1572872 | tf_op jit(solution)/shard_map/ppermute | solution.py:429
  104.0 15.6 %collective-permute-start.14 = (bf16[128,2048]{1,0:T(8,128)(2,1)S(1)}, bf16[128,2048]{1,0:T(8,128)(2,1)S(1)}, u32[]{:S(2)}, u32[]{:S(2)}) collective-permute-start(bf16[128,2048]{1,0:T(8,128)(2,1)S(1)} %add_convert_fusion.6), channel_id=1, source_target_pairs={{0,2},{1,3},{2,4},{3,5},{4,6},{5,7},{6,0},{7,1},{8,10},{9,11},{10,... | collective-permute-start | bytes 1572872 | tf_op jit(solution)/shard_map/ppermute | solution.py:429
  119.7 3.2 %collective-permute-start.18 = (bf16[128,2048]{1,0:T(8,128)(2,1)S(1)}, bf16[128,2048]{1,0:T(8,128)(2,1)S(1)}, u32[]{:S(2)}, u32[]{:S(2)}) collective-permute-start(bf16[128,2048]{1,0:T(8,128)(2,1)S(1)} %get-tuple-element.165), channel_id=1, source_target_pairs={{0,1},{1,0},{2,3},{3,2},{4,5},{5,4},{6,7},{7,6},{8,9},{9,8},{10,11... | collective-permute-start | bytes 1572872 | tf_op jit(solution)/shard_map/ppermute | solution.py:429
  119.7 10.8 %collective-permute-start.20 = (bf16[1408,128]{1,0:T(8,128)(2,1)S(1)}, bf16[1408,128]{1,0:T(8,128)(2,1)S(1)}, u32[]{:S(2)}, u32[]{:S(2)}) collective-permute-start(bf16[1408,128]{1,0:T(8,128)(2,1)S(1)} %get-tuple-element.173.refs_0_), channel_id=1, source_target_pairs={{0,8},{8,0},{16,24},{24,16},{1,9},{9,1},{17,25},{25,17},{2,10},{10... | collective-permute-start | bytes 1081352 | tf_op jit(solution)/shard_map/ppermute | solution.py:448
  121.2 10.5 %collective-permute-start.21 = (bf16[1408,128]{1,0:T(8,128)(2,1)S(1)}, bf16[1408,128]{1,0:T(8,128)(2,1)S(1)}, u32[]{:S(2)}, u32[]{:S(2)}) collective-permute-start(bf16[1408,128]{1,0:T(8,128)(2,1)S(1)} %get-tuple-element.174.refs_1_), channel_id=1, source_target_pairs={{0,16},{8,24},{16,0},{24,8},{1,17},{9,25},{17,1},{25,9},{2,18},{10... | collective-permute-start | bytes 1081352 | tf_op jit(solution)/shard_map/ppermute | solution.py:448
  122.7 1.9 %collective-permute-start.19 = (bf16[128,2048]{1,0:T(8,128)(2,1)S(1)}, bf16[128,2048]{1,0:T(8,128)(2,1)S(1)}, u32[]{:S(2)}, u32[]{:S(2)}) collective-permute-start(bf16[128,2048]{1,0:T(8,128)(2,1)S(1)} %get-tuple-element.167), channel_id=1, source_target_pairs={{0,1},{1,0},{2,3},{3,2},{4,5},{5,4},{6,7},{7,6},{8,9},{9,8},{10,11... | collective-permute-start | bytes 1572872 | tf_op jit(solution)/shard_map/ppermute | solution.py:429
  122.8 16.2 %collective-permute-start.17 = (bf16[128,2048]{1,0:T(8,128)(2,1)S(1)}, bf16[128,2048]{1,0:T(8,128)(2,1)S(1)}, u32[]{:S(2)}, u32[]{:S(2)}) collective-permute-start(bf16[128,2048]{1,0:T(8,128)(2,1)S(1)} %add_convert_fusion.4), channel_id=1, source_target_pairs={{0,2},{1,3},{2,4},{3,5},{4,6},{5,7},{6,0},{7,1},{8,10},{9,11},{10,... | collective-permute-start | bytes 1572872 | tf_op jit(solution)/shard_map/ppermute | solution.py:429
  139.1 16.6 %collective-permute-start.22 = (bf16[128,2048]{1,0:T(8,128)(2,1)S(1)}, bf16[128,2048]{1,0:T(8,128)(2,1)S(1)}, u32[]{:S(2)}, u32[]{:S(2)}) collective-permute-start(bf16[128,2048]{1,0:T(8,128)(2,1)S(1)} %add_convert_fusion.1), channel_id=1, source_target_pairs={{0,2},{1,3},{2,4},{3,5},{4,6},{5,7},{6,0},{7,1},{8,10},{9,11},{10,... | collective-permute-start | bytes 1572872 | tf_op jit(solution)/shard_map/ppermute | solution.py:429
  141.5 10.3 %collective-permute-start.23 = (bf16[1408,128]{1,0:T(8,128)(2,1)}, bf16[1408,128]{1,0:T(8,128)(2,1)S(1)}, u32[]{:S(2)}, u32[]{:S(2)}) collective-permute-start(bf16[1408,128]{1,0:T(8,128)(2,1)} %get-tuple-element.177.one_x), channel_id=1, source_target_pairs={{0,16},{8,24},{16,0},{24,8},{1,17},{9,25},{17,1},{25,9},{2,18},{10... | collective-permute-start | bytes 1081352 | tf_op jit(solution)/shard_map/ppermute | solution.py:448
  142.0 10.0 %collective-permute-start.24 = (bf16[1408,128]{1,0:T(8,128)(2,1)}, bf16[1408,128]{1,0:T(8,128)(2,1)S(1)}, u32[]{:S(2)}, u32[]{:S(2)}) collective-permute-start(bf16[1408,128]{1,0:T(8,128)(2,1)} %get-tuple-element.178.one_y), channel_id=1, source_target_pairs={{0,8},{8,0},{16,24},{24,16},{1,9},{9,1},{17,25},{25,17},{2,10},{10... | collective-permute-start | bytes 1081352 | tf_op jit(solution)/shard_map/ppermute | solution.py:448
  (17 other events, 193.6 us)

commit v13 on v12

--- a/solution.py
+++ b/solution.py
@@ -482,51 +482,36 @@
     tokens = tagged_tokens(
         tokens, routing, router_route_weights, route_replica_choice, device_expert_table, capacity
     )
-    tok1 = step(tokens)
-    rows0 = (tokens, sibling(tokens))
-    tok1, rows0, cotangent = fence(tok1, rows0, cotangent)
-
-    tok2 = step(tok1)
-    rows1 = (tok1, sibling(tok1))
+    tok1, cot1 = step(tokens), step(cotangent)
+    rows0, cots0 = (tokens, sibling(tokens)), (cotangent, sibling(cotangent))
     saved0, part0, away0 = forward(*rows0)
-    tok2, rows1, part0, away0, cotangent = fence(tok2, rows1, part0, away0, cotangent)
-
-    tok3 = step(tok2)
-    rows2 = (tok2, sibling(tok2))
+    tok1, cot1, cots0, part0, away0 = fence(tok1, cot1, cots0, part0, away0)
+
+    tok2, cot2 = step(tok1), step(cot1)
+    rows1, cots1 = (tok1, sibling(tok1)), (cot1, sibling(cot1))
     saved1, part1, away1 = forward(*rows1)
-    tok3, rows2, part1, away1, cotangent = fence(tok3, rows2, part1, away1, cotangent)
-
-    cot1 = step(cotangent)
-    rows3 = (tok3, sibling(tok3))
-    cots0 = (cotangent, sibling(cotangent))
+    grads = backward(cots0, rows0, saved0)
+    tok2, cot2, cots1, part1, away1, grads = fence(tok2, cot2, cots1, part1, away1, grads)
+
+    tok3, cot3 = step(tok2), step(cot2)
+    rows2, cots2 = (tok2, sibling(tok2)), (cot2, sibling(cot2))
+    part1 = add_rounded(part1, sibling(away1))
     saved2, part2, away2 = forward(*rows2)
-    cot1, rows3, cots0, part2, away2 = fence(cot1, rows3, cots0, part2, away2)
-
-    cot2 = step(cot1)
-    cots1 = (cot1, sibling(cot1))
+    grads = backward(cots1, rows1, saved1, grads)
+    tok3, cot3, cots2, part1, part2, away2, grads = fence(
+        tok3, cot3, cots2, part1, part2, away2, grads
+    )
+
+    sum1 = step(part1)
+    rows3, cots3 = (tok3, sibling(tok3)), (cot3, sibling(cot3))
+    part2 = add_rounded(part2, sibling(away2))
     saved3, part3, away3 = forward(*rows3)
-    grads = backward(cots0, rows0, saved0)
-    cot2, cots1, part1, away1, part2, away2, part3, away3, grads = fence(
-        cot2, cots1, part1, away1, part2, away2, part3, away3, grads
-    )
-
-    cot3 = step(cot2)
-    cots2 = (cot2, sibling(cot2))
-    part1 = add_rounded(part1, sibling(away1))
-    grads = backward(cots1, rows1, saved1, grads)
     grads = backward(cots2, rows2, saved2, grads)
-    cot3, part1, part2, away2, part3, away3, grads = fence(
-        cot3, part1, part2, away2, part3, away3, grads
-    )
-
-    sum1 = step(part1)
-    cots3 = (cot3, sibling(cot3))
-    part2 = add_rounded(part2, sibling(away2))
     features, hidden_width = adapt_a.shape[0], adapt_b.shape[1]
     cut = (features + hidden_width) // 2
     grads = backward(cots3, rows3, saved3, grads, cut)
-    sum1, part2, part0, away0, part3, away3, grads = fence(
-        sum1, part2, part0, away0, part3, away3, grads
+    sum1, part0, away0, part2, part3, away3, grads = fence(
+        sum1, part0, away0, part2, part3, away3, grads
     )
 
     sum2 = step(add_rounded(part2, sum1))

time: 157 us -> 143 us (0.911)
  waiting for transfers between devices: 97.6 us -> 77 us
  starting transfers between devices: 8.76 us -> 11.3 us
  local copies, waits for them, and re-layouts: 8.98 us -> 10.9 us
  Pallas kernels: 38.6 us -> 40.3 us
    ppermute x21, waiting for transfers between devices: 81.2 us -> 60.6 us  [send(): return lax.ppermute(array, 'expert', pairs)]
    ppermute x21, starting transfers between devices: 4.7 us -> 7.28 us  [send(): return lax.ppermute(array, 'expert', pairs)]
    unnamed x32 -> x40, local copies, waits for them, and re-layouts: 8.98 us -> 10.9 us
    pallas_call x8, Pallas kernels: 31.6 us -> 33.3 us  [stage_call(): pl.pallas_call(kernel, out_shape=out_shape, in_specs=[SMEM] + [VMEM] * (l...]
  transfers between devices with their start and end apart: 25 -> 25, of which waited for: 14 -> 11; matrix products, arithmetic and copies ran while one was open for 0% -> 1% of each run, Pallas kernels for 23% -> 27%
where the time goes in v13:
time: 143 us; the launch traced here: 142 us
  waiting for transfers between devices  77 us (54%)
  Pallas kernels  40.3 us (28%)
  starting transfers between devices  11.3 us (8%)
  local copies, waits for them, and re-layouts  10.9 us (8%)
  other arithmetic  1.79 us (1%)
    ppermute x21, waiting for transfers between devices, send(): return lax.ppermute(array, 'expert', pairs)  60.6 us
    pallas_call x8, Pallas kernels, stage_call(): pl.pallas_call(kernel, out_shape=out_shape, in_specs=[SMEM] + [VMEM] * (l...  33.3 us
    ppermute x4, waiting for transfers between devices, dp_swap(): return lax.ppermute(array, 'dp', [(d, d ^ bit) for d in range(4)])  16.4 us
    unnamed x40, local copies, waits for them, and re-layouts  10.9 us
    ppermute x21, starting transfers between devices, send(): return lax.ppermute(array, 'expert', pairs)  7.28 us
    ppermute x4, starting transfers between devices, dp_swap(): return lax.ppermute(array, 'dp', [(d, d ^ bit) for d in range(4)])  4.05 us
  transfers between devices with their start and end apart: 25, of which 11 were waited for; matrix products, arithmetic and copies ran while one was open for 1% of the time, Pallas kernels for 27%

profile of v13, /device:TPU:0, one launch (start us, length us, event | category | flops | bytes accessed | tf_op | source)
XLA Modules:
  0.0 142.2 jit_solution(12624236733074229956)
XLA Ops:
  0.6 2.2 %shard_map.121.mine_ref.refs_3_ = bf16[128,2176]{1,0:T(8,128)(2,1)} custom-call(s32[8]{0:T(128)} %table_ref.1, s32[8,128]{1,0:T(8,128)} %bitcast.34, s32[8,128]{1,0:T(8,128)} %bitcast.35, f32[8,128]{1,0:T(8,128)} %bitcast.36, bf16[128,2048]{1,0:T(8,128)(2,1)} %tokens_ref.1), custom_call_target="tpu_custom_call" | custom-call | tf_op jit(solution)/shard_map/pallas_call | solution.py:258
  3.3 2.6 %collective-permute-start = (bf16[128,2176]{1,0:T(8,128)(2,1)}, bf16[128,2176]{1,0:T(8,128)(2,1)}, u32[]{:S(2)}, u32[]{:S(2)}) collective-permute-start(bf16[128,2176]{1,0:T(8,128)(2,1)} %shard_map.121.mine_ref.refs_3_), channel_id=1, source_target_pairs={{0,2},{1,3},{2,4},{3,5},{4,6},{5,7},{6,0},{7,1},{8,10},{9,11},{10,... | collective-permute-start | bytes 1671176 | tf_op jit(solution)/shard_map/ppermute | solution.py:429
  5.9 1.6 %collective-permute-start.1 = (bf16[128,2048]{1,0:T(8,128)(2,1)}, bf16[128,2048]{1,0:T(8,128)(2,1)}, u32[]{:S(2)}, u32[]{:S(2)}) collective-permute-start(bf16[128,2048]{1,0:T(8,128)(2,1)} %refs_1_), channel_id=1, source_target_pairs={{0,2},{1,3},{2,4},{3,5},{4,6},{5,7},{6,0},{7,1},{8,10},{9,11},{10,... | collective-permute-start | bytes 1572872 | tf_op jit(solution)/shard_map/ppermute | solution.py:429
  8.4 1.9 %copy-done = bf16[1,768,2048]{2,1,0:T(8,128)(2,1)S(1)} copy-done((bf16[1,768,2048]{2,1,0:T(8,128)(2,1)S(1)}, bf16[1,768,2048]{2,1,0:T(8,128)(2,1)}, u32[]{:S(2)}) %copy-start) | copy-done | bytes 3145752
  10.2 2.8 %copy-done.2 = bf16[1,2048,1536]{2,1,0:T(8,128)(2,1)S(1)} copy-done((bf16[1,2048,1536]{2,1,0:T(8,128)(2,1)S(1)}, bf16[1,2048,1536]{2,1,0:T(8,128)(2,1)}, u32[]{:S(2)}) %copy-start.2) | copy-done | bytes 6291480
  17.1 4.3 %shard_map.122 = (bf16[256,128]{1,0:T(8,128)(2,1)S(1)}, f32[256,768]{1,0:T(8,128)S(1)}, f32[256,768]{1,0:T(8,128)S(1)}, bf16[128,2048]{1,0:T(8,128)(2,1)S(1)}, bf16[128,2048]{1,0:T(8,128)(2,1)S(1)}) custom-call(s32[2]{0:T(128)S(1)} %pad_add_fusion.slot_ref.refs_0_, bf16[128,2176]{1,0:T(8,128)(2,1)S(1)} %copy-done.8, bf16[128,2176]{1,0:T(8,128)(2,1)S(1)} %copy-done.11, ...), custom_call_target="tpu_custom_call" | custom-call | flops 2550136832 | bytes 13959176 | tf_op jit(solution)/shard_map/pallas_call | solution.py:269
  21.4 11.3 %collective-permute-done.1.refs_1_ = bf16[128,2048]{1,0:T(8,128)(2,1)} collective-permute-done((bf16[128,2048]{1,0:T(8,128)(2,1)}, bf16[128,2048]{1,0:T(8,128)(2,1)}, u32[]{:S(2)}, u32[]{:S(2)}) %collective-permute-start.1) | collective-permute-done | bytes 524320 | tf_op jit(solution)/shard_map/ppermute | solution.py:429
  34.3 4.1 %shard_map.124 = (f32[2048,128]{1,0:T(8,128)S(1)}, f32[128,768]{1,0:T(8,128)S(1)}) custom-call(s32[2]{0:T(128)S(1)} %pad_add_fusion.slot_ref.refs_0_, bf16[128,2048]{1,0:T(8,128)(2,1)S(1)} %copy-done.13, bf16[128,2048]{1,0:T(8,128)(2,1)} %collective-permute-done.2.refs_2_, bf16[128,2176]{1,0:T(8,128)(2,1)S(1)} %copy-done.9, ...), custom_call_target="tpu_custom_call" | custom-call | flops 1140850688 | bytes 8585224 | tf_op jit(solution)/shard_map/pallas_call | solution.py:269
  38.5 4.8 %shard_map.123 = (bf16[256,128]{1,0:T(8,128)(2,1)S(1)}, f32[256,768]{1,0:T(8,128)S(1)}, f32[256,768]{1,0:T(8,128)S(1)}, bf16[128,2048]{1,0:T(8,128)(2,1)S(1)}, bf16[128,2048]{1,0:T(8,128)(2,1)S(1)}) custom-call(s32[2]{0:T(128)S(1)} %pad_add_fusion.slot_ref.refs_0_, bf16[128,2176]{1,0:T(8,128)(2,1)} %collective-permute-done.mine_ref.refs_3_, ...), custom_call_target="tpu_custom_call" | custom-call | flops 2550136832 | bytes 13959176 | tf_op jit(solution)/shard_map/pallas_call | solution.py:269
  43.3 17.7 %collective-permute-done.5.refs_1_ = bf16[128,2048]{1,0:T(8,128)(2,1)S(1)} collective-permute-done((bf16[128,2048]{1,0:T(8,128)(2,1)}, bf16[128,2048]{1,0:T(8,128)(2,1)S(1)}, u32[]{:S(2)}, u32[]{:S(2)}) %collective-permute-start.5) | collective-permute-done | bytes 524320 | tf_op jit(solution)/shard_map/ppermute | solution.py:429
  61.6 4.3 %shard_map.126 = (f32[2048,128]{1,0:T(8,128)S(1)}, f32[128,768]{1,0:T(8,128)S(1)}) custom-call(s32[2]{0:T(128)S(1)} %pad_add_fusion.slot_ref.refs_0_, bf16[128,2048]{1,0:T(8,128)(2,1)} %collective-permute-done.1.refs_1_, bf16[128,2048]{1,0:T(8,128)(2,1)S(1)} %collective-permute-done.6.refs_2_, bf16[128,2176]{1,0:T(8,128)(2,1)} %collective-permute-done.mine_ref.refs_3_, ...), custom_call_target="tpu_custom_call" | custom-call | flops 1140850688 | bytes 10027016 | tf_op jit(solution)/shard_map/pallas_call | solution.py:269
  66.0 4.3 %shard_map.125 = (bf16[256,128]{1,0:T(8,128)(2,1)S(1)}, f32[256,768]{1,0:T(8,128)S(1)}, f32[256,768]{1,0:T(8,128)S(1)}, bf16[128,2048]{1,0:T(8,128)(2,1)S(1)}, bf16[128,2048]{1,0:T(8,128)(2,1)S(1)}) custom-call(s32[2]{0:T(128)S(1)} %pad_add_fusion.slot_ref.refs_0_, bf16[128,2176]{1,0:T(8,128)(2,1)S(1)} %collective-permute-done.4.mine_ref.refs_3_, ...), custom_call_target="tpu_custom_call" | custom-call | flops 2550136832 | bytes 13959176 | tf_op jit(solution)/shard_map/pallas_call | solution.py:269
  70.4 7.8 %collective-permute-done.9.refs_1_ = bf16[128,2048]{1,0:T(8,128)(2,1)S(1)} collective-permute-done((bf16[128,2048]{1,0:T(8,128)(2,1)S(1)}, bf16[128,2048]{1,0:T(8,128)(2,1)S(1)}, u32[]{:S(2)}, u32[]{:S(2)}) %collective-permute-start.9) | collective-permute-done | bytes 524320 | tf_op jit(solution)/shard_map/ppermute | solution.py:429
  78.1 11.0 %collective-permute-done.8.mine_ref.refs_3_ = bf16[128,2176]{1,0:T(8,128)(2,1)S(1)} collective-permute-done((bf16[128,2176]{1,0:T(8,128)(2,1)S(1)}, bf16[128,2176]{1,0:T(8,128)(2,1)S(1)}, u32[]{:S(2)}, u32[]{:S(2)}) %collective-permute-start.8) | collective-permute-done | bytes 557088 | tf_op jit(solution)/shard_map/ppermute | solution.py:429
  89.6 3.6 %shard_map.128 = (f32[2048,128]{1,0:T(8,128)S(1)}, f32[128,768]{1,0:T(8,128)S(1)}) custom-call(s32[2]{0:T(128)S(1)} %pad_add_fusion.slot_ref.refs_0_, bf16[128,2048]{1,0:T(8,128)(2,1)S(1)} %collective-permute-done.5.refs_1_, bf16[128,2048]{1,0:T(8,128)(2,1)S(1)} %collective-permute-done.10.refs_2_, ...), custom_call_target="tpu_custom_call" | custom-call | flops 1140850688 | bytes 10027016 | tf_op jit(solution)/shard_map/pallas_call | solution.py:269
  93.4 4.3 %shard_map.127 = (bf16[256,128]{1,0:T(8,128)(2,1)S(1)}, f32[256,768]{1,0:T(8,128)S(1)}, f32[256,768]{1,0:T(8,128)S(1)}, bf16[128,2048]{1,0:T(8,128)(2,1)S(1)}, bf16[128,2048]{1,0:T(8,128)(2,1)S(1)}) custom-call(s32[2]{0:T(128)S(1)} %pad_add_fusion.slot_ref.refs_0_, bf16[128,2176]{1,0:T(8,128)(2,1)S(1)} %collective-permute-done.8.mine_ref.refs_3_, ...), custom_call_target="tpu_custom_call" | custom-call | flops 2550136832 | bytes 13959176 | tf_op jit(solution)/shard_map/pallas_call | solution.py:269
  97.7 3.6 %shard_map.129 = (bf16[1408,128]{1,0:T(8,128)(2,1)S(1)}, bf16[1408,128]{1,0:T(8,128)(2,1)S(1)}) custom-call(s32[2]{0:T(128)S(1)} %pad_add_fusion.slot_ref.refs_0_, bf16[128,2048]{1,0:T(8,128)(2,1)S(1)} %collective-permute-done.9.refs_1_, bf16[128,2048]{1,0:T(8,128)(2,1)S(1)} %collective-permute-done.16.refs_2_, ...), custom_call_target="tpu_custom_call" | custom-call | flops 1140850688 | bytes 9306120 | tf_op jit(solution)/shard_map/pallas_call | solution.py:269
  101.3 3.9 %collective-permute-done.13 = bf16[128,2048]{1,0:T(8,128)(2,1)S(1)} collective-permute-done((bf16[128,2048]{1,0:T(8,128)(2,1)S(1)}, bf16[128,2048]{1,0:T(8,128)(2,1)S(1)}, u32[]{:S(2)}, u32[]{:S(2)}) %collective-permute-start.13) | collective-permute-done | bytes 524320 | tf_op jit(solution)/shard_map/ppermute | solution.py:429
  108.6 1.6 %collective-permute-done.19 = bf16[128,2048]{1,0:T(8,128)(2,1)S(1)} collective-permute-done((bf16[128,2048]{1,0:T(8,128)(2,1)S(1)}, bf16[128,2048]{1,0:T(8,128)(2,1)S(1)}, u32[]{:S(2)}, u32[]{:S(2)}) %collective-permute-start.19) | collective-permute-done | bytes 524320 | tf_op jit(solution)/shard_map/ppermute | solution.py:429
  110.3 5.8 %collective-permute-done.20.refs_2_ = bf16[1408,128]{1,0:T(8,128)(2,1)S(1)} collective-permute-done((bf16[1408,128]{1,0:T(8,128)(2,1)S(1)}, bf16[1408,128]{1,0:T(8,128)(2,1)S(1)}, u32[]{:S(2)}, u32[]{:S(2)}) %collective-permute-start.20) | collective-permute-done | bytes 360480 | tf_op jit(solution)/shard_map/ppermute | solution.py:448
  117.3 7.3 %collective-permute-done.17 = bf16[128,2048]{1,0:T(8,128)(2,1)S(1)} collective-permute-done((bf16[128,2048]{1,0:T(8,128)(2,1)S(1)}, bf16[128,2048]{1,0:T(8,128)(2,1)S(1)}, u32[]{:S(2)}, u32[]{:S(2)}) %collective-permute-start.17) | collective-permute-done | bytes 524320 | tf_op jit(solution)/shard_map/ppermute | solution.py:429
  124.8 2.3 %shard_map.130 = (bf16[1408,128]{1,0:T(8,128)(2,1)}, bf16[1408,128]{1,0:T(8,128)(2,1)}) custom-call(bf16[1408,128]{1,0:T(8,128)(2,1)} %copy-done.14, bf16[1408,128]{1,0:T(8,128)(2,1)} %copy-done.15, bf16[1408,128]{1,0:T(8,128)(2,1)} %copy-done.16, bf16[1408,128]{1,0:T(8,128)(2,1)} %copy-done.17), custom_call_target="tpu_custom_call" | custom-call | tf_op jit(solution)/shard_map/pallas_call | solution.py:394
  128.1 9.2 %collective-permute-done.23.other_x = bf16[1408,128]{1,0:T(8,128)(2,1)S(1)} collective-permute-done((bf16[1408,128]{1,0:T(8,128)(2,1)}, bf16[1408,128]{1,0:T(8,128)(2,1)S(1)}, u32[]{:S(2)}, u32[]{:S(2)}) %collective-permute-start.23) | collective-permute-done | bytes 360480 | tf_op jit(solution)/shard_map/ppermute | solution.py:448
  138.8 2.5 %shard_map.131 = (f32[2048,128]{1,0:T(8,128)}, f32[128,768]{1,0:T(8,128)}) custom-call(bf16[1408,128]{1,0:T(8,128)(2,1)} %get-tuple-element.139.one_x, bf16[1408,128]{1,0:T(8,128)(2,1)} %get-tuple-element.140.one_y, bf16[1408,128]{1,0:T(8,128)(2,1)} %copy-done.18, bf16[1408,128]{1,0:T(8,128)(2,1)} %copy-done.19), custom_call_target="tpu_custom_call" | custom-call | tf_op jit(solution)/shard_map/pallas_call | solution.py:415
  (85 shorter events, 16.6 us)
Async XLA Ops:
  2.8 4.7 %collective-permute-start.3 = (bf16[128,2176]{1,0:T(8,128)(2,1)}, bf16[128,2176]{1,0:T(8,128)(2,1)S(1)}, u32[]{:S(2)}, u32[]{:S(2)}) collective-permute-start(bf16[128,2176]{1,0:T(8,128)(2,1)} %shard_map.121.mine_ref.refs_3_), channel_id=1, source_target_pairs={{0,1},{1,0},{2,3},{3,2},{4,5},{5,4},{6,7},{7,6},{8,9},{9,8},{10,11... | collective-permute-start | bytes 1671176 | tf_op jit(solution)/shard_map/ppermute | solution.py:429
  3.3 29.5 %collective-permute-start = (bf16[128,2176]{1,0:T(8,128)(2,1)}, bf16[128,2176]{1,0:T(8,128)(2,1)}, u32[]{:S(2)}, u32[]{:S(2)}) collective-permute-start(bf16[128,2176]{1,0:T(8,128)(2,1)} %shard_map.121.mine_ref.refs_3_), channel_id=1, source_target_pairs={{0,2},{1,3},{2,4},{3,5},{4,6},{5,7},{6,0},{7,1},{8,10},{9,11},{10,... | collective-permute-start | bytes 1671176 | tf_op jit(solution)/shard_map/ppermute | solution.py:429
  5.9 26.9 %collective-permute-start.1 = (bf16[128,2048]{1,0:T(8,128)(2,1)}, bf16[128,2048]{1,0:T(8,128)(2,1)}, u32[]{:S(2)}, u32[]{:S(2)}) collective-permute-start(bf16[128,2048]{1,0:T(8,128)(2,1)} %refs_1_), channel_id=1, source_target_pairs={{0,2},{1,3},{2,4},{3,5},{4,6},{5,7},{6,0},{7,1},{8,10},{9,11},{10,... | collective-permute-start | bytes 1572872 | tf_op jit(solution)/shard_map/ppermute | solution.py:429
  7.4 25.3 %collective-permute-start.2 = (bf16[128,2048]{1,0:T(8,128)(2,1)}, bf16[128,2048]{1,0:T(8,128)(2,1)}, u32[]{:S(2)}, u32[]{:S(2)}) collective-permute-start(bf16[128,2048]{1,0:T(8,128)(2,1)} %refs_1_), channel_id=1, source_target_pairs={{0,1},{1,0},{2,3},{3,2},{4,5},{5,4},{6,7},{7,6},{8,9},{9,8},{10,11... | collective-permute-start | bytes 1572872 | tf_op jit(solution)/shard_map/ppermute | solution.py:429
  32.7 5.7 %collective-permute-start.7 = (bf16[128,2176]{1,0:T(8,128)(2,1)}, bf16[128,2176]{1,0:T(8,128)(2,1)S(1)}, u32[]{:S(2)}, u32[]{:S(2)}) collective-permute-start(bf16[128,2176]{1,0:T(8,128)(2,1)} %collective-permute-done.mine_ref.refs_3_), channel_id=1, source_target_pairs={{0,1},{1,0},{2,3},{3,2},{4,5},{5,4},{6,7},{7,6},{8,9},{9,8},{10,11... | collective-permute-start | bytes 1671176 | tf_op jit(solution)/shard_map/ppermute | solution.py:429
  32.8 28.3 %collective-permute-start.4 = (bf16[128,2176]{1,0:T(8,128)(2,1)}, bf16[128,2176]{1,0:T(8,128)(2,1)S(1)}, u32[]{:S(2)}, u32[]{:S(2)}) collective-permute-start(bf16[128,2176]{1,0:T(8,128)(2,1)} %collective-permute-done.mine_ref.refs_3_), channel_id=1, source_target_pairs={{0,2},{1,3},{2,4},{3,5},{4,6},{5,7},{6,0},{7,1},{8,10},{9,11},{10,... | collective-permute-start | bytes 1671176 | tf_op jit(solution)/shard_map/ppermute | solution.py:429
  32.8 10.5 %collective-permute-start.6 = (bf16[128,2048]{1,0:T(8,128)(2,1)}, bf16[128,2048]{1,0:T(8,128)(2,1)S(1)}, u32[]{:S(2)}, u32[]{:S(2)}) collective-permute-start(bf16[128,2048]{1,0:T(8,128)(2,1)} %collective-permute-done.1.refs_1_), channel_id=1, source_target_pairs={{0,1},{1,0},{2,3},{3,2},{4,5},{5,4},{6,7},{7,6},{8,9},{9,8},{10,11... | collective-permute-start | bytes 1572872 | tf_op jit(solution)/shard_map/ppermute | solution.py:429
  33.3 27.8 %collective-permute-start.5 = (bf16[128,2048]{1,0:T(8,128)(2,1)}, bf16[128,2048]{1,0:T(8,128)(2,1)S(1)}, u32[]{:S(2)}, u32[]{:S(2)}) collective-permute-start(bf16[128,2048]{1,0:T(8,128)(2,1)} %collective-permute-done.1.refs_1_), channel_id=1, source_target_pairs={{0,2},{1,3},{2,4},{3,5},{4,6},{5,7},{6,0},{7,1},{8,10},{9,11},{10,... | collective-permute-start | bytes 1572872 | tf_op jit(solution)/shard_map/ppermute | solution.py:429
  61.0 4.8 %collective-permute-start.11 = (bf16[128,2048]{1,0:T(8,128)(2,1)S(1)}, bf16[128,2048]{1,0:T(8,128)(2,1)S(1)}, u32[]{:S(2)}, u32[]{:S(2)}) collective-permute-start(bf16[128,2048]{1,0:T(8,128)(2,1)S(1)} %get-tuple-element.89), channel_id=1, source_target_pairs={{0,1},{1,0},{2,3},{3,2},{4,5},{5,4},{6,7},{7,6},{8,9},{9,8},{10,11... | collective-permute-start | bytes 1572872 | tf_op jit(solution)/shard_map/ppermute | solution.py:429
  61.0 9.3 %collective-permute-start.10 = (bf16[128,2048]{1,0:T(8,128)(2,1)S(1)}, bf16[128,2048]{1,0:T(8,128)(2,1)S(1)}, u32[]{:S(2)}, u32[]{:S(2)}) collective-permute-start(bf16[128,2048]{1,0:T(8,128)(2,1)S(1)} %collective-permute-done.5.refs_1_), channel_id=1, source_target_pairs={{0,1},{1,0},{2,3},{3,2},{4,5},{5,4},{6,7},{7,6},{8,9},{9,8},{10,11... | collective-permute-start | bytes 1572872 | tf_op jit(solution)/shard_map/ppermute | solution.py:429
  61.6 16.6 %collective-permute-start.9 = (bf16[128,2048]{1,0:T(8,128)(2,1)S(1)}, bf16[128,2048]{1,0:T(8,128)(2,1)S(1)}, u32[]{:S(2)}, u32[]{:S(2)}) collective-permute-start(bf16[128,2048]{1,0:T(8,128)(2,1)S(1)} %collective-permute-done.5.refs_1_), channel_id=1, source_target_pairs={{0,2},{1,3},{2,4},{3,5},{4,6},{5,7},{6,0},{7,1},{8,10},{9,11},{10,... | collective-permute-start | bytes 1572872 | tf_op jit(solution)/shard_map/ppermute | solution.py:429
  61.6 4.5 %collective-permute-start.12 = (bf16[128,2176]{1,0:T(8,128)(2,1)S(1)}, bf16[128,2176]{1,0:T(8,128)(2,1)S(1)}, u32[]{:S(2)}, u32[]{:S(2)}) collective-permute-start(bf16[128,2176]{1,0:T(8,128)(2,1)S(1)} %collective-permute-done.4.mine_ref.refs_3_), channel_id=1, source_target_pairs={{0,1},{1,0},{2,3},{3,2},{4,5},{5,4},{6,7},{7,6},{8,9},{9,8},{10,11... | collective-permute-start | bytes 1671176 | tf_op jit(solution)/shard_map/ppermute | solution.py:429
  61.6 27.6 %collective-permute-start.8 = (bf16[128,2176]{1,0:T(8,128)(2,1)S(1)}, bf16[128,2176]{1,0:T(8,128)(2,1)S(1)}, u32[]{:S(2)}, u32[]{:S(2)}) collective-permute-start(bf16[128,2176]{1,0:T(8,128)(2,1)S(1)} %collective-permute-done.4.mine_ref.refs_3_), channel_id=1, source_target_pairs={{0,2},{1,3},{2,4},{3,5},{4,6},{5,7},{6,0},{7,1},{8,10},{9,11},{10,... | collective-permute-start | bytes 1671176 | tf_op jit(solution)/shard_map/ppermute | solution.py:429
  89.1 4.1 %collective-permute-start.14 = (bf16[128,2048]{1,0:T(8,128)(2,1)S(1)}, bf16[128,2048]{1,0:T(8,128)(2,1)S(1)}, u32[]{:S(2)}, u32[]{:S(2)}) collective-permute-start(bf16[128,2048]{1,0:T(8,128)(2,1)S(1)} %get-tuple-element.105), channel_id=1, source_target_pairs={{0,1},{1,0},{2,3},{3,2},{4,5},{5,4},{6,7},{7,6},{8,9},{9,8},{10,11... | collective-permute-start | bytes 1572872 | tf_op jit(solution)/shard_map/ppermute | solution.py:429
  89.1 16.1 %collective-permute-start.13 = (bf16[128,2048]{1,0:T(8,128)(2,1)S(1)}, bf16[128,2048]{1,0:T(8,128)(2,1)S(1)}, u32[]{:S(2)}, u32[]{:S(2)}) collective-permute-start(bf16[128,2048]{1,0:T(8,128)(2,1)S(1)} %add_convert_fusion.6), channel_id=1, source_target_pairs={{0,2},{1,3},{2,4},{3,5},{4,6},{5,7},{6,0},{7,1},{8,10},{9,11},{10,... | collective-permute-start | bytes 1572872 | tf_op jit(solution)/shard_map/ppermute | solution.py:429
  89.1 8.6 %collective-permute-start.16 = (bf16[128,2048]{1,0:T(8,128)(2,1)S(1)}, bf16[128,2048]{1,0:T(8,128)(2,1)S(1)}, u32[]{:S(2)}, u32[]{:S(2)}) collective-permute-start(bf16[128,2048]{1,0:T(8,128)(2,1)S(1)} %collective-permute-done.9.refs_1_), channel_id=1, source_target_pairs={{0,1},{1,0},{2,3},{3,2},{4,5},{5,4},{6,7},{7,6},{8,9},{9,8},{10,11... | collective-permute-start | bytes 1572872 | tf_op jit(solution)/shard_map/ppermute | solution.py:429
  89.6 3.7 %collective-permute-start.15 = (bf16[128,2176]{1,0:T(8,128)(2,1)S(1)}, bf16[128,2176]{1,0:T(8,128)(2,1)S(1)}, u32[]{:S(2)}, u32[]{:S(2)}) collective-permute-start(bf16[128,2176]{1,0:T(8,128)(2,1)S(1)} %collective-permute-done.8.mine_ref.refs_3_), channel_id=1, source_target_pairs={{0,1},{1,0},{2,3},{3,2},{4,5},{5,4},{6,7},{7,6},{8,9},{9,8},{10,11... | collective-permute-start | bytes 1671176 | tf_op jit(solution)/shard_map/ppermute | solution.py:429
  105.3 3.2 %collective-permute-start.18 = (bf16[128,2048]{1,0:T(8,128)(2,1)S(1)}, bf16[128,2048]{1,0:T(8,128)(2,1)S(1)}, u32[]{:S(2)}, u32[]{:S(2)}) collective-permute-start(bf16[128,2048]{1,0:T(8,128)(2,1)S(1)} %get-tuple-element.127), channel_id=1, source_target_pairs={{0,1},{1,0},{2,3},{3,2},{4,5},{5,4},{6,7},{7,6},{8,9},{9,8},{10,11... | collective-permute-start | bytes 1572872 | tf_op jit(solution)/shard_map/ppermute | solution.py:429
  105.3 10.8 %collective-permute-start.20 = (bf16[1408,128]{1,0:T(8,128)(2,1)S(1)}, bf16[1408,128]{1,0:T(8,128)(2,1)S(1)}, u32[]{:S(2)}, u32[]{:S(2)}) collective-permute-start(bf16[1408,128]{1,0:T(8,128)(2,1)S(1)} %get-tuple-element.135.refs_0_), channel_id=1, source_target_pairs={{0,8},{8,0},{16,24},{24,16},{1,9},{9,1},{17,25},{25,17},{2,10},{10... | collective-permute-start | bytes 1081352 | tf_op jit(solution)/shard_map/ppermute | solution.py:448
  106.8 10.5 %collective-permute-start.21 = (bf16[1408,128]{1,0:T(8,128)(2,1)S(1)}, bf16[1408,128]{1,0:T(8,128)(2,1)S(1)}, u32[]{:S(2)}, u32[]{:S(2)}) collective-permute-start(bf16[1408,128]{1,0:T(8,128)(2,1)S(1)} %get-tuple-element.136.refs_1_), channel_id=1, source_target_pairs={{0,16},{8,24},{16,0},{24,8},{1,17},{9,25},{17,1},{25,9},{2,18},{10... | collective-permute-start | bytes 1081352 | tf_op jit(solution)/shard_map/ppermute | solution.py:448
  108.4 16.2 %collective-permute-start.17 = (bf16[128,2048]{1,0:T(8,128)(2,1)S(1)}, bf16[128,2048]{1,0:T(8,128)(2,1)S(1)}, u32[]{:S(2)}, u32[]{:S(2)}) collective-permute-start(bf16[128,2048]{1,0:T(8,128)(2,1)S(1)} %add_convert_fusion.4), channel_id=1, source_target_pairs={{0,2},{1,3},{2,4},{3,5},{4,6},{5,7},{6,0},{7,1},{8,10},{9,11},{10,... | collective-permute-start | bytes 1572872 | tf_op jit(solution)/shard_map/ppermute | solution.py:429
  124.7 16.6 %collective-permute-start.22 = (bf16[128,2048]{1,0:T(8,128)(2,1)S(1)}, bf16[128,2048]{1,0:T(8,128)(2,1)S(1)}, u32[]{:S(2)}, u32[]{:S(2)}) collective-permute-start(bf16[128,2048]{1,0:T(8,128)(2,1)S(1)} %add_convert_fusion.1), channel_id=1, source_target_pairs={{0,2},{1,3},{2,4},{3,5},{4,6},{5,7},{6,0},{7,1},{8,10},{9,11},{10,... | collective-permute-start | bytes 1572872 | tf_op jit(solution)/shard_map/ppermute | solution.py:429
  127.1 10.3 %collective-permute-start.23 = (bf16[1408,128]{1,0:T(8,128)(2,1)}, bf16[1408,128]{1,0:T(8,128)(2,1)S(1)}, u32[]{:S(2)}, u32[]{:S(2)}) collective-permute-start(bf16[1408,128]{1,0:T(8,128)(2,1)} %get-tuple-element.139.one_x), channel_id=1, source_target_pairs={{0,16},{8,24},{16,0},{24,8},{1,17},{9,25},{17,1},{25,9},{2,18},{10... | collective-permute-start | bytes 1081352 | tf_op jit(solution)/shard_map/ppermute | solution.py:448
  127.6 10.0 %collective-permute-start.24 = (bf16[1408,128]{1,0:T(8,128)(2,1)}, bf16[1408,128]{1,0:T(8,128)(2,1)S(1)}, u32[]{:S(2)}, u32[]{:S(2)}) collective-permute-start(bf16[1408,128]{1,0:T(8,128)(2,1)} %get-tuple-element.140.one_y), channel_id=1, source_target_pairs={{0,8},{8,0},{16,24},{24,16},{1,9},{9,1},{17,25},{25,17},{2,10},{10... | collective-permute-start | bytes 1081352 | tf_op jit(solution)/shard_map/ppermute | solution.py:448
  (21 other events, 189.4 us)

commit v14 on v13

--- a/solution.py
+++ b/solution.py
@@ -485,28 +485,31 @@
     tok1, cot1 = step(tokens), step(cotangent)
     rows0, cots0 = (tokens, sibling(tokens)), (cotangent, sibling(cotangent))
     saved0, part0, away0 = forward(*rows0)
-    tok1, cot1, cots0, part0, away0 = fence(tok1, cot1, cots0, part0, away0)
-
-    tok2, cot2 = step(tok1), step(cot1)
-    rows1, cots1 = (tok1, sibling(tok1)), (cot1, sibling(cot1))
+
+    tok1, cots0, part0, away0 = fence(tok1, cots0, part0, away0)
+    tok2 = step(tok1)
+    rows1 = (tok1, sibling(tok1))
+    cots1, rows1 = fence((cot1, sibling(cot1)), rows1)
+    cot2 = step(cots1[0])
     saved1, part1, away1 = forward(*rows1)
     grads = backward(cots0, rows0, saved0)
-    tok2, cot2, cots1, part1, away1, grads = fence(tok2, cot2, cots1, part1, away1, grads)
-
-    tok3, cot3 = step(tok2), step(cot2)
-    rows2, cots2 = (tok2, sibling(tok2)), (cot2, sibling(cot2))
+
+    tok2, part1, away1, grads = fence(tok2, part1, away1, grads)
+    tok3 = step(tok2)
+    rows2 = (tok2, sibling(tok2))
+    cots2, rows2 = fence((cot2, sibling(cot2)), rows2)
+    cot3 = step(cots2[0])
     part1 = add_rounded(part1, sibling(away1))
     saved2, part2, away2 = forward(*rows2)
     grads = backward(cots1, rows1, saved1, grads)
-    tok3, cot3, cots2, part1, part2, away2, grads = fence(
-        tok3, cot3, cots2, part1, part2, away2, grads
-    )
-
+
+    tok3, part1, part2, away2, grads = fence(tok3, part1, part2, away2, grads)
     sum1 = step(part1)
-    rows3, cots3 = (tok3, sibling(tok3)), (cot3, sibling(cot3))
+    rows3 = (tok3, sibling(tok3))
+    cots3, rows3 = fence((cot3, sibling(cot3)), rows3)
     part2 = add_rounded(part2, sibling(away2))
+    grads = backward(cots2, rows2, saved2, grads)
     saved3, part3, away3 = forward(*rows3)
-    grads = backward(cots2, rows2, saved2, grads)
     features, hidden_width = adapt_a.shape[0], adapt_b.shape[1]
     cut = (features + hidden_width) // 2
     grads = backward(cots3, rows3, saved3, grads, cut)

time: 143 us -> 132 us (0.923)
  waiting for transfers between devices: 77 us -> 63.5 us
  starting transfers between devices: 11.3 us -> 14.3 us
    ppermute x21, waiting for transfers between devices: 60.6 us -> 46.5 us  [send(): return lax.ppermute(array, 'expert', pairs)]
    ppermute x4, starting transfers between devices: 4.05 us -> 6.11 us  [dp_swap(): return lax.ppermute(array, 'dp', [(d, d ^ bit) for d in range(4)])]
  transfers between devices with their start and end apart: 25 -> 25, of which waited for: 11 -> 10; matrix products, arithmetic and copies ran while one was open for 1% -> 1% of each run, Pallas kernels for 27% -> 29%
where the time goes in v14:
time: 132 us; the launch traced here: 131 us
  waiting for transfers between devices  63.5 us (48%)
  Pallas kernels  40.3 us (31%)
  starting transfers between devices  14.3 us (11%)
  local copies, waits for them, and re-layouts  10.4 us (8%)
  other arithmetic  1.82 us (1%)
    ppermute x21, waiting for transfers between devices, send(): return lax.ppermute(array, 'expert', pairs)  46.5 us
    pallas_call x8, Pallas kernels, stage_call(): pl.pallas_call(kernel, out_shape=out_shape, in_specs=[SMEM] + [VMEM] * (l...  33.4 us
    ppermute x4, waiting for transfers between devices, dp_swap(): return lax.ppermute(array, 'dp', [(d, d ^ bit) for d in range(4)])  17 us
    unnamed x40, local copies, waits for them, and re-layouts  10.4 us
    ppermute x21, starting transfers between devices, send(): return lax.ppermute(array, 'expert', pairs)  8.22 us
    ppermute x4, starting transfers between devices, dp_swap(): return lax.ppermute(array, 'dp', [(d, d ^ bit) for d in range(4)])  6.11 us
  transfers between devices with their start and end apart: 25, of which 10 were waited for; matrix products, arithmetic and copies ran while one was open for 1% of the time, Pallas kernels for 29%

profile of v14, /device:TPU:0, one launch (start us, length us, event | category | flops | bytes accessed | tf_op | source)
XLA Modules:
  0.0 131.3 jit_solution(16054335770410325567)
XLA Ops:
  0.6 2.2 %shard_map.121.mine_ref.refs_3_ = bf16[128,2176]{1,0:T(8,128)(2,1)} custom-call(s32[8]{0:T(128)} %table_ref.1, s32[8,128]{1,0:T(8,128)} %bitcast.34, s32[8,128]{1,0:T(8,128)} %bitcast.35, f32[8,128]{1,0:T(8,128)} %bitcast.36, bf16[128,2048]{1,0:T(8,128)(2,1)} %tokens_ref.1), custom_call_target="tpu_custom_call" | custom-call | tf_op jit(solution)/shard_map/pallas_call | solution.py:258
  3.3 2.6 %collective-permute-start = (bf16[128,2176]{1,0:T(8,128)(2,1)}, bf16[128,2176]{1,0:T(8,128)(2,1)}, u32[]{:S(2)}, u32[]{:S(2)}) collective-permute-start(bf16[128,2176]{1,0:T(8,128)(2,1)} %shard_map.121.mine_ref.refs_3_), channel_id=1, source_target_pairs={{0,2},{1,3},{2,4},{3,5},{4,6},{5,7},{6,0},{7,1},{8,10},{9,11},{10,... | collective-permute-start | bytes 1671176 | tf_op jit(solution)/shard_map/ppermute | solution.py:429
  6.1 1.6 %collective-permute-start.4 = (bf16[128,2048]{1,0:T(8,128)(2,1)}, bf16[128,2048]{1,0:T(8,128)(2,1)}, u32[]{:S(2)}, u32[]{:S(2)}) collective-permute-start(bf16[128,2048]{1,0:T(8,128)(2,1)} %refs_1_), channel_id=1, source_target_pairs={{0,2},{1,3},{2,4},{3,5},{4,6},{5,7},{6,0},{7,1},{8,10},{9,11},{10,... | collective-permute-start | bytes 1572872 | tf_op jit(solution)/shard_map/ppermute | solution.py:429
  8.6 1.9 %copy-done = bf16[1,768,2048]{2,1,0:T(8,128)(2,1)S(1)} copy-done((bf16[1,768,2048]{2,1,0:T(8,128)(2,1)S(1)}, bf16[1,768,2048]{2,1,0:T(8,128)(2,1)}, u32[]{:S(2)}) %copy-start) | copy-done | bytes 3145752
  10.5 2.8 %copy-done.2 = bf16[1,2048,1536]{2,1,0:T(8,128)(2,1)S(1)} copy-done((bf16[1,2048,1536]{2,1,0:T(8,128)(2,1)S(1)}, bf16[1,2048,1536]{2,1,0:T(8,128)(2,1)}, u32[]{:S(2)}) %copy-start.2) | copy-done | bytes 6291480
  17.3 4.3 %shard_map.122 = (bf16[256,128]{1,0:T(8,128)(2,1)S(1)}, f32[256,768]{1,0:T(8,128)S(1)}, f32[256,768]{1,0:T(8,128)S(1)}, bf16[128,2048]{1,0:T(8,128)(2,1)S(1)}, bf16[128,2048]{1,0:T(8,128)(2,1)S(1)}) custom-call(s32[2]{0:T(128)S(1)} %pad_add_fusion.slot_ref.refs_0_, bf16[128,2176]{1,0:T(8,128)(2,1)S(1)} %copy-done.8, bf16[128,2176]{1,0:T(8,128)(2,1)S(1)} %copy-done.11, ...), custom_call_target="tpu_custom_call" | custom-call | flops 2550136832 | bytes 13959176 | tf_op jit(solution)/shard_map/pallas_call | solution.py:269
  21.7 11.0 %collective-permute-done.4.refs_1_ = bf16[128,2048]{1,0:T(8,128)(2,1)} collective-permute-done((bf16[128,2048]{1,0:T(8,128)(2,1)}, bf16[128,2048]{1,0:T(8,128)(2,1)}, u32[]{:S(2)}, u32[]{:S(2)}) %collective-permute-start.4) | collective-permute-done | bytes 524320 | tf_op jit(solution)/shard_map/ppermute | solution.py:429
  32.8 4.1 %shard_map.124 = (f32[2048,128]{1,0:T(8,128)S(1)}, f32[128,768]{1,0:T(8,128)S(1)}) custom-call(s32[2]{0:T(128)S(1)} %pad_add_fusion.slot_ref.refs_0_, bf16[128,2048]{1,0:T(8,128)(2,1)S(1)} %copy-done.13, bf16[128,2048]{1,0:T(8,128)(2,1)} %collective-permute-done.1.refs_2_, bf16[128,2176]{1,0:T(8,128)(2,1)S(1)} %copy-done.9, ...), custom_call_target="tpu_custom_call" | custom-call | flops 1140850688 | bytes 8585224 | tf_op jit(solution)/shard_map/pallas_call | solution.py:269
  38.3 4.8 %shard_map.123 = (bf16[256,128]{1,0:T(8,128)(2,1)S(1)}, f32[256,768]{1,0:T(8,128)S(1)}, f32[256,768]{1,0:T(8,128)S(1)}, bf16[128,2048]{1,0:T(8,128)(2,1)S(1)}, bf16[128,2048]{1,0:T(8,128)(2,1)S(1)}) custom-call(s32[2]{0:T(128)S(1)} %pad_add_fusion.slot_ref.refs_0_, bf16[128,2176]{1,0:T(8,128)(2,1)} %collective-permute-done.mine_ref.refs_3_, ...), custom_call_target="tpu_custom_call" | custom-call | flops 2550136832 | bytes 13959176 | tf_op jit(solution)/shard_map/pallas_call | solution.py:269
  43.1 7.1 %collective-permute-done.3.mine_ref.refs_3_ = bf16[128,2176]{1,0:T(8,128)(2,1)S(1)} collective-permute-done((bf16[128,2176]{1,0:T(8,128)(2,1)}, bf16[128,2176]{1,0:T(8,128)(2,1)S(1)}, u32[]{:S(2)}, u32[]{:S(2)}) %collective-permute-start.3) | collective-permute-done | bytes 557088 | tf_op jit(solution)/shard_map/ppermute | solution.py:429
  50.7 10.7 %collective-permute-done.9.refs_1_ = bf16[128,2048]{1,0:T(8,128)(2,1)S(1)} collective-permute-done((bf16[128,2048]{1,0:T(8,128)(2,1)}, bf16[128,2048]{1,0:T(8,128)(2,1)S(1)}, u32[]{:S(2)}, u32[]{:S(2)}) %collective-permute-start.9) | collective-permute-done | bytes 524320 | tf_op jit(solution)/shard_map/ppermute | solution.py:429
  61.4 4.3 %shard_map.126 = (f32[2048,128]{1,0:T(8,128)S(1)}, f32[128,768]{1,0:T(8,128)S(1)}) custom-call(s32[2]{0:T(128)S(1)} %pad_add_fusion.slot_ref.refs_0_, bf16[128,2048]{1,0:T(8,128)(2,1)} %collective-permute-done.4.refs_1_, bf16[128,2048]{1,0:T(8,128)(2,1)S(1)} %collective-permute-done.5.refs_2_, bf16[128,2176]{1,0:T(8,128)(2,1)} %collective-permute-done.mine_ref.refs_3_, ...), custom_call_target="tpu_custom_call" | custom-call | flops 1140850688 | bytes 10027016 | tf_op jit(solution)/shard_map/pallas_call | solution.py:269
  66.1 4.3 %shard_map.125 = (bf16[256,128]{1,0:T(8,128)(2,1)S(1)}, f32[256,768]{1,0:T(8,128)S(1)}, f32[256,768]{1,0:T(8,128)S(1)}, bf16[128,2048]{1,0:T(8,128)(2,1)S(1)}, bf16[128,2048]{1,0:T(8,128)(2,1)S(1)}) custom-call(s32[2]{0:T(128)S(1)} %pad_add_fusion.slot_ref.refs_0_, bf16[128,2176]{1,0:T(8,128)(2,1)S(1)} %collective-permute-done.3.mine_ref.refs_3_, ...), custom_call_target="tpu_custom_call" | custom-call | flops 2550136832 | bytes 13959176 | tf_op jit(solution)/shard_map/pallas_call | solution.py:269
  70.5 2.9 %collective-permute-done.7.mine_ref.refs_3_ = bf16[128,2176]{1,0:T(8,128)(2,1)S(1)} collective-permute-done((bf16[128,2176]{1,0:T(8,128)(2,1)S(1)}, bf16[128,2176]{1,0:T(8,128)(2,1)S(1)}, u32[]{:S(2)}, u32[]{:S(2)}) %collective-permute-start.7) | collective-permute-done | bytes 557088 | tf_op jit(solution)/shard_map/ppermute | solution.py:429
  73.9 10.7 %collective-permute-done.14.refs_1_ = bf16[128,2048]{1,0:T(8,128)(2,1)S(1)} collective-permute-done((bf16[128,2048]{1,0:T(8,128)(2,1)S(1)}, bf16[128,2048]{1,0:T(8,128)(2,1)S(1)}, u32[]{:S(2)}, u32[]{:S(2)}) %collective-permute-start.14) | collective-permute-done | bytes 524320 | tf_op jit(solution)/shard_map/ppermute | solution.py:429
  84.6 3.6 %shard_map.128 = (f32[2048,128]{1,0:T(8,128)S(1)}, f32[128,768]{1,0:T(8,128)S(1)}) custom-call(s32[2]{0:T(128)S(1)} %pad_add_fusion.slot_ref.refs_0_, bf16[128,2048]{1,0:T(8,128)(2,1)S(1)} %collective-permute-done.9.refs_1_, bf16[128,2048]{1,0:T(8,128)(2,1)S(1)} %collective-permute-done.10.refs_2_, ...), custom_call_target="tpu_custom_call" | custom-call | flops 1140850688 | bytes 10027016 | tf_op jit(solution)/shard_map/pallas_call | solution.py:269
  88.4 4.3 %shard_map.127 = (bf16[256,128]{1,0:T(8,128)(2,1)S(1)}, f32[256,768]{1,0:T(8,128)S(1)}, f32[256,768]{1,0:T(8,128)S(1)}, bf16[128,2048]{1,0:T(8,128)(2,1)S(1)}, bf16[128,2048]{1,0:T(8,128)(2,1)S(1)}) custom-call(s32[2]{0:T(128)S(1)} %pad_add_fusion.slot_ref.refs_0_, bf16[128,2176]{1,0:T(8,128)(2,1)S(1)} %collective-permute-done.7.mine_ref.refs_3_, ...), custom_call_target="tpu_custom_call" | custom-call | flops 2550136832 | bytes 13959176 | tf_op jit(solution)/shard_map/pallas_call | solution.py:269
  92.7 3.6 %shard_map.129 = (bf16[1408,128]{1,0:T(8,128)(2,1)S(1)}, bf16[1408,128]{1,0:T(8,128)(2,1)S(1)}) custom-call(s32[2]{0:T(128)S(1)} %pad_add_fusion.slot_ref.refs_0_, bf16[128,2048]{1,0:T(8,128)(2,1)S(1)} %collective-permute-done.14.refs_1_, bf16[128,2048]{1,0:T(8,128)(2,1)S(1)} %collective-permute-done.15.refs_2_, ...), custom_call_target="tpu_custom_call" | custom-call | flops 1140850688 | bytes 9306120 | tf_op jit(solution)/shard_map/pallas_call | solution.py:269
  97.2 1.6 %collective-permute-start.20 = (bf16[1408,128]{1,0:T(8,128)(2,1)S(1)}, bf16[1408,128]{1,0:T(8,128)(2,1)S(1)}, u32[]{:S(2)}, u32[]{:S(2)}) collective-permute-start(bf16[1408,128]{1,0:T(8,128)(2,1)S(1)} %get-tuple-element.145.refs_0_), channel_id=1, source_target_pairs={{0,8},{8,0},{16,24},{24,16},{1,9},{9,1},{17,25},{25,17},{2,10},{10... | collective-permute-start | bytes 1081352 | tf_op jit(solution)/shard_map/ppermute | solution.py:448
  100.6 7.4 %collective-permute-done.20.refs_2_ = bf16[1408,128]{1,0:T(8,128)(2,1)S(1)} collective-permute-done((bf16[1408,128]{1,0:T(8,128)(2,1)S(1)}, bf16[1408,128]{1,0:T(8,128)(2,1)S(1)}, u32[]{:S(2)}, u32[]{:S(2)}) %collective-permute-start.20) | collective-permute-done | bytes 360480 | tf_op jit(solution)/shard_map/ppermute | solution.py:448
  109.2 4.0 %collective-permute-done.17 = bf16[128,2048]{1,0:T(8,128)(2,1)S(1)} collective-permute-done((bf16[128,2048]{1,0:T(8,128)(2,1)S(1)}, bf16[128,2048]{1,0:T(8,128)(2,1)S(1)}, u32[]{:S(2)}, u32[]{:S(2)}) %collective-permute-start.17) | collective-permute-done | bytes 524320 | tf_op jit(solution)/shard_map/ppermute | solution.py:429
  113.5 2.3 %shard_map.130 = (bf16[1408,128]{1,0:T(8,128)(2,1)}, bf16[1408,128]{1,0:T(8,128)(2,1)}) custom-call(bf16[1408,128]{1,0:T(8,128)(2,1)} %copy-done.14, bf16[1408,128]{1,0:T(8,128)(2,1)} %copy-done.15, bf16[1408,128]{1,0:T(8,128)(2,1)} %copy-done.16, bf16[1408,128]{1,0:T(8,128)(2,1)} %copy-done.17), custom_call_target="tpu_custom_call" | custom-call | tf_op jit(solution)/shard_map/pallas_call | solution.py:394
  118.8 7.2 %collective-permute-done.23.other_x = bf16[1408,128]{1,0:T(8,128)(2,1)S(1)} collective-permute-done((bf16[1408,128]{1,0:T(8,128)(2,1)}, bf16[1408,128]{1,0:T(8,128)(2,1)S(1)}, u32[]{:S(2)}, u32[]{:S(2)}) %collective-permute-start.23) | collective-permute-done | bytes 360480 | tf_op jit(solution)/shard_map/ppermute | solution.py:448
  127.9 2.5 %shard_map.131 = (f32[2048,128]{1,0:T(8,128)}, f32[128,768]{1,0:T(8,128)}) custom-call(bf16[1408,128]{1,0:T(8,128)(2,1)} %get-tuple-element.149.one_x, bf16[1408,128]{1,0:T(8,128)(2,1)} %get-tuple-element.150.one_y, bf16[1408,128]{1,0:T(8,128)(2,1)} %copy-done.18, bf16[1408,128]{1,0:T(8,128)(2,1)} %copy-done.19), custom_call_target="tpu_custom_call" | custom-call | tf_op jit(solution)/shard_map/pallas_call | solution.py:415
  (85 shorter events, 18.6 us)
Async XLA Ops:
  2.8 4.9 %collective-permute-start.2 = (bf16[128,2176]{1,0:T(8,128)(2,1)}, bf16[128,2176]{1,0:T(8,128)(2,1)S(1)}, u32[]{:S(2)}, u32[]{:S(2)}) collective-permute-start(bf16[128,2176]{1,0:T(8,128)(2,1)} %shard_map.121.mine_ref.refs_3_), channel_id=1, source_target_pairs={{0,1},{1,0},{2,3},{3,2},{4,5},{5,4},{6,7},{7,6},{8,9},{9,8},{10,11... | collective-permute-start | bytes 1671176 | tf_op jit(solution)/shard_map/ppermute | solution.py:429
  3.3 18.4 %collective-permute-start = (bf16[128,2176]{1,0:T(8,128)(2,1)}, bf16[128,2176]{1,0:T(8,128)(2,1)}, u32[]{:S(2)}, u32[]{:S(2)}) collective-permute-start(bf16[128,2176]{1,0:T(8,128)(2,1)} %shard_map.121.mine_ref.refs_3_), channel_id=1, source_target_pairs={{0,2},{1,3},{2,4},{3,5},{4,6},{5,7},{6,0},{7,1},{8,10},{9,11},{10,... | collective-permute-start | bytes 1671176 | tf_op jit(solution)/shard_map/ppermute | solution.py:429
  5.9 15.8 %collective-permute-start.1 = (bf16[128,2048]{1,0:T(8,128)(2,1)}, bf16[128,2048]{1,0:T(8,128)(2,1)}, u32[]{:S(2)}, u32[]{:S(2)}) collective-permute-start(bf16[128,2048]{1,0:T(8,128)(2,1)} %refs_1_), channel_id=1, source_target_pairs={{0,1},{1,0},{2,3},{3,2},{4,5},{5,4},{6,7},{7,6},{8,9},{9,8},{10,11... | collective-permute-start | bytes 1572872 | tf_op jit(solution)/shard_map/ppermute | solution.py:429
  6.1 26.6 %collective-permute-start.4 = (bf16[128,2048]{1,0:T(8,128)(2,1)}, bf16[128,2048]{1,0:T(8,128)(2,1)}, u32[]{:S(2)}, u32[]{:S(2)}) collective-permute-start(bf16[128,2048]{1,0:T(8,128)(2,1)} %refs_1_), channel_id=1, source_target_pairs={{0,2},{1,3},{2,4},{3,5},{4,6},{5,7},{6,0},{7,1},{8,10},{9,11},{10,... | collective-permute-start | bytes 1572872 | tf_op jit(solution)/shard_map/ppermute | solution.py:429
  21.7 15.3 %collective-permute-start.6 = (bf16[128,2176]{1,0:T(8,128)(2,1)}, bf16[128,2176]{1,0:T(8,128)(2,1)S(1)}, u32[]{:S(2)}, u32[]{:S(2)}) collective-permute-start(bf16[128,2176]{1,0:T(8,128)(2,1)} %collective-permute-done.mine_ref.refs_3_), channel_id=1, source_target_pairs={{0,1},{1,0},{2,3},{3,2},{4,5},{5,4},{6,7},{7,6},{8,9},{9,8},{10,11... | collective-permute-start | bytes 1671176 | tf_op jit(solution)/shard_map/ppermute | solution.py:429
  32.7 4.2 %collective-permute-start.5 = (bf16[128,2048]{1,0:T(8,128)(2,1)}, bf16[128,2048]{1,0:T(8,128)(2,1)S(1)}, u32[]{:S(2)}, u32[]{:S(2)}) collective-permute-start(bf16[128,2048]{1,0:T(8,128)(2,1)} %collective-permute-done.4.refs_1_), channel_id=1, source_target_pairs={{0,1},{1,0},{2,3},{3,2},{4,5},{5,4},{6,7},{7,6},{8,9},{9,8},{10,11... | collective-permute-start | bytes 1572872 | tf_op jit(solution)/shard_map/ppermute | solution.py:429
  32.7 17.4 %collective-permute-start.3 = (bf16[128,2176]{1,0:T(8,128)(2,1)}, bf16[128,2176]{1,0:T(8,128)(2,1)S(1)}, u32[]{:S(2)}, u32[]{:S(2)}) collective-permute-start(bf16[128,2176]{1,0:T(8,128)(2,1)} %collective-permute-done.mine_ref.refs_3_), channel_id=1, source_target_pairs={{0,2},{1,3},{2,4},{3,5},{4,6},{5,7},{6,0},{7,1},{8,10},{9,11},{10,... | collective-permute-start | bytes 1671176 | tf_op jit(solution)/shard_map/ppermute | solution.py:429
  37.0 24.4 %collective-permute-start.9 = (bf16[128,2048]{1,0:T(8,128)(2,1)}, bf16[128,2048]{1,0:T(8,128)(2,1)S(1)}, u32[]{:S(2)}, u32[]{:S(2)}) collective-permute-start(bf16[128,2048]{1,0:T(8,128)(2,1)} %collective-permute-done.4.refs_1_), channel_id=1, source_target_pairs={{0,2},{1,3},{2,4},{3,5},{4,6},{5,7},{6,0},{7,1},{8,10},{9,11},{10,... | collective-permute-start | bytes 1572872 | tf_op jit(solution)/shard_map/ppermute | solution.py:429
  50.2 15.5 %collective-permute-start.8 = (bf16[128,2048]{1,0:T(8,128)(2,1)S(1)}, bf16[128,2048]{1,0:T(8,128)(2,1)S(1)}, u32[]{:S(2)}, u32[]{:S(2)}) collective-permute-start(bf16[128,2048]{1,0:T(8,128)(2,1)S(1)} %get-tuple-element.94), channel_id=1, source_target_pairs={{0,1},{1,0},{2,3},{3,2},{4,5},{5,4},{6,7},{7,6},{8,9},{9,8},{10,11... | collective-permute-start | bytes 1572872 | tf_op jit(solution)/shard_map/ppermute | solution.py:429
  50.2 15.7 %collective-permute-start.11 = (bf16[128,2176]{1,0:T(8,128)(2,1)S(1)}, bf16[128,2176]{1,0:T(8,128)(2,1)S(1)}, u32[]{:S(2)}, u32[]{:S(2)}) collective-permute-start(bf16[128,2176]{1,0:T(8,128)(2,1)S(1)} %collective-permute-done.3.mine_ref.refs_3_), channel_id=1, source_target_pairs={{0,1},{1,0},{2,3},{3,2},{4,5},{5,4},{6,7},{7,6},{8,9},{9,8},{10,11... | collective-permute-start | bytes 1671176 | tf_op jit(solution)/shard_map/ppermute | solution.py:429
  50.7 22.7 %collective-permute-start.7 = (bf16[128,2176]{1,0:T(8,128)(2,1)S(1)}, bf16[128,2176]{1,0:T(8,128)(2,1)S(1)}, u32[]{:S(2)}, u32[]{:S(2)}) collective-permute-start(bf16[128,2176]{1,0:T(8,128)(2,1)S(1)} %collective-permute-done.3.mine_ref.refs_3_), channel_id=1, source_target_pairs={{0,2},{1,3},{2,4},{3,5},{4,6},{5,7},{6,0},{7,1},{8,10},{9,11},{10,... | collective-permute-start | bytes 1671176 | tf_op jit(solution)/shard_map/ppermute | solution.py:429
  61.4 4.5 %collective-permute-start.10 = (bf16[128,2048]{1,0:T(8,128)(2,1)S(1)}, bf16[128,2048]{1,0:T(8,128)(2,1)S(1)}, u32[]{:S(2)}, u32[]{:S(2)}) collective-permute-start(bf16[128,2048]{1,0:T(8,128)(2,1)S(1)} %collective-permute-done.9.refs_1_), channel_id=1, source_target_pairs={{0,1},{1,0},{2,3},{3,2},{4,5},{5,4},{6,7},{7,6},{8,9},{9,8},{10,11... | collective-permute-start | bytes 1572872 | tf_op jit(solution)/shard_map/ppermute | solution.py:429
  65.9 18.7 %collective-permute-start.14 = (bf16[128,2048]{1,0:T(8,128)(2,1)S(1)}, bf16[128,2048]{1,0:T(8,128)(2,1)S(1)}, u32[]{:S(2)}, u32[]{:S(2)}) collective-permute-start(bf16[128,2048]{1,0:T(8,128)(2,1)S(1)} %collective-permute-done.9.refs_1_), channel_id=1, source_target_pairs={{0,2},{1,3},{2,4},{3,5},{4,6},{5,7},{6,0},{7,1},{8,10},{9,11},{10,... | collective-permute-start | bytes 1572872 | tf_op jit(solution)/shard_map/ppermute | solution.py:429
  73.3 14.8 %collective-permute-start.13 = (bf16[128,2048]{1,0:T(8,128)(2,1)S(1)}, bf16[128,2048]{1,0:T(8,128)(2,1)S(1)}, u32[]{:S(2)}, u32[]{:S(2)}) collective-permute-start(bf16[128,2048]{1,0:T(8,128)(2,1)S(1)} %get-tuple-element.112), channel_id=1, source_target_pairs={{0,1},{1,0},{2,3},{3,2},{4,5},{5,4},{6,7},{7,6},{8,9},{9,8},{10,11... | collective-permute-start | bytes 1572872 | tf_op jit(solution)/shard_map/ppermute | solution.py:429
  73.4 15.0 %collective-permute-start.16 = (bf16[128,2176]{1,0:T(8,128)(2,1)S(1)}, bf16[128,2176]{1,0:T(8,128)(2,1)S(1)}, u32[]{:S(2)}, u32[]{:S(2)}) collective-permute-start(bf16[128,2176]{1,0:T(8,128)(2,1)S(1)} %collective-permute-done.7.mine_ref.refs_3_), channel_id=1, source_target_pairs={{0,1},{1,0},{2,3},{3,2},{4,5},{5,4},{6,7},{7,6},{8,9},{9,8},{10,11... | collective-permute-start | bytes 1671176 | tf_op jit(solution)/shard_map/ppermute | solution.py:429
  73.9 22.5 %collective-permute-start.12 = (bf16[128,2048]{1,0:T(8,128)(2,1)S(1)}, bf16[128,2048]{1,0:T(8,128)(2,1)S(1)}, u32[]{:S(2)}, u32[]{:S(2)}) collective-permute-start(bf16[128,2048]{1,0:T(8,128)(2,1)S(1)} %add_convert_fusion.6), channel_id=1, source_target_pairs={{0,2},{1,3},{2,4},{3,5},{4,6},{5,7},{6,0},{7,1},{8,10},{9,11},{10,... | collective-permute-start | bytes 1572872 | tf_op jit(solution)/shard_map/ppermute | solution.py:429
  84.6 3.8 %collective-permute-start.15 = (bf16[128,2048]{1,0:T(8,128)(2,1)S(1)}, bf16[128,2048]{1,0:T(8,128)(2,1)S(1)}, u32[]{:S(2)}, u32[]{:S(2)}) collective-permute-start(bf16[128,2048]{1,0:T(8,128)(2,1)S(1)} %collective-permute-done.14.refs_1_), channel_id=1, source_target_pairs={{0,1},{1,0},{2,3},{3,2},{4,5},{5,4},{6,7},{7,6},{8,9},{9,8},{10,11... | collective-permute-start | bytes 1572872 | tf_op jit(solution)/shard_map/ppermute | solution.py:429
  96.3 3.9 %collective-permute-start.19 = (bf16[128,2048]{1,0:T(8,128)(2,1)S(1)}, bf16[128,2048]{1,0:T(8,128)(2,1)S(1)}, u32[]{:S(2)}, u32[]{:S(2)}) collective-permute-start(bf16[128,2048]{1,0:T(8,128)(2,1)S(1)} %get-tuple-element.139), channel_id=1, source_target_pairs={{0,1},{1,0},{2,3},{3,2},{4,5},{5,4},{6,7},{7,6},{8,9},{9,8},{10,11... | collective-permute-start | bytes 1572872 | tf_op jit(solution)/shard_map/ppermute | solution.py:429
  97.1 16.1 %collective-permute-start.17 = (bf16[128,2048]{1,0:T(8,128)(2,1)S(1)}, bf16[128,2048]{1,0:T(8,128)(2,1)S(1)}, u32[]{:S(2)}, u32[]{:S(2)}) collective-permute-start(bf16[128,2048]{1,0:T(8,128)(2,1)S(1)} %add_convert_fusion.4), channel_id=1, source_target_pairs={{0,2},{1,3},{2,4},{3,5},{4,6},{5,7},{6,0},{7,1},{8,10},{9,11},{10,... | collective-permute-start | bytes 1572872 | tf_op jit(solution)/shard_map/ppermute | solution.py:429
  97.2 10.8 %collective-permute-start.20 = (bf16[1408,128]{1,0:T(8,128)(2,1)S(1)}, bf16[1408,128]{1,0:T(8,128)(2,1)S(1)}, u32[]{:S(2)}, u32[]{:S(2)}) collective-permute-start(bf16[1408,128]{1,0:T(8,128)(2,1)S(1)} %get-tuple-element.145.refs_0_), channel_id=1, source_target_pairs={{0,8},{8,0},{16,24},{24,16},{1,9},{9,1},{17,25},{25,17},{2,10},{10... | collective-permute-start | bytes 1081352 | tf_op jit(solution)/shard_map/ppermute | solution.py:448
  98.7 10.5 %collective-permute-start.21 = (bf16[1408,128]{1,0:T(8,128)(2,1)S(1)}, bf16[1408,128]{1,0:T(8,128)(2,1)S(1)}, u32[]{:S(2)}, u32[]{:S(2)}) collective-permute-start(bf16[1408,128]{1,0:T(8,128)(2,1)S(1)} %get-tuple-element.146.refs_1_), channel_id=1, source_target_pairs={{0,16},{8,24},{16,0},{24,8},{1,17},{9,25},{17,1},{25,9},{2,18},{10... | collective-permute-start | bytes 1081352 | tf_op jit(solution)/shard_map/ppermute | solution.py:448
  113.4 17.0 %collective-permute-start.22 = (bf16[128,2048]{1,0:T(8,128)(2,1)S(1)}, bf16[128,2048]{1,0:T(8,128)(2,1)S(1)}, u32[]{:S(2)}, u32[]{:S(2)}) collective-permute-start(bf16[128,2048]{1,0:T(8,128)(2,1)S(1)} %add_convert_fusion.1), channel_id=1, source_target_pairs={{0,2},{1,3},{2,4},{3,5},{4,6},{5,7},{6,0},{7,1},{8,10},{9,11},{10,... | collective-permute-start | bytes 1572872 | tf_op jit(solution)/shard_map/ppermute | solution.py:429
  115.7 10.2 %collective-permute-start.23 = (bf16[1408,128]{1,0:T(8,128)(2,1)}, bf16[1408,128]{1,0:T(8,128)(2,1)S(1)}, u32[]{:S(2)}, u32[]{:S(2)}) collective-permute-start(bf16[1408,128]{1,0:T(8,128)(2,1)} %get-tuple-element.149.one_x), channel_id=1, source_target_pairs={{0,16},{8,24},{16,0},{24,8},{1,17},{9,25},{17,1},{25,9},{2,18},{10... | collective-permute-start | bytes 1081352 | tf_op jit(solution)/shard_map/ppermute | solution.py:448
  117.3 9.9 %collective-permute-start.24 = (bf16[1408,128]{1,0:T(8,128)(2,1)}, bf16[1408,128]{1,0:T(8,128)(2,1)S(1)}, u32[]{:S(2)}, u32[]{:S(2)}) collective-permute-start(bf16[1408,128]{1,0:T(8,128)(2,1)} %get-tuple-element.150.one_y), channel_id=1, source_target_pairs={{0,8},{8,0},{16,24},{24,16},{1,9},{9,1},{17,25},{25,17},{2,10},{10... | collective-permute-start | bytes 1081352 | tf_op jit(solution)/shard_map/ppermute | solution.py:448
  (21 other events, 167.9 us)
